TPU v7x, 32 devices: a whole 2x2x4 slice. The times are simulated.
32 devices in a mesh: lon: 8 (over y, x, core), lat: 4 (over z).
Axes of the slice: x: 2, y: 2, z: 4, core: 2. Of those that a mesh axis runs over, the one named last changes fastest.
Arguments:
- tracers: float32 [12, 256, 4096], P(None, 'lat', 'lon'), may hold values from -6 to 6
- lon_shift: int32 [2, 12, 256], P(None, None, 'lat'), may hold values from -127 to 127, as said below
- lon_frac: float32 [2, 12, 256], P(None, None, 'lat'), may hold values from 0 to 1
- lat_shift: int32 [2, 12, 256], P(None, None, 'lat'), may hold values from -1 to 1
- lat_frac: float32 [2, 12, 256], P(None, None, 'lat'), may hold values from 0 to 1
- remap_frac: float32 [2, 12, 256], P(None, None, 'lat'), may hold values from 0 to 1
- diffusivity: float32 [12, 256], P(None, 'lat'), may hold values from 0.1 to 3
Outputs:
- advected: float32 [12, 256, 4096], P(None, 'lat', 'lon')
Inputs may be any that keep to these rules, and one draw needn't show every extreme that they name: In latitude row j, with e = |2 * j - 255|, |lon_shift| is at most min(127, 64 * 256 // (257 - e)).
All inputs are finite; a program needn't handle non-finite values.
Results may differ from a plain program's by a relative error of at most 0.00002.
Values sent between devices are 32-bit elements; how exact they have to be, the bound alone decides.
No kernel may reach another device: no remote copies, remote signals or barrier semaphores. Data moves between devices by JAX's collectives and lax.ppermute only.
A program may use at most 64 MiB of HBM per device.

v0:
```python
import jax
import jax.numpy as jnp
from jax import lax
from jax.sharding import PartitionSpec as P

NTR = 8
STEPS = 2


def from_behind(x, axis, by):
    peers = lax.axis_size(axis)
    return lax.ppermute(x, axis, [(i, (i + by) % peers) for i in range(peers)])


def with_halo(block, sides, width, periodic):
    for axis, dim in sides:
        count = lax.axis_size(axis)
        forward = [(i, i + 1) for i in range(count - 1)]
        if periodic:
            forward.append((count - 1, 0))
        backward = [(target, source) for source, target in forward]
        low = lax.ppermute(
            lax.slice_in_dim(block, block.shape[dim] - width, None, axis=dim), axis, forward
        )
        high = lax.ppermute(lax.slice_in_dim(block, 0, width, axis=dim), axis, backward)
        block = jnp.concatenate([low, block, high], axis=dim)
    return block


def cubic_weights(fraction):
    w_zero = -fraction * (fraction - 1.0) * (fraction - 2.0) / 6.0
    w_one = (fraction + 1.0) * (fraction - 1.0) * (fraction - 2.0) / 2.0
    w_two = -(fraction + 1.0) * fraction * (fraction - 2.0) / 2.0
    w_three = (fraction + 1.0) * fraction * (fraction - 1.0) / 6.0
    return (w_zero, w_one, w_two, w_three)


def lat_step(padded, offset, fraction, row_count):
    weights = cubic_weights(fraction)
    summed = None
    for place_index in range(6):
        row_delta = place_index - 2
        coeff = jnp.zeros_like(fraction)
        for tap_index in range(4):
            coeff = coeff + jnp.where(offset == tap_index - 1 - row_delta, weights[tap_index], 0.0)
        addend = coeff[:, :, None] * padded[:, 1 + place_index : 1 + place_index + row_count, :]
        summed = addend if summed is None else summed + addend
    return summed


def lon_step(wrapped, fraction, tracer_count):
    weights = cubic_weights(fraction)
    width_cols = wrapped.shape[2] - 4 * tracer_count
    summed = None
    for tap_index in range(4):
        offset_cols = (1 + tap_index) * tracer_count
        addend = (
            weights[tap_index][:, :, None] * wrapped[:, :, offset_cols : offset_cols + width_cols]
        )
        summed = addend if summed is None else summed + addend
    return summed


def remap(tracer_field, fraction):
    level_above = jnp.concatenate([tracer_field[1:], tracer_field[-1:]], axis=0)
    return (1.0 - fraction)[:, :, None] * tracer_field + fraction[:, :, None] * level_above


def diffuse(tracer_field, kappa):
    levels = tracer_field.shape[0]
    face_kappa = 0.5 * (kappa[:-1] + kappa[1:])
    zero_face = jnp.zeros_like(kappa[:1])
    face_below = jnp.concatenate([zero_face, face_kappa], axis=0)
    face_above = jnp.concatenate([face_kappa, zero_face], axis=0)
    ratio_prev = jnp.zeros_like(kappa[0])
    solved_prev = jnp.zeros_like(tracer_field[0])
    ratios = []
    solveds = []
    for level_index in range(levels):
        below = face_below[level_index]
        above = face_above[level_index]
        pivot_value = 1.0 + below + above + below * ratio_prev
        ratio_now = -above / pivot_value
        solved_now = (tracer_field[level_index] + below[:, None] * solved_prev) / pivot_value[
            :, None
        ]
        ratios.append(ratio_now)
        solveds.append(solved_now)
        ratio_prev = ratio_now
        solved_prev = solved_now
    results = [None] * levels
    results[levels - 1] = solveds[levels - 1]
    for level_index in range(levels - 2, -1, -1):
        results[level_index] = (
            solveds[level_index] - ratios[level_index][:, None] * results[level_index + 1]
        )
    return jnp.stack(results, axis=0)


def bit_mask(amount, position):
    return (amount // 2**position % 2 == 1)[:, :, None]


def move_rows(tracer_field, shift_cells):
    tracer_count = NTR
    width_cols = tracer_field.shape[2]
    cell_count = width_cols // tracer_count
    devices = lax.axis_size("lon")
    low_bits = cell_count.bit_length() - 1
    ahead_amount = jnp.remainder(shift_cells, cell_count * devices)
    high_bits = devices.bit_length() - 1
    current = tracer_field
    for position in range(low_bits):
        step_cols = 2**position * tracer_count
        from_west = from_behind(current[:, :, width_cols - step_cols :], "lon", 1)
        forward = jnp.concatenate([from_west, current[:, :, : width_cols - step_cols]], axis=2)
        current = jnp.where(bit_mask(ahead_amount, position), forward, current)
    for position in range(high_bits):
        hops = 2**position
        digit = low_bits + position
        ahead_block = from_behind(current, "lon", hops)
        current = jnp.where(bit_mask(ahead_amount, digit), ahead_block, current)
    return current


def per_device(tracers, lon_shift, lon_frac, lat_shift, lat_frac, remap_frac, diffusivity):
    tracer_field = tracers
    row_count = tracer_field.shape[1]
    for time_step in range(STEPS):
        padded = with_halo(tracer_field, (("lat", 1),), 3, False)
        tracer_field = lat_step(padded, lat_shift[time_step], lat_frac[time_step], row_count)
        shifted = move_rows(tracer_field, lon_shift[time_step])
        wrapped = with_halo(shifted, (("lon", 2),), 2 * NTR, True)
        tracer_field = lon_step(wrapped, lon_frac[time_step], NTR)
        tracer_field = remap(tracer_field, remap_frac[time_step])
        tracer_field = diffuse(tracer_field, diffusivity)
    return tracer_field


def solution(mesh):
    in_specs = (
        P(None, "lat", "lon"),
        P(None, None, "lat"),
        P(None, None, "lat"),
        P(None, None, "lat"),
        P(None, None, "lat"),
        P(None, None, "lat"),
        P(None, "lat"),
    )
    out_specs = P(None, "lat", "lon")
    return jax.shard_map(
        per_device, mesh=mesh, in_specs=in_specs, out_specs=out_specs, check_vma=False
    )
```

profile of v0, /device:TPU:9, one launch (start us, length us, event | category | flops | bytes accessed | tf_op | source)
XLA Modules:
  0.0 351.6 jit_solution(13389767223782837860)
XLA Ops:
  1.1 1.9 collective-permute-start.1
  3.0 3.4 collective-permute-start
  8.8 1.7 constant_dynamic-update-slice_fusion.1
  10.7 1.4 fusion.17
  12.2 2.4 collective-permute-start.2
  14.7 4.6 %collective-permute-done.2 = f32[12,64,8]{2,1,0:T(8,128)S(1)} collective-permute-done((f32[12,64,8]{2,1,0:T(8,128)S(1)}, f32[12,64,8]{2,1,0:T(8,128)S(1)}, u32[]{:S(2)}, u32[]{:S(2)}) %collective-permute-start.2) | collective-permute-done | bytes 24608 | tf_op jit(solution)/shard_map/ppermute | solution.py:12
  20.1 2.5 collective-permute-start.3
  22.7 4.7 %collective-permute-done.3 = f32[12,64,16]{2,1,0:T(8,128)S(1)} collective-permute-done((f32[12,64,16]{2,1,0:T(8,128)S(1)}, f32[12,64,16]{2,1,0:T(8,128)S(1)}, u32[]{:S(2)}, u32[]{:S(2)}) %collective-permute-start.3) | collective-permute-done | bytes 49184 | tf_op jit(solution)/shard_map/ppermute | solution.py:12
  28.2 2.5 collective-permute-start.4
  30.7 4.7 %collective-permute-done.4 = f32[12,64,32]{2,1,0:T(8,128)S(1)} collective-permute-done((f32[12,64,32]{2,1,0:T(8,128)S(1)}, f32[12,64,32]{2,1,0:T(8,128)S(1)}, u32[]{:S(2)}, u32[]{:S(2)}) %collective-permute-start.4) | collective-permute-done | bytes 98336 | tf_op jit(solution)/shard_map/ppermute | solution.py:12
  36.3 2.5 collective-permute-start.5
  38.8 4.7 %collective-permute-done.5 = f32[12,64,64]{2,1,0:T(8,128)S(1)} collective-permute-done((f32[12,64,64]{2,1,0:T(8,128)S(1)}, f32[12,64,64]{2,1,0:T(8,128)S(1)}, u32[]{:S(2)}, u32[]{:S(2)}) %collective-permute-start.5) | collective-permute-done | bytes 196640 | tf_op jit(solution)/shard_map/ppermute | solution.py:12
  44.2 2.5 collective-permute-start.6
  46.9 4.6 %collective-permute-done.6 = f32[12,64,128]{2,1,0:T(8,128)S(1)} collective-permute-done((f32[12,64,128]{2,1,0:T(8,128)S(1)}, f32[12,64,128]{2,1,0:T(8,128)S(1)}, u32[]{:S(2)}, u32[]{:S(2)}) %collective-permute-start.6) | collective-permute-done | bytes 393248 | tf_op jit(solution)/shard_map/ppermute | solution.py:12
  51.9 2.5 collective-permute-start.7
  54.4 8.9 %collective-permute-done.7 = f32[12,64,256]{2,1,0:T(8,128)S(1)} collective-permute-done((f32[12,64,256]{2,1,0:T(8,128)S(1)}, f32[12,64,256]{2,1,0:T(8,128)S(1)}, u32[]{:S(2)}, u32[]{:S(2)}) %collective-permute-start.7) | collective-permute-done | bytes 786464 | tf_op jit(solution)/shard_map/ppermute | solution.py:12
  63.6 2.5 collective-permute-start.8
  66.1 17.4 %collective-permute-done.8 = f32[12,64,512]{2,1,0:T(8,128)S(1)} collective-permute-done((f32[12,64,512]{2,1,0:T(8,128)S(1)}, f32[12,64,512]{2,1,0:T(8,128)S(1)}, u32[]{:S(2)}, u32[]{:S(2)}) %collective-permute-start.8) | collective-permute-done | bytes 1572896 | tf_op jit(solution)/shard_map/ppermute | solution.py:12
  83.7 6.7 %collective-permute-start.9 = (f32[12,64,512]{2,1,0:T(8,128)S(1)}, f32[12,64,512]{2,1,0:T(8,128)S(1)}, u32[]{:S(2)}, u32[]{:S(2)}) collective-permute-start(f32[12,64,512]{2,1,0:T(8,128)S(1)} %broadcast_select_fusion), channel_id=1, source_target_pairs={{0,8},{4,12},{8,16},{12,20},{16,24},{20,28},{24,0},{28,4},{1,9},{5... | collective-permute-start | bytes 4718600 | tf_op jit(solution)/shard_map/ppermute | solution.py:12
  90.3 32.9 %collective-permute-done.9 = f32[12,64,512]{2,1,0:T(8,128)S(1)} collective-permute-done((f32[12,64,512]{2,1,0:T(8,128)S(1)}, f32[12,64,512]{2,1,0:T(8,128)S(1)}, u32[]{:S(2)}, u32[]{:S(2)}) %collective-permute-start.9) | collective-permute-done | bytes 1572896 | tf_op jit(solution)/shard_map/ppermute | solution.py:12
  124.2 32.9 %collective-permute-done.10 = f32[12,64,512]{2,1,0:T(8,128)S(1)} collective-permute-done((f32[12,64,512]{2,1,0:T(8,128)S(1)}, f32[12,64,512]{2,1,0:T(8,128)S(1)}, u32[]{:S(2)}, u32[]{:S(2)}) %collective-permute-start.10) | collective-permute-done | bytes 1572896 | tf_op jit(solution)/shard_map/ppermute | solution.py:12
  157.5 5.4 %collective-permute-start.11 = (f32[12,64,16]{2,1,0:T(8,128)S(1)}, f32[12,64,16]{2,1,0:T(8,128)S(1)}, u32[]{:S(2)}, u32[]{:S(2)}) collective-permute-start(f32[12,64,16]{2,1,0:T(8,128)S(1)} %get-tuple-element.55), channel_id=1, source_target_pairs={{0,4},{4,8},{8,12},{12,16},{16,20},{20,24},{24,28},{28,0},{1,5},{5... | collective-permute-start | bytes 147464 | tf_op jit(solution)/shard_map/ppermute | solution.py:22
  162.9 8.2 %collective-permute-done.11 = f32[12,64,16]{2,1,0:T(8,128)S(1)} collective-permute-done((f32[12,64,16]{2,1,0:T(8,128)S(1)}, f32[12,64,16]{2,1,0:T(8,128)S(1)}, u32[]{:S(2)}, u32[]{:S(2)}) %collective-permute-start.11) | collective-permute-done | bytes 49184 | tf_op jit(solution)/shard_map/ppermute | solution.py:22
  171.5 2.5 fusion.25
  175.6 3.2 collective-permute-start.13
  178.8 2.1 collective-permute-start.14
  180.9 3.2 collective-permute-done.14
  184.1 1.5 fusion.3
  185.8 3.7 %collective-permute-start.15 = (f32[12,64,8]{2,1,0:T(8,128)S(1)}, f32[12,64,8]{2,1,0:T(8,128)S(1)}, u32[]{:S(2)}, u32[]{:S(2)}) collective-permute-start(f32[12,64,8]{2,1,0:T(8,128)S(1)} %slice.501), channel_id=1, source_target_pairs={{0,4},{4,8},{8,12},{12,16},{16,20},{20,24},{24,28},{28,0},{1,5},{5... | collective-permute-start | bytes 73736 | tf_op jit(solution)/shard_map/ppermute | solution.py:12
  189.6 4.6 %collective-permute-done.15 = f32[12,64,8]{2,1,0:T(8,128)S(1)} collective-permute-done((f32[12,64,8]{2,1,0:T(8,128)S(1)}, f32[12,64,8]{2,1,0:T(8,128)S(1)}, u32[]{:S(2)}, u32[]{:S(2)}) %collective-permute-start.15) | collective-permute-done | bytes 24608 | tf_op jit(solution)/shard_map/ppermute | solution.py:12
  195.0 2.5 collective-permute-start.16
  197.6 4.7 %collective-permute-done.16 = f32[12,64,16]{2,1,0:T(8,128)S(1)} collective-permute-done((f32[12,64,16]{2,1,0:T(8,128)S(1)}, f32[12,64,16]{2,1,0:T(8,128)S(1)}, u32[]{:S(2)}, u32[]{:S(2)}) %collective-permute-start.16) | collective-permute-done | bytes 49184 | tf_op jit(solution)/shard_map/ppermute | solution.py:12
  203.1 2.7 collective-permute-start.17
  205.8 4.7 %collective-permute-done.17 = f32[12,64,32]{2,1,0:T(8,128)S(1)} collective-permute-done((f32[12,64,32]{2,1,0:T(8,128)S(1)}, f32[12,64,32]{2,1,0:T(8,128)S(1)}, u32[]{:S(2)}, u32[]{:S(2)}) %collective-permute-start.17) | collective-permute-done | bytes 98336 | tf_op jit(solution)/shard_map/ppermute | solution.py:12
  211.3 2.5 collective-permute-start.18
  213.9 4.7 %collective-permute-done.18 = f32[12,64,64]{2,1,0:T(8,128)S(1)} collective-permute-done((f32[12,64,64]{2,1,0:T(8,128)S(1)}, f32[12,64,64]{2,1,0:T(8,128)S(1)}, u32[]{:S(2)}, u32[]{:S(2)}) %collective-permute-start.18) | collective-permute-done | bytes 196640 | tf_op jit(solution)/shard_map/ppermute | solution.py:12
  219.3 2.5 collective-permute-start.19
  221.9 4.6 %collective-permute-done.19 = f32[12,64,128]{2,1,0:T(8,128)S(1)} collective-permute-done((f32[12,64,128]{2,1,0:T(8,128)S(1)}, f32[12,64,128]{2,1,0:T(8,128)S(1)}, u32[]{:S(2)}, u32[]{:S(2)}) %collective-permute-start.19) | collective-permute-done | bytes 393248 | tf_op jit(solution)/shard_map/ppermute | solution.py:12
  227.0 2.5 collective-permute-start.20
  229.5 8.9 %collective-permute-done.20 = f32[12,64,256]{2,1,0:T(8,128)S(1)} collective-permute-done((f32[12,64,256]{2,1,0:T(8,128)S(1)}, f32[12,64,256]{2,1,0:T(8,128)S(1)}, u32[]{:S(2)}, u32[]{:S(2)}) %collective-permute-start.20) | collective-permute-done | bytes 786464 | tf_op jit(solution)/shard_map/ppermute | solution.py:12
  238.6 2.5 collective-permute-start.21
  241.2 17.4 %collective-permute-done.21 = f32[12,64,512]{2,1,0:T(8,128)S(1)} collective-permute-done((f32[12,64,512]{2,1,0:T(8,128)S(1)}, f32[12,64,512]{2,1,0:T(8,128)S(1)}, u32[]{:S(2)}, u32[]{:S(2)}) %collective-permute-start.21) | collective-permute-done | bytes 1572896 | tf_op jit(solution)/shard_map/ppermute | solution.py:12
  258.8 5.9 %collective-permute-start.22 = (f32[12,64,512]{2,1,0:T(8,128)S(1)}, f32[12,64,512]{2,1,0:T(8,128)S(1)}, u32[]{:S(2)}, u32[]{:S(2)}) collective-permute-start(f32[12,64,512]{2,1,0:T(8,128)S(1)} %broadcast_select_fusion.3), channel_id=1, source_target_pairs={{0,8},{4,12},{8,16},{12,20},{16,24},{20,28},{24,0},{28,4},{1,9},{5... | collective-permute-start | bytes 4718600 | tf_op jit(solution)/shard_map/ppermute | solution.py:12
  264.7 32.5 %collective-permute-done.22 = f32[12,64,512]{2,1,0:T(8,128)S(1)} collective-permute-done((f32[12,64,512]{2,1,0:T(8,128)S(1)}, f32[12,64,512]{2,1,0:T(8,128)S(1)}, u32[]{:S(2)}, u32[]{:S(2)}) %collective-permute-start.22) | collective-permute-done | bytes 1572896 | tf_op jit(solution)/shard_map/ppermute | solution.py:12
  297.9 32.1 %collective-permute-done.23 = f32[12,64,512]{2,1,0:T(8,128)S(1)} collective-permute-done((f32[12,64,512]{2,1,0:T(8,128)S(1)}, f32[12,64,512]{2,1,0:T(8,128)S(1)}, u32[]{:S(2)}, u32[]{:S(2)}) %collective-permute-start.23) | collective-permute-done | bytes 1572896 | tf_op jit(solution)/shard_map/ppermute | solution.py:12
  330.4 6.3 %collective-permute-start.24 = (f32[12,64,16]{2,1,0:T(8,128)S(1)}, f32[12,64,16]{2,1,0:T(8,128)S(1)}, u32[]{:S(2)}, u32[]{:S(2)}) collective-permute-start(f32[12,64,16]{2,1,0:T(8,128)S(1)} %get-tuple-element.49), channel_id=1, source_target_pairs={{0,4},{4,8},{8,12},{12,16},{16,20},{20,24},{24,28},{28,0},{1,5},{5... | collective-permute-start | bytes 147464 | tf_op jit(solution)/shard_map/ppermute | solution.py:22
  336.8 8.2 %collective-permute-done.24 = f32[12,64,16]{2,1,0:T(8,128)S(1)} collective-permute-done((f32[12,64,16]{2,1,0:T(8,128)S(1)}, f32[12,64,16]{2,1,0:T(8,128)S(1)}, u32[]{:S(2)}, u32[]{:S(2)}) %collective-permute-start.24) | collective-permute-done | bytes 49184 | tf_op jit(solution)/shard_map/ppermute | solution.py:22
  345.8 2.5 fusion.21
  (104 shorter events, 20.4 us)
Async XLA Ops:
  1.1 9.4 %collective-permute-start.1 = (f32[12,3,512]{2,1,0:T(4,128)S(1)}, f32[12,3,512]{2,1,0:T(4,128)S(1)}, u32[]{:S(2)}, u32[]{:S(2)}) collective-permute-start(f32[12,3,512]{2,1,0:T(4,128)S(1)} %get-tuple-element.59), channel_id=1, source_target_pairs={{1,0},{2,1},{3,2},{5,4},{6,5},{7,6},{9,8},{10,9},{11,10},{13,12},{... | collective-permute-start | bytes 221192 | tf_op jit(solution)/shard_map/ppermute | solution.py:25
  3.0 7.6 %collective-permute-start = (f32[12,3,512]{2,1,0:T(4,128)S(1)}, f32[12,3,512]{2,1,0:T(4,128)S(1)}, u32[]{:S(2)}, u32[]{:S(2)}) collective-permute-start(f32[12,3,512]{2,1,0:T(4,128)S(1)} %get-tuple-element.60), channel_id=1, source_target_pairs={{0,1},{1,2},{2,3},{4,5},{5,6},{6,7},{8,9},{9,10},{10,11},{12,13},{... | collective-permute-start | bytes 221192 | tf_op jit(solution)/shard_map/ppermute | solution.py:22
  8.8 1.9 copy-start
  12.2 7.1 %collective-permute-start.2 = (f32[12,64,8]{2,1,0:T(8,128)S(1)}, f32[12,64,8]{2,1,0:T(8,128)S(1)}, u32[]{:S(2)}, u32[]{:S(2)}) collective-permute-start(f32[12,64,8]{2,1,0:T(8,128)S(1)} %slice.452), channel_id=1, source_target_pairs={{0,4},{4,8},{8,12},{12,16},{16,20},{20,24},{24,28},{28,0},{1,5},{5... | collective-permute-start | bytes 73736 | tf_op jit(solution)/shard_map/ppermute | solution.py:12
  20.1 7.3 %collective-permute-start.3 = (f32[12,64,16]{2,1,0:T(8,128)S(1)}, f32[12,64,16]{2,1,0:T(8,128)S(1)}, u32[]{:S(2)}, u32[]{:S(2)}) collective-permute-start(f32[12,64,16]{2,1,0:T(8,128)S(1)} %slice.454), channel_id=1, source_target_pairs={{0,4},{4,8},{8,12},{12,16},{16,20},{20,24},{24,28},{28,0},{1,5},{5... | collective-permute-start | bytes 147464 | tf_op jit(solution)/shard_map/ppermute | solution.py:12
  28.2 7.3 %collective-permute-start.4 = (f32[12,64,32]{2,1,0:T(8,128)S(1)}, f32[12,64,32]{2,1,0:T(8,128)S(1)}, u32[]{:S(2)}, u32[]{:S(2)}) collective-permute-start(f32[12,64,32]{2,1,0:T(8,128)S(1)} %slice.456), channel_id=1, source_target_pairs={{0,4},{4,8},{8,12},{12,16},{16,20},{20,24},{24,28},{28,0},{1,5},{5... | collective-permute-start | bytes 294920 | tf_op jit(solution)/shard_map/ppermute | solution.py:12
  36.3 7.3 %collective-permute-start.5 = (f32[12,64,64]{2,1,0:T(8,128)S(1)}, f32[12,64,64]{2,1,0:T(8,128)S(1)}, u32[]{:S(2)}, u32[]{:S(2)}) collective-permute-start(f32[12,64,64]{2,1,0:T(8,128)S(1)} %slice.458), channel_id=1, source_target_pairs={{0,4},{4,8},{8,12},{12,16},{16,20},{20,24},{24,28},{28,0},{1,5},{5... | collective-permute-start | bytes 589832 | tf_op jit(solution)/shard_map/ppermute | solution.py:12
  44.2 7.3 %collective-permute-start.6 = (f32[12,64,128]{2,1,0:T(8,128)S(1)}, f32[12,64,128]{2,1,0:T(8,128)S(1)}, u32[]{:S(2)}, u32[]{:S(2)}) collective-permute-start(f32[12,64,128]{2,1,0:T(8,128)S(1)} %slice.460), channel_id=1, source_target_pairs={{0,4},{4,8},{8,12},{12,16},{16,20},{20,24},{24,28},{28,0},{1,5},{5... | collective-permute-start | bytes 1179656 | tf_op jit(solution)/shard_map/ppermute | solution.py:12
  51.9 11.5 %collective-permute-start.7 = (f32[12,64,256]{2,1,0:T(8,128)S(1)}, f32[12,64,256]{2,1,0:T(8,128)S(1)}, u32[]{:S(2)}, u32[]{:S(2)}) collective-permute-start(f32[12,64,256]{2,1,0:T(8,128)S(1)} %get-tuple-element.57), channel_id=1, source_target_pairs={{0,4},{4,8},{8,12},{12,16},{16,20},{20,24},{24,28},{28,0},{1,5},{5... | collective-permute-start | bytes 2359304 | tf_op jit(solution)/shard_map/ppermute | solution.py:12
  63.6 19.9 %collective-permute-start.8 = (f32[12,64,512]{2,1,0:T(8,128)S(1)}, f32[12,64,512]{2,1,0:T(8,128)S(1)}, u32[]{:S(2)}, u32[]{:S(2)}) collective-permute-start(f32[12,64,512]{2,1,0:T(8,128)S(1)} %maximum_select_fusion.5), channel_id=1, source_target_pairs={{0,4},{4,8},{8,12},{12,16},{16,20},{20,24},{24,28},{28,0},{1,5},{5... | collective-permute-start | bytes 4718600 | tf_op jit(solution)/shard_map/ppermute | solution.py:12
  83.7 39.6 %collective-permute-start.9 = (f32[12,64,512]{2,1,0:T(8,128)S(1)}, f32[12,64,512]{2,1,0:T(8,128)S(1)}, u32[]{:S(2)}, u32[]{:S(2)}) collective-permute-start(f32[12,64,512]{2,1,0:T(8,128)S(1)} %broadcast_select_fusion), channel_id=1, source_target_pairs={{0,8},{4,12},{8,16},{12,20},{16,24},{20,28},{24,0},{28,4},{1,9},{5... | collective-permute-start | bytes 4718600 | tf_op jit(solution)/shard_map/ppermute | solution.py:12
  123.3 0.7 copy-start.1
  123.3 0.8 copy-start.2
  123.3 0.8 copy-start.3
  123.5 33.6 %collective-permute-start.10 = (f32[12,64,512]{2,1,0:T(8,128)S(1)}, f32[12,64,512]{2,1,0:T(8,128)S(1)}, u32[]{:S(2)}, u32[]{:S(2)}) collective-permute-start(f32[12,64,512]{2,1,0:T(8,128)S(1)} %broadcast_select_fusion.1), channel_id=1, source_target_pairs={{0,16},{4,20},{8,24},{12,28},{16,0},{20,4},{24,8},{28,12},{1,17},{... | collective-permute-start | bytes 4718600 | tf_op jit(solution)/shard_map/ppermute | solution.py:12
  157.5 13.7 %collective-permute-start.11 = (f32[12,64,16]{2,1,0:T(8,128)S(1)}, f32[12,64,16]{2,1,0:T(8,128)S(1)}, u32[]{:S(2)}, u32[]{:S(2)}) collective-permute-start(f32[12,64,16]{2,1,0:T(8,128)S(1)} %get-tuple-element.55), channel_id=1, source_target_pairs={{0,4},{4,8},{8,12},{12,16},{16,20},{20,24},{24,28},{28,0},{1,5},{5... | collective-permute-start | bytes 147464 | tf_op jit(solution)/shard_map/ppermute | solution.py:22
  162.9 8.6 %collective-permute-start.12 = (f32[12,64,16]{2,1,0:T(8,128)S(1)}, f32[12,64,16]{2,1,0:T(8,128)S(1)}, u32[]{:S(2)}, u32[]{:S(2)}) collective-permute-start(f32[12,64,16]{2,1,0:T(8,128)S(1)} %get-tuple-element.56), channel_id=1, source_target_pairs={{4,0},{8,4},{12,8},{16,12},{20,16},{24,20},{28,24},{0,28},{5,1},{9... | collective-permute-start | bytes 147464 | tf_op jit(solution)/shard_map/ppermute | solution.py:25
  175.6 5.4 %collective-permute-start.13 = (f32[12,3,512]{2,1,0:T(4,128)S(1)}, f32[12,3,512]{2,1,0:T(4,128)S(1)}, u32[]{:S(2)}, u32[]{:S(2)}) collective-permute-start(f32[12,3,512]{2,1,0:T(4,128)S(1)} %get-tuple-element.54), channel_id=1, source_target_pairs={{0,1},{1,2},{2,3},{4,5},{5,6},{6,7},{8,9},{9,10},{10,11},{12,13},{... | collective-permute-start | bytes 221192 | tf_op jit(solution)/shard_map/ppermute | solution.py:22
  178.8 5.4 %collective-permute-start.14 = (f32[12,3,512]{2,1,0:T(4,128)S(1)}, f32[12,3,512]{2,1,0:T(4,128)S(1)}, u32[]{:S(2)}, u32[]{:S(2)}) collective-permute-start(f32[12,3,512]{2,1,0:T(4,128)S(1)} %get-tuple-element.53), channel_id=1, source_target_pairs={{1,0},{2,1},{3,2},{5,4},{6,5},{7,6},{9,8},{10,9},{11,10},{13,12},{... | collective-permute-start | bytes 221192 | tf_op jit(solution)/shard_map/ppermute | solution.py:25
  185.8 8.4 %collective-permute-start.15 = (f32[12,64,8]{2,1,0:T(8,128)S(1)}, f32[12,64,8]{2,1,0:T(8,128)S(1)}, u32[]{:S(2)}, u32[]{:S(2)}) collective-permute-start(f32[12,64,8]{2,1,0:T(8,128)S(1)} %slice.501), channel_id=1, source_target_pairs={{0,4},{4,8},{8,12},{12,16},{16,20},{20,24},{24,28},{28,0},{1,5},{5... | collective-permute-start | bytes 73736 | tf_op jit(solution)/shard_map/ppermute | solution.py:12
  195.0 7.3 %collective-permute-start.16 = (f32[12,64,16]{2,1,0:T(8,128)S(1)}, f32[12,64,16]{2,1,0:T(8,128)S(1)}, u32[]{:S(2)}, u32[]{:S(2)}) collective-permute-start(f32[12,64,16]{2,1,0:T(8,128)S(1)} %slice.503), channel_id=1, source_target_pairs={{0,4},{4,8},{8,12},{12,16},{16,20},{20,24},{24,28},{28,0},{1,5},{5... | collective-permute-start | bytes 147464 | tf_op jit(solution)/shard_map/ppermute | solution.py:12
  203.1 7.4 %collective-permute-start.17 = (f32[12,64,32]{2,1,0:T(8,128)S(1)}, f32[12,64,32]{2,1,0:T(8,128)S(1)}, u32[]{:S(2)}, u32[]{:S(2)}) collective-permute-start(f32[12,64,32]{2,1,0:T(8,128)S(1)} %slice.505), channel_id=1, source_target_pairs={{0,4},{4,8},{8,12},{12,16},{16,20},{20,24},{24,28},{28,0},{1,5},{5... | collective-permute-start | bytes 294920 | tf_op jit(solution)/shard_map/ppermute | solution.py:12
  211.3 7.3 %collective-permute-start.18 = (f32[12,64,64]{2,1,0:T(8,128)S(1)}, f32[12,64,64]{2,1,0:T(8,128)S(1)}, u32[]{:S(2)}, u32[]{:S(2)}) collective-permute-start(f32[12,64,64]{2,1,0:T(8,128)S(1)} %slice.507), channel_id=1, source_target_pairs={{0,4},{4,8},{8,12},{12,16},{16,20},{20,24},{24,28},{28,0},{1,5},{5... | collective-permute-start | bytes 589832 | tf_op jit(solution)/shard_map/ppermute | solution.py:12
  219.3 7.3 %collective-permute-start.19 = (f32[12,64,128]{2,1,0:T(8,128)S(1)}, f32[12,64,128]{2,1,0:T(8,128)S(1)}, u32[]{:S(2)}, u32[]{:S(2)}) collective-permute-start(f32[12,64,128]{2,1,0:T(8,128)S(1)} %slice.509), channel_id=1, source_target_pairs={{0,4},{4,8},{8,12},{12,16},{16,20},{20,24},{24,28},{28,0},{1,5},{5... | collective-permute-start | bytes 1179656 | tf_op jit(solution)/shard_map/ppermute | solution.py:12
  227.0 11.5 %collective-permute-start.20 = (f32[12,64,256]{2,1,0:T(8,128)S(1)}, f32[12,64,256]{2,1,0:T(8,128)S(1)}, u32[]{:S(2)}, u32[]{:S(2)}) collective-permute-start(f32[12,64,256]{2,1,0:T(8,128)S(1)} %get-tuple-element.51), channel_id=1, source_target_pairs={{0,4},{4,8},{8,12},{12,16},{16,20},{20,24},{24,28},{28,0},{1,5},{5... | collective-permute-start | bytes 2359304 | tf_op jit(solution)/shard_map/ppermute | solution.py:12
  238.6 19.9 %collective-permute-start.21 = (f32[12,64,512]{2,1,0:T(8,128)S(1)}, f32[12,64,512]{2,1,0:T(8,128)S(1)}, u32[]{:S(2)}, u32[]{:S(2)}) collective-permute-start(f32[12,64,512]{2,1,0:T(8,128)S(1)} %maximum_select_fusion.11), channel_id=1, source_target_pairs={{0,4},{4,8},{8,12},{12,16},{16,20},{20,24},{24,28},{28,0},{1,5},{5... | collective-permute-start | bytes 4718600 | tf_op jit(solution)/shard_map/ppermute | solution.py:12
  258.8 38.3 %collective-permute-start.22 = (f32[12,64,512]{2,1,0:T(8,128)S(1)}, f32[12,64,512]{2,1,0:T(8,128)S(1)}, u32[]{:S(2)}, u32[]{:S(2)}) collective-permute-start(f32[12,64,512]{2,1,0:T(8,128)S(1)} %broadcast_select_fusion.3), channel_id=1, source_target_pairs={{0,8},{4,12},{8,16},{12,20},{16,24},{20,28},{24,0},{28,4},{1,9},{5... | collective-permute-start | bytes 4718600 | tf_op jit(solution)/shard_map/ppermute | solution.py:12
  297.3 32.7 %collective-permute-start.23 = (f32[12,64,512]{2,1,0:T(8,128)S(1)}, f32[12,64,512]{2,1,0:T(8,128)S(1)}, u32[]{:S(2)}, u32[]{:S(2)}) collective-permute-start(f32[12,64,512]{2,1,0:T(8,128)S(1)} %broadcast_select_fusion.4), channel_id=1, source_target_pairs={{0,16},{4,20},{8,24},{12,28},{16,0},{20,4},{24,8},{28,12},{1,17},{... | collective-permute-start | bytes 4718600 | tf_op jit(solution)/shard_map/ppermute | solution.py:12
  330.4 14.6 %collective-permute-start.24 = (f32[12,64,16]{2,1,0:T(8,128)S(1)}, f32[12,64,16]{2,1,0:T(8,128)S(1)}, u32[]{:S(2)}, u32[]{:S(2)}) collective-permute-start(f32[12,64,16]{2,1,0:T(8,128)S(1)} %get-tuple-element.49), channel_id=1, source_target_pairs={{0,4},{4,8},{8,12},{12,16},{16,20},{20,24},{24,28},{28,0},{1,5},{5... | collective-permute-start | bytes 147464 | tf_op jit(solution)/shard_map/ppermute | solution.py:22
  336.8 9.0 %collective-permute-start.25 = (f32[12,64,16]{2,1,0:T(8,128)S(1)}, f32[12,64,16]{2,1,0:T(8,128)S(1)}, u32[]{:S(2)}, u32[]{:S(2)}) collective-permute-start(f32[12,64,16]{2,1,0:T(8,128)S(1)} %get-tuple-element.50), channel_id=1, source_target_pairs={{4,0},{8,4},{12,8},{16,12},{20,16},{24,20},{28,24},{0,28},{5,1},{9... | collective-permute-start | bytes 147464 | tf_op jit(solution)/shard_map/ppermute | solution.py:25
  349.7 1.1 copy-start.4
where the time goes:
time: 353 us; the launch traced here: 352 us
  waiting for transfers between devices  251 us (71%)
  starting transfers between devices  72.2 us (20%)
  other arithmetic  18.3 us (5%)
  local copies, waits for them, and re-layouts  9.81 us (3%)
    ppermute x18, waiting for transfers between devices, from_behind(): return lax.ppermute(x, axis, [(i, (i + by) % peers) for i in range(peers)])  230 us
    ppermute x18, starting transfers between devices, from_behind(): return lax.ppermute(x, axis, [(i, (i + by) % peers) for i in range(peers)])  49.8 us
    ppermute x4, starting transfers between devices, with_halo(): lax.ppermute(lax.slice_in_dim(block, block.shape[dim] - width, None, axis...  18.3 us
    ppermute x4, waiting for transfers between devices, with_halo(): lax.ppermute(lax.slice_in_dim(block, block.shape[dim] - width, None, axis...  16.5 us
  transfers between devices with their start and end apart: 26, of which 23 were waited for; matrix products, arithmetic and copies ran while one was open for 1% of the time, Pallas kernels for 0%

commit v1 on v0

--- a/solution.py
+++ b/solution.py
@@ -1,6 +1,8 @@
 import jax
 import jax.numpy as jnp
 from jax import lax
+from jax.experimental import pallas as pl
+from jax.experimental.pallas import tpu as pltpu
 from jax.sharding import PartitionSpec as P
 
 NTR = 8
@@ -137,6 +139,316 @@
     return tracer_field
 
 
+LANES = 128
+TILE = 8
+PLANES = 4
+LOW = 2
+HIGH = 3
+
+
+def lane_index():
+    return lax.broadcasted_iota(jnp.int32, (TILE, LANES), 1)
+
+
+def pick(values, index):
+    return jnp.take_along_axis(values, index, axis=1)
+
+
+def swap_blocks(items, masks):
+    for bit, mask in enumerate(masks):
+        items = [
+            jnp.where(mask, items[place ^ (1 << bit)], items[place])
+            for place in range(len(items))
+        ]
+    return items
+
+
+def lane_masks(lane, first, count):
+    return [(lane >> (first + bit)) & 1 == 1 for bit in range(count)]
+
+
+def pack_kernel(field_ref, *message_refs):
+    me = lax.axis_index("lon")
+    lane = lane_index()
+    cell_masks = lane_masks(lane, 2, 2)
+    device_masks = lane_masks(lane, 4, 3)
+    base = ((lane & 3) << 5) | (((lane >> 2) & 3) << 3) | ((lane >> 4) ^ me)
+
+    def level(k, carry):
+        by_tile = []
+        for tile in range(8):
+            rows = slice(TILE * tile, TILE * tile + TILE)
+            parts = [
+                pick(field_ref[k, rows, LANES * q : LANES * q + LANES], base ^ ((q << 3) | tile))
+                for q in range(PLANES)
+            ]
+            by_tile.append(swap_blocks(parts, cell_masks))
+        for plane in range(PLANES):
+            sent = swap_blocks([parts[plane] for parts in by_tile], device_masks)
+            for mate in range(8):
+                message_refs[mate][k, plane] = sent[mate]
+        return carry
+
+    lax.fori_loop(0, field_ref.shape[0], level, 0)
+
+
+def unpack_kernel(*refs):
+    message_refs, field_ref = refs[:8], refs[8]
+    me = lax.axis_index("lon")
+    lane = lane_index()
+    cell_masks = lane_masks(lane, 2, 2)
+    device_masks = lane_masks(lane, 4, 3)
+    base = (((lane & 7) ^ me) << 4) | (((lane >> 3) & 3) << 2) | (lane >> 5)
+
+    def level(k, carry):
+        by_plane = [
+            swap_blocks([ref[k, plane] for ref in message_refs], device_masks)
+            for plane in range(PLANES)
+        ]
+        for tile in range(8):
+            rows = slice(TILE * tile, TILE * tile + TILE)
+            parts = swap_blocks([planes[tile] for planes in by_plane], cell_masks)
+            for q in range(PLANES):
+                field_ref[k, rows, LANES * q : LANES * q + LANES] = pick(
+                    parts[q], base ^ ((tile << 4) | (q << 2))
+                )
+        return carry
+
+    lax.fori_loop(0, field_ref.shape[0], level, 0)
+
+
+def put_edges(k, plane, first, last, up_ref, down_ref):
+    up_ref[pl.ds((k * PLANES + plane) * HIGH, HIGH), :] = first[:HIGH]
+    down_ref[pl.ds((k * PLANES + plane) * LOW, LOW), :] = last[TILE - LOW :]
+
+
+def gather_kernel(*refs):
+    message_refs, (moved_ref, up_ref, down_ref) = refs[:8], refs[8:]
+    me = lax.axis_index("lon")
+    lane = lane_index()
+    device_masks = lane_masks(lane, 4, 3)
+    base = lane ^ (me << 4)
+
+    def level(k, carry):
+        for plane in range(PLANES):
+            tiles = swap_blocks([ref[k, plane] for ref in message_refs], device_masks)
+            tiles = [
+                pick(values, base ^ ((tile << 4) | (plane << 2)))
+                for tile, values in enumerate(tiles)
+            ]
+            for tile, values in enumerate(tiles):
+                moved_ref[k, plane, TILE * tile : TILE * tile + TILE, :] = values
+            put_edges(k, plane, tiles[0], tiles[-1], up_ref, down_ref)
+        return carry
+
+    lax.fori_loop(0, moved_ref.shape[0], level, 0)
+
+
+def advance(field_ref, low_ref, high_ref, coeff_ref, padded, moved, step, put):
+    levels, _, rows, _ = field_ref.shape
+    tiles = rows // TILE
+    lane = lane_index()
+
+    def level(k, carry):
+        for plane in range(PLANES):
+            place = k * PLANES + plane
+            padded[k, plane, TILE - LOW : TILE, :] = low_ref[pl.ds(place * LOW, LOW), :]
+            padded[k, plane, TILE : TILE + rows, :] = field_ref[k, plane]
+            padded[k, plane, TILE + rows : TILE + rows + HIGH, :] = high_ref[
+                pl.ds(place * HIGH, HIGH), :
+            ]
+        for tile in range(tiles):
+            start = TILE * tile
+            own = coeff_ref[k, start : start + TILE, :]
+
+            def coeff(which):
+                which = which + 16 * step
+                return jnp.broadcast_to(own[:, which : which + 1], (TILE, LANES))
+
+            weights = [coeff(which) for which in range(LOW + HIGH + 1)]
+            planes = []
+            for plane in range(PLANES):
+                summed = None
+                for which, weight in enumerate(weights):
+                    first = TILE + start + which - LOW
+                    addend = weight * padded[k, plane, first : first + TILE, :]
+                    summed = addend if summed is None else summed + addend
+                planes.append(summed)
+            shift = coeff(10).astype(jnp.int32)
+            bit = shift & 1 == 1
+            behind = [pltpu.roll(planes[3], 1, 1)] + planes[:3]
+            planes = [jnp.where(bit, a, b) for a, b in zip(behind, planes)]
+            bit = shift & 2 == 2
+            behind = [pltpu.roll(planes[2], 1, 1), pltpu.roll(planes[3], 1, 1)] + planes[:2]
+            planes = [jnp.where(bit, a, b) for a, b in zip(behind, planes)]
+            index = (lane - (shift >> 2)) & (LANES - 1)
+            planes = [pick(values, index) for values in planes]
+            wide = (
+                [pltpu.roll(planes[3], 1, 1)]
+                + planes
+                + [pltpu.roll(planes[0], LANES - 1, 1), pltpu.roll(planes[1], LANES - 1, 1)]
+            )
+            taps = [coeff(which) for which in range(6, 10)]
+            for plane in range(PLANES):
+                summed = taps[0] * wide[plane]
+                for which in range(1, 4):
+                    summed = summed + taps[which] * wide[plane + which]
+                moved[k, plane, start : start + TILE, :] = summed
+        return carry
+
+    lax.fori_loop(0, levels, level, 0)
+
+    def column(tile, carry):
+        rows_of = pl.ds(pl.multiple_of(TILE * tile, TILE), TILE)
+        own = [coeff_ref[k, rows_of, :] for k in range(levels)]
+
+        def coeff(k, which):
+            which = which + 16 * step
+            return jnp.broadcast_to(own[k][:, which : which + 1], (TILE, LANES))
+
+        solved = [[None] * PLANES for _ in range(levels)]
+        values = [moved[0, plane, rows_of, :] for plane in range(PLANES)]
+        for k in range(levels):
+            above = values
+            if k + 1 < levels:
+                above = [moved[k + 1, plane, rows_of, :] for plane in range(PLANES)]
+            c_own, c_above, c_before = coeff(k, 11), coeff(k, 12), coeff(k, 13)
+            for plane in range(PLANES):
+                now = c_own * values[plane] + c_above * above[plane]
+                if k:
+                    now = now + c_before * solved[k - 1][plane]
+                solved[k][plane] = now
+            values = above
+        for k in range(levels - 2, -1, -1):
+            c_next = coeff(k, 14)
+            for plane in range(PLANES):
+                solved[k][plane] = solved[k][plane] + c_next * solved[k + 1][plane]
+        for k in range(levels):
+            for plane in range(PLANES):
+                put(k, plane, rows_of, solved[k][plane])
+        return carry
+
+    lax.fori_loop(0, tiles, column, 0)
+
+
+def first_kernel(
+    field_ref, low_ref, high_ref, coeff_ref, next_ref, up_ref, down_ref, padded, moved
+):
+    def put(k, plane, rows_of, values):
+        next_ref[k, plane, rows_of, :] = values
+
+    advance(field_ref, low_ref, high_ref, coeff_ref, padded, moved, 0, put)
+
+    def level(k, carry):
+        for plane in range(PLANES):
+            first = next_ref[k, plane, :TILE, :]
+            last = next_ref[k, plane, next_ref.shape[2] - TILE :, :]
+            put_edges(k, plane, first, last, up_ref, down_ref)
+        return carry
+
+    lax.fori_loop(0, next_ref.shape[0], level, 0)
+
+
+def second_kernel(field_ref, low_ref, high_ref, coeff_ref, *refs):
+    message_refs, (padded, moved) = refs[:8], refs[8:]
+    me = lax.axis_index("lon")
+    lane = lane_index()
+    device_masks = lane_masks(lane, 4, 3)
+    base = lane ^ (me << 4)
+
+    def put(k, plane, rows_of, values):
+        moved[k, plane, rows_of, :] = values
+
+    advance(field_ref, low_ref, high_ref, coeff_ref, padded, moved, 1, put)
+
+    def level(k, carry):
+        for plane in range(PLANES):
+            tiles = [
+                pick(
+                    moved[k, plane, TILE * tile : TILE * tile + TILE, :],
+                    base ^ ((tile << 4) | (plane << 2)),
+                )
+                for tile in range(8)
+            ]
+            for mate, values in enumerate(swap_blocks(tiles, device_masks)):
+                message_refs[mate][k, plane] = values
+        return carry
+
+    lax.fori_loop(0, moved.shape[0], level, 0)
+
+
+def coefficients(lon_shift, lon_frac, lat_shift, lat_frac, remap_frac, diffusivity):
+    face = 0.5 * (diffusivity[:-1] + diffusivity[1:])
+    zero = jnp.zeros_like(diffusivity[:1])
+    below = jnp.concatenate([zero, face], axis=0)
+    above = jnp.concatenate([face, zero], axis=0)
+    ratio = jnp.zeros_like(diffusivity[0])
+    pivots, ratios = [], []
+    for k in range(diffusivity.shape[0]):
+        pivot = 1.0 + below[k] + above[k] + below[k] * ratio
+        ratio = -above[k] / pivot
+        pivots.append(pivot)
+        ratios.append(ratio)
+    pivot = jnp.stack(pivots)
+    back = -jnp.stack(ratios)
+    lat_weights = cubic_weights(lat_frac)
+    columns = []
+    for row_delta in range(-LOW, HIGH + 1):
+        coeff = jnp.zeros_like(lat_frac)
+        for tap in range(4):
+            coeff = coeff + jnp.where(lat_shift == tap - 1 - row_delta, lat_weights[tap], 0.0)
+        columns.append(coeff)
+    columns.extend(cubic_weights(lon_frac))
+    columns.append(lon_shift.astype(jnp.float32))
+    columns.append((1.0 - remap_frac) / pivot)
+    columns.append(remap_frac / pivot)
+    columns.append(jnp.broadcast_to(below / pivot, lat_frac.shape))
+    columns.append(jnp.broadcast_to(back, lat_frac.shape))
+    columns.append(jnp.zeros_like(lat_frac))
+    stacked = jnp.stack(columns, axis=-1)
+    return jnp.concatenate([stacked[0], stacked[1]], axis=-1)
+
+
+def call(kernel, out_shapes, scratch=()):
+    return pl.pallas_call(
+        kernel,
+        out_shape=[jax.ShapeDtypeStruct(shape, jnp.float32) for shape in out_shapes],
+        scratch_shapes=[pltpu.VMEM(shape, jnp.float32) for shape in scratch],
+        compiler_params=pltpu.CompilerParams(vmem_limit_bytes=40 * 2**20),
+    )
+
+
+def exchange(messages):
+    peers = lax.axis_size("lon")
+    received = [messages[0]]
+    for mate in range(1, peers):
+        received.append(lax.ppermute(messages[mate], "lon", [(i, i ^ mate) for i in range(peers)]))
+    return received
+
+
+def exchange_rows(up, down):
+    count = lax.axis_size("lat")
+    high = lax.ppermute(up, "lat", [(i + 1, i) for i in range(count - 1)])
+    low = lax.ppermute(down, "lat", [(i, i + 1) for i in range(count - 1)])
+    return low, high
+
+
+def by_tracer(tracers, lon_shift, lon_frac, lat_shift, lat_frac, remap_frac, diffusivity):
+    levels, rows, _ = tracers.shape
+    block = (levels, PLANES, rows, LANES)
+    message = (levels, PLANES, TILE, LANES)
+    edges = [(levels * PLANES * HIGH, LANES), (levels * PLANES * LOW, LANES)]
+    scratch = [(levels, PLANES, rows + 2 * TILE, LANES), block]
+    coeff = coefficients(lon_shift, lon_frac, lat_shift, lat_frac, remap_frac, diffusivity)
+    messages = call(pack_kernel, [message] * 8)(tracers)
+    field, up, down = call(gather_kernel, [block] + edges)(*exchange(messages))
+    low, high = exchange_rows(up, down)
+    field, up, down = call(first_kernel, [block] + edges, scratch)(field, low, high, coeff)
+    low, high = exchange_rows(up, down)
+    messages = call(second_kernel, [message] * 8, scratch)(field, low, high, coeff)
+    return call(unpack_kernel, [tracers.shape])(*exchange(messages))[0]
+
+
 def solution(mesh):
     in_specs = (
         P(None, "lat", "lon"),
@@ -148,6 +460,11 @@
         P(None, "lat"),
     )
     out_specs = P(None, "lat", "lon")
+    def per_part(tracers, *fields):
+        _, rows, columns = tracers.shape
+        fits = mesh.shape["lon"] == NTR and columns == PLANES * LANES and rows == TILE * NTR
+        return (by_tracer if fits else per_device)(tracers, *fields)
+
     return jax.shard_map(
-        per_device, mesh=mesh, in_specs=in_specs, out_specs=out_specs, check_vma=False
+        per_part, mesh=mesh, in_specs=in_specs, out_specs=out_specs, check_vma=False
     )

time: 353 us -> 110 us (0.31)
  waiting for transfers between devices: 251 us -> 24.7 us
  starting transfers between devices: 72.2 us -> 29.4 us
  Pallas kernels: 0 us -> 24 us
  local copies, waits for them, and re-layouts: 9.81 us -> 30.2 us
  other arithmetic: 18.3 us -> 0.99 us
    ppermute x26 -> x18, waiting for transfers between devices: 251 us -> 24.7 us  [the longest x14 19.9 us: exchange(): lax.ppermute(messages[mate], 'lon', [(i, i ^ mate) for i in range(peers)])]
    ppermute x26 -> x18, starting transfers between devices: 72.2 us -> 29.4 us  [the longest x14 18.8 us: exchange(): lax.ppermute(messages[mate], 'lon', [(i, i ^ mate) for i in range(peers)])]
    another operation x0 -> x19, local copies, waits for them, and re-layouts: none -> 27.6 us  [the longest x17 26.8 us: coefficients(): stacked = jnp.stack(columns, axis=-1)]
    pallas_call x0 -> x5, Pallas kernels: none -> 24 us  [the longest x1 9.39 us: by_tracer(): call(second_kernel, [message] * 8, scratch)(field, low, high, coeff)]
    add x9 -> x0, other arithmetic: 8.57 us -> none  [the longest x2 5.04 us: lon_step(): summed = addend if summed is None else summed + addend]
    select_n x18 -> x0, other arithmetic: 7.05 us -> none  [the longest x12 5.76 us: move_rows(): current = jnp.where(bit_mask(ahead_amount, position), forward, current)]
    slice x27 -> x0, local copies, waits for them, and re-layouts: 6.31 us -> none  [the longest x12 1.92 us: move_rows(): from_west = from_behind(current[:, :, width_cols - step_cols:], 'lon', 1)]
  transfers between devices with their start and end apart: 26 -> 18, of which waited for: 23 -> 7; matrix products, arithmetic and copies ran while one was open for 1% -> 27% of each run, Pallas kernels for 0% -> 0%
where the time goes in v1:
time: 110 us; the launch traced here: 109 us
  local copies, waits for them, and re-layouts  30.2 us (27%)
  starting transfers between devices  29.4 us (27%)
  waiting for transfers between devices  24.7 us (22%)
  Pallas kernels  24 us (22%)
    another operation x17, local copies, waits for them, and re-layouts, coefficients(): stacked = jnp.stack(columns, axis=-1)  26.8 us
    ppermute x14, waiting for transfers between devices, exchange(): lax.ppermute(messages[mate], 'lon', [(i, i ^ mate) for i in range(peers)])  19.9 us
    ppermute x14, starting transfers between devices, exchange(): lax.ppermute(messages[mate], 'lon', [(i, i ^ mate) for i in range(peers)])  18.8 us
    pallas_call x1, Pallas kernels, by_tracer(): call(second_kernel, [message] * 8, scratch)(field, low, high, coeff)  9.39 us
    pallas_call x1, Pallas kernels, by_tracer(): call(first_kernel, [block] + edges, scratch)(field, low, high, coeff)  7.54 us
    ppermute x2, starting transfers between devices, exchange_rows(): low = lax.ppermute(down, 'lat', [(i, i + 1) for i in range(count - 1)])  6.41 us
    ppermute x2, starting transfers between devices, exchange_rows(): high = lax.ppermute(up, 'lat', [(i + 1, i) for i in range(count - 1)])  4.15 us
    pallas_call x1, Pallas kernels, by_tracer(): return call(unpack_kernel, [tracers.shape])(*exchange(messages))[0]  3.12 us
  transfers between devices with their start and end apart: 18, of which 7 were waited for; matrix products, arithmetic and copies ran while one was open for 27% of the time, Pallas kernels for 0%

profile of v1, /device:TPU:9, one launch (start us, length us, event | category | flops | bytes accessed | tf_op | source)
XLA Modules:
  0.0 109.4 jit_solution(15917806587696330909)
XLA Ops:
  0.0 1.4 %copy-done = f32[12,64,512]{2,1,0:T(8,128)S(1)} copy-done((f32[12,64,512]{2,1,0:T(8,128)S(1)}, f32[12,64,512]{2,1,0:T(8,128)}, u32[]{:S(2)}) %copy-start) | copy-done | bytes 1572888
  1.4 2.0 %shard_map.73 = (f32[12,4,8,128]{3,2,1,0:T(8,128)S(1)}, f32[12,4,8,128]{3,2,1,0:T(8,128)S(1)}, f32[12,4,8,128]{3,2,1,0:T(8,128)S(1)}, f32[12,4,8,128]{3,2,1,0:T(...) custom-call(f32[12,64,512]{2,1,0:T(8,128)S(1)} %copy-done), custom_call_target="tpu_custom_call" | custom-call | tf_op jit(solution)/shard_map/pallas_call | solution.py:443
  3.5 0.7 collective-permute-start
  4.2 1.2 %collective-permute-start.1 = (f32[12,4,8,128]{3,2,1,0:T(8,128)S(1)}, f32[12,4,8,128]{3,2,1,0:T(8,128)S(1)}, u32[]{:S(2)}, u32[]{:S(2)}) collective-permute-start(f32[12,4,8,128]{3,2,1,0:T(8,128)S(1)} %get-tuple-element.29), channel_id=1, source_target_pairs={{0,8},{4,12},{8,0},{12,4},{16,24},{20,28},{24,16},{28,20},{1,9},{5... | collective-permute-start | bytes 589832 | tf_op jit(solution)/shard_map/ppermute | solution.py:425
  5.5 0.5 collective-permute-start.2
  5.9 1.2 %collective-permute-start.3 = (f32[12,4,8,128]{3,2,1,0:T(8,128)S(1)}, f32[12,4,8,128]{3,2,1,0:T(8,128)S(1)}, u32[]{:S(2)}, u32[]{:S(2)}) collective-permute-start(f32[12,4,8,128]{3,2,1,0:T(8,128)S(1)} %get-tuple-element.31), channel_id=1, source_target_pairs={{0,16},{4,20},{8,24},{12,28},{16,0},{20,4},{24,8},{28,12},{1,17},{... | collective-permute-start | bytes 589832 | tf_op jit(solution)/shard_map/ppermute | solution.py:425
  7.2 0.6 collective-permute-start.4
  7.8 0.6 broadcast_divide_fusion
  9.0 1.2 %copy.531 = f32[2,12,64,1]{3,2,1,0:T(8,128)} copy(f32[2,12,64,1]{2,0,1,3:T(2,128)S(1)} %get-tuple-element.82) | data formatting | bytes 12288 | tf_op jit(solution)/shard_map/stack | solution.py:408
  10.2 0.7 stack.83
  10.9 1.3 %copy.534 = f32[2,12,64,1]{3,2,1,0:T(8,128)} copy(f32[2,12,64,1]{2,0,1,3:T(2,128)S(1)} %get-tuple-element.80) | data formatting | bytes 12288 | tf_op jit(solution)/shard_map/stack | solution.py:408
  12.2 1.2 %copy.532 = f32[2,12,64,1]{3,2,1,0:T(8,128)} copy(f32[2,12,64,1]{2,0,1,3:T(2,128)S(1)} %convert_bitcast_fusion) | data formatting | bytes 12288 | tf_op jit(solution)/shard_map/stack | solution.py:408
  13.4 1.2 %copy.522 = f32[2,12,64,1]{3,2,1,0:T(8,128)} copy(f32[2,12,64,1]{2,0,1,3:T(2,128)S(1)} %get-tuple-element.75) | data formatting | bytes 12288 | tf_op jit(solution)/shard_map/stack | solution.py:408
  14.6 1.2 %copy.525 = f32[2,12,64,1]{3,2,1,0:T(8,128)} copy(f32[2,12,64,1]{2,0,1,3:T(2,128)S(1)} %get-tuple-element.76) | data formatting | bytes 12288 | tf_op jit(solution)/shard_map/stack | solution.py:408
  15.8 1.2 %copy.524 = f32[2,12,64,1]{3,2,1,0:T(8,128)} copy(f32[2,12,64,1]{2,0,1,3:T(2,128)S(1)} %get-tuple-element.77) | data formatting | bytes 12288 | tf_op jit(solution)/shard_map/stack | solution.py:408
  17.1 1.3 %copy.523 = f32[2,12,64,1]{3,2,1,0:T(8,128)} copy(f32[2,12,64,1]{2,0,1,3:T(2,128)S(1)} %get-tuple-element.78) | data formatting | bytes 12288 | tf_op jit(solution)/shard_map/stack | solution.py:408
  18.3 1.2 %copy.526 = f32[2,12,64,1]{3,2,1,0:T(8,128)} copy(f32[2,12,64,1]{2,0,1,3:T(2,128)S(1)} %get-tuple-element.79) | data formatting | bytes 12288 | tf_op jit(solution)/shard_map/stack | solution.py:408
  19.5 1.2 %copy.529 = f32[2,12,64,1]{3,2,1,0:T(8,128)} copy(f32[2,12,64,1]{2,0,1,3:T(2,128)S(1)} %get-tuple-element.83) | data formatting | bytes 12288 | tf_op jit(solution)/shard_map/stack | solution.py:408
  20.8 1.2 %copy.528 = f32[2,12,64,1]{3,2,1,0:T(8,128)} copy(f32[2,12,64,1]{2,0,1,3:T(2,128)S(1)} %get-tuple-element.84) | data formatting | bytes 12288 | tf_op jit(solution)/shard_map/stack | solution.py:408
  22.0 1.2 %copy.530 = f32[2,12,64,1]{3,2,1,0:T(8,128)} copy(f32[2,12,64,1]{2,0,1,3:T(2,128)S(1)} %get-tuple-element.85) | data formatting | bytes 12288 | tf_op jit(solution)/shard_map/stack | solution.py:408
  23.2 1.2 %copy.533 = f32[2,12,64,1]{3,2,1,0:T(8,128)} copy(f32[2,12,64,1]{2,0,1,3:T(2,128)S(1)} %get-tuple-element.81) | data formatting | bytes 12288 | tf_op jit(solution)/shard_map/stack | solution.py:408
  24.5 1.1 stack_broadcast_in_dim.9
  25.5 1.1 stack_broadcast_in_dim.10
  26.6 1.0 stack_broadcast_in_dim.11
  27.6 8.6 %stack.87 = f32[2,12,64,16]{3,2,1,0:T(8,128)} concatenate(f32[2,12,64,1]{3,2,1,0:T(8,128)} %copy.522, f32[2,12,64,1]{3,2,1,0:T(8,128)} %copy.523, f32[2,12,64,1]{3,2,1,0:T(8,128)} %copy.524, f32[2,12,64,1]{3,2,1,0:T(8,128)} %copy.525, f32[2,12,64,1]{3,2,1,0:T(8,128)} %copy.526, f32[2,12,64,1]{3,2,1,0:T(8,128)S(1)} %copy.527, f32[2,12,64,1]{3,2,1,0:T(8,128)} %copy.528, ...), dimensions={3} | concatenate | bytes 196608 | tf_op jit(solution)/shard_map/stack | solution.py:408
  36.2 2.2 %collective-permute-start.5 = (f32[12,4,8,128]{3,2,1,0:T(8,128)S(1)}, f32[12,4,8,128]{3,2,1,0:T(8,128)S(1)}, u32[]{:S(2)}, u32[]{:S(2)}) collective-permute-start(f32[12,4,8,128]{3,2,1,0:T(8,128)S(1)} %get-tuple-element.33), channel_id=1, source_target_pairs={{0,24},{4,28},{8,16},{12,20},{16,8},{20,12},{24,0},{28,4},{1,25},{... | collective-permute-start | bytes 589832 | tf_op jit(solution)/shard_map/ppermute | solution.py:425
  38.9 1.2 %slice_bitcast_fusion.1 = (f32[12,64,16]{2,1,0:T(8,128)S(1)}, f32[12,64,16]{2,1,0:T(8,128)S(1)}) fusion(f32[2,12,64,16]{3,2,1,0:T(8,128)} %stack.87), kind=kLoop, calls=%fused_computation.1 | loop fusion | bytes 196608 | tf_op jit(solution)/shard_map/squeeze | solution.py:409
  40.1 3.6 %collective-permute-done.5.refs_6_ = f32[12,4,8,128]{3,2,1,0:T(8,128)S(1)} collective-permute-done((f32[12,4,8,128]{3,2,1,0:T(8,128)S(1)}, f32[12,4,8,128]{3,2,1,0:T(8,128)S(1)}, u32[]{:S(2)}, u32[]{:S(2)}) %collective-permute-start.5) | collective-permute-done | bytes 196640 | tf_op jit(solution)/shard_map/ppermute | solution.py:425
  43.7 4.4 %collective-permute-done.6.refs_7_ = f32[12,4,8,128]{3,2,1,0:T(8,128)S(1)} collective-permute-done((f32[12,4,8,128]{3,2,1,0:T(8,128)S(1)}, f32[12,4,8,128]{3,2,1,0:T(8,128)S(1)}, u32[]{:S(2)}, u32[]{:S(2)}) %collective-permute-start.6) | collective-permute-done | bytes 196640 | tf_op jit(solution)/shard_map/ppermute | solution.py:425
  48.0 1.9 %shard_map.74 = (f32[12,4,64,128]{3,2,1,0:T(8,128)S(1)}, f32[144,128]{1,0:T(8,128)S(1)}, f32[96,128]{1,0:T(8,128)S(1)}) custom-call(f32[12,4,8,128]{3,2,1,0:T(8,128)S(1)} %get-tuple-element.27.refs_0_, f32[12,4,8,128]{3,2,1,0:T(8,128)S(1)} %collective-permute-done.refs_1_, f32[12,4,8,128]{3,2,1,0:T(8,128)S(1)} %collective-permute-done.1.refs_2_, ...), custom_call_target="tpu_custom_call" | custom-call | tf_op jit(solution)/shard_map/pallas_call | solution.py:444
  49.9 3.2 %collective-permute-start.7 = (f32[96,128]{1,0:T(8,128)S(1)}, f32[96,128]{1,0:T(8,128)S(1)}, u32[]{:S(2)}, u32[]{:S(2)}) collective-permute-start(f32[96,128]{1,0:T(8,128)S(1)} %get-tuple-element.36), channel_id=1, source_target_pairs={{0,1},{1,2},{2,3},{4,5},{5,6},{6,7},{8,9},{9,10},{10,11},{12,13},{... | collective-permute-start | bytes 147464 | tf_op jit(solution)/shard_map/ppermute | solution.py:432
  53.1 2.1 %collective-permute-start.8 = (f32[144,128]{1,0:T(8,128)S(1)}, f32[144,128]{1,0:T(8,128)S(1)}, u32[]{:S(2)}, u32[]{:S(2)}) collective-permute-start(f32[144,128]{1,0:T(8,128)S(1)} %get-tuple-element.37), channel_id=1, source_target_pairs={{1,0},{2,1},{3,2},{5,4},{6,5},{7,6},{9,8},{10,9},{11,10},{13,12},{... | collective-permute-start | bytes 221192 | tf_op jit(solution)/shard_map/ppermute | solution.py:431
  55.4 2.8 %collective-permute-done.8.high_ref = f32[144,128]{1,0:T(8,128)S(1)} collective-permute-done((f32[144,128]{1,0:T(8,128)S(1)}, f32[144,128]{1,0:T(8,128)S(1)}, u32[]{:S(2)}, u32[]{:S(2)}) %collective-permute-start.8) | collective-permute-done | bytes 73760 | tf_op jit(solution)/shard_map/ppermute | solution.py:431
  58.2 7.5 %shard_map.75 = (f32[12,4,64,128]{3,2,1,0:T(8,128)S(1)}, f32[144,128]{1,0:T(8,128)S(1)}, f32[96,128]{1,0:T(8,128)S(1)}) custom-call(f32[12,4,64,128]{3,2,1,0:T(8,128)S(1)} %get-tuple-element.35.field_ref, f32[96,128]{1,0:T(8,128)S(1)} %collective-permute-done.7.low_ref, f32[144,128]{1,0:T(8,128)S(1)} %collective-permute-done.8.high_ref, ...), custom_call_target="tpu_custom_call" | custom-call | tf_op jit(solution)/shard_map/pallas_call | solution.py:446
  65.8 2.1 %collective-permute-start.10 = (f32[144,128]{1,0:T(8,128)S(1)}, f32[144,128]{1,0:T(8,128)S(1)}, u32[]{:S(2)}, u32[]{:S(2)}) collective-permute-start(f32[144,128]{1,0:T(8,128)S(1)} %get-tuple-element.40), channel_id=1, source_target_pairs={{1,0},{2,1},{3,2},{5,4},{6,5},{7,6},{9,8},{10,9},{11,10},{13,12},{... | collective-permute-start | bytes 221192 | tf_op jit(solution)/shard_map/ppermute | solution.py:431
  67.9 3.2 %collective-permute-start.9 = (f32[96,128]{1,0:T(8,128)S(1)}, f32[96,128]{1,0:T(8,128)S(1)}, u32[]{:S(2)}, u32[]{:S(2)}) collective-permute-start(f32[96,128]{1,0:T(8,128)S(1)} %get-tuple-element.39), channel_id=1, source_target_pairs={{0,1},{1,2},{2,3},{4,5},{5,6},{6,7},{8,9},{9,10},{10,11},{12,13},{... | collective-permute-start | bytes 147464 | tf_op jit(solution)/shard_map/ppermute | solution.py:432
  71.1 1.9 %collective-permute-done.9.low_ref = f32[96,128]{1,0:T(8,128)S(1)} collective-permute-done((f32[96,128]{1,0:T(8,128)S(1)}, f32[96,128]{1,0:T(8,128)S(1)}, u32[]{:S(2)}, u32[]{:S(2)}) %collective-permute-start.9) | collective-permute-done | bytes 49184 | tf_op jit(solution)/shard_map/ppermute | solution.py:432
  73.0 9.4 %shard_map.76 = (f32[12,4,8,128]{3,2,1,0:T(8,128)S(1)}, f32[12,4,8,128]{3,2,1,0:T(8,128)S(1)}, f32[12,4,8,128]{3,2,1,0:T(8,128)S(1)}, f32[12,4,8,128]{3,2,1,0:T(...) custom-call(f32[12,4,64,128]{3,2,1,0:T(8,128)S(1)} %get-tuple-elemen, ...), custom_call_target="tpu_custom_call" | custom-call | tf_op jit(solution)/shard_map/pallas_call | solution.py:448
  82.4 2.9 %collective-permute-start.11 = (f32[12,4,8,128]{3,2,1,0:T(8,128)S(1)}, f32[12,4,8,128]{3,2,1,0:T(8,128)S(1)}, u32[]{:S(2)}, u32[]{:S(2)}) collective-permute-start(f32[12,4,8,128]{3,2,1,0:T(8,128)S(1)} %get-tuple-element.42), channel_id=1, source_target_pairs={{0,4},{4,0},{8,12},{12,8},{16,20},{20,16},{24,28},{28,24},{1,5},{5... | collective-permute-start | bytes 589832 | tf_op jit(solution)/shard_map/ppermute | solution.py:425
  85.3 1.2 %collective-permute-start.12 = (f32[12,4,8,128]{3,2,1,0:T(8,128)S(1)}, f32[12,4,8,128]{3,2,1,0:T(8,128)S(1)}, u32[]{:S(2)}, u32[]{:S(2)}) collective-permute-start(f32[12,4,8,128]{3,2,1,0:T(8,128)S(1)} %get-tuple-element.43), channel_id=1, source_target_pairs={{0,8},{4,12},{8,0},{12,4},{16,24},{20,28},{24,16},{28,20},{1,9},{5... | collective-permute-start | bytes 589832 | tf_op jit(solution)/shard_map/ppermute | solution.py:425
  87.0 1.2 %collective-permute-start.14 = (f32[12,4,8,128]{3,2,1,0:T(8,128)S(1)}, f32[12,4,8,128]{3,2,1,0:T(8,128)S(1)}, u32[]{:S(2)}, u32[]{:S(2)}) collective-permute-start(f32[12,4,8,128]{3,2,1,0:T(8,128)S(1)} %get-tuple-element.45), channel_id=1, source_target_pairs={{0,16},{4,20},{8,24},{12,28},{16,0},{20,4},{24,8},{28,12},{1,17},{... | collective-permute-start | bytes 589832 | tf_op jit(solution)/shard_map/ppermute | solution.py:425
  88.2 0.6 collective-permute-start.15
  88.8 2.2 %collective-permute-start.16 = (f32[12,4,8,128]{3,2,1,0:T(8,128)S(1)}, f32[12,4,8,128]{3,2,1,0:T(8,128)S(1)}, u32[]{:S(2)}, u32[]{:S(2)}) collective-permute-start(f32[12,4,8,128]{3,2,1,0:T(8,128)S(1)} %get-tuple-element.47), channel_id=1, source_target_pairs={{0,24},{4,28},{8,16},{12,20},{16,8},{20,12},{24,0},{28,4},{1,25},{... | collective-permute-start | bytes 589832 | tf_op jit(solution)/shard_map/ppermute | solution.py:425
  90.9 0.8 collective-permute-done.12.refs_2_
  91.8 3.4 %collective-permute-start.17 = (f32[12,4,8,128]{3,2,1,0:T(8,128)S(1)}, f32[12,4,8,128]{3,2,1,0:T(8,128)S(1)}, u32[]{:S(2)}, u32[]{:S(2)}) collective-permute-start(f32[12,4,8,128]{3,2,1,0:T(8,128)S(1)} %get-tuple-element.48), channel_id=1, source_target_pairs={{0,28},{4,24},{8,20},{12,16},{16,12},{20,8},{24,4},{28,0},{1,29},{... | collective-permute-start | bytes 589832 | tf_op jit(solution)/shard_map/ppermute | solution.py:425
  95.1 1.8 %collective-permute-done.13.refs_3_ = f32[12,4,8,128]{3,2,1,0:T(8,128)S(1)} collective-permute-done((f32[12,4,8,128]{3,2,1,0:T(8,128)S(1)}, f32[12,4,8,128]{3,2,1,0:T(8,128)S(1)}, u32[]{:S(2)}, u32[]{:S(2)}) %collective-permute-start.13) | collective-permute-done | bytes 196640 | tf_op jit(solution)/shard_map/ppermute | solution.py:425
  96.9 9.4 %collective-permute-done.15.refs_5_ = f32[12,4,8,128]{3,2,1,0:T(8,128)S(1)} collective-permute-done((f32[12,4,8,128]{3,2,1,0:T(8,128)S(1)}, f32[12,4,8,128]{3,2,1,0:T(8,128)S(1)}, u32[]{:S(2)}, u32[]{:S(2)}) %collective-permute-start.15) | collective-permute-done | bytes 196640 | tf_op jit(solution)/shard_map/ppermute | solution.py:425
  106.3 3.1 %shard_map.77 = f32[12,64,512]{2,1,0:T(8,128)} custom-call(f32[12,4,8,128]{3,2,1,0:T(8,128)S(1)} %get-tuple-element.41.refs_0_, f32[12,4,8,128]{3,2,1,0:T(8,128)S(1)} %collective-permute-done.11.refs_1_, f32[12,4,8,128]{3,2,1,0:T(8,128)S(1)} %collective-permute-done.12.refs_2_, f32[12,4,8,128]{3,2,1,0:T(8,128)S(1)} %collective-permute-done.13.refs_3_, ...), custom_call_target="tpu_custom_call" | custom-call | tf_op jit(solution)/shard_map/pallas_call | solution.py:449
  (36 shorter events, 1.7 us)
Async XLA Ops:
  0.0 1.4 %copy-start = (f32[12,64,512]{2,1,0:T(8,128)S(1)}, f32[12,64,512]{2,1,0:T(8,128)}, u32[]{:S(2)}) copy-start(f32[12,64,512]{2,1,0:T(8,128)} %field_ref.1) | copy-start | bytes 4718596
  1.4 6.3 %copy-start.1 = (f32[12,64]{1,0:T(8,128)S(1)}, f32[12,64]{1,0:T(8,128)}, u32[]{:S(2)}) copy-start(f32[12,64]{1,0:T(8,128)} %param.13) | copy-start | bytes 9220
  1.4 6.3 %copy-start.4 = (s32[2,12,64]{2,0,1:T(2,128)S(1)}, s32[2,12,64]{2,0,1:T(2,128)}, u32[]{:S(2)}) copy-start(s32[2,12,64]{2,0,1:T(2,128)} %param.8) | copy-start | bytes 18436
  1.4 7.0 %copy-start.6 = (f32[2,12,64]{2,0,1:T(2,128)S(1)}, f32[2,12,64]{2,0,1:T(2,128)}, u32[]{:S(2)}) copy-start(f32[2,12,64]{2,0,1:T(2,128)} %param.9) | copy-start | bytes 18436
  1.4 7.1 %copy-start.2 = (s32[2,12,64]{2,0,1:T(2,128)S(1)}, s32[2,12,64]{2,0,1:T(2,128)}, u32[]{:S(2)}) copy-start(s32[2,12,64]{2,0,1:T(2,128)} %param.10) | copy-start | bytes 18436
  1.4 7.1 %copy-start.3 = (f32[2,12,64]{2,0,1:T(2,128)S(1)}, f32[2,12,64]{2,0,1:T(2,128)}, u32[]{:S(2)}) copy-start(f32[2,12,64]{2,0,1:T(2,128)} %param.11) | copy-start | bytes 18436
  1.4 9.5 %copy-start.5 = (f32[2,12,64]{2,0,1:T(2,128)S(1)}, f32[2,12,64]{2,0,1:T(2,128)}, u32[]{:S(2)}) copy-start(f32[2,12,64]{2,0,1:T(2,128)} %param.12) | copy-start | bytes 18436
  3.5 32.7 %collective-permute-start = (f32[12,4,8,128]{3,2,1,0:T(8,128)S(1)}, f32[12,4,8,128]{3,2,1,0:T(8,128)S(1)}, u32[]{:S(2)}, u32[]{:S(2)}) collective-permute-start(f32[12,4,8,128]{3,2,1,0:T(8,128)S(1)} %get-tuple-element.28), channel_id=1, source_target_pairs={{0,4},{4,0},{8,12},{12,8},{16,20},{20,16},{24,28},{28,24},{1,5},{5... | collective-permute-start | bytes 589832 | tf_op jit(solution)/shard_map/ppermute | solution.py:425
  4.2 34.2 %collective-permute-start.1 = (f32[12,4,8,128]{3,2,1,0:T(8,128)S(1)}, f32[12,4,8,128]{3,2,1,0:T(8,128)S(1)}, u32[]{:S(2)}, u32[]{:S(2)}) collective-permute-start(f32[12,4,8,128]{3,2,1,0:T(8,128)S(1)} %get-tuple-element.29), channel_id=1, source_target_pairs={{0,8},{4,12},{8,0},{12,4},{16,24},{20,28},{24,16},{28,20},{1,9},{5... | collective-permute-start | bytes 589832 | tf_op jit(solution)/shard_map/ppermute | solution.py:425
  5.5 34.6 %collective-permute-start.2 = (f32[12,4,8,128]{3,2,1,0:T(8,128)S(1)}, f32[12,4,8,128]{3,2,1,0:T(8,128)S(1)}, u32[]{:S(2)}, u32[]{:S(2)}) collective-permute-start(f32[12,4,8,128]{3,2,1,0:T(8,128)S(1)} %get-tuple-element.30), channel_id=1, source_target_pairs={{0,12},{4,8},{8,4},{12,0},{16,28},{20,24},{24,20},{28,16},{1,13},{... | collective-permute-start | bytes 589832 | tf_op jit(solution)/shard_map/ppermute | solution.py:425
  5.9 34.1 %collective-permute-start.3 = (f32[12,4,8,128]{3,2,1,0:T(8,128)S(1)}, f32[12,4,8,128]{3,2,1,0:T(8,128)S(1)}, u32[]{:S(2)}, u32[]{:S(2)}) collective-permute-start(f32[12,4,8,128]{3,2,1,0:T(8,128)S(1)} %get-tuple-element.31), channel_id=1, source_target_pairs={{0,16},{4,20},{8,24},{12,28},{16,0},{20,4},{24,8},{28,12},{1,17},{... | collective-permute-start | bytes 589832 | tf_op jit(solution)/shard_map/ppermute | solution.py:425
  7.2 32.9 %collective-permute-start.4 = (f32[12,4,8,128]{3,2,1,0:T(8,128)S(1)}, f32[12,4,8,128]{3,2,1,0:T(8,128)S(1)}, u32[]{:S(2)}, u32[]{:S(2)}) collective-permute-start(f32[12,4,8,128]{3,2,1,0:T(8,128)S(1)} %get-tuple-element.32), channel_id=1, source_target_pairs={{0,20},{4,16},{8,28},{12,24},{16,4},{20,0},{24,12},{28,8},{1,21},{... | collective-permute-start | bytes 589832 | tf_op jit(solution)/shard_map/ppermute | solution.py:425
  36.2 7.4 %collective-permute-start.5 = (f32[12,4,8,128]{3,2,1,0:T(8,128)S(1)}, f32[12,4,8,128]{3,2,1,0:T(8,128)S(1)}, u32[]{:S(2)}, u32[]{:S(2)}) collective-permute-start(f32[12,4,8,128]{3,2,1,0:T(8,128)S(1)} %get-tuple-element.33), channel_id=1, source_target_pairs={{0,24},{4,28},{8,16},{12,20},{16,8},{20,12},{24,0},{28,4},{1,25},{... | collective-permute-start | bytes 589832 | tf_op jit(solution)/shard_map/ppermute | solution.py:425
  38.5 9.6 %collective-permute-start.6 = (f32[12,4,8,128]{3,2,1,0:T(8,128)S(1)}, f32[12,4,8,128]{3,2,1,0:T(8,128)S(1)}, u32[]{:S(2)}, u32[]{:S(2)}) collective-permute-start(f32[12,4,8,128]{3,2,1,0:T(8,128)S(1)} %get-tuple-element.34), channel_id=1, source_target_pairs={{0,28},{4,24},{8,20},{12,16},{16,12},{20,8},{24,4},{28,0},{1,29},{... | collective-permute-start | bytes 589832 | tf_op jit(solution)/shard_map/ppermute | solution.py:425
  49.9 5.5 %collective-permute-start.7 = (f32[96,128]{1,0:T(8,128)S(1)}, f32[96,128]{1,0:T(8,128)S(1)}, u32[]{:S(2)}, u32[]{:S(2)}) collective-permute-start(f32[96,128]{1,0:T(8,128)S(1)} %get-tuple-element.36), channel_id=1, source_target_pairs={{0,1},{1,2},{2,3},{4,5},{5,6},{6,7},{8,9},{9,10},{10,11},{12,13},{... | collective-permute-start | bytes 147464 | tf_op jit(solution)/shard_map/ppermute | solution.py:432
  53.1 5.1 %collective-permute-start.8 = (f32[144,128]{1,0:T(8,128)S(1)}, f32[144,128]{1,0:T(8,128)S(1)}, u32[]{:S(2)}, u32[]{:S(2)}) collective-permute-start(f32[144,128]{1,0:T(8,128)S(1)} %get-tuple-element.37), channel_id=1, source_target_pairs={{1,0},{2,1},{3,2},{5,4},{6,5},{7,6},{9,8},{10,9},{11,10},{13,12},{... | collective-permute-start | bytes 221192 | tf_op jit(solution)/shard_map/ppermute | solution.py:431
  65.8 7.2 %collective-permute-start.10 = (f32[144,128]{1,0:T(8,128)S(1)}, f32[144,128]{1,0:T(8,128)S(1)}, u32[]{:S(2)}, u32[]{:S(2)}) collective-permute-start(f32[144,128]{1,0:T(8,128)S(1)} %get-tuple-element.40), channel_id=1, source_target_pairs={{1,0},{2,1},{3,2},{5,4},{6,5},{7,6},{9,8},{10,9},{11,10},{13,12},{... | collective-permute-start | bytes 221192 | tf_op jit(solution)/shard_map/ppermute | solution.py:431
  67.9 5.1 %collective-permute-start.9 = (f32[96,128]{1,0:T(8,128)S(1)}, f32[96,128]{1,0:T(8,128)S(1)}, u32[]{:S(2)}, u32[]{:S(2)}) collective-permute-start(f32[96,128]{1,0:T(8,128)S(1)} %get-tuple-element.39), channel_id=1, source_target_pairs={{0,1},{1,2},{2,3},{4,5},{5,6},{6,7},{8,9},{9,10},{10,11},{12,13},{... | collective-permute-start | bytes 147464 | tf_op jit(solution)/shard_map/ppermute | solution.py:432
  82.4 6.4 %collective-permute-start.11 = (f32[12,4,8,128]{3,2,1,0:T(8,128)S(1)}, f32[12,4,8,128]{3,2,1,0:T(8,128)S(1)}, u32[]{:S(2)}, u32[]{:S(2)}) collective-permute-start(f32[12,4,8,128]{3,2,1,0:T(8,128)S(1)} %get-tuple-element.42), channel_id=1, source_target_pairs={{0,4},{4,0},{8,12},{12,8},{16,20},{20,16},{24,28},{28,24},{1,5},{5... | collective-permute-start | bytes 589832 | tf_op jit(solution)/shard_map/ppermute | solution.py:425
  85.3 6.5 %collective-permute-start.12 = (f32[12,4,8,128]{3,2,1,0:T(8,128)S(1)}, f32[12,4,8,128]{3,2,1,0:T(8,128)S(1)}, u32[]{:S(2)}, u32[]{:S(2)}) collective-permute-start(f32[12,4,8,128]{3,2,1,0:T(8,128)S(1)} %get-tuple-element.43), channel_id=1, source_target_pairs={{0,8},{4,12},{8,0},{12,4},{16,24},{20,28},{24,16},{28,20},{1,9},{5... | collective-permute-start | bytes 589832 | tf_op jit(solution)/shard_map/ppermute | solution.py:425
  86.5 10.4 %collective-permute-start.13 = (f32[12,4,8,128]{3,2,1,0:T(8,128)S(1)}, f32[12,4,8,128]{3,2,1,0:T(8,128)S(1)}, u32[]{:S(2)}, u32[]{:S(2)}) collective-permute-start(f32[12,4,8,128]{3,2,1,0:T(8,128)S(1)} %get-tuple-element.44), channel_id=1, source_target_pairs={{0,12},{4,8},{8,4},{12,0},{16,28},{20,24},{24,20},{28,16},{1,13},{... | collective-permute-start | bytes 589832 | tf_op jit(solution)/shard_map/ppermute | solution.py:425
  87.0 9.9 %collective-permute-start.14 = (f32[12,4,8,128]{3,2,1,0:T(8,128)S(1)}, f32[12,4,8,128]{3,2,1,0:T(8,128)S(1)}, u32[]{:S(2)}, u32[]{:S(2)}) collective-permute-start(f32[12,4,8,128]{3,2,1,0:T(8,128)S(1)} %get-tuple-element.45), channel_id=1, source_target_pairs={{0,16},{4,20},{8,24},{12,28},{16,0},{20,4},{24,8},{28,12},{1,17},{... | collective-permute-start | bytes 589832 | tf_op jit(solution)/shard_map/ppermute | solution.py:425
  88.2 18.0 %collective-permute-start.15 = (f32[12,4,8,128]{3,2,1,0:T(8,128)S(1)}, f32[12,4,8,128]{3,2,1,0:T(8,128)S(1)}, u32[]{:S(2)}, u32[]{:S(2)}) collective-permute-start(f32[12,4,8,128]{3,2,1,0:T(8,128)S(1)} %get-tuple-element.46), channel_id=1, source_target_pairs={{0,20},{4,16},{8,28},{12,24},{16,4},{20,0},{24,12},{28,8},{1,21},{... | collective-permute-start | bytes 589832 | tf_op jit(solution)/shard_map/ppermute | solution.py:425
  88.8 17.5 %collective-permute-start.16 = (f32[12,4,8,128]{3,2,1,0:T(8,128)S(1)}, f32[12,4,8,128]{3,2,1,0:T(8,128)S(1)}, u32[]{:S(2)}, u32[]{:S(2)}) collective-permute-start(f32[12,4,8,128]{3,2,1,0:T(8,128)S(1)} %get-tuple-element.47), channel_id=1, source_target_pairs={{0,24},{4,28},{8,16},{12,20},{16,8},{20,12},{24,0},{28,4},{1,25},{... | collective-permute-start | bytes 589832 | tf_op jit(solution)/shard_map/ppermute | solution.py:425
  91.8 14.5 %collective-permute-start.17 = (f32[12,4,8,128]{3,2,1,0:T(8,128)S(1)}, f32[12,4,8,128]{3,2,1,0:T(8,128)S(1)}, u32[]{:S(2)}, u32[]{:S(2)}) collective-permute-start(f32[12,4,8,128]{3,2,1,0:T(8,128)S(1)} %get-tuple-element.48), channel_id=1, source_target_pairs={{0,28},{4,24},{8,20},{12,16},{16,12},{20,8},{24,4},{28,0},{1,29},{... | collective-permute-start | bytes 589832 | tf_op jit(solution)/shard_map/ppermute | solution.py:425

commit v2 on v0

--- a/solution.py
+++ b/solution.py
@@ -1,6 +1,10 @@
+import functools
+
 import jax
 import jax.numpy as jnp
 from jax import lax
+from jax.experimental import pallas as pl
+from jax.experimental.pallas import tpu as pltpu
 from jax.sharding import PartitionSpec as P
 
 NTR = 8
@@ -137,6 +141,515 @@
     return tracer_field
 
 
+LANES = 128
+TILE = 8
+PLANES = 4
+LOW = 2
+HIGH = 3
+TAPS = LOW + HIGH + 1
+OUTER = (0, 1, 6, 7)
+INNER = (2, 3, 4, 5)
+PAD = TILE
+COEFFS = 14
+MESH_LON = "lon"
+
+
+def lane_index():
+    return lax.broadcasted_iota(jnp.int32, (TILE, LANES), 1)
+
+
+def pick(values, index):
+    return jnp.take_along_axis(values, index, axis=1)
+
+
+def swap_blocks(items, masks):
+    for bit, mask in enumerate(masks):
+        items = [
+            jnp.where(mask, items[place ^ (1 << bit)], items[place])
+            for place in range(len(items))
+        ]
+    return items
+
+
+def lane_masks(lane, first, count):
+    return [(lane >> (first + bit)) & 1 == 1 for bit in range(count)]
+
+
+def at(tile, offset=0):
+    return slice(TILE * tile + offset, TILE * tile + offset + TILE)
+
+
+def row_runs(tiles):
+    runs = []
+    for place, tile in enumerate(tiles):
+        if runs and tiles[place - 1] + 1 == tile:
+            runs[-1][2] += 1
+        else:
+            runs.append([tile, place, 1])
+    return [(TILE * tile, TILE * place, TILE * count) for tile, place, count in runs]
+
+
+def pack_kernel(tiles, field_ref, *refs):
+    message_refs, (held, sems) = refs[:8], refs[8:]
+    levels = held.shape[0]
+    runs = row_runs(tiles)
+
+    def copies(k):
+        return [
+            pltpu.make_async_copy(
+                field_ref.at[k, pl.ds(source, count), :],
+                held.at[k, pl.ds(target, count), :],
+                sems.at[k, which],
+            )
+            for which, (source, target, count) in enumerate(runs)
+        ]
+
+    def begin(k, carry):
+        for copy in copies(k):
+            copy.start()
+        return carry
+
+    lax.fori_loop(0, levels, begin, 0)
+    me = lax.axis_index(MESH_LON)
+    lane = lane_index()
+    cell_masks = lane_masks(lane, 2, 2)
+    device_masks = lane_masks(lane, 4, 3)
+    base = ((lane & 3) << 5) | (((lane >> 2) & 3) << 3) | ((lane >> 4) ^ me)
+
+    def unit(u, carry):
+        by_group = []
+        for group in range(8):
+            k = 2 * u + group // 4
+            if group % 4 == 0:
+                for copy in copies(k):
+                    copy.wait()
+            parts = [
+                pick(
+                    held[k, at(group % 4), LANES * q : LANES * q + LANES],
+                    base ^ ((q << 3) | group),
+                )
+                for q in range(PLANES)
+            ]
+            by_group.append(swap_blocks(parts, cell_masks))
+        for plane in range(PLANES):
+            sent = swap_blocks([parts[plane] for parts in by_group], device_masks)
+            for mate in range(8):
+                message_refs[mate][u, plane] = sent[mate]
+        return carry
+
+    lax.fori_loop(0, levels // 2, unit, 0)
+
+
+def unpack_kernel(tiles, *refs):
+    message_refs, (field_ref, held, sems) = refs[:8], refs[-3:]
+    levels = held.shape[0]
+    runs = row_runs(tiles)
+
+    def copies(k):
+        return [
+            pltpu.make_async_copy(
+                held.at[k, pl.ds(source, count), :],
+                field_ref.at[k, pl.ds(target, count), :],
+                sems.at[k, which],
+            )
+            for which, (target, source, count) in enumerate(runs)
+        ]
+
+    me = lax.axis_index(MESH_LON)
+    lane = lane_index()
+    cell_masks = lane_masks(lane, 2, 2)
+    device_masks = lane_masks(lane, 4, 3)
+    base = (((lane & 7) ^ me) << 4) | (((lane >> 3) & 3) << 2) | (lane >> 5)
+
+    def unit(u, carry):
+        by_plane = [
+            swap_blocks([ref[u, plane] for ref in message_refs], device_masks)
+            for plane in range(PLANES)
+        ]
+        for group in range(8):
+            k = 2 * u + group // 4
+            parts = swap_blocks([planes[group] for planes in by_plane], cell_masks)
+            for q in range(PLANES):
+                held[k, at(group % 4), LANES * q : LANES * q + LANES] = pick(
+                    parts[q], base ^ ((group << 4) | (q << 2))
+                )
+            if group % 4 == 3:
+                for copy in copies(k):
+                    copy.start()
+        return carry
+
+    lax.fori_loop(0, levels // 2, unit, 0)
+
+    def end(k, carry):
+        for copy in copies(k):
+            copy.wait()
+        return carry
+
+    lax.fori_loop(0, levels, end, 0)
+
+
+def take_messages(message_refs, put):
+    me = lax.axis_index(MESH_LON)
+    lane = lane_index()
+    device_masks = lane_masks(lane, 4, 3)
+    base = lane ^ (me << 4)
+
+    def unit(u, carry):
+        for plane in range(PLANES):
+            groups = swap_blocks([ref[u, plane] for ref in message_refs], device_masks)
+            for group, values in enumerate(groups):
+                put(
+                    2 * u + group // 4,
+                    plane,
+                    group % 4,
+                    pick(values, base ^ ((group << 4) | (plane << 2))),
+                )
+        return carry
+
+    lax.fori_loop(0, message_refs[0].shape[0], unit, 0)
+
+
+def give_messages(message_refs, take):
+    me = lax.axis_index(MESH_LON)
+    lane = lane_index()
+    device_masks = lane_masks(lane, 4, 3)
+    base = lane ^ (me << 4)
+
+    def unit(u, carry):
+        for plane in range(PLANES):
+            groups = [
+                pick(
+                    take(2 * u + group // 4, plane, group % 4),
+                    base ^ ((group << 4) | (plane << 2)),
+                )
+                for group in range(8)
+            ]
+            for mate, values in enumerate(swap_blocks(groups, device_masks)):
+                message_refs[mate][u, plane] = values
+        return carry
+
+    lax.fori_loop(0, message_refs[0].shape[0], unit, 0)
+
+
+def put_up(up_ref, k, plane, first):
+    up_ref[pl.ds((k * PLANES + plane) * HIGH, HIGH), :] = first[:HIGH]
+
+
+def put_down(down_ref, k, plane, last):
+    down_ref[pl.ds((k * PLANES + plane) * LOW, LOW), :] = last[TILE - LOW :]
+
+
+def take_edges(low_ref, high_ref, padded, rows):
+    def level(k, carry):
+        for plane in range(PLANES):
+            place = k * PLANES + plane
+            padded[k, plane, PAD - LOW : PAD, :] = low_ref[pl.ds(place * LOW, LOW), :]
+            padded[k, plane, PAD + rows : PAD + rows + HIGH, :] = high_ref[
+                pl.ds(place * HIGH, HIGH), :
+            ]
+        return carry
+
+    lax.fori_loop(0, padded.shape[0], level, 0)
+
+
+def copy_tiles(source, target, pairs):
+    def level(k, carry):
+        for plane in range(PLANES):
+            for source_row, target_row, count in pairs:
+                target[k, plane, target_row : target_row + count, :] = source[
+                    k, plane, source_row : source_row + count, :
+                ]
+        return carry
+
+    lax.fori_loop(0, target.shape[0], level, 0)
+
+
+def interpolate(step, tiles, padded, coeff_ref, shift_ref, moved):
+    lane = lane_index()
+
+    def level(k, carry):
+        for tile in tiles:
+            weights = [coeff_ref[step, k, which, at(tile), :] for which in range(TAPS)]
+            planes = []
+            for plane in range(PLANES):
+                summed = None
+                for which, weight in enumerate(weights):
+                    addend = weight * padded[k, plane, at(tile, PAD + which - LOW), :]
+                    summed = addend if summed is None else summed + addend
+                planes.append(summed)
+            shift = shift_ref[step, k, at(tile), :]
+            low_bit = shift & 1 == 1
+            high_bit = shift & 2 == 2
+            planes = [jnp.where(low_bit, planes[v - 1], planes[v]) for v in range(PLANES)]
+            planes = [jnp.where(high_bit, planes[v - 2], planes[v]) for v in range(PLANES)]
+            first = lane - (shift >> 2)
+            least = shift & 3
+            planes = [
+                pick(values, jnp.where(least > v, first - 1, first) & (LANES - 1))
+                for v, values in enumerate(planes)
+            ]
+            wide = (
+                [pltpu.roll(planes[3], 1, 1)]
+                + planes
+                + [pltpu.roll(planes[0], LANES - 1, 1), pltpu.roll(planes[1], LANES - 1, 1)]
+            )
+            taps = [coeff_ref[step, k, which, at(tile), :] for which in range(TAPS, TAPS + 4)]
+            for plane in range(PLANES):
+                summed = taps[0] * wide[plane]
+                for which in range(1, 4):
+                    summed = summed + taps[which] * wide[plane + which]
+                moved[k, plane, at(tile), :] = summed
+        return carry
+
+    lax.fori_loop(0, padded.shape[0], level, 0)
+
+
+def solve(step, tiles, moved, coeff_ref, put):
+    levels = moved.shape[0]
+    for tile in tiles:
+        def column(plane, carry):
+            def coeff(k, which):
+                return coeff_ref[step, k, which, at(tile), :]
+
+            solved = []
+            values = moved[0, plane, at(tile), :]
+            for k in range(levels):
+                above = moved[k + 1, plane, at(tile), :] if k + 1 < levels else values
+                now = coeff(k, TAPS + 4) * values + coeff(k, TAPS + 5) * above
+                if k:
+                    now = now + coeff(k, TAPS + 6) * solved[k - 1]
+                solved.append(now)
+                values = above
+            for k in range(levels - 2, -1, -1):
+                solved[k] = solved[k] + coeff(k, TAPS + 7) * solved[k + 1]
+            for k in range(levels):
+                put(k, plane, tile, solved[k])
+            return carry
+
+        for plane in range(PLANES):
+            column(plane, 0)
+
+
+def outer_kernel(*refs):
+    message_refs, (field_ref, up_ref, down_ref) = refs[:8], refs[8:]
+
+    def put(k, plane, place, values):
+        field_ref[k, plane, at(place), :] = values
+        if place == 0:
+            put_up(up_ref, k, plane, values)
+        if place == len(OUTER) - 1:
+            put_down(down_ref, k, plane, values)
+
+    take_messages(message_refs, put)
+
+
+def edge_kernel(
+    field_ref, low_ref, high_ref, coeff_ref, shift_ref, next_ref, up_ref, down_ref, padded, moved
+):
+    take_edges(low_ref, high_ref, padded, 8 * TILE)
+    copy_tiles(field_ref, padded, [(0, PAD, 16), (16, PAD + 6 * TILE, 16)])
+    interpolate(0, (0, 7), padded, coeff_ref, shift_ref, moved)
+
+    def put(k, plane, tile, values):
+        next_ref[k, plane, at(tile and 1), :] = values
+        if tile == 0:
+            put_up(up_ref, k, plane, values)
+        else:
+            put_down(down_ref, k, plane, values)
+
+    solve(0, (0, 7), moved, coeff_ref, put)
+
+
+def inner_kernel(*refs):
+    incoming, outgoing = refs[:8], refs[11:19]
+    field_ref, coeff_ref, shift_ref = refs[8:11]
+    next_ref, padded, moved = refs[19:]
+
+    def put_field(k, plane, place, values):
+        padded[k, plane, at(INNER[place], PAD), :] = values
+
+    take_messages(incoming, put_field)
+    copy_tiles(field_ref, padded, [(0, PAD, 16), (16, PAD + 6 * TILE, 16)])
+    interpolate(0, (1, 2, 3, 4, 5, 6), padded, coeff_ref, shift_ref, moved)
+
+    def put_next(k, plane, tile, values):
+        padded[k, plane, at(tile, PAD), :] = values
+        if tile not in (3, 4):
+            next_ref[k, plane, at(tile if tile < 3 else tile - 2), :] = values
+
+    solve(0, (1, 2, 3, 4, 5, 6), moved, coeff_ref, put_next)
+    interpolate(1, INNER, padded, coeff_ref, shift_ref, moved)
+
+    def put_last(k, plane, tile, values):
+        moved[k, plane, at(tile), :] = values
+
+    solve(1, INNER, moved, coeff_ref, put_last)
+    give_messages(outgoing, lambda k, plane, place: moved[k, plane, at(INNER[place]), :])
+
+
+def last_kernel(near_ref, edge_ref, low_ref, high_ref, coeff_ref, shift_ref, *refs):
+    outgoing, (padded, moved) = refs[:8], refs[8:]
+    take_edges(low_ref, high_ref, padded, 8 * TILE)
+    copy_tiles(near_ref, padded, [(8, PAD + 8, 16), (24, PAD + 40, 16)])
+    copy_tiles(edge_ref, padded, [(0, PAD, 8), (8, PAD + 56, 8)])
+    interpolate(1, OUTER, padded, coeff_ref, shift_ref, moved)
+
+    def put_last(k, plane, tile, values):
+        moved[k, plane, at(tile), :] = values
+
+    solve(1, OUTER, moved, coeff_ref, put_last)
+    give_messages(outgoing, lambda k, plane, place: moved[k, plane, at(OUTER[place]), :])
+
+
+def coeff_kernel(
+    lon_shift_ref,
+    lon_frac_ref,
+    lat_shift_ref,
+    lat_frac_ref,
+    remap_ref,
+    diffusivity_ref,
+    coeff_ref,
+    shift_ref,
+    held,
+):
+    kappa = diffusivity_ref[...]
+    levels, rows = kappa.shape
+    steps = lon_frac_ref.shape[0]
+    face = 0.5 * (kappa[:-1] + kappa[1:])
+    zero = jnp.zeros_like(kappa[:1])
+    below = jnp.concatenate([zero, face], axis=0)
+    above = jnp.concatenate([face, zero], axis=0)
+    ratio = zero
+    pivots, ratios = [], []
+    for k in range(levels):
+        pivot = 1.0 + below[k : k + 1] + above[k : k + 1] + below[k : k + 1] * ratio
+        ratio = -above[k : k + 1] / pivot
+        pivots.append(pivot)
+        ratios.append(ratio)
+    pivot = jnp.concatenate(pivots, axis=0)
+    back = -jnp.concatenate(ratios, axis=0)
+    for step in range(steps):
+        lat_weights = cubic_weights(lat_frac_ref[step])
+        offset = lat_shift_ref[step]
+        columns = []
+        for row_delta in range(-LOW, HIGH + 1):
+            coeff = jnp.zeros_like(kappa)
+            for tap in range(4):
+                coeff = coeff + jnp.where(offset == tap - 1 - row_delta, lat_weights[tap], 0.0)
+            columns.append(coeff)
+        columns.extend(cubic_weights(lon_frac_ref[step]))
+        fraction = remap_ref[step]
+        columns.append((1.0 - fraction) / pivot)
+        columns.append(fraction / pivot)
+        columns.append(below / pivot)
+        columns.append(back)
+        columns.append(lon_shift_ref[step].astype(jnp.float32))
+        for which, column in enumerate(columns):
+            for k in range(levels):
+                held[step * levels + k, which : which + 1, :rows] = column[k : k + 1]
+
+    def spread(place, carry):
+        step, k = place // levels, place % levels
+        turned = held[place].T
+        for which in range(COEFFS + 1):
+            for tile in range(rows // TILE):
+                wide = jnp.broadcast_to(turned[at(tile), which : which + 1], (TILE, LANES))
+                if which < COEFFS:
+                    coeff_ref[step, k, which, at(tile), :] = wide
+                else:
+                    shift_ref[step, k, at(tile), :] = wide.astype(jnp.int32)
+        return carry
+
+    held[:, COEFFS + 1 :, :] = jnp.zeros((steps * levels, LANES - COEFFS - 1, LANES), jnp.float32)
+    lax.fori_loop(0, steps * levels, spread, 0)
+
+
+def call(kernel, out_shapes, scratch=(), **options):
+    return pl.pallas_call(
+        kernel,
+        out_shape=[
+            shape if isinstance(shape, jax.ShapeDtypeStruct) else jax.ShapeDtypeStruct(shape, jnp.float32)
+            for shape in out_shapes
+        ],
+        scratch_shapes=[
+            pltpu.VMEM(shape, jnp.float32) if isinstance(shape, tuple) else shape
+            for shape in scratch
+        ],
+        compiler_params=pltpu.CompilerParams(vmem_limit_bytes=40 * 2**20),
+        **options,
+    )
+
+
+def exchange(messages):
+    peers = lax.axis_size(MESH_LON)
+    received = [messages[0]]
+    for mate in range(1, peers):
+        received.append(
+            lax.ppermute(messages[mate], MESH_LON, [(i, i ^ mate) for i in range(peers)])
+        )
+    return received
+
+
+def exchange_rows(up, down):
+    count = lax.axis_size("lat")
+    high = lax.ppermute(up, "lat", [(i + 1, i) for i in range(count - 1)])
+    low = lax.ppermute(down, "lat", [(i, i + 1) for i in range(count - 1)])
+    return low, high
+
+
+def by_tracer(tracers, lon_shift, lon_frac, lat_shift, lat_frac, remap_frac, diffusivity):
+    levels, rows, columns = tracers.shape
+    steps = lon_shift.shape[0]
+    messages = [(levels // 2, PLANES, TILE, LANES)] * 8
+    half = (levels, PLANES, rows // 2, LANES)
+    edges = [(levels * PLANES * HIGH, LANES), (levels * PLANES * LOW, LANES)]
+    scratch = [
+        (levels, PLANES, rows + 2 * TILE, LANES),
+        (levels, PLANES, rows, LANES),
+    ]
+    held = [(levels, rows // 2, columns), pltpu.SemaphoreType.DMA((levels, 2))]
+    anywhere = pl.BlockSpec(memory_space=pl.ANY)
+    vmem = pl.BlockSpec(memory_space=pltpu.VMEM)
+
+    def pack(tiles):
+        return call(
+            functools.partial(pack_kernel, tiles), messages, held, in_specs=[anywhere]
+        )(tracers)
+
+    outer = exchange(pack(OUTER))
+    inner = exchange(pack(INNER))
+    coeff, shift = call(
+        coeff_kernel,
+        [
+            (steps, levels, COEFFS, rows, LANES),
+            jax.ShapeDtypeStruct((steps, levels, rows, LANES), jnp.int32),
+        ],
+        [(steps * levels, LANES, LANES)],
+    )(lon_shift, lon_frac, lat_shift, lat_frac, remap_frac, diffusivity)
+    field, up, down = call(outer_kernel, [half] + edges)(*outer)
+    low, high = exchange_rows(up, down)
+    edge, up, down = call(
+        edge_kernel, [(levels, PLANES, 2 * TILE, LANES)] + edges, scratch
+    )(field, low, high, coeff, shift)
+    low, high = exchange_rows(up, down)
+    *inner, near = call(inner_kernel, messages + [(levels, PLANES, 5 * TILE, LANES)], scratch)(
+        *inner, field, coeff, shift
+    )
+    inner = exchange(inner)
+    outer = exchange(call(last_kernel, messages, scratch)(near, edge, low, high, coeff, shift))
+    done = call(
+        functools.partial(unpack_kernel, INNER), [tracers.shape], held, out_specs=[anywhere]
+    )(*inner)[0]
+    return call(
+        functools.partial(unpack_kernel, OUTER),
+        [tracers.shape],
+        held,
+        in_specs=[vmem] * 8 + [anywhere],
+        out_specs=[anywhere],
+        input_output_aliases={8: 0},
+    )(*outer, done)[0]
+
+
 def solution(mesh):
     in_specs = (
         P(None, "lat", "lon"),
@@ -148,6 +661,11 @@
         P(None, "lat"),
     )
     out_specs = P(None, "lat", "lon")
+    def per_part(tracers, *fields):
+        _, rows, columns = tracers.shape
+        fits = mesh.shape["lon"] == NTR and columns == PLANES * LANES and rows == TILE * NTR
+        return (by_tracer if fits else per_device)(tracers, *fields)
+
     return jax.shard_map(
-        per_device, mesh=mesh, in_specs=in_specs, out_specs=out_specs, check_vma=False
+        per_part, mesh=mesh, in_specs=in_specs, out_specs=out_specs, check_vma=False
     )

time: 353 us -> 91.8 us (0.26)
  waiting for transfers between devices: 251 us -> 10.9 us
  Pallas kernels: 0 us -> 36.3 us
  starting transfers between devices: 72.2 us -> 39.7 us
  other arithmetic: 18.3 us -> 0 us
  local copies, waits for them, and re-layouts: 9.81 us -> 3.28 us
    ppermute x26 -> x32, waiting for transfers between devices: 251 us -> 10.9 us  [the longest x28 7.85 us: exchange(): lax.ppermute(messages[mate], MESH_LON, [(i, i ^ mate) for i in range(peer...]
    pallas_call x0 -> x9, Pallas kernels: none -> 36.3 us  [the longest x1 11.9 us: by_tracer(): call(inner_kernel, messages + [(levels, PLANES, 5 * TILE, LANES)], scratch)]
    ppermute x26 -> x32, starting transfers between devices: 72.2 us -> 39.7 us  [the longest x28 29.1 us: exchange(): lax.ppermute(messages[mate], MESH_LON, [(i, i ^ mate) for i in range(peer...]
    add x9 -> x0, other arithmetic: 8.57 us -> none  [the longest x2 5.04 us: lon_step(): summed = addend if summed is None else summed + addend]
    select_n x18 -> x0, other arithmetic: 7.05 us -> none  [the longest x12 5.76 us: move_rows(): current = jnp.where(bit_mask(ahead_amount, position), forward, current)]
    slice x27 -> x0, local copies, waits for them, and re-layouts: 6.31 us -> none  [the longest x12 1.92 us: move_rows(): from_west = from_behind(current[:, :, width_cols - step_cols:], 'lon', 1)]
  transfers between devices with their start and end apart: 26 -> 32, of which waited for: 23 -> 6; matrix products, arithmetic and copies ran while one was open for 1% -> 0% of each run, Pallas kernels for 0% -> 35%
where the time goes in v2:
time: 91.8 us; the launch traced here: 90.4 us
  starting transfers between devices  39.7 us (43%)
  Pallas kernels  36.3 us (40%)
  waiting for transfers between devices  10.9 us (12%)
  local copies, waits for them, and re-layouts  3.28 us (4%)
    ppermute x28, starting transfers between devices, exchange(): lax.ppermute(messages[mate], MESH_LON, [(i, i ^ mate) for i in range(peer...  29.1 us
    pallas_call x1, Pallas kernels, by_tracer(): call(inner_kernel, messages + [(levels, PLANES, 5 * TILE, LANES)], scratch)  11.9 us
    pallas_call x1, Pallas kernels, by_tracer(): call(coeff_kernel, [(steps, levels, COEFFS, rows, LANES), jax.ShapeDtypeS...  8.12 us
    ppermute x28, waiting for transfers between devices, exchange(): lax.ppermute(messages[mate], MESH_LON, [(i, i ^ mate) for i in range(peer...  7.85 us
    ppermute x2, starting transfers between devices, exchange_rows(): low = lax.ppermute(down, 'lat', [(i, i + 1) for i in range(count - 1)])  6.56 us
    pallas_call x2, Pallas kernels, pack(): call(functools.partial(pack_kernel, tiles), messages, held, in_specs=[any...  5.42 us
    ppermute x2, starting transfers between devices, exchange_rows(): high = lax.ppermute(up, 'lat', [(i + 1, i) for i in range(count - 1)])  3.99 us
    pallas_call x1, Pallas kernels, by_tracer(): call(last_kernel, messages, scratch)(near, edge, low, high, coeff, shift)  3.87 us
  transfers between devices with their start and end apart: 32, of which 6 were waited for; matrix products, arithmetic and copies ran while one was open for 0% of the time, Pallas kernels for 35%

profile of v2, /device:TPU:9, one launch (start us, length us, event | category | flops | bytes accessed | tf_op | source)
XLA Modules:
  0.0 90.4 jit_solution(12025781362504860247)
XLA Ops:
  0.0 1.4 %copy-done.2 = f32[12,64,512]{2,1,0:T(8,128)S(1)} copy-done((f32[12,64,512]{2,1,0:T(8,128)S(1)}, f32[12,64,512]{2,1,0:T(8,128)}, u32[]{:S(2)}) %copy-start.2) | copy-done | bytes 1572888
  1.4 2.7 %shard_map.74 = (f32[6,4,8,128]{3,2,1,0:T(8,128)S(1)}, f32[6,4,8,128]{3,2,1,0:T(8,128)S(1)}, f32[6,4,8,128]{3,2,1,0:T(8,128)S(1)}, f32[6,4,8,128]{3,2,1,0:T(8,12...) custom-call(f32[12,64,512]{2,1,0:T(8,128)S(1)} %copy-done.2), custom_call_target="tpu_custom_call" | custom-call | tf_op jit(solution)/shard_map/pallas_call | solution.py:615
  4.2 0.7 collective-permute-start.7
  5.0 1.2 %collective-permute-start.8 = (f32[6,4,8,128]{3,2,1,0:T(8,128)S(1)}, f32[6,4,8,128]{3,2,1,0:T(8,128)S(1)}, u32[]{:S(2)}, u32[]{:S(2)}) collective-permute-start(f32[6,4,8,128]{3,2,1,0:T(8,128)S(1)} %get-tuple-element.56), channel_id=1, source_target_pairs={{0,8},{4,12},{8,0},{12,4},{16,24},{20,28},{24,16},{28,20},{1,9},{5... | collective-permute-start | bytes 294920 | tf_op jit(solution)/shard_map/ppermute | solution.py:588
  6.2 0.5 collective-permute-start.9
  6.7 1.2 %collective-permute-start.10 = (f32[6,4,8,128]{3,2,1,0:T(8,128)S(1)}, f32[6,4,8,128]{3,2,1,0:T(8,128)S(1)}, u32[]{:S(2)}, u32[]{:S(2)}) collective-permute-start(f32[6,4,8,128]{3,2,1,0:T(8,128)S(1)} %get-tuple-element.58), channel_id=1, source_target_pairs={{0,16},{4,20},{8,24},{12,28},{16,0},{20,4},{24,8},{28,12},{1,17},{... | collective-permute-start | bytes 294920 | tf_op jit(solution)/shard_map/ppermute | solution.py:588
  7.9 0.6 collective-permute-start.11
  8.5 2.2 %collective-permute-start.12 = (f32[6,4,8,128]{3,2,1,0:T(8,128)S(1)}, f32[6,4,8,128]{3,2,1,0:T(8,128)S(1)}, u32[]{:S(2)}, u32[]{:S(2)}) collective-permute-start(f32[6,4,8,128]{3,2,1,0:T(8,128)S(1)} %get-tuple-element.60), channel_id=1, source_target_pairs={{0,24},{4,28},{8,16},{12,20},{16,8},{20,12},{24,0},{28,4},{1,25},{... | collective-permute-start | bytes 294920 | tf_op jit(solution)/shard_map/ppermute | solution.py:588
  10.6 2.0 %collective-permute-start.13 = (f32[6,4,8,128]{3,2,1,0:T(8,128)S(1)}, f32[6,4,8,128]{3,2,1,0:T(8,128)S(1)}, u32[]{:S(2)}, u32[]{:S(2)}) collective-permute-start(f32[6,4,8,128]{3,2,1,0:T(8,128)S(1)} %get-tuple-element.61), channel_id=1, source_target_pairs={{0,28},{4,24},{8,20},{12,16},{16,12},{20,8},{24,4},{28,0},{1,29},{... | collective-permute-start | bytes 294920 | tf_op jit(solution)/shard_map/ppermute | solution.py:588
  12.7 2.7 %shard_map.73 = (f32[6,4,8,128]{3,2,1,0:T(8,128)S(1)}, f32[6,4,8,128]{3,2,1,0:T(8,128)S(1)}, f32[6,4,8,128]{3,2,1,0:T(8,128)S(1)}, f32[6,4,8,128]{3,2,1,0:T(8,12...) custom-call(f32[12,64,512]{2,1,0:T(8,128)S(1)} %copy-done.2), custom_call_target="tpu_custom_call" | custom-call | tf_op jit(solution)/shard_map/pallas_call | solution.py:615
  15.5 0.3 collective-permute-start.1
  15.8 1.7 %collective-permute-done.11.refs_5_ = f32[6,4,8,128]{3,2,1,0:T(8,128)S(1)} collective-permute-done((f32[6,4,8,128]{3,2,1,0:T(8,128)S(1)}, f32[6,4,8,128]{3,2,1,0:T(8,128)S(1)}, u32[]{:S(2)}, u32[]{:S(2)}) %collective-permute-start.11) | collective-permute-done | bytes 98336 | tf_op jit(solution)/shard_map/ppermute | solution.py:588
  17.5 0.9 %shard_map.75 = (f32[12,4,32,128]{3,2,1,0:T(8,128)S(1)}, f32[144,128]{1,0:T(8,128)S(1)}, f32[96,128]{1,0:T(8,128)S(1)}) custom-call(f32[6,4,8,128]{3,2,1,0:T(8,128)S(1)} %get-tuple-element.54.refs_0_, f32[6,4,8,128]{3,2,1,0:T(8,128)S(1)} %collective-permute-done.7.refs_1_, f32[6,4,8,128]{3,2,1,0:T(8,128)S(1)} %collective-permute-done.8.refs_2_, ...), custom_call_target="tpu_custom_call" | custom-call | tf_op jit(solution)/shard_map/pallas_call | solution.py:629
  18.5 1.9 %collective-permute-start.15 = (f32[144,128]{1,0:T(8,128)S(1)}, f32[144,128]{1,0:T(8,128)S(1)}, u32[]{:S(2)}, u32[]{:S(2)}) collective-permute-start(f32[144,128]{1,0:T(8,128)S(1)} %get-tuple-element.67), channel_id=1, source_target_pairs={{1,0},{2,1},{3,2},{5,4},{6,5},{7,6},{9,8},{10,9},{11,10},{13,12},{... | collective-permute-start | bytes 221192 | tf_op jit(solution)/shard_map/ppermute | solution.py:595
  20.4 3.4 %collective-permute-start.14 = (f32[96,128]{1,0:T(8,128)S(1)}, f32[96,128]{1,0:T(8,128)S(1)}, u32[]{:S(2)}, u32[]{:S(2)}) collective-permute-start(f32[96,128]{1,0:T(8,128)S(1)} %get-tuple-element.66), channel_id=1, source_target_pairs={{0,1},{1,2},{2,3},{4,5},{5,6},{6,7},{8,9},{9,10},{10,11},{12,13},{... | collective-permute-start | bytes 147464 | tf_op jit(solution)/shard_map/ppermute | solution.py:596
  23.8 1.9 %collective-permute-start.2 = (f32[6,4,8,128]{3,2,1,0:T(8,128)S(1)}, f32[6,4,8,128]{3,2,1,0:T(8,128)S(1)}, u32[]{:S(2)}, u32[]{:S(2)}) collective-permute-start(f32[6,4,8,128]{3,2,1,0:T(8,128)S(1)} %get-tuple-element.49), channel_id=1, source_target_pairs={{0,12},{4,8},{8,4},{12,0},{16,28},{20,24},{24,20},{28,16},{1,13},{... | collective-permute-start | bytes 294920 | tf_op jit(solution)/shard_map/ppermute | solution.py:588
  25.6 1.2 %collective-permute-start.3 = (f32[6,4,8,128]{3,2,1,0:T(8,128)S(1)}, f32[6,4,8,128]{3,2,1,0:T(8,128)S(1)}, u32[]{:S(2)}, u32[]{:S(2)}) collective-permute-start(f32[6,4,8,128]{3,2,1,0:T(8,128)S(1)} %get-tuple-element.50), channel_id=1, source_target_pairs={{0,16},{4,20},{8,24},{12,28},{16,0},{20,4},{24,8},{28,12},{1,17},{... | collective-permute-start | bytes 294920 | tf_op jit(solution)/shard_map/ppermute | solution.py:588
  26.8 0.2 collective-permute-start.4
  27.1 1.3 %collective-permute-start.5 = (f32[6,4,8,128]{3,2,1,0:T(8,128)S(1)}, f32[6,4,8,128]{3,2,1,0:T(8,128)S(1)}, u32[]{:S(2)}, u32[]{:S(2)}) collective-permute-start(f32[6,4,8,128]{3,2,1,0:T(8,128)S(1)} %get-tuple-element.52), channel_id=1, source_target_pairs={{0,24},{4,28},{8,16},{12,20},{16,8},{20,12},{24,0},{28,4},{1,25},{... | collective-permute-start | bytes 294920 | tf_op jit(solution)/shard_map/ppermute | solution.py:588
  28.4 1.6 %collective-permute-start.6 = (f32[6,4,8,128]{3,2,1,0:T(8,128)S(1)}, f32[6,4,8,128]{3,2,1,0:T(8,128)S(1)}, u32[]{:S(2)}, u32[]{:S(2)}) collective-permute-start(f32[6,4,8,128]{3,2,1,0:T(8,128)S(1)} %get-tuple-element.53), channel_id=1, source_target_pairs={{0,28},{4,24},{8,20},{12,16},{16,12},{20,8},{24,4},{28,0},{1,29},{... | collective-permute-start | bytes 294920 | tf_op jit(solution)/shard_map/ppermute | solution.py:588
  30.1 8.1 %shard_map.76 = (f32[2,12,14,64,128]{4,3,2,1,0:T(8,128)S(1)}, s32[2,12,64,128]{3,2,1,0:T(8,128)S(1)}) custom-call(s32[2,12,64]{2,1,0:T(8,128)S(1)} %copy.9.lon_shift_ref, f32[2,12,64]{2,1,0:T(8,128)S(1)} %copy.10.lon_frac_ref, s32[2,12,64]{2,1,0:T(8,128)S(1)} %copy.11.lat_shift_ref, f32[2,12,64]{2,1,0:T(8,128)S(1)} %copy.12.lat_frac_ref, ...), custom_call_target="tpu_custom_call" | custom-call | tf_op jit(solution)/shard_map/pallas_call | solution.py:621
  38.3 2.4 %shard_map.78 = (f32[12,4,16,128]{3,2,1,0:T(8,128)S(1)}, f32[144,128]{1,0:T(8,128)S(1)}, f32[96,128]{1,0:T(8,128)S(1)}) custom-call(f32[12,4,32,128]{3,2,1,0:T(8,128)S(1)} %get-tuple-element.62.refs_8_.field_ref, f32[96,128]{1,0:T(8,128)S(1)} %collective-permute-done.14.low_ref, f32[144,128]{1,0:T(8,128)S(1)} %collective-permute-done.15.high_ref, ...), custom_call_target="tpu_custom_call" | custom-call | tf_op jit(solution)/shard_map/pallas_call | solution.py:631
  40.6 1.8 %copy-done = f32[2,12,14,64,128]{4,3,2,1,0:T(8,128)} copy-done((f32[2,12,14,64,128]{4,3,2,1,0:T(8,128)}, f32[2,12,14,64,128]{4,3,2,1,0:T(8,128)S(1)}, u32[]{:S(2)}) %copy-start) | copy-done | bytes 11010072
  42.4 3.2 %collective-permute-start.16 = (f32[96,128]{1,0:T(8,128)S(1)}, f32[96,128]{1,0:T(8,128)S(1)}, u32[]{:S(2)}, u32[]{:S(2)}) collective-permute-start(f32[96,128]{1,0:T(8,128)S(1)} %get-tuple-element.69), channel_id=1, source_target_pairs={{0,1},{1,2},{2,3},{4,5},{5,6},{6,7},{8,9},{9,10},{10,11},{12,13},{... | collective-permute-start | bytes 147464 | tf_op jit(solution)/shard_map/ppermute | solution.py:596
  45.7 11.9 %shard_map.77 = (f32[6,4,8,128]{3,2,1,0:T(8,128)S(1)}, f32[6,4,8,128]{3,2,1,0:T(8,128)S(1)}, f32[6,4,8,128]{3,2,1,0:T(8,128)S(1)}, f32[6,4,8,128]{3,2,1,0:T(8,12...) custom-call(f32[6,4,8,128]{3,2,1,0:T(8,128)S(1)} %get-tuple-element., ...), custom_call_target="tpu_custom_call" | custom-call | tf_op jit(solution)/shard_map/pallas_call | solution.py:635
  57.6 0.1 collective-permute-start.25
  57.7 0.7 collective-permute-start.26
  58.4 1.4 %collective-permute-start.27 = (f32[6,4,8,128]{3,2,1,0:T(8,128)S(1)}, f32[6,4,8,128]{3,2,1,0:T(8,128)S(1)}, u32[]{:S(2)}, u32[]{:S(2)}) collective-permute-start(f32[6,4,8,128]{3,2,1,0:T(8,128)S(1)} %get-tuple-element.82), channel_id=1, source_target_pairs={{0,12},{4,8},{8,4},{12,0},{16,28},{20,24},{24,20},{28,16},{1,13},{... | collective-permute-start | bytes 294920 | tf_op jit(solution)/shard_map/ppermute | solution.py:588
  59.8 1.2 %collective-permute-start.28 = (f32[6,4,8,128]{3,2,1,0:T(8,128)S(1)}, f32[6,4,8,128]{3,2,1,0:T(8,128)S(1)}, u32[]{:S(2)}, u32[]{:S(2)}) collective-permute-start(f32[6,4,8,128]{3,2,1,0:T(8,128)S(1)} %get-tuple-element.83), channel_id=1, source_target_pairs={{0,16},{4,20},{8,24},{12,28},{16,0},{20,4},{24,8},{28,12},{1,17},{... | collective-permute-start | bytes 294920 | tf_op jit(solution)/shard_map/ppermute | solution.py:588
  61.0 2.1 %collective-permute-start.17 = (f32[144,128]{1,0:T(8,128)S(1)}, f32[144,128]{1,0:T(8,128)S(1)}, u32[]{:S(2)}, u32[]{:S(2)}) collective-permute-start(f32[144,128]{1,0:T(8,128)S(1)} %get-tuple-element.70), channel_id=1, source_target_pairs={{1,0},{2,1},{3,2},{5,4},{6,5},{7,6},{9,8},{10,9},{11,10},{13,12},{... | collective-permute-start | bytes 221192 | tf_op jit(solution)/shard_map/ppermute | solution.py:595
  63.1 3.0 %collective-permute-done.17.high_ref = f32[144,128]{1,0:T(8,128)S(1)} collective-permute-done((f32[144,128]{1,0:T(8,128)S(1)}, f32[144,128]{1,0:T(8,128)S(1)}, u32[]{:S(2)}, u32[]{:S(2)}) %collective-permute-start.17) | collective-permute-done | bytes 73760 | tf_op jit(solution)/shard_map/ppermute | solution.py:595
  66.1 1.6 %collective-permute-start.29 = (f32[6,4,8,128]{3,2,1,0:T(8,128)S(1)}, f32[6,4,8,128]{3,2,1,0:T(8,128)S(1)}, u32[]{:S(2)}, u32[]{:S(2)}) collective-permute-start(f32[6,4,8,128]{3,2,1,0:T(8,128)S(1)} %get-tuple-element.84), channel_id=1, source_target_pairs={{0,20},{4,16},{8,28},{12,24},{16,4},{20,0},{24,12},{28,8},{1,21},{... | collective-permute-start | bytes 294920 | tf_op jit(solution)/shard_map/ppermute | solution.py:588
  67.7 3.9 %shard_map.79 = (f32[6,4,8,128]{3,2,1,0:T(8,128)S(1)}, f32[6,4,8,128]{3,2,1,0:T(8,128)S(1)}, f32[6,4,8,128]{3,2,1,0:T(8,128)S(1)}, f32[6,4,8,128]{3,2,1,0:T(8,12...) custom-call(f32[12,4,40,128]{3,2,1,0:T(8,128)S(1)} %get-tuple-elemen, ...), custom_call_target="tpu_custom_call" | custom-call | tf_op jit(solution)/shard_map/pallas_call | solution.py:639
  71.6 1.7 %collective-permute-start.30 = (f32[6,4,8,128]{3,2,1,0:T(8,128)S(1)}, f32[6,4,8,128]{3,2,1,0:T(8,128)S(1)}, u32[]{:S(2)}, u32[]{:S(2)}) collective-permute-start(f32[6,4,8,128]{3,2,1,0:T(8,128)S(1)} %get-tuple-element.85), channel_id=1, source_target_pairs={{0,24},{4,28},{8,16},{12,20},{16,8},{20,12},{24,0},{28,4},{1,25},{... | collective-permute-start | bytes 294920 | tf_op jit(solution)/shard_map/ppermute | solution.py:588
  73.3 0.9 %collective-permute-start.31 = (f32[6,4,8,128]{3,2,1,0:T(8,128)S(1)}, f32[6,4,8,128]{3,2,1,0:T(8,128)S(1)}, u32[]{:S(2)}, u32[]{:S(2)}) collective-permute-start(f32[6,4,8,128]{3,2,1,0:T(8,128)S(1)} %get-tuple-element.86), channel_id=1, source_target_pairs={{0,28},{4,24},{8,20},{12,16},{16,12},{20,8},{24,4},{28,0},{1,29},{... | collective-permute-start | bytes 294920 | tf_op jit(solution)/shard_map/ppermute | solution.py:588
  74.2 0.3 collective-permute-start.18
  74.5 0.7 collective-permute-start.19
  75.1 1.2 %collective-permute-start.20 = (f32[6,4,8,128]{3,2,1,0:T(8,128)S(1)}, f32[6,4,8,128]{3,2,1,0:T(8,128)S(1)}, u32[]{:S(2)}, u32[]{:S(2)}) collective-permute-start(f32[6,4,8,128]{3,2,1,0:T(8,128)S(1)} %get-tuple-element.74), channel_id=1, source_target_pairs={{0,12},{4,8},{8,4},{12,0},{16,28},{20,24},{24,20},{28,16},{1,13},{... | collective-permute-start | bytes 294920 | tf_op jit(solution)/shard_map/ppermute | solution.py:588
  76.4 0.7 collective-permute-done.30.refs_6_
  77.1 1.1 %collective-permute-start.21 = (f32[6,4,8,128]{3,2,1,0:T(8,128)S(1)}, f32[6,4,8,128]{3,2,1,0:T(8,128)S(1)}, u32[]{:S(2)}, u32[]{:S(2)}) collective-permute-start(f32[6,4,8,128]{3,2,1,0:T(8,128)S(1)} %get-tuple-element.75), channel_id=1, source_target_pairs={{0,16},{4,20},{8,24},{12,28},{16,0},{20,4},{24,8},{28,12},{1,17},{... | collective-permute-start | bytes 294920 | tf_op jit(solution)/shard_map/ppermute | solution.py:588
  78.2 1.4 %collective-permute-done.31.refs_7_ = f32[6,4,8,128]{3,2,1,0:T(8,128)S(1)} collective-permute-done((f32[6,4,8,128]{3,2,1,0:T(8,128)S(1)}, f32[6,4,8,128]{3,2,1,0:T(8,128)S(1)}, u32[]{:S(2)}, u32[]{:S(2)}) %collective-permute-start.31) | collective-permute-done | bytes 98336 | tf_op jit(solution)/shard_map/ppermute | solution.py:588
  79.6 1.3 %collective-permute-start.22 = (f32[6,4,8,128]{3,2,1,0:T(8,128)S(1)}, f32[6,4,8,128]{3,2,1,0:T(8,128)S(1)}, u32[]{:S(2)}, u32[]{:S(2)}) collective-permute-start(f32[6,4,8,128]{3,2,1,0:T(8,128)S(1)} %get-tuple-element.76), channel_id=1, source_target_pairs={{0,20},{4,16},{8,28},{12,24},{16,4},{20,0},{24,12},{28,8},{1,21},{... | collective-permute-start | bytes 294920 | tf_op jit(solution)/shard_map/ppermute | solution.py:588
  80.8 0.5 collective-permute-start.23
  81.3 0.2 collective-permute-done.19.refs_2_
  81.5 1.4 %collective-permute-start.24 = (f32[6,4,8,128]{3,2,1,0:T(8,128)S(1)}, f32[6,4,8,128]{3,2,1,0:T(8,128)S(1)}, u32[]{:S(2)}, u32[]{:S(2)}) collective-permute-start(f32[6,4,8,128]{3,2,1,0:T(8,128)S(1)} %get-tuple-element.78), channel_id=1, source_target_pairs={{0,28},{4,24},{8,20},{12,16},{16,12},{20,8},{24,4},{28,0},{1,29},{... | collective-permute-start | bytes 294920 | tf_op jit(solution)/shard_map/ppermute | solution.py:588
  82.9 1.8 %shard_map.80.refs_8_ = f32[12,64,512]{2,1,0:T(8,128)} custom-call(f32[6,4,8,128]{3,2,1,0:T(8,128)S(1)} %get-tuple-element.79.refs_0_, f32[6,4,8,128]{3,2,1,0:T(8,128)S(1)} %collective-permute-done.25.refs_1_, f32[6,4,8,128]{3,2,1,0:T(8,128)S(1)} %collective-permute-done.26.refs_2_, f32[6,4,8,128]{3,2,1,0:T(8,128)S(1)} %collective-permute-done.27.refs_3_, ...), custom_call_target="tpu_custom_call" | custom-call | tf_op jit(solution)/shard_map/pallas_call | solution.py:640
  84.8 3.8 %collective-permute-done.22.refs_5_ = f32[6,4,8,128]{3,2,1,0:T(8,128)S(1)} collective-permute-done((f32[6,4,8,128]{3,2,1,0:T(8,128)S(1)}, f32[6,4,8,128]{3,2,1,0:T(8,128)S(1)}, u32[]{:S(2)}, u32[]{:S(2)}) %collective-permute-start.22) | collective-permute-done | bytes 98336 | tf_op jit(solution)/shard_map/ppermute | solution.py:588
  88.6 1.8 %shard_map.81 = f32[12,64,512]{2,1,0:T(8,128)} custom-call(f32[6,4,8,128]{3,2,1,0:T(8,128)S(1)} %get-tuple-element.71.refs_0_, f32[6,4,8,128]{3,2,1,0:T(8,128)S(1)} %collective-permute-done.18.refs_1_, f32[6,4,8,128]{3,2,1,0:T(8,128)S(1)} %collective-permute-done.19.refs_2_, ...), custom_call_target="tpu_custom_call", output_to_operand_aliasing={{}: (8, {})} | custom-call | tf_op jit(solution)/shard_map/pallas_call | solution.py:643
  (48 shorter events, 0.2 us)
Async XLA Ops:
  0.0 1.4 %copy-start.2 = (f32[12,64,512]{2,1,0:T(8,128)S(1)}, f32[12,64,512]{2,1,0:T(8,128)}, u32[]{:S(2)}) copy-start(f32[12,64,512]{2,1,0:T(8,128)} %field_ref.3) | copy-start | bytes 4718596
  4.1 25.9 %copy-start.4 = (s32[2,12,64]{2,0,1:T(2,128)S(1)}, s32[2,12,64]{2,0,1:T(2,128)}, u32[]{:S(2)}) copy-start(s32[2,12,64]{2,0,1:T(2,128)} %param.8) | copy-start | bytes 18436
  4.2 25.9 %copy-start.5 = (f32[2,12,64]{2,0,1:T(2,128)S(1)}, f32[2,12,64]{2,0,1:T(2,128)}, u32[]{:S(2)}) copy-start(f32[2,12,64]{2,0,1:T(2,128)} %param.9) | copy-start | bytes 18436
  4.2 25.9 %copy-start.6 = (s32[2,12,64]{2,0,1:T(2,128)S(1)}, s32[2,12,64]{2,0,1:T(2,128)}, u32[]{:S(2)}) copy-start(s32[2,12,64]{2,0,1:T(2,128)} %param.10) | copy-start | bytes 18436
  4.2 25.9 %copy-start.7 = (f32[2,12,64]{2,0,1:T(2,128)S(1)}, f32[2,12,64]{2,0,1:T(2,128)}, u32[]{:S(2)}) copy-start(f32[2,12,64]{2,0,1:T(2,128)} %param.11) | copy-start | bytes 18436
  4.2 25.9 %copy-start.8 = (f32[2,12,64]{2,0,1:T(2,128)S(1)}, f32[2,12,64]{2,0,1:T(2,128)}, u32[]{:S(2)}) copy-start(f32[2,12,64]{2,0,1:T(2,128)} %param.12) | copy-start | bytes 18436
  4.2 25.9 %copy-start.3 = (f32[12,64]{1,0:T(8,128)S(1)}, f32[12,64]{1,0:T(8,128)}, u32[]{:S(2)}) copy-start(f32[12,64]{1,0:T(8,128)} %diffusivity_ref.1) | copy-start | bytes 9220
  4.2 4.3 %collective-permute-start.7 = (f32[6,4,8,128]{3,2,1,0:T(8,128)S(1)}, f32[6,4,8,128]{3,2,1,0:T(8,128)S(1)}, u32[]{:S(2)}, u32[]{:S(2)}) collective-permute-start(f32[6,4,8,128]{3,2,1,0:T(8,128)S(1)} %get-tuple-element.55), channel_id=1, source_target_pairs={{0,4},{4,0},{8,12},{12,8},{16,20},{20,16},{24,28},{28,24},{1,5},{5... | collective-permute-start | bytes 294920 | tf_op jit(solution)/shard_map/ppermute | solution.py:588
  5.0 5.7 %collective-permute-start.8 = (f32[6,4,8,128]{3,2,1,0:T(8,128)S(1)}, f32[6,4,8,128]{3,2,1,0:T(8,128)S(1)}, u32[]{:S(2)}, u32[]{:S(2)}) collective-permute-start(f32[6,4,8,128]{3,2,1,0:T(8,128)S(1)} %get-tuple-element.56), channel_id=1, source_target_pairs={{0,8},{4,12},{8,0},{12,4},{16,24},{20,28},{24,16},{28,20},{1,9},{5... | collective-permute-start | bytes 294920 | tf_op jit(solution)/shard_map/ppermute | solution.py:588
  6.2 9.2 %collective-permute-start.9 = (f32[6,4,8,128]{3,2,1,0:T(8,128)S(1)}, f32[6,4,8,128]{3,2,1,0:T(8,128)S(1)}, u32[]{:S(2)}, u32[]{:S(2)}) collective-permute-start(f32[6,4,8,128]{3,2,1,0:T(8,128)S(1)} %get-tuple-element.57), channel_id=1, source_target_pairs={{0,12},{4,8},{8,4},{12,0},{16,28},{20,24},{24,20},{28,16},{1,13},{... | collective-permute-start | bytes 294920 | tf_op jit(solution)/shard_map/ppermute | solution.py:588
  6.7 8.8 %collective-permute-start.10 = (f32[6,4,8,128]{3,2,1,0:T(8,128)S(1)}, f32[6,4,8,128]{3,2,1,0:T(8,128)S(1)}, u32[]{:S(2)}, u32[]{:S(2)}) collective-permute-start(f32[6,4,8,128]{3,2,1,0:T(8,128)S(1)} %get-tuple-element.58), channel_id=1, source_target_pairs={{0,16},{4,20},{8,24},{12,28},{16,0},{20,4},{24,8},{28,12},{1,17},{... | collective-permute-start | bytes 294920 | tf_op jit(solution)/shard_map/ppermute | solution.py:588
  7.9 9.6 %collective-permute-start.11 = (f32[6,4,8,128]{3,2,1,0:T(8,128)S(1)}, f32[6,4,8,128]{3,2,1,0:T(8,128)S(1)}, u32[]{:S(2)}, u32[]{:S(2)}) collective-permute-start(f32[6,4,8,128]{3,2,1,0:T(8,128)S(1)} %get-tuple-element.59), channel_id=1, source_target_pairs={{0,20},{4,16},{8,28},{12,24},{16,4},{20,0},{24,12},{28,8},{1,21},{... | collective-permute-start | bytes 294920 | tf_op jit(solution)/shard_map/ppermute | solution.py:588
  8.5 9.0 %collective-permute-start.12 = (f32[6,4,8,128]{3,2,1,0:T(8,128)S(1)}, f32[6,4,8,128]{3,2,1,0:T(8,128)S(1)}, u32[]{:S(2)}, u32[]{:S(2)}) collective-permute-start(f32[6,4,8,128]{3,2,1,0:T(8,128)S(1)} %get-tuple-element.60), channel_id=1, source_target_pairs={{0,24},{4,28},{8,16},{12,20},{16,8},{20,12},{24,0},{28,4},{1,25},{... | collective-permute-start | bytes 294920 | tf_op jit(solution)/shard_map/ppermute | solution.py:588
  10.6 6.9 %collective-permute-start.13 = (f32[6,4,8,128]{3,2,1,0:T(8,128)S(1)}, f32[6,4,8,128]{3,2,1,0:T(8,128)S(1)}, u32[]{:S(2)}, u32[]{:S(2)}) collective-permute-start(f32[6,4,8,128]{3,2,1,0:T(8,128)S(1)} %get-tuple-element.61), channel_id=1, source_target_pairs={{0,28},{4,24},{8,20},{12,16},{16,12},{20,8},{24,4},{28,0},{1,29},{... | collective-permute-start | bytes 294920 | tf_op jit(solution)/shard_map/ppermute | solution.py:588
  15.4 10.2 %collective-permute-start = (f32[6,4,8,128]{3,2,1,0:T(8,128)S(1)}, f32[6,4,8,128]{3,2,1,0:T(8,128)S(1)}, u32[]{:S(2)}, u32[]{:S(2)}) collective-permute-start(f32[6,4,8,128]{3,2,1,0:T(8,128)S(1)} %get-tuple-element.47), channel_id=1, source_target_pairs={{0,4},{4,0},{8,12},{12,8},{16,20},{20,16},{24,28},{28,24},{1,5},{5... | collective-permute-start | bytes 294920 | tf_op jit(solution)/shard_map/ppermute | solution.py:588
  15.5 11.4 %collective-permute-start.1 = (f32[6,4,8,128]{3,2,1,0:T(8,128)S(1)}, f32[6,4,8,128]{3,2,1,0:T(8,128)S(1)}, u32[]{:S(2)}, u32[]{:S(2)}) collective-permute-start(f32[6,4,8,128]{3,2,1,0:T(8,128)S(1)} %get-tuple-element.48), channel_id=1, source_target_pairs={{0,8},{4,12},{8,0},{12,4},{16,24},{20,28},{24,16},{28,20},{1,9},{5... | collective-permute-start | bytes 294920 | tf_op jit(solution)/shard_map/ppermute | solution.py:588
  18.5 9.9 %collective-permute-start.15 = (f32[144,128]{1,0:T(8,128)S(1)}, f32[144,128]{1,0:T(8,128)S(1)}, u32[]{:S(2)}, u32[]{:S(2)}) collective-permute-start(f32[144,128]{1,0:T(8,128)S(1)} %get-tuple-element.67), channel_id=1, source_target_pairs={{1,0},{2,1},{3,2},{5,4},{6,5},{7,6},{9,8},{10,9},{11,10},{13,12},{... | collective-permute-start | bytes 221192 | tf_op jit(solution)/shard_map/ppermute | solution.py:595
  20.4 6.7 %collective-permute-start.14 = (f32[96,128]{1,0:T(8,128)S(1)}, f32[96,128]{1,0:T(8,128)S(1)}, u32[]{:S(2)}, u32[]{:S(2)}) collective-permute-start(f32[96,128]{1,0:T(8,128)S(1)} %get-tuple-element.66), channel_id=1, source_target_pairs={{0,1},{1,2},{2,3},{4,5},{5,6},{6,7},{8,9},{9,10},{10,11},{12,13},{... | collective-permute-start | bytes 147464 | tf_op jit(solution)/shard_map/ppermute | solution.py:596
  23.8 18.7 %collective-permute-start.2 = (f32[6,4,8,128]{3,2,1,0:T(8,128)S(1)}, f32[6,4,8,128]{3,2,1,0:T(8,128)S(1)}, u32[]{:S(2)}, u32[]{:S(2)}) collective-permute-start(f32[6,4,8,128]{3,2,1,0:T(8,128)S(1)} %get-tuple-element.49), channel_id=1, source_target_pairs={{0,12},{4,8},{8,4},{12,0},{16,28},{20,24},{24,20},{28,16},{1,13},{... | collective-permute-start | bytes 294920 | tf_op jit(solution)/shard_map/ppermute | solution.py:588
  25.6 20.0 %collective-permute-start.3 = (f32[6,4,8,128]{3,2,1,0:T(8,128)S(1)}, f32[6,4,8,128]{3,2,1,0:T(8,128)S(1)}, u32[]{:S(2)}, u32[]{:S(2)}) collective-permute-start(f32[6,4,8,128]{3,2,1,0:T(8,128)S(1)} %get-tuple-element.50), channel_id=1, source_target_pairs={{0,16},{4,20},{8,24},{12,28},{16,0},{20,4},{24,8},{28,12},{1,17},{... | collective-permute-start | bytes 294920 | tf_op jit(solution)/shard_map/ppermute | solution.py:588
  26.8 18.8 %collective-permute-start.4 = (f32[6,4,8,128]{3,2,1,0:T(8,128)S(1)}, f32[6,4,8,128]{3,2,1,0:T(8,128)S(1)}, u32[]{:S(2)}, u32[]{:S(2)}) collective-permute-start(f32[6,4,8,128]{3,2,1,0:T(8,128)S(1)} %get-tuple-element.51), channel_id=1, source_target_pairs={{0,20},{4,16},{8,28},{12,24},{16,4},{20,0},{24,12},{28,8},{1,21},{... | collective-permute-start | bytes 294920 | tf_op jit(solution)/shard_map/ppermute | solution.py:588
  27.1 18.6 %collective-permute-start.5 = (f32[6,4,8,128]{3,2,1,0:T(8,128)S(1)}, f32[6,4,8,128]{3,2,1,0:T(8,128)S(1)}, u32[]{:S(2)}, u32[]{:S(2)}) collective-permute-start(f32[6,4,8,128]{3,2,1,0:T(8,128)S(1)} %get-tuple-element.52), channel_id=1, source_target_pairs={{0,24},{4,28},{8,16},{12,20},{16,8},{20,12},{24,0},{28,4},{1,25},{... | collective-permute-start | bytes 294920 | tf_op jit(solution)/shard_map/ppermute | solution.py:588
  28.4 17.3 %collective-permute-start.6 = (f32[6,4,8,128]{3,2,1,0:T(8,128)S(1)}, f32[6,4,8,128]{3,2,1,0:T(8,128)S(1)}, u32[]{:S(2)}, u32[]{:S(2)}) collective-permute-start(f32[6,4,8,128]{3,2,1,0:T(8,128)S(1)} %get-tuple-element.53), channel_id=1, source_target_pairs={{0,28},{4,24},{8,20},{12,16},{16,12},{20,8},{24,4},{28,0},{1,29},{... | collective-permute-start | bytes 294920 | tf_op jit(solution)/shard_map/ppermute | solution.py:588
  38.3 4.2 %copy-start = (f32[2,12,14,64,128]{4,3,2,1,0:T(8,128)}, f32[2,12,14,64,128]{4,3,2,1,0:T(8,128)S(1)}, u32[]{:S(2)}) copy-start(f32[2,12,14,64,128]{4,3,2,1,0:T(8,128)S(1)} %get-tuple-element.63.refs_9_.coeff_ref) | copy-start | bytes 33030148
  42.4 18.6 %collective-permute-start.16 = (f32[96,128]{1,0:T(8,128)S(1)}, f32[96,128]{1,0:T(8,128)S(1)}, u32[]{:S(2)}, u32[]{:S(2)}) collective-permute-start(f32[96,128]{1,0:T(8,128)S(1)} %get-tuple-element.69), channel_id=1, source_target_pairs={{0,1},{1,2},{2,3},{4,5},{5,6},{6,7},{8,9},{9,10},{10,11},{12,13},{... | collective-permute-start | bytes 147464 | tf_op jit(solution)/shard_map/ppermute | solution.py:596
  45.7 22.1 %copy-start.1 = (f32[2,12,14,64,128]{4,3,2,1,0:T(8,128)S(1)}, f32[2,12,14,64,128]{4,3,2,1,0:T(8,128)}, u32[]{:S(2)}) copy-start(f32[2,12,14,64,128]{4,3,2,1,0:T(8,128)} %copy-done) | copy-start | bytes 33030148
  57.6 14.0 %collective-permute-start.25 = (f32[6,4,8,128]{3,2,1,0:T(8,128)S(1)}, f32[6,4,8,128]{3,2,1,0:T(8,128)S(1)}, u32[]{:S(2)}, u32[]{:S(2)}) collective-permute-start(f32[6,4,8,128]{3,2,1,0:T(8,128)S(1)} %get-tuple-element.80), channel_id=1, source_target_pairs={{0,4},{4,0},{8,12},{12,8},{16,20},{20,16},{24,28},{28,24},{1,5},{5... | collective-permute-start | bytes 294920 | tf_op jit(solution)/shard_map/ppermute | solution.py:588
  57.7 15.6 %collective-permute-start.26 = (f32[6,4,8,128]{3,2,1,0:T(8,128)S(1)}, f32[6,4,8,128]{3,2,1,0:T(8,128)S(1)}, u32[]{:S(2)}, u32[]{:S(2)}) collective-permute-start(f32[6,4,8,128]{3,2,1,0:T(8,128)S(1)} %get-tuple-element.81), channel_id=1, source_target_pairs={{0,8},{4,12},{8,0},{12,4},{16,24},{20,28},{24,16},{28,20},{1,9},{5... | collective-permute-start | bytes 294920 | tf_op jit(solution)/shard_map/ppermute | solution.py:588
  58.4 15.8 %collective-permute-start.27 = (f32[6,4,8,128]{3,2,1,0:T(8,128)S(1)}, f32[6,4,8,128]{3,2,1,0:T(8,128)S(1)}, u32[]{:S(2)}, u32[]{:S(2)}) collective-permute-start(f32[6,4,8,128]{3,2,1,0:T(8,128)S(1)} %get-tuple-element.82), channel_id=1, source_target_pairs={{0,12},{4,8},{8,4},{12,0},{16,28},{20,24},{24,20},{28,16},{1,13},{... | collective-permute-start | bytes 294920 | tf_op jit(solution)/shard_map/ppermute | solution.py:588
  59.8 14.7 %collective-permute-start.28 = (f32[6,4,8,128]{3,2,1,0:T(8,128)S(1)}, f32[6,4,8,128]{3,2,1,0:T(8,128)S(1)}, u32[]{:S(2)}, u32[]{:S(2)}) collective-permute-start(f32[6,4,8,128]{3,2,1,0:T(8,128)S(1)} %get-tuple-element.83), channel_id=1, source_target_pairs={{0,16},{4,20},{8,24},{12,28},{16,0},{20,4},{24,8},{28,12},{1,17},{... | collective-permute-start | bytes 294920 | tf_op jit(solution)/shard_map/ppermute | solution.py:588
  61.0 5.1 %collective-permute-start.17 = (f32[144,128]{1,0:T(8,128)S(1)}, f32[144,128]{1,0:T(8,128)S(1)}, u32[]{:S(2)}, u32[]{:S(2)}) collective-permute-start(f32[144,128]{1,0:T(8,128)S(1)} %get-tuple-element.70), channel_id=1, source_target_pairs={{1,0},{2,1},{3,2},{5,4},{6,5},{7,6},{9,8},{10,9},{11,10},{13,12},{... | collective-permute-start | bytes 221192 | tf_op jit(solution)/shard_map/ppermute | solution.py:595
  66.1 9.0 %collective-permute-start.29 = (f32[6,4,8,128]{3,2,1,0:T(8,128)S(1)}, f32[6,4,8,128]{3,2,1,0:T(8,128)S(1)}, u32[]{:S(2)}, u32[]{:S(2)}) collective-permute-start(f32[6,4,8,128]{3,2,1,0:T(8,128)S(1)} %get-tuple-element.84), channel_id=1, source_target_pairs={{0,20},{4,16},{8,28},{12,24},{16,4},{20,0},{24,12},{28,8},{1,21},{... | collective-permute-start | bytes 294920 | tf_op jit(solution)/shard_map/ppermute | solution.py:588
  71.6 5.4 %collective-permute-start.30 = (f32[6,4,8,128]{3,2,1,0:T(8,128)S(1)}, f32[6,4,8,128]{3,2,1,0:T(8,128)S(1)}, u32[]{:S(2)}, u32[]{:S(2)}) collective-permute-start(f32[6,4,8,128]{3,2,1,0:T(8,128)S(1)} %get-tuple-element.85), channel_id=1, source_target_pairs={{0,24},{4,28},{8,16},{12,20},{16,8},{20,12},{24,0},{28,4},{1,25},{... | collective-permute-start | bytes 294920 | tf_op jit(solution)/shard_map/ppermute | solution.py:588
  73.3 6.3 %collective-permute-start.31 = (f32[6,4,8,128]{3,2,1,0:T(8,128)S(1)}, f32[6,4,8,128]{3,2,1,0:T(8,128)S(1)}, u32[]{:S(2)}, u32[]{:S(2)}) collective-permute-start(f32[6,4,8,128]{3,2,1,0:T(8,128)S(1)} %get-tuple-element.86), channel_id=1, source_target_pairs={{0,28},{4,24},{8,20},{12,16},{16,12},{20,8},{24,4},{28,0},{1,29},{... | collective-permute-start | bytes 294920 | tf_op jit(solution)/shard_map/ppermute | solution.py:588
  74.2 6.6 %collective-permute-start.18 = (f32[6,4,8,128]{3,2,1,0:T(8,128)S(1)}, f32[6,4,8,128]{3,2,1,0:T(8,128)S(1)}, u32[]{:S(2)}, u32[]{:S(2)}) collective-permute-start(f32[6,4,8,128]{3,2,1,0:T(8,128)S(1)} %get-tuple-element.72), channel_id=1, source_target_pairs={{0,4},{4,0},{8,12},{12,8},{16,20},{20,16},{24,28},{28,24},{1,5},{5... | collective-permute-start | bytes 294920 | tf_op jit(solution)/shard_map/ppermute | solution.py:588
  74.5 7.0 %collective-permute-start.19 = (f32[6,4,8,128]{3,2,1,0:T(8,128)S(1)}, f32[6,4,8,128]{3,2,1,0:T(8,128)S(1)}, u32[]{:S(2)}, u32[]{:S(2)}) collective-permute-start(f32[6,4,8,128]{3,2,1,0:T(8,128)S(1)} %get-tuple-element.73), channel_id=1, source_target_pairs={{0,8},{4,12},{8,0},{12,4},{16,24},{20,28},{24,16},{28,20},{1,9},{5... | collective-permute-start | bytes 294920 | tf_op jit(solution)/shard_map/ppermute | solution.py:588
  75.1 9.6 %collective-permute-start.20 = (f32[6,4,8,128]{3,2,1,0:T(8,128)S(1)}, f32[6,4,8,128]{3,2,1,0:T(8,128)S(1)}, u32[]{:S(2)}, u32[]{:S(2)}) collective-permute-start(f32[6,4,8,128]{3,2,1,0:T(8,128)S(1)} %get-tuple-element.74), channel_id=1, source_target_pairs={{0,12},{4,8},{8,4},{12,0},{16,28},{20,24},{24,20},{28,16},{1,13},{... | collective-permute-start | bytes 294920 | tf_op jit(solution)/shard_map/ppermute | solution.py:588
  77.1 7.7 %collective-permute-start.21 = (f32[6,4,8,128]{3,2,1,0:T(8,128)S(1)}, f32[6,4,8,128]{3,2,1,0:T(8,128)S(1)}, u32[]{:S(2)}, u32[]{:S(2)}) collective-permute-start(f32[6,4,8,128]{3,2,1,0:T(8,128)S(1)} %get-tuple-element.75), channel_id=1, source_target_pairs={{0,16},{4,20},{8,24},{12,28},{16,0},{20,4},{24,8},{28,12},{1,17},{... | collective-permute-start | bytes 294920 | tf_op jit(solution)/shard_map/ppermute | solution.py:588
  79.6 9.0 %collective-permute-start.22 = (f32[6,4,8,128]{3,2,1,0:T(8,128)S(1)}, f32[6,4,8,128]{3,2,1,0:T(8,128)S(1)}, u32[]{:S(2)}, u32[]{:S(2)}) collective-permute-start(f32[6,4,8,128]{3,2,1,0:T(8,128)S(1)} %get-tuple-element.76), channel_id=1, source_target_pairs={{0,20},{4,16},{8,28},{12,24},{16,4},{20,0},{24,12},{28,8},{1,21},{... | collective-permute-start | bytes 294920 | tf_op jit(solution)/shard_map/ppermute | solution.py:588
  80.8 7.7 %collective-permute-start.23 = (f32[6,4,8,128]{3,2,1,0:T(8,128)S(1)}, f32[6,4,8,128]{3,2,1,0:T(8,128)S(1)}, u32[]{:S(2)}, u32[]{:S(2)}) collective-permute-start(f32[6,4,8,128]{3,2,1,0:T(8,128)S(1)} %get-tuple-element.77), channel_id=1, source_target_pairs={{0,24},{4,28},{8,16},{12,20},{16,8},{20,12},{24,0},{28,4},{1,25},{... | collective-permute-start | bytes 294920 | tf_op jit(solution)/shard_map/ppermute | solution.py:588
  81.5 7.1 %collective-permute-start.24 = (f32[6,4,8,128]{3,2,1,0:T(8,128)S(1)}, f32[6,4,8,128]{3,2,1,0:T(8,128)S(1)}, u32[]{:S(2)}, u32[]{:S(2)}) collective-permute-start(f32[6,4,8,128]{3,2,1,0:T(8,128)S(1)} %get-tuple-element.78), channel_id=1, source_target_pairs={{0,28},{4,24},{8,20},{12,16},{16,12},{20,8},{24,4},{28,0},{1,29},{... | collective-permute-start | bytes 294920 | tf_op jit(solution)/shard_map/ppermute | solution.py:588

commit v3 on v2

v3 whole, which is shorter than its diff:
```python
import functools

import jax
import jax.numpy as jnp
from jax import lax
from jax.experimental import pallas as pl
from jax.experimental.pallas import tpu as pltpu
from jax.sharding import PartitionSpec as P

NTR = 8
STEPS = 2


def from_behind(x, axis, by):
    peers = lax.axis_size(axis)
    return lax.ppermute(x, axis, [(i, (i + by) % peers) for i in range(peers)])


def with_halo(block, sides, width, periodic):
    for axis, dim in sides:
        count = lax.axis_size(axis)
        forward = [(i, i + 1) for i in range(count - 1)]
        if periodic:
            forward.append((count - 1, 0))
        backward = [(target, source) for source, target in forward]
        low = lax.ppermute(
            lax.slice_in_dim(block, block.shape[dim] - width, None, axis=dim), axis, forward
        )
        high = lax.ppermute(lax.slice_in_dim(block, 0, width, axis=dim), axis, backward)
        block = jnp.concatenate([low, block, high], axis=dim)
    return block


def cubic_weights(fraction):
    w_zero = -fraction * (fraction - 1.0) * (fraction - 2.0) / 6.0
    w_one = (fraction + 1.0) * (fraction - 1.0) * (fraction - 2.0) / 2.0
    w_two = -(fraction + 1.0) * fraction * (fraction - 2.0) / 2.0
    w_three = (fraction + 1.0) * fraction * (fraction - 1.0) / 6.0
    return (w_zero, w_one, w_two, w_three)


def lat_step(padded, offset, fraction, row_count):
    weights = cubic_weights(fraction)
    summed = None
    for place_index in range(6):
        row_delta = place_index - 2
        coeff = jnp.zeros_like(fraction)
        for tap_index in range(4):
            coeff = coeff + jnp.where(offset == tap_index - 1 - row_delta, weights[tap_index], 0.0)
        addend = coeff[:, :, None] * padded[:, 1 + place_index : 1 + place_index + row_count, :]
        summed = addend if summed is None else summed + addend
    return summed


def lon_step(wrapped, fraction, tracer_count):
    weights = cubic_weights(fraction)
    width_cols = wrapped.shape[2] - 4 * tracer_count
    summed = None
    for tap_index in range(4):
        offset_cols = (1 + tap_index) * tracer_count
        addend = (
            weights[tap_index][:, :, None] * wrapped[:, :, offset_cols : offset_cols + width_cols]
        )
        summed = addend if summed is None else summed + addend
    return summed


def remap(tracer_field, fraction):
    level_above = jnp.concatenate([tracer_field[1:], tracer_field[-1:]], axis=0)
    return (1.0 - fraction)[:, :, None] * tracer_field + fraction[:, :, None] * level_above


def diffuse(tracer_field, kappa):
    levels = tracer_field.shape[0]
    face_kappa = 0.5 * (kappa[:-1] + kappa[1:])
    zero_face = jnp.zeros_like(kappa[:1])
    face_below = jnp.concatenate([zero_face, face_kappa], axis=0)
    face_above = jnp.concatenate([face_kappa, zero_face], axis=0)
    ratio_prev = jnp.zeros_like(kappa[0])
    solved_prev = jnp.zeros_like(tracer_field[0])
    ratios = []
    solveds = []
    for level_index in range(levels):
        below = face_below[level_index]
        above = face_above[level_index]
        pivot_value = 1.0 + below + above + below * ratio_prev
        ratio_now = -above / pivot_value
        solved_now = (tracer_field[level_index] + below[:, None] * solved_prev) / pivot_value[
            :, None
        ]
        ratios.append(ratio_now)
        solveds.append(solved_now)
        ratio_prev = ratio_now
        solved_prev = solved_now
    results = [None] * levels
    results[levels - 1] = solveds[levels - 1]
    for level_index in range(levels - 2, -1, -1):
        results[level_index] = (
            solveds[level_index] - ratios[level_index][:, None] * results[level_index + 1]
        )
    return jnp.stack(results, axis=0)


def bit_mask(amount, position):
    return (amount // 2**position % 2 == 1)[:, :, None]


def move_rows(tracer_field, shift_cells):
    tracer_count = NTR
    width_cols = tracer_field.shape[2]
    cell_count = width_cols // tracer_count
    devices = lax.axis_size("lon")
    low_bits = cell_count.bit_length() - 1
    ahead_amount = jnp.remainder(shift_cells, cell_count * devices)
    high_bits = devices.bit_length() - 1
    current = tracer_field
    for position in range(low_bits):
        step_cols = 2**position * tracer_count
        from_west = from_behind(current[:, :, width_cols - step_cols :], "lon", 1)
        forward = jnp.concatenate([from_west, current[:, :, : width_cols - step_cols]], axis=2)
        current = jnp.where(bit_mask(ahead_amount, position), forward, current)
    for position in range(high_bits):
        hops = 2**position
        digit = low_bits + position
        ahead_block = from_behind(current, "lon", hops)
        current = jnp.where(bit_mask(ahead_amount, digit), ahead_block, current)
    return current


def per_device(tracers, lon_shift, lon_frac, lat_shift, lat_frac, remap_frac, diffusivity):
    tracer_field = tracers
    row_count = tracer_field.shape[1]
    for time_step in range(STEPS):
        padded = with_halo(tracer_field, (("lat", 1),), 3, False)
        tracer_field = lat_step(padded, lat_shift[time_step], lat_frac[time_step], row_count)
        shifted = move_rows(tracer_field, lon_shift[time_step])
        wrapped = with_halo(shifted, (("lon", 2),), 2 * NTR, True)
        tracer_field = lon_step(wrapped, lon_frac[time_step], NTR)
        tracer_field = remap(tracer_field, remap_frac[time_step])
        tracer_field = diffuse(tracer_field, diffusivity)
    return tracer_field


LANES = 128
TILE = 8
PLANES = 4
LOW = 2
HIGH = 3
TAPS = LOW + HIGH + 1
OUTER = (0, 1, 6, 7)
INNER = (2, 3, 4, 5)
PAD = 2 * TILE
COEFFS = TAPS + 9
MESH_LON = "lon"


def lane_index():
    return lax.broadcasted_iota(jnp.int32, (TILE, LANES), 1)


def pick(values, index):
    return jnp.take_along_axis(values, index, axis=1)


def swap_blocks(items, masks):
    for bit, mask in enumerate(masks):
        items = [
            jnp.where(mask, items[place ^ (1 << bit)], items[place])
            for place in range(len(items))
        ]
    return items


def lane_masks(lane, first, count):
    return [(lane >> (first + bit)) & 1 == 1 for bit in range(count)]


def at(tile, offset=0):
    return slice(TILE * tile + offset, TILE * tile + offset + TILE)


def row_runs(tiles):
    runs = []
    for place, tile in enumerate(tiles):
        if runs and tiles[place - 1] + 1 == tile:
            runs[-1][2] += 1
        else:
            runs.append([tile, place, 1])
    return [(TILE * tile, TILE * place, TILE * count) for tile, place, count in runs]


def pack_kernel(tiles, field_ref, *pair_refs):
    levels = field_ref.shape[0]
    me = lax.axis_index(MESH_LON)
    lane = lane_index()
    cell_masks = lane_masks(lane, 2, 2)
    device_masks = lane_masks(lane, 4, 3)
    base = ((lane & 3) << 5) | (((lane >> 2) & 3) << 3) | ((lane >> 4) ^ me)

    def unit(u, carry):
        by_group = []
        for group in range(8):
            k = 2 * u + group // 4
            parts = [
                pick(
                    field_ref[k, at(tiles[group % 4]), LANES * q : LANES * q + LANES],
                    base ^ ((q << 3) | group),
                )
                for q in range(PLANES)
            ]
            by_group.append(swap_blocks(parts, cell_masks))
        for plane in range(PLANES):
            sent = swap_blocks([parts[plane] for parts in by_group], device_masks)
            for mate in range(8):
                pair_refs[mate >> 1][mate & 1, u, plane] = sent[mate]
        return carry

    lax.fori_loop(0, levels // 2, unit, 0)


def unpack_kernel(tiles, *refs):
    message_refs, (field_ref, held, sems) = refs[:5], refs[-3:]
    levels = held.shape[0]
    runs = row_runs(tiles)

    def copies(k):
        return [
            pltpu.make_async_copy(
                held.at[k, pl.ds(source, count), :],
                field_ref.at[k, pl.ds(target, count), :],
                sems.at[k, which],
            )
            for which, (target, source, count) in enumerate(runs)
        ]

    me = lax.axis_index(MESH_LON)
    lane = lane_index()
    cell_masks = lane_masks(lane, 2, 2)
    device_masks = lane_masks(lane, 4, 3)
    base = (((lane & 7) ^ me) << 4) | (((lane >> 3) & 3) << 2) | (lane >> 5)

    def unit(u, carry):
        by_plane = [
            swap_blocks(arrived(message_refs, u, plane), device_masks)
            for plane in range(PLANES)
        ]
        for group in range(8):
            k = 2 * u + group // 4
            parts = swap_blocks([planes[group] for planes in by_plane], cell_masks)
            for q in range(PLANES):
                held[k, at(group % 4), LANES * q : LANES * q + LANES] = pick(
                    parts[q], base ^ ((group << 4) | (q << 2))
                )
            if group % 4 == 3:
                for copy in copies(k):
                    copy.start()
        return carry

    lax.fori_loop(0, levels // 2, unit, 0)

    def end(k, carry):
        for copy in copies(k):
            copy.wait()
        return carry

    lax.fori_loop(0, levels, end, 0)


def arrived(refs, u, plane):
    return [
        refs[4][mate >> 1, u, plane] if mate & 1 else refs[mate >> 1][0, u, plane]
        for mate in range(8)
    ]


def take_messages(message_refs, put):
    me = lax.axis_index(MESH_LON)
    lane = lane_index()
    device_masks = lane_masks(lane, 4, 3)
    base = lane ^ (me << 4)

    def unit(u, carry):
        for plane in range(PLANES):
            groups = swap_blocks(arrived(message_refs, u, plane), device_masks)
            for group, values in enumerate(groups):
                put(
                    2 * u + group // 4,
                    plane,
                    group % 4,
                    pick(values, base ^ ((group << 4) | (plane << 2))),
                )
        return carry

    lax.fori_loop(0, message_refs[0].shape[1], unit, 0)


def give_messages(message_refs, take):
    me = lax.axis_index(MESH_LON)
    lane = lane_index()
    device_masks = lane_masks(lane, 4, 3)
    base = lane ^ (me << 4)

    def unit(u, carry):
        for plane in range(PLANES):
            groups = [
                pick(
                    take(2 * u + group // 4, plane, group % 4),
                    base ^ ((group << 4) | (plane << 2)),
                )
                for group in range(8)
            ]
            for mate, values in enumerate(swap_blocks(groups, device_masks)):
                message_refs[mate >> 1][mate & 1, u, plane] = values
        return carry

    lax.fori_loop(0, message_refs[0].shape[1], unit, 0)


def copy_tiles(source, target, pairs):
    def level(k, carry):
        for plane in range(PLANES):
            for source_row, target_row, count in pairs:
                target[k, plane, target_row : target_row + count, :] = source[
                    k, plane, source_row : source_row + count, :
                ]
        return carry

    lax.fori_loop(0, source.shape[0], level, 0)


def advance(tile, padded, coeff_ref, coeff_row, moved, put):
    levels = moved.shape[0]
    lane = lane_index()
    first_row = pl.multiple_of(TILE * tile + PAD, TILE)
    rows_of = pl.ds(pl.multiple_of(coeff_row, TILE), TILE)

    def coeff(k, which):
        return coeff_ref[k, which, rows_of, :]

    for k in range(levels):
        weights = [coeff(k, which) for which in range(TAPS)]
        planes = []
        for plane in range(PLANES):
            summed = None
            for which, weight in enumerate(weights):
                addend = weight * padded[k, plane, pl.ds(first_row + (which - LOW), TILE), :]
                summed = addend if summed is None else summed + addend
            planes.append(summed)
        shift = coeff(k, COEFFS - 1).astype(jnp.int32)
        low_bit = shift & 1 == 1
        high_bit = shift & 2 == 2
        planes = [jnp.where(low_bit, planes[v - 1], planes[v]) for v in range(PLANES)]
        planes = [jnp.where(high_bit, planes[v - 2], planes[v]) for v in range(PLANES)]
        first = lane - (shift >> 2)
        least = shift & 3
        planes = [
            pick(values, jnp.where(least > v, first - 1, first) & (LANES - 1))
            for v, values in enumerate(planes)
        ]
        wide = (
            [pltpu.roll(planes[3], 1, 1)]
            + planes
            + [pltpu.roll(planes[0], LANES - 1, 1), pltpu.roll(planes[1], LANES - 1, 1)]
        )
        taps = [coeff(k, which) for which in range(TAPS, TAPS + 4)]
        for plane in range(PLANES):
            summed = taps[0] * wide[plane]
            for which in range(1, 4):
                summed = summed + taps[which] * wide[plane + which]
            moved[k, plane] = summed
    solved = []
    values = [moved[0, plane] for plane in range(PLANES)]
    for k in range(levels):
        above = values
        if k + 1 < levels:
            above = [moved[k + 1, plane] for plane in range(PLANES)]
        c_own, c_above, c_before = [coeff(k, TAPS + 4 + which) for which in range(3)]
        now = [c_own * a + c_above * b for a, b in zip(values, above)]
        if k:
            now = [a + c_before * b for a, b in zip(now, solved[-1])]
        solved.append(now)
        values = above
    for k in range(levels - 1, -1, -1):
        if k + 1 < levels:
            c_next = coeff(k, TAPS + 7)
            solved[k] = [a + c_next * b for a, b in zip(solved[k], solved[k + 1])]
        for plane in range(PLANES):
            put(k, plane, first_row, solved[k][plane])


def outer_kernel(*refs):
    message_refs, edge_ref, (field_ref, even_ref, odd_ref) = refs[:5], refs[5], refs[6:]

    def put(k, plane, place, values):
        field_ref[k, plane, at(place), :] = values

    take_messages(message_refs, put)
    levels = field_ref.shape[0]
    is_even = lax.axis_index("lat") % 2 == 0

    def choose(place, first, last):
        even_ref[place] = jnp.where(is_even, last, first)
        odd_ref[place] = jnp.where(is_even, first, last)

    def level(k, carry):
        for plane in range(PLANES):
            choose(k * PLANES + plane, field_ref[k, plane, at(0), :], field_ref[k, plane, at(3), :])
        return carry

    lax.fori_loop(0, levels, level, 0)
    for pair in range(levels // 2):
        choose(levels * PLANES + pair, edge_ref[0, pair], edge_ref[1, pair])


def inner_kernel(*refs):
    incoming, outgoing = refs[:5], refs[7:11]
    field_ref, coeff_ref = refs[5:7]
    next_ref, padded, moved = refs[11:]

    def put_field(k, plane, place, values):
        padded[0, k, plane, at(INNER[place], PAD), :] = values

    take_messages(incoming, put_field)
    copy_tiles(field_ref, padded.at[0], [(0, PAD, 16), (16, PAD + 6 * TILE, 16)])

    def one(place, carry):
        step = jnp.where(place < 6, 0, 1)
        tile = place + jnp.where(place < 6, 1, -4)

        def put(k, plane, row, values):
            padded[step + 1, k, plane, pl.ds(row, TILE), :] = values

        advance(tile, padded.at[step], coeff_ref.at[step], TILE * tile, moved, put)
        return carry

    lax.fori_loop(0, 10, one, 0)
    copy_tiles(padded.at[1], next_ref, [(PAD + 8, 0, 16), (PAD + 40, 16, 16)])
    give_messages(
        outgoing, lambda k, plane, place: padded[2, k, plane, at(INNER[place], PAD), :]
    )


def last_kernel(near_ref, field_ref, even_ref, odd_ref, coeff_ref, spread_ref, *refs):
    outgoing, (padded, moved, nearby) = refs[:4], refs[4:]
    levels = near_ref.shape[0]
    is_even = lax.axis_index("lat") % 2 == 0

    def choose(place):
        even, odd = even_ref[place], odd_ref[place]
        return jnp.where(is_even, odd, even), jnp.where(is_even, even, odd)

    def level(k, carry):
        for plane in range(PLANES):
            low, high = choose(k * PLANES + plane)
            padded[0, k, plane, at(-1, PAD), :] = low
            padded[0, k, plane, at(8, PAD), :] = high
        return carry

    lax.fori_loop(0, levels, level, 0)
    copy_tiles(field_ref, padded.at[0], [(0, PAD, 16), (16, PAD + 6 * TILE, 16)])
    copy_tiles(near_ref, padded.at[1], [(0, PAD + 8, 16), (16, PAD + 40, 16)])
    sides = [choose(levels * PLANES + pair) for pair in range(levels // 2)]
    turned = jnp.concatenate([low for low, _ in sides] + [high for _, high in sides], axis=0)
    turned = turned.astype(jnp.bfloat16)

    def widen(group, carry):
        for which in [group * 3 + i for i in range(3)]:
            for parity in range(2):
                wide = jnp.dot(
                    turned, spread_ref[which, parity], preferred_element_type=jnp.float32
                )
                for side in range(2):
                    for pair in range(levels // 2):
                        nearby[2 * pair + parity, which, at(3 * side), :] = wide[
                            at(side * levels // 2 + pair)
                        ]
            for k in range(levels):
                nearby[k, which, at(1), :] = coeff_ref[0, k, which, at(0), :]
                nearby[k, which, at(2), :] = coeff_ref[0, k, which, at(7), :]
        return carry

    lax.fori_loop(0, COEFFS // 3, widen, 0)

    def first(place, carry):
        tile = jnp.where(place < 2, place - 1, place + 5)

        def put(k, plane, row, values):
            padded[1, k, plane, pl.ds(row, TILE), :] = values

        advance(tile, padded.at[0], nearby, TILE * place, moved, put)
        return carry

    lax.fori_loop(0, 4, first, 0)

    def second(place, carry):
        tile = place + jnp.where(place < 2, 0, 4)

        def put(k, plane, row, values):
            padded[0, k, plane, pl.ds(row, TILE), :] = values

        advance(tile, padded.at[1], coeff_ref.at[1], TILE * tile, moved, put)
        return carry

    lax.fori_loop(0, 4, second, 0)
    give_messages(
        outgoing, lambda k, plane, place: padded[0, k, plane, at(OUTER[place], PAD), :]
    )


def coeff_kernel(
    lon_shift_ref,
    lon_frac_ref,
    lat_shift_ref,
    lat_frac_ref,
    remap_ref,
    diffusivity_ref,
    coeff_ref,
    edge_ref,
    spread_ref,
    held,
    turned_ref,
):
    held[...] = jnp.zeros_like(held)
    kappa = diffusivity_ref[...]
    levels, rows = kappa.shape
    steps = lon_frac_ref.shape[0]
    face = 0.5 * (kappa[:-1] + kappa[1:])
    zero = jnp.zeros_like(kappa[:1])
    below = jnp.concatenate([zero, face], axis=0)
    above = jnp.concatenate([face, zero], axis=0)
    ratio = zero
    pivots, ratios = [], []
    for k in range(levels):
        pivot = 1.0 + below[k : k + 1] + above[k : k + 1] + below[k : k + 1] * ratio
        ratio = -above[k : k + 1] / pivot
        pivots.append(pivot)
        ratios.append(ratio)
    pivot = jnp.concatenate(pivots, axis=0)
    back = -jnp.concatenate(ratios, axis=0)
    for step in range(steps):
        lat_weights = cubic_weights(lat_frac_ref[step])
        offset = lat_shift_ref[step]
        columns = []
        for row_delta in range(-LOW, HIGH + 1):
            coeff = jnp.zeros_like(kappa)
            for tap in range(4):
                coeff = coeff + jnp.where(offset == tap - 1 - row_delta, lat_weights[tap], 0.0)
            columns.append(coeff)
        columns.extend(cubic_weights(lon_frac_ref[step]))
        fraction = remap_ref[step]
        columns.append((1.0 - fraction) / pivot)
        columns.append(fraction / pivot)
        columns.append(below / pivot)
        columns.append(back)
        columns.append(lon_shift_ref[step].astype(jnp.float32))
        for which, column in enumerate(columns):
            for part in range(3):
                piece = column.astype(jnp.bfloat16).astype(jnp.float32)
                column = column - piece
                for k in range(levels):
                    place = 64 * (k & 1) + 16 * part + which
                    held[(step * levels + k) // 2, place : place + 1, :rows] = piece[k : k + 1]
    row = lax.broadcasted_iota(jnp.int32, (LANES, LANES), 0)

    def choose(which, carry):
        wanted = jnp.logical_and(row & 15 == which, row & 63 < 48)
        for parity in range(2):
            chosen = jnp.logical_and(wanted, row >> 6 == parity)
            spread_ref[which, parity] = chosen.astype(jnp.float32).astype(jnp.bfloat16)
        return carry

    lax.fori_loop(0, COEFFS, choose, 0)
    pairs = steps * levels // 2

    def turn(place, carry):
        turned = held[place].T[:rows]
        turned_ref[pl.ds(pl.multiple_of(place * rows, rows), rows), :] = turned.astype(jnp.bfloat16)

        @pl.when(place < levels // 2)
        def _():
            edge_ref[0, place] = turned[:TILE]
            edge_ref[1, place] = turned[rows - TILE :]

        return carry

    lax.fori_loop(0, pairs, turn, 0)

    def spread(group, carry):
        for which in [group * 3 + i for i in range(3)]:
            for parity in range(2):
                wide = jnp.dot(
                    turned_ref[...], spread_ref[which, parity], preferred_element_type=jnp.float32
                )
                for pair in range(pairs):
                    both = 2 * pair + parity
                    coeff_ref[both // levels, both % levels, which] = wide[
                        pair * rows : pair * rows + rows
                    ]
        return carry

    lax.fori_loop(0, COEFFS // 3, spread, 0)


def call(kernel, micros, out_shapes, scratch=(), **options):
    return pl.pallas_call(
        kernel,
        cost_estimate=pl.CostEstimate(
            flops=micros * 10**9, bytes_accessed=micros * 3 * 10**6, transcendentals=0
        ),
        out_shape=[
            shape if isinstance(shape, jax.ShapeDtypeStruct) else jax.ShapeDtypeStruct(shape, jnp.float32)
            for shape in out_shapes
        ],
        scratch_shapes=[
            pltpu.VMEM(shape, jnp.float32) if isinstance(shape, tuple) else shape
            for shape in scratch
        ],
        compiler_params=pltpu.CompilerParams(vmem_limit_bytes=20 * 2**20),
        **options,
    )


def between_chips(pairs, chip):
    peers = lax.axis_size(MESH_LON)
    return lax.ppermute(pairs[chip], MESH_LON, [(i, i ^ (2 * chip)) for i in range(peers)])


def arrive(pairs):
    return pairs[:1] + [between_chips(pairs, chip) for chip in range(1, len(pairs))]


def between_cores(pairs):
    peers = lax.axis_size(MESH_LON)
    away = jnp.concatenate([pair[1:] for pair in pairs], axis=0)
    return pairs + [lax.ppermute(away, MESH_LON, [(i, i ^ 1) for i in range(peers)])]


def exchange_edges(even, odd):
    count = lax.axis_size("lat")
    near = [(i, i ^ 1) for i in range(count) if i ^ 1 < count]
    far = [(i, ((i + 1) ^ 1) - 1) for i in range(1, count) if ((i + 1) ^ 1) - 1 < count]
    return lax.ppermute(even, "lat", near), lax.ppermute(odd, "lat", far)


def by_tracer(tracers, lon_shift, lon_frac, lat_shift, lat_frac, remap_frac, diffusivity):
    levels, rows, columns = tracers.shape
    steps = lon_shift.shape[0]
    pairs = levels // 2
    messages = [(2, pairs, PLANES, TILE, LANES)] * 4
    half = (levels, PLANES, rows // 2, LANES)
    edges = (levels * PLANES + pairs, TILE, LANES)
    work = (levels, PLANES, rows + 4 * TILE, LANES)
    moved = (levels, PLANES, TILE, LANES)
    held = [(levels, rows // 2, columns), pltpu.SemaphoreType.DMA((levels, 2))]
    anywhere = pl.BlockSpec(memory_space=pl.ANY)
    vmem = pl.BlockSpec(memory_space=pltpu.VMEM)

    def pack(tiles):
        kernel = functools.partial(pack_kernel, tiles)
        return list(call(kernel, 2, messages)(tracers))

    outer, inner = pack(OUTER), pack(INNER)
    coeff, edge, spread = call(
        coeff_kernel,
        6,
        [
            (steps, levels, COEFFS, rows, LANES),
            (2, pairs, TILE, LANES),
            jax.ShapeDtypeStruct((COEFFS, 2, LANES, LANES), jnp.bfloat16),
        ],
        [
            (steps * pairs, LANES, LANES),
            pltpu.VMEM((steps * pairs * rows, LANES), jnp.bfloat16),
        ],
    )(lon_shift, lon_frac, lat_shift, lat_frac, remap_frac, diffusivity)
    outer = between_cores(arrive(outer))
    *inner, coeff = lax.optimization_barrier((*inner, coeff))
    inner = arrive(inner)
    field, even, odd = call(outer_kernel, 1, [half, edges, edges])(*outer, edge)
    inner = between_cores(inner)
    even, odd = exchange_edges(even, odd)
    *inner, near = call(inner_kernel, 6, messages + [half], [(3,) + work, moved])(
        *inner, field, coeff
    )
    *inner, even, odd = lax.optimization_barrier((*inner, even, odd))
    inner = arrive(inner)
    outer = call(
        last_kernel,
        6,
        messages,
        [(2,) + work, moved, (levels, COEFFS, rows // 2, LANES)],
    )(near, field, even, odd, coeff, spread)
    *inner, outer = lax.optimization_barrier((*inner, list(outer)))
    inner = between_cores(inner)
    done = call(
        functools.partial(unpack_kernel, INNER), 2, [tracers.shape], held, out_specs=[anywhere]
    )(*inner)[0]
    outer[3], done = lax.optimization_barrier((outer[3], done))
    outer = between_cores(arrive(outer))
    return call(
        functools.partial(unpack_kernel, OUTER),
        2,
        [tracers.shape],
        held,
        in_specs=[vmem] * 5 + [anywhere],
        out_specs=[anywhere],
        input_output_aliases={5: 0},
    )(*outer, done)[0]


def solution(mesh):
    in_specs = (
        P(None, "lat", "lon"),
        P(None, None, "lat"),
        P(None, None, "lat"),
        P(None, None, "lat"),
        P(None, None, "lat"),
        P(None, None, "lat"),
        P(None, "lat"),
    )
    out_specs = P(None, "lat", "lon")
    def per_part(tracers, *fields):
        _, rows, columns = tracers.shape
        fits = mesh.shape["lon"] == NTR and columns == PLANES * LANES and rows == TILE * NTR
        return (by_tracer if fits else per_device)(tracers, *fields)

    return jax.shard_map(
        per_part, mesh=mesh, in_specs=in_specs, out_specs=out_specs, check_vma=False
    )
```

time: 91.8 us -> 64 us (0.70); the launches traced: 90.4 us -> 63.9 us
  starting transfers between devices: 39.7 us -> 23.1 us
  Pallas kernels: 36.3 us -> 22.8 us
  waiting for transfers between devices: 10.9 us -> 15.9 us
  local copies, waits for them, and re-layouts: 3.28 us -> 1.58 us
    ppermute x32 -> x18, starting transfers between devices: 39.7 us -> 23.1 us  [the longest x12 11 us: between_chips(): lax.ppermute(pairs[chip], MESH_LON, [(i, i ^ 2 * chip) for i in range(pee...]
    pallas_call x9 -> x8, Pallas kernels: 36.3 us -> 22.8 us  [the longest x1 6.29 us: by_tracer(): call(inner_kernel, 6, messages + [half], [(3,) + work, moved])]
    ppermute x32 -> x18, waiting for transfers between devices: 10.9 us -> 15.9 us  [the longest x12 14.6 us: between_chips(): lax.ppermute(pairs[chip], MESH_LON, [(i, i ^ 2 * chip) for i in range(pee...]
    unnamed x23 -> x21, local copies, waits for them, and re-layouts: 3.28 us -> 1.45 us
  transfers between devices with their start and end apart: 32 -> 18, of which waited for: 6 -> 9; matrix products, arithmetic and copies ran while one was open for 0% -> 0% of each run, Pallas kernels for 35% -> 31%
where the time goes in v3:
time: 64 us; the launch traced here: 63.9 us
  starting transfers between devices  23.1 us (36%)
  Pallas kernels  22.8 us (36%)
  waiting for transfers between devices  15.9 us (25%)
  local copies, waits for them, and re-layouts  1.58 us (2%)
    ppermute x12, waiting for transfers between devices, between_chips(): lax.ppermute(pairs[chip], MESH_LON, [(i, i ^ 2 * chip) for i in range(pee...  14.6 us
    ppermute x12, starting transfers between devices, between_chips(): lax.ppermute(pairs[chip], MESH_LON, [(i, i ^ 2 * chip) for i in range(pee...  11 us
    ppermute x4, starting transfers between devices, between_cores(): lax.ppermute(away, MESH_LON, [(i, i ^ 1) for i in range(peers)])  7.57 us
    pallas_call x1, Pallas kernels, by_tracer(): call(inner_kernel, 6, messages + [half], [(3,) + work, moved])  6.29 us
    pallas_call x1, Pallas kernels, by_tracer(): call(last_kernel, 6, messages, [(2,) + work, moved, (levels, COEFFS, rows...  5.59 us
    ppermute x2, starting transfers between devices, exchange_edges(): return (lax.ppermute(even, 'lat', near), lax.ppermute(odd, 'lat', far))  4.55 us
    pallas_call x1, Pallas kernels, by_tracer(): call(coeff_kernel, 6, [(steps, levels, COEFFS, rows, LANES), (2, pairs, T...  4.13 us
    pallas_call x2, Pallas kernels, pack(): return list(call(kernel, 2, messages)(tracers))  2.04 us
  transfers between devices with their start and end apart: 18, of which 9 were waited for; matrix products, arithmetic and copies ran while one was open for 0% of the time, Pallas kernels for 31%

profile of v3, /device:TPU:9, one launch (start us, length us, event | category | flops | bytes accessed | tf_op | source)
XLA Modules:
  0.0 63.9 jit_solution(8361065134243457915)
XLA Ops:
  0.0 1.4 %copy-done = f32[12,64,512]{2,1,0:T(8,128)S(1)} copy-done((f32[12,64,512]{2,1,0:T(8,128)S(1)}, f32[12,64,512]{2,1,0:T(8,128)}, u32[]{:S(2)}) %copy-start) | copy-done | bytes 1572888
  1.4 0.0 copy-start.7
  1.4 1.0 %shard_map.75 = (f32[2,6,4,8,128]{4,3,2,1,0:T(8,128)S(1)}, f32[2,6,4,8,128]{4,3,2,1,0:T(8,128)S(1)}, f32[2,6,4,8,128]{4,3,2,1,0:T(8,128)S(1)}, f32[2,6,4,8,128]{4,3,2,1,0:T(8,128)S(1)}) custom-call(f32[12,64,512]{2,1,0:T(8,128)S(1)} %copy-done), custom_call_target="tpu_custom_call" | custom-call | flops 2000000000 | bytes 6000000 | tf_op jit(solution)/shard_map/pallas_call | solution.py:660
  2.5 1.3 %collective-permute-start.4 = (f32[2,6,4,8,128]{4,3,2,1,0:T(8,128)S(1)}, f32[2,6,4,8,128]{4,3,2,1,0:T(8,128)S(1)}, u32[]{:S(2)}, u32[]{:S(2)}) collective-permute-start(f32[2,6,4,8,128]{4,3,2,1,0:T(8,128)S(1)} %get-tuple-element.59), channel_id=1, source_target_pairs={{0,8},{4,12},{8,0},{12,4},{16,24},{20,28},{24,16},{28,20},{1,9},{5... | collective-permute-start | bytes 589832 | tf_op jit(solution)/shard_map/ppermute | solution.py:625
  3.7 1.2 %collective-permute-start.5 = (f32[2,6,4,8,128]{4,3,2,1,0:T(8,128)S(1)}, f32[2,6,4,8,128]{4,3,2,1,0:T(8,128)S(1)}, u32[]{:S(2)}, u32[]{:S(2)}) collective-permute-start(f32[2,6,4,8,128]{4,3,2,1,0:T(8,128)S(1)} %get-tuple-element.60), channel_id=1, source_target_pairs={{0,16},{4,20},{8,24},{12,28},{16,0},{20,4},{24,8},{28,12},{1,17},{... | collective-permute-start | bytes 589832 | tf_op jit(solution)/shard_map/ppermute | solution.py:625
  5.0 0.2 collective-permute-start.6
  5.2 0.0 copy-done.3
  5.3 0.0 copy-start.1
  5.3 4.1 %shard_map.74 = (f32[2,12,15,64,128]{4,3,2,1,0:T(8,128)S(1)}, f32[2,6,8,128]{3,2,1,0:T(8,128)S(1)}, bf16[15,2,128,128]{3,2,1,0:T(8,128)(2,1)S(1)}) custom-call(s32[2,12,64]{2,1,0:T(8,128)S(1)} %copy.9.lon_shift_ref, f32[2,12,64]{2,1,0:T(8,128)S(1)} %copy.10.lon_frac_ref, s32[2,12,64]{2,1,0:T(8,128)S(1)} %copy.11.lat_shift_ref, ...), custom_call_target="tpu_custom_call" | custom-call | flops 6000000000 | bytes 18000000 | tf_op jit(solution)/shard_map/pallas_call | solution.py:663
  9.4 1.0 %shard_map.73 = (f32[2,6,4,8,128]{4,3,2,1,0:T(8,128)S(1)}, f32[2,6,4,8,128]{4,3,2,1,0:T(8,128)S(1)}, f32[2,6,4,8,128]{4,3,2,1,0:T(8,128)S(1)}, f32[2,6,4,8,128]{4,3,2,1,0:T(8,128)S(1)}) custom-call(f32[12,64,512]{2,1,0:T(8,128)S(1)} %copy-done.1), custom_call_target="tpu_custom_call" | custom-call | flops 2000000000 | bytes 6000000 | tf_op jit(solution)/shard_map/pallas_call | solution.py:660
  10.5 1.3 %collective-permute-start = (f32[2,6,4,8,128]{4,3,2,1,0:T(8,128)S(1)}, f32[2,6,4,8,128]{4,3,2,1,0:T(8,128)S(1)}, u32[]{:S(2)}, u32[]{:S(2)}) collective-permute-start(f32[2,6,4,8,128]{4,3,2,1,0:T(8,128)S(1)} %get-tuple-element.55), channel_id=1, source_target_pairs={{0,8},{4,12},{8,0},{12,4},{16,24},{20,28},{24,16},{28,20},{1,9},{5... | collective-permute-start | bytes 589832 | tf_op jit(solution)/shard_map/ppermute | solution.py:625
  11.7 1.2 %collective-permute-start.1 = (f32[2,6,4,8,128]{4,3,2,1,0:T(8,128)S(1)}, f32[2,6,4,8,128]{4,3,2,1,0:T(8,128)S(1)}, u32[]{:S(2)}, u32[]{:S(2)}) collective-permute-start(f32[2,6,4,8,128]{4,3,2,1,0:T(8,128)S(1)} %get-tuple-element.56), channel_id=1, source_target_pairs={{0,16},{4,20},{8,24},{12,28},{16,0},{20,4},{24,8},{28,12},{1,17},{... | collective-permute-start | bytes 589832 | tf_op jit(solution)/shard_map/ppermute | solution.py:625
  13.0 0.0 collective-permute-done.4.refs_1_
  13.0 0.2 collective-permute-start.2
  13.2 0.0 collective-permute-done.5.refs_2_
  13.2 0.3 collective-permute-done.6.refs_3_
  13.6 2.2 %collective-permute-start.7 = (f32[4,6,4,8,128]{4,3,2,1,0:T(8,128)S(1)}, f32[4,6,4,8,128]{4,3,2,1,0:T(8,128)S(1)}, u32[]{:S(2)}, u32[]{:S(2)}) collective-permute-start(f32[4,6,4,8,128]{4,3,2,1,0:T(8,128)S(1)} %pad_maximum_fusion.1), channel_id=1, source_target_pairs={{0,4},{4,0},{8,12},{12,8},{16,20},{20,16},{24,28},{28,24},{1,5},{5... | collective-permute-start | bytes 1179656 | tf_op jit(solution)/shard_map/ppermute | solution.py:635
  15.7 0.6 collective-permute-done.refs_1_
  16.4 0.8 %collective-permute-done.1.refs_2_ = f32[2,6,4,8,128]{4,3,2,1,0:T(8,128)S(1)} collective-permute-done((f32[2,6,4,8,128]{4,3,2,1,0:T(8,128)S(1)}, f32[2,6,4,8,128]{4,3,2,1,0:T(8,128)S(1)}, u32[]{:S(2)}, u32[]{:S(2)}) %collective-permute-start.1) | collective-permute-done | bytes 196640 | tf_op jit(solution)/shard_map/ppermute | solution.py:625
  17.2 4.4 %collective-permute-done.2.refs_3_ = f32[2,6,4,8,128]{4,3,2,1,0:T(8,128)S(1)} collective-permute-done((f32[2,6,4,8,128]{4,3,2,1,0:T(8,128)S(1)}, f32[2,6,4,8,128]{4,3,2,1,0:T(8,128)S(1)}, u32[]{:S(2)}, u32[]{:S(2)}) %collective-permute-start.2) | collective-permute-done | bytes 196640 | tf_op jit(solution)/shard_map/ppermute | solution.py:625
  21.6 2.2 %collective-permute-start.3 = (f32[4,6,4,8,128]{4,3,2,1,0:T(8,128)S(1)}, f32[4,6,4,8,128]{4,3,2,1,0:T(8,128)S(1)}, u32[]{:S(2)}, u32[]{:S(2)}) collective-permute-start(f32[4,6,4,8,128]{4,3,2,1,0:T(8,128)S(1)} %pad_maximum_fusion), channel_id=1, source_target_pairs={{0,4},{4,0},{8,12},{12,8},{16,20},{20,16},{24,28},{28,24},{1,5},{5... | collective-permute-start | bytes 1179656 | tf_op jit(solution)/shard_map/ppermute | solution.py:635
  23.8 0.0 collective-permute-done.7.refs_4_
  23.8 1.0 %shard_map.76 = (f32[12,4,32,128]{3,2,1,0:T(8,128)S(1)}, f32[54,8,128]{2,1,0:T(8,128)S(1)}, f32[54,8,128]{2,1,0:T(8,128)S(1)}) custom-call(f32[2,6,4,8,128]{4,3,2,1,0:T(8,128)S(1)} %get-tuple-element.58.refs_0_, f32[2,6,4,8,128]{4,3,2,1,0:T(8,128)S(1)} %collective-permute-done.4.refs_1_, f32[2,6,4,8,128]{4,3,2,1,0:T(8,128)S(1)} %collective-permute-done.5.refs_2_, ...), custom_call_target="tpu_custom_call" | custom-call | flops 1000000000 | bytes 3000000 | tf_op jit(solution)/shard_map/pallas_call | solution.py:679
  24.9 0.2 collective-permute-start.8
  25.1 4.3 %collective-permute-start.9 = (f32[54,8,128]{2,1,0:T(8,128)S(1)}, f32[54,8,128]{2,1,0:T(8,128)S(1)}, u32[]{:S(2)}, u32[]{:S(2)}) collective-permute-start(f32[54,8,128]{2,1,0:T(8,128)S(1)} %get-tuple-element.70), channel_id=1, source_target_pairs={{1,2},{2,1},{5,6},{6,5},{9,10},{10,9},{13,14},{14,13},{17,18},{18,... | collective-permute-start | bytes 663560 | tf_op jit(solution)/shard_map/ppermute | solution.py:642
  29.5 0.0 collective-permute-done.3.refs_4_
  29.5 6.3 %shard_map.77 = (f32[2,6,4,8,128]{4,3,2,1,0:T(8,128)S(1)}, f32[2,6,4,8,128]{4,3,2,1,0:T(8,128)S(1)}, f32[2,6,4,8,128]{4,3,2,1,0:T(8,128)S(1)}, f32[2,6,4,8,128]{4,3,2,1,0:T(8,128)S(1)}, f32[12,4,32,128]{3,2,1,0:T(8,128)S(1)}) custom-call(f32[2,6,4,8,128]{4,3,2,1,0:T(8,128)S(1)} %get-tuple-element.54.refs_0_, ...), custom_call_target="tpu_custom_call" | custom-call | flops 6000000000 | bytes 18000000 | tf_op jit(solution)/shard_map/pallas_call | solution.py:682
  35.8 0.0 collective-permute-done.8.even_ref
  35.8 0.0 collective-permute-done.9.odd_ref
  35.8 1.0 %collective-permute-start.10 = (f32[2,6,4,8,128]{4,3,2,1,0:T(8,128)S(1)}, f32[2,6,4,8,128]{4,3,2,1,0:T(8,128)S(1)}, u32[]{:S(2)}, u32[]{:S(2)}) collective-permute-start(f32[2,6,4,8,128]{4,3,2,1,0:T(8,128)S(1)} %get-tuple-element.72), channel_id=1, source_target_pairs={{0,8},{4,12},{8,0},{12,4},{16,24},{20,28},{24,16},{28,20},{1,9},{5... | collective-permute-start | bytes 589832 | tf_op jit(solution)/shard_map/ppermute | solution.py:625
  36.8 0.6 collective-permute-start.11
  37.4 1.2 %collective-permute-start.12 = (f32[2,6,4,8,128]{4,3,2,1,0:T(8,128)S(1)}, f32[2,6,4,8,128]{4,3,2,1,0:T(8,128)S(1)}, u32[]{:S(2)}, u32[]{:S(2)}) collective-permute-start(f32[2,6,4,8,128]{4,3,2,1,0:T(8,128)S(1)} %get-tuple-element.74), channel_id=1, source_target_pairs={{0,24},{4,28},{8,16},{12,20},{16,8},{20,12},{24,0},{28,4},{1,25},{... | collective-permute-start | bytes 589832 | tf_op jit(solution)/shard_map/ppermute | solution.py:625
  38.5 5.6 %shard_map.78 = (f32[2,6,4,8,128]{4,3,2,1,0:T(8,128)S(1)}, f32[2,6,4,8,128]{4,3,2,1,0:T(8,128)S(1)}, f32[2,6,4,8,128]{4,3,2,1,0:T(8,128)S(1)}, f32[2,6,4,8,128]{4,3,2,1,0:T(8,128)S(1)}) custom-call(f32[12,4,32,128]{3,2,1,0:T(8,128)S(1)} %get-tuple-element.75.near_ref, f32[12,4,32,128]{3,2,1,0:T(8,128)S(1)} %get-tuple-element.63.refs_5_.field_ref, ...), custom_call_target="tpu_custom_call" | custom-call | flops 6000000000 | bytes 18000000 | tf_op jit(solution)/shard_map/pallas_call | solution.py:687
  44.1 0.0 collective-permute-done.10.refs_1_
  44.1 0.0 collective-permute-done.11.refs_2_
  44.1 2.8 %collective-permute-done.12.refs_3_ = f32[2,6,4,8,128]{4,3,2,1,0:T(8,128)S(1)} collective-permute-done((f32[2,6,4,8,128]{4,3,2,1,0:T(8,128)S(1)}, f32[2,6,4,8,128]{4,3,2,1,0:T(8,128)S(1)}, u32[]{:S(2)}, u32[]{:S(2)}) %collective-permute-start.12) | collective-permute-done | bytes 196640 | tf_op jit(solution)/shard_map/ppermute | solution.py:625
  47.0 1.5 %collective-permute-start.15 = (f32[4,6,4,8,128]{4,3,2,1,0:T(8,128)S(1)}, f32[4,6,4,8,128]{4,3,2,1,0:T(8,128)S(1)}, u32[]{:S(2)}, u32[]{:S(2)}) collective-permute-start(f32[4,6,4,8,128]{4,3,2,1,0:T(8,128)S(1)} %pad_maximum_fusion.2), channel_id=1, source_target_pairs={{0,4},{4,0},{8,12},{12,8},{16,20},{20,16},{24,28},{28,24},{1,5},{5... | collective-permute-start | bytes 1179656 | tf_op jit(solution)/shard_map/ppermute | solution.py:635
  48.5 0.5 collective-permute-start.13
  49.0 1.2 %collective-permute-start.14 = (f32[2,6,4,8,128]{4,3,2,1,0:T(8,128)S(1)}, f32[2,6,4,8,128]{4,3,2,1,0:T(8,128)S(1)}, u32[]{:S(2)}, u32[]{:S(2)}) collective-permute-start(f32[2,6,4,8,128]{4,3,2,1,0:T(8,128)S(1)} %get-tuple-element.85), channel_id=1, source_target_pairs={{0,16},{4,20},{8,24},{12,28},{16,0},{20,4},{24,8},{28,12},{1,17},{... | collective-permute-start | bytes 589832 | tf_op jit(solution)/shard_map/ppermute | solution.py:625
  50.3 0.0 collective-permute-done.15.refs_4_
  50.3 1.8 %shard_map.79.refs_5_ = f32[12,64,512]{2,1,0:T(8,128)} custom-call(f32[2,6,4,8,128]{4,3,2,1,0:T(8,128)S(1)} %get-tuple-element.87.refs_0_, f32[2,6,4,8,128]{4,3,2,1,0:T(8,128)S(1)} %collective-permute-done.10.refs_1_, f32[2,6,4,8,128]{4,3,2,1,0:T(8,128)S(1)} %collective-permute-done.11.refs_2_, f32[2,6,4,8,128]{4,3,2,1,0:T(8,128)S(1)} %collective-permute-done.12.refs_3_, ...), custom_call_target="tpu_custom_call" | custom-call | flops 2000000000 | bytes 6000000 | tf_op jit(solution)/shard_map/pallas_call | solution.py:695
  52.1 1.1 %collective-permute-start.16 = (f32[2,6,4,8,128]{4,3,2,1,0:T(8,128)S(1)}, f32[2,6,4,8,128]{4,3,2,1,0:T(8,128)S(1)}, u32[]{:S(2)}, u32[]{:S(2)}) collective-permute-start(f32[2,6,4,8,128]{4,3,2,1,0:T(8,128)S(1)} %get-tuple-element.91), channel_id=1, source_target_pairs={{0,24},{4,28},{8,16},{12,20},{16,8},{20,12},{24,0},{28,4},{1,25},{... | collective-permute-start | bytes 589832 | tf_op jit(solution)/shard_map/ppermute | solution.py:625
  53.2 1.7 %collective-permute-done.13.refs_1_ = f32[2,6,4,8,128]{4,3,2,1,0:T(8,128)S(1)} collective-permute-done((f32[2,6,4,8,128]{4,3,2,1,0:T(8,128)S(1)}, f32[2,6,4,8,128]{4,3,2,1,0:T(8,128)S(1)}, u32[]{:S(2)}, u32[]{:S(2)}) %collective-permute-start.13) | collective-permute-done | bytes 196640 | tf_op jit(solution)/shard_map/ppermute | solution.py:625
  55.0 0.2 collective-permute-done.14.refs_2_
  55.2 3.8 %collective-permute-done.16.refs_3_ = f32[2,6,4,8,128]{4,3,2,1,0:T(8,128)S(1)} collective-permute-done((f32[2,6,4,8,128]{4,3,2,1,0:T(8,128)S(1)}, f32[2,6,4,8,128]{4,3,2,1,0:T(8,128)S(1)}, u32[]{:S(2)}, u32[]{:S(2)}) %collective-permute-start.16) | collective-permute-done | bytes 196640 | tf_op jit(solution)/shard_map/ppermute | solution.py:625
  59.0 1.7 %collective-permute-start.17 = (f32[4,6,4,8,128]{4,3,2,1,0:T(8,128)S(1)}, f32[4,6,4,8,128]{4,3,2,1,0:T(8,128)S(1)}, u32[]{:S(2)}, u32[]{:S(2)}) collective-permute-start(f32[4,6,4,8,128]{4,3,2,1,0:T(8,128)S(1)} %pad_maximum_fusion.3), channel_id=1, source_target_pairs={{0,4},{4,0},{8,12},{12,8},{16,20},{20,16},{24,28},{28,24},{1,5},{5... | collective-permute-start | bytes 1179656 | tf_op jit(solution)/shard_map/ppermute | solution.py:635
  60.7 1.3 %collective-permute-done.17.refs_4_ = f32[4,6,4,8,128]{4,3,2,1,0:T(8,128)S(1)} collective-permute-done((f32[4,6,4,8,128]{4,3,2,1,0:T(8,128)S(1)}, f32[4,6,4,8,128]{4,3,2,1,0:T(8,128)S(1)}, u32[]{:S(2)}, u32[]{:S(2)}) %collective-permute-start.17) | collective-permute-done | bytes 393248 | tf_op jit(solution)/shard_map/ppermute | solution.py:635
  62.1 1.8 %shard_map.80 = f32[12,64,512]{2,1,0:T(8,128)} custom-call(f32[2,6,4,8,128]{4,3,2,1,0:T(8,128)S(1)} %get-tuple-element.83.refs_0_, f32[2,6,4,8,128]{4,3,2,1,0:T(8,128)S(1)} %collective-permute-done.13.refs_1_, f32[2,6,4,8,128]{4,3,2,1,0:T(8,128)S(1)} %collective-permute-done.14.refs_2_, ...), custom_call_target="tpu_custom_call", output_to_operand_aliasing={{}: (5, {})} | custom-call | flops 2000000000 | bytes 6000000 | tf_op jit(solution)/shard_map/pallas_call | solution.py:700
  (37 shorter events, 0.3 us)
Async XLA Ops:
  0.0 1.4 %copy-start = (f32[12,64,512]{2,1,0:T(8,128)S(1)}, f32[12,64,512]{2,1,0:T(8,128)}, u32[]{:S(2)}) copy-start(f32[12,64,512]{2,1,0:T(8,128)} %field_ref.3) | copy-start | bytes 4718596
  1.4 3.8 %copy-start.3 = (s32[2,12,64]{2,0,1:T(2,128)S(1)}, s32[2,12,64]{2,0,1:T(2,128)}, u32[]{:S(2)}) copy-start(s32[2,12,64]{2,0,1:T(2,128)} %param.8) | copy-start | bytes 18436
  1.4 3.8 %copy-start.4 = (f32[2,12,64]{2,0,1:T(2,128)S(1)}, f32[2,12,64]{2,0,1:T(2,128)}, u32[]{:S(2)}) copy-start(f32[2,12,64]{2,0,1:T(2,128)} %param.9) | copy-start | bytes 18436
  1.4 3.8 %copy-start.5 = (s32[2,12,64]{2,0,1:T(2,128)S(1)}, s32[2,12,64]{2,0,1:T(2,128)}, u32[]{:S(2)}) copy-start(s32[2,12,64]{2,0,1:T(2,128)} %param.10) | copy-start | bytes 18436
  1.4 3.8 %copy-start.6 = (f32[2,12,64]{2,0,1:T(2,128)S(1)}, f32[2,12,64]{2,0,1:T(2,128)}, u32[]{:S(2)}) copy-start(f32[2,12,64]{2,0,1:T(2,128)} %param.11) | copy-start | bytes 18436
  1.4 3.8 %copy-start.7 = (f32[2,12,64]{2,0,1:T(2,128)S(1)}, f32[2,12,64]{2,0,1:T(2,128)}, u32[]{:S(2)}) copy-start(f32[2,12,64]{2,0,1:T(2,128)} %param.12) | copy-start | bytes 18436
  1.4 3.8 %copy-start.2 = (f32[12,64]{1,0:T(8,128)S(1)}, f32[12,64]{1,0:T(8,128)}, u32[]{:S(2)}) copy-start(f32[12,64]{1,0:T(8,128)} %diffusivity_ref.1) | copy-start | bytes 9220
  2.5 10.5 %collective-permute-start.4 = (f32[2,6,4,8,128]{4,3,2,1,0:T(8,128)S(1)}, f32[2,6,4,8,128]{4,3,2,1,0:T(8,128)S(1)}, u32[]{:S(2)}, u32[]{:S(2)}) collective-permute-start(f32[2,6,4,8,128]{4,3,2,1,0:T(8,128)S(1)} %get-tuple-element.59), channel_id=1, source_target_pairs={{0,8},{4,12},{8,0},{12,4},{16,24},{20,28},{24,16},{28,20},{1,9},{5... | collective-permute-start | bytes 589832 | tf_op jit(solution)/shard_map/ppermute | solution.py:625
  3.7 9.5 %collective-permute-start.5 = (f32[2,6,4,8,128]{4,3,2,1,0:T(8,128)S(1)}, f32[2,6,4,8,128]{4,3,2,1,0:T(8,128)S(1)}, u32[]{:S(2)}, u32[]{:S(2)}) collective-permute-start(f32[2,6,4,8,128]{4,3,2,1,0:T(8,128)S(1)} %get-tuple-element.60), channel_id=1, source_target_pairs={{0,16},{4,20},{8,24},{12,28},{16,0},{20,4},{24,8},{28,12},{1,17},{... | collective-permute-start | bytes 589832 | tf_op jit(solution)/shard_map/ppermute | solution.py:625
  5.0 8.5 %collective-permute-start.6 = (f32[2,6,4,8,128]{4,3,2,1,0:T(8,128)S(1)}, f32[2,6,4,8,128]{4,3,2,1,0:T(8,128)S(1)}, u32[]{:S(2)}, u32[]{:S(2)}) collective-permute-start(f32[2,6,4,8,128]{4,3,2,1,0:T(8,128)S(1)} %get-tuple-element.61), channel_id=1, source_target_pairs={{0,24},{4,28},{8,16},{12,20},{16,8},{20,12},{24,0},{28,4},{1,25},{... | collective-permute-start | bytes 589832 | tf_op jit(solution)/shard_map/ppermute | solution.py:625
  5.3 4.1 %copy-start.1 = (f32[12,64,512]{2,1,0:T(8,128)S(1)}, f32[12,64,512]{2,1,0:T(8,128)}, u32[]{:S(2)}) copy-start(f32[12,64,512]{2,1,0:T(8,128)} %field_ref.3) | copy-start | bytes 4718596
  10.5 5.9 %collective-permute-start = (f32[2,6,4,8,128]{4,3,2,1,0:T(8,128)S(1)}, f32[2,6,4,8,128]{4,3,2,1,0:T(8,128)S(1)}, u32[]{:S(2)}, u32[]{:S(2)}) collective-permute-start(f32[2,6,4,8,128]{4,3,2,1,0:T(8,128)S(1)} %get-tuple-element.55), channel_id=1, source_target_pairs={{0,8},{4,12},{8,0},{12,4},{16,24},{20,28},{24,16},{28,20},{1,9},{5... | collective-permute-start | bytes 589832 | tf_op jit(solution)/shard_map/ppermute | solution.py:625
  11.7 5.4 %collective-permute-start.1 = (f32[2,6,4,8,128]{4,3,2,1,0:T(8,128)S(1)}, f32[2,6,4,8,128]{4,3,2,1,0:T(8,128)S(1)}, u32[]{:S(2)}, u32[]{:S(2)}) collective-permute-start(f32[2,6,4,8,128]{4,3,2,1,0:T(8,128)S(1)} %get-tuple-element.56), channel_id=1, source_target_pairs={{0,16},{4,20},{8,24},{12,28},{16,0},{20,4},{24,8},{28,12},{1,17},{... | collective-permute-start | bytes 589832 | tf_op jit(solution)/shard_map/ppermute | solution.py:625
  13.0 8.6 %collective-permute-start.2 = (f32[2,6,4,8,128]{4,3,2,1,0:T(8,128)S(1)}, f32[2,6,4,8,128]{4,3,2,1,0:T(8,128)S(1)}, u32[]{:S(2)}, u32[]{:S(2)}) collective-permute-start(f32[2,6,4,8,128]{4,3,2,1,0:T(8,128)S(1)} %get-tuple-element.57), channel_id=1, source_target_pairs={{0,24},{4,28},{8,16},{12,20},{16,8},{20,12},{24,0},{28,4},{1,25},{... | collective-permute-start | bytes 589832 | tf_op jit(solution)/shard_map/ppermute | solution.py:625
  13.6 10.3 %collective-permute-start.7 = (f32[4,6,4,8,128]{4,3,2,1,0:T(8,128)S(1)}, f32[4,6,4,8,128]{4,3,2,1,0:T(8,128)S(1)}, u32[]{:S(2)}, u32[]{:S(2)}) collective-permute-start(f32[4,6,4,8,128]{4,3,2,1,0:T(8,128)S(1)} %pad_maximum_fusion.1), channel_id=1, source_target_pairs={{0,4},{4,0},{8,12},{12,8},{16,20},{20,16},{24,28},{28,24},{1,5},{5... | collective-permute-start | bytes 1179656 | tf_op jit(solution)/shard_map/ppermute | solution.py:635
  21.6 7.9 %collective-permute-start.3 = (f32[4,6,4,8,128]{4,3,2,1,0:T(8,128)S(1)}, f32[4,6,4,8,128]{4,3,2,1,0:T(8,128)S(1)}, u32[]{:S(2)}, u32[]{:S(2)}) collective-permute-start(f32[4,6,4,8,128]{4,3,2,1,0:T(8,128)S(1)} %pad_maximum_fusion), channel_id=1, source_target_pairs={{0,4},{4,0},{8,12},{12,8},{16,20},{20,16},{24,28},{28,24},{1,5},{5... | collective-permute-start | bytes 1179656 | tf_op jit(solution)/shard_map/ppermute | solution.py:635
  24.9 10.9 %collective-permute-start.8 = (f32[54,8,128]{2,1,0:T(8,128)S(1)}, f32[54,8,128]{2,1,0:T(8,128)S(1)}, u32[]{:S(2)}, u32[]{:S(2)}) collective-permute-start(f32[54,8,128]{2,1,0:T(8,128)S(1)} %get-tuple-element.69), channel_id=1, source_target_pairs={{0,1},{1,0},{2,3},{3,2},{4,5},{5,4},{6,7},{7,6},{8,9},{9,8},{10,11... | collective-permute-start | bytes 663560 | tf_op jit(solution)/shard_map/ppermute | solution.py:642
  25.1 10.6 %collective-permute-start.9 = (f32[54,8,128]{2,1,0:T(8,128)S(1)}, f32[54,8,128]{2,1,0:T(8,128)S(1)}, u32[]{:S(2)}, u32[]{:S(2)}) collective-permute-start(f32[54,8,128]{2,1,0:T(8,128)S(1)} %get-tuple-element.70), channel_id=1, source_target_pairs={{1,2},{2,1},{5,6},{6,5},{9,10},{10,9},{13,14},{14,13},{17,18},{18,... | collective-permute-start | bytes 663560 | tf_op jit(solution)/shard_map/ppermute | solution.py:642
  35.8 8.3 %collective-permute-start.10 = (f32[2,6,4,8,128]{4,3,2,1,0:T(8,128)S(1)}, f32[2,6,4,8,128]{4,3,2,1,0:T(8,128)S(1)}, u32[]{:S(2)}, u32[]{:S(2)}) collective-permute-start(f32[2,6,4,8,128]{4,3,2,1,0:T(8,128)S(1)} %get-tuple-element.72), channel_id=1, source_target_pairs={{0,8},{4,12},{8,0},{12,4},{16,24},{20,28},{24,16},{28,20},{1,9},{5... | collective-permute-start | bytes 589832 | tf_op jit(solution)/shard_map/ppermute | solution.py:625
  36.8 7.3 %collective-permute-start.11 = (f32[2,6,4,8,128]{4,3,2,1,0:T(8,128)S(1)}, f32[2,6,4,8,128]{4,3,2,1,0:T(8,128)S(1)}, u32[]{:S(2)}, u32[]{:S(2)}) collective-permute-start(f32[2,6,4,8,128]{4,3,2,1,0:T(8,128)S(1)} %get-tuple-element.73), channel_id=1, source_target_pairs={{0,16},{4,20},{8,24},{12,28},{16,0},{20,4},{24,8},{28,12},{1,17},{... | collective-permute-start | bytes 589832 | tf_op jit(solution)/shard_map/ppermute | solution.py:625
  37.4 9.5 %collective-permute-start.12 = (f32[2,6,4,8,128]{4,3,2,1,0:T(8,128)S(1)}, f32[2,6,4,8,128]{4,3,2,1,0:T(8,128)S(1)}, u32[]{:S(2)}, u32[]{:S(2)}) collective-permute-start(f32[2,6,4,8,128]{4,3,2,1,0:T(8,128)S(1)} %get-tuple-element.74), channel_id=1, source_target_pairs={{0,24},{4,28},{8,16},{12,20},{16,8},{20,12},{24,0},{28,4},{1,25},{... | collective-permute-start | bytes 589832 | tf_op jit(solution)/shard_map/ppermute | solution.py:625
  47.0 3.3 %collective-permute-start.15 = (f32[4,6,4,8,128]{4,3,2,1,0:T(8,128)S(1)}, f32[4,6,4,8,128]{4,3,2,1,0:T(8,128)S(1)}, u32[]{:S(2)}, u32[]{:S(2)}) collective-permute-start(f32[4,6,4,8,128]{4,3,2,1,0:T(8,128)S(1)} %pad_maximum_fusion.2), channel_id=1, source_target_pairs={{0,4},{4,0},{8,12},{12,8},{16,20},{20,16},{24,28},{28,24},{1,5},{5... | collective-permute-start | bytes 1179656 | tf_op jit(solution)/shard_map/ppermute | solution.py:635
  48.5 6.5 %collective-permute-start.13 = (f32[2,6,4,8,128]{4,3,2,1,0:T(8,128)S(1)}, f32[2,6,4,8,128]{4,3,2,1,0:T(8,128)S(1)}, u32[]{:S(2)}, u32[]{:S(2)}) collective-permute-start(f32[2,6,4,8,128]{4,3,2,1,0:T(8,128)S(1)} %get-tuple-element.84), channel_id=1, source_target_pairs={{0,8},{4,12},{8,0},{12,4},{16,24},{20,28},{24,16},{28,20},{1,9},{5... | collective-permute-start | bytes 589832 | tf_op jit(solution)/shard_map/ppermute | solution.py:625
  49.0 6.1 %collective-permute-start.14 = (f32[2,6,4,8,128]{4,3,2,1,0:T(8,128)S(1)}, f32[2,6,4,8,128]{4,3,2,1,0:T(8,128)S(1)}, u32[]{:S(2)}, u32[]{:S(2)}) collective-permute-start(f32[2,6,4,8,128]{4,3,2,1,0:T(8,128)S(1)} %get-tuple-element.85), channel_id=1, source_target_pairs={{0,16},{4,20},{8,24},{12,28},{16,0},{20,4},{24,8},{28,12},{1,17},{... | collective-permute-start | bytes 589832 | tf_op jit(solution)/shard_map/ppermute | solution.py:625
  52.1 6.9 %collective-permute-start.16 = (f32[2,6,4,8,128]{4,3,2,1,0:T(8,128)S(1)}, f32[2,6,4,8,128]{4,3,2,1,0:T(8,128)S(1)}, u32[]{:S(2)}, u32[]{:S(2)}) collective-permute-start(f32[2,6,4,8,128]{4,3,2,1,0:T(8,128)S(1)} %get-tuple-element.91), channel_id=1, source_target_pairs={{0,24},{4,28},{8,16},{12,20},{16,8},{20,12},{24,0},{28,4},{1,25},{... | collective-permute-start | bytes 589832 | tf_op jit(solution)/shard_map/ppermute | solution.py:625
  59.0 3.0 %collective-permute-start.17 = (f32[4,6,4,8,128]{4,3,2,1,0:T(8,128)S(1)}, f32[4,6,4,8,128]{4,3,2,1,0:T(8,128)S(1)}, u32[]{:S(2)}, u32[]{:S(2)}) collective-permute-start(f32[4,6,4,8,128]{4,3,2,1,0:T(8,128)S(1)} %pad_maximum_fusion.3), channel_id=1, source_target_pairs={{0,4},{4,0},{8,12},{12,8},{16,20},{20,16},{24,28},{28,24},{1,5},{5... | collective-permute-start | bytes 1179656 | tf_op jit(solution)/shard_map/ppermute | solution.py:635

commit v4 on v3

--- a/solution.py
+++ b/solution.py
@@ -267,8 +267,11 @@
 
 
 def arrived(refs, u, plane):
+    swapped = refs[4]
+    if len(swapped.shape) == 6:
+        swapped = swapped.at[1 - lax.axis_index(MESH_LON) % 2]
     return [
-        refs[4][mate >> 1, u, plane] if mate & 1 else refs[mate >> 1][0, u, plane]
+        swapped[mate >> 1, u, plane] if mate & 1 else refs[mate >> 1][0, u, plane]
         for mate in range(8)
     ]
 
@@ -629,6 +632,13 @@
     return pairs[:1] + [between_chips(pairs, chip) for chip in range(1, len(pairs))]
 
 
+def core_pairs(pairs):
+    peers = lax.axis_size(MESH_LON)
+    away = jnp.concatenate([pair[1:] for pair in pairs], axis=0)
+    groups = [[i, i + 1] for i in range(0, peers, 2)]
+    return pairs + [lax.all_gather(away, MESH_LON, axis_index_groups=groups)]
+
+
 def between_cores(pairs):
     peers = lax.axis_size(MESH_LON)
     away = jnp.concatenate([pair[1:] for pair in pairs], axis=0)
@@ -673,10 +683,11 @@
             pltpu.VMEM((steps * pairs * rows, LANES), jnp.bfloat16),
         ],
     )(lon_shift, lon_frac, lat_shift, lat_frac, remap_frac, diffusivity)
-    outer = between_cores(arrive(outer))
+    outer = core_pairs(arrive(outer))
     *inner, coeff = lax.optimization_barrier((*inner, coeff))
     inner = arrive(inner)
     field, even, odd = call(outer_kernel, 1, [half, edges, edges])(*outer, edge)
+    inner, _ = lax.optimization_barrier((inner, field))
     inner = between_cores(inner)
     even, odd = exchange_edges(even, odd)
     *inner, near = call(inner_kernel, 6, messages + [half], [(3,) + work, moved])(
@@ -690,13 +701,14 @@
         messages,
         [(2,) + work, moved, (levels, COEFFS, rows // 2, LANES)],
     )(near, field, even, odd, coeff, spread)
-    *inner, outer = lax.optimization_barrier((*inner, list(outer)))
-    inner = between_cores(inner)
+    *inner, _ = lax.optimization_barrier((*inner, list(outer)))
+    outer = list(outer)
+    inner = core_pairs(inner)
     done = call(
         functools.partial(unpack_kernel, INNER), 2, [tracers.shape], held, out_specs=[anywhere]
     )(*inner)[0]
-    outer[3], done = lax.optimization_barrier((outer[3], done))
-    outer = between_cores(arrive(outer))
+    outer, done = lax.optimization_barrier((arrive(outer), done))
+    outer = between_cores(outer)
     return call(
         functools.partial(unpack_kernel, OUTER),
         2,

time: 64 us -> 58.8 us (0.919)
  waiting for transfers between devices: 15.9 us -> 6.49 us
  blocking collectives: 0 us -> 8.2 us
  starting transfers between devices: 23.1 us -> 19.7 us
  Pallas kernels: 22.8 us -> 22.1 us
    ppermute x12, waiting for transfers between devices: 14.6 us -> 5.13 us  [between_chips(): lax.ppermute(pairs[chip], MESH_LON, [(i, i ^ 2 * chip) for i in range(pee...]
    all_gather x0 -> x2, blocking collectives: none -> 8.2 us  [core_pairs(): return pairs + [lax.all_gather(away, MESH_LON, axis_index_groups=groups)]]
    ppermute x4 -> x2, starting transfers between devices: 7.57 us -> 4.31 us  [between_cores(): lax.ppermute(away, MESH_LON, [(i, i ^ 1) for i in range(peers)])]
    ppermute x4 -> x2, waiting for transfers between devices: 1.36 us -> 1.35 us  [between_cores(): lax.ppermute(away, MESH_LON, [(i, i ^ 1) for i in range(peers)])]
  transfers between devices with their start and end apart: 18 -> 16, of which waited for: 9 -> 5; matrix products, arithmetic and copies ran while one was open for 0% -> 0% of each run, Pallas kernels for 31% -> 33%
where the time goes in v4:
time: 58.8 us; the launch traced here: 58.6 us
  Pallas kernels  22.1 us (38%)
  starting transfers between devices  19.7 us (34%)
  blocking collectives  8.2 us (14%)
  waiting for transfers between devices  6.49 us (11%)
  local copies, waits for them, and re-layouts  1.58 us (3%)
    ppermute x12, starting transfers between devices, between_chips(): lax.ppermute(pairs[chip], MESH_LON, [(i, i ^ 2 * chip) for i in range(pee...  10.9 us
    all_gather x2, blocking collectives, core_pairs(): return pairs + [lax.all_gather(away, MESH_LON, axis_index_groups=groups)]  8.2 us
    pallas_call x1, Pallas kernels, by_tracer(): call(inner_kernel, 6, messages + [half], [(3,) + work, moved])  5.86 us
    pallas_call x1, Pallas kernels, by_tracer(): call(last_kernel, 6, messages, [(2,) + work, moved, (levels, COEFFS, rows...  5.37 us
    ppermute x12, waiting for transfers between devices, between_chips(): lax.ppermute(pairs[chip], MESH_LON, [(i, i ^ 2 * chip) for i in range(pee...  5.13 us
    ppermute x2, starting transfers between devices, exchange_edges(): return (lax.ppermute(even, 'lat', near), lax.ppermute(odd, 'lat', far))  4.5 us
    ppermute x2, starting transfers between devices, between_cores(): lax.ppermute(away, MESH_LON, [(i, i ^ 1) for i in range(peers)])  4.31 us
    pallas_call x1, Pallas kernels, by_tracer(): call(coeff_kernel, 6, [(steps, levels, COEFFS, rows, LANES), (2, pairs, T...  4.12 us
  transfers between devices with their start and end apart: 16, of which 5 were waited for; matrix products, arithmetic and copies ran while one was open for 0% of the time, Pallas kernels for 33%

profile of v4, /device:TPU:9, one launch (start us, length us, event | category | flops | bytes accessed | tf_op | source)
XLA Modules:
  0.0 58.6 jit_solution(13713055320188216276)
XLA Ops:
  0.0 1.4 %copy-done = f32[12,64,512]{2,1,0:T(8,128)S(1)} copy-done((f32[12,64,512]{2,1,0:T(8,128)S(1)}, f32[12,64,512]{2,1,0:T(8,128)}, u32[]{:S(2)}) %copy-start) | copy-done | bytes 1572888
  1.4 0.0 copy-start.7
  1.4 0.0 copy-start.2
  1.4 1.0 %shard_map.75 = (f32[2,6,4,8,128]{4,3,2,1,0:T(8,128)S(1)}, f32[2,6,4,8,128]{4,3,2,1,0:T(8,128)S(1)}, f32[2,6,4,8,128]{4,3,2,1,0:T(8,128)S(1)}, f32[2,6,4,8,128]{4,3,2,1,0:T(8,128)S(1)}) custom-call(f32[12,64,512]{2,1,0:T(8,128)S(1)} %copy-done), custom_call_target="tpu_custom_call" | custom-call | flops 2000000000 | bytes 6000000 | tf_op jit(solution)/shard_map/pallas_call | solution.py:670
  2.5 1.3 %collective-permute-start.3 = (f32[2,6,4,8,128]{4,3,2,1,0:T(8,128)S(1)}, f32[2,6,4,8,128]{4,3,2,1,0:T(8,128)S(1)}, u32[]{:S(2)}, u32[]{:S(2)}) collective-permute-start(f32[2,6,4,8,128]{4,3,2,1,0:T(8,128)S(1)} %get-tuple-element.62), channel_id=1, source_target_pairs={{0,8},{4,12},{8,0},{12,4},{16,24},{20,28},{24,16},{28,20},{1,9},{5... | collective-permute-start | bytes 589832 | tf_op jit(solution)/shard_map/ppermute | solution.py:628
  3.7 1.2 %collective-permute-start.4 = (f32[2,6,4,8,128]{4,3,2,1,0:T(8,128)S(1)}, f32[2,6,4,8,128]{4,3,2,1,0:T(8,128)S(1)}, u32[]{:S(2)}, u32[]{:S(2)}) collective-permute-start(f32[2,6,4,8,128]{4,3,2,1,0:T(8,128)S(1)} %get-tuple-element.63), channel_id=1, source_target_pairs={{0,16},{4,20},{8,24},{12,28},{16,0},{20,4},{24,8},{28,12},{1,17},{... | collective-permute-start | bytes 589832 | tf_op jit(solution)/shard_map/ppermute | solution.py:628
  5.0 0.2 collective-permute-start.5
  5.2 0.0 copy-done.3
  5.2 0.0 copy-done.4
  5.3 0.0 copy-start.1
  5.3 4.1 %shard_map.74 = (f32[2,12,15,64,128]{4,3,2,1,0:T(8,128)S(1)}, f32[2,6,8,128]{3,2,1,0:T(8,128)S(1)}, bf16[15,2,128,128]{3,2,1,0:T(8,128)(2,1)S(1)}) custom-call(s32[2,12,64]{2,1,0:T(8,128)S(1)} %copy.14.lon_shift_ref, f32[2,12,64]{2,1,0:T(8,128)S(1)} %copy.15.lon_frac_ref, s32[2,12,64]{2,1,0:T(8,128)S(1)} %copy.16.lat_shift_ref, ...), custom_call_target="tpu_custom_call" | custom-call | flops 6000000000 | bytes 18000000 | tf_op jit(solution)/shard_map/pallas_call | solution.py:673
  9.4 1.0 %shard_map.73 = (f32[2,6,4,8,128]{4,3,2,1,0:T(8,128)S(1)}, f32[2,6,4,8,128]{4,3,2,1,0:T(8,128)S(1)}, f32[2,6,4,8,128]{4,3,2,1,0:T(8,128)S(1)}, f32[2,6,4,8,128]{4,3,2,1,0:T(8,128)S(1)}) custom-call(f32[12,64,512]{2,1,0:T(8,128)S(1)} %copy-done.1), custom_call_target="tpu_custom_call" | custom-call | flops 2000000000 | bytes 6000000 | tf_op jit(solution)/shard_map/pallas_call | solution.py:670
  10.5 1.3 %collective-permute-start = (f32[2,6,4,8,128]{4,3,2,1,0:T(8,128)S(1)}, f32[2,6,4,8,128]{4,3,2,1,0:T(8,128)S(1)}, u32[]{:S(2)}, u32[]{:S(2)}) collective-permute-start(f32[2,6,4,8,128]{4,3,2,1,0:T(8,128)S(1)} %get-tuple-element.58), channel_id=1, source_target_pairs={{0,8},{4,12},{8,0},{12,4},{16,24},{20,28},{24,16},{28,20},{1,9},{5... | collective-permute-start | bytes 589832 | tf_op jit(solution)/shard_map/ppermute | solution.py:628
  11.7 1.2 %collective-permute-start.1 = (f32[2,6,4,8,128]{4,3,2,1,0:T(8,128)S(1)}, f32[2,6,4,8,128]{4,3,2,1,0:T(8,128)S(1)}, u32[]{:S(2)}, u32[]{:S(2)}) collective-permute-start(f32[2,6,4,8,128]{4,3,2,1,0:T(8,128)S(1)} %get-tuple-element.59), channel_id=1, source_target_pairs={{0,16},{4,20},{8,24},{12,28},{16,0},{20,4},{24,8},{28,12},{1,17},{... | collective-permute-start | bytes 589832 | tf_op jit(solution)/shard_map/ppermute | solution.py:628
  13.0 0.0 collective-permute-done.3.refs_1_
  13.0 0.3 collective-permute-start.2
  13.3 0.0 collective-permute-done.4.refs_2_
  13.3 0.2 collective-permute-done.5.refs_3_
  13.6 4.1 %all-gather = f32[8,6,4,8,128]{4,3,2,1,0:T(8,128)S(1)} all-gather(f32[4,6,4,8,128]{4,3,2,1,0:T(8,128)S(1)} %pad_maximum_fusion), channel_id=2, replica_groups={{0,4},{8,12},{16,20},{24,28},{1,5},{9,13},{17,21},{25,29},{2,6},{10,14}..., dimensions={0}, use_global_device_ids=true | all-gather | bytes 1179648 | tf_op jit(solution)/shard_map/all_gather | solution.py:639
  17.7 1.0 %shard_map.76 = (f32[12,4,32,128]{3,2,1,0:T(8,128)S(1)}, f32[54,8,128]{2,1,0:T(8,128)S(1)}, f32[54,8,128]{2,1,0:T(8,128)S(1)}) custom-call(f32[2,6,4,8,128]{4,3,2,1,0:T(8,128)S(1)} %get-tuple-element.61.refs_0_, f32[2,6,4,8,128]{4,3,2,1,0:T(8,128)S(1)} %collective-permute-done.3.refs_1_, f32[2,6,4,8,128]{4,3,2,1,0:T(8,128)S(1)} %collective-permute-done.4.refs_2_, ...), custom_call_target="tpu_custom_call" | custom-call | flops 1000000000 | bytes 3000000 | tf_op jit(solution)/shard_map/pallas_call | solution.py:689
  18.8 0.0 collective-permute-done.refs_1_
  18.8 0.0 collective-permute-done.1.refs_2_
  18.8 2.8 %collective-permute-done.2.refs_3_ = f32[2,6,4,8,128]{4,3,2,1,0:T(8,128)S(1)} collective-permute-done((f32[2,6,4,8,128]{4,3,2,1,0:T(8,128)S(1)}, f32[2,6,4,8,128]{4,3,2,1,0:T(8,128)S(1)}, u32[]{:S(2)}, u32[]{:S(2)}) %collective-permute-start.2) | collective-permute-done | bytes 196640 | tf_op jit(solution)/shard_map/ppermute | solution.py:628
  21.7 2.2 %collective-permute-start.6 = (f32[4,6,4,8,128]{4,3,2,1,0:T(8,128)S(1)}, f32[4,6,4,8,128]{4,3,2,1,0:T(8,128)S(1)}, u32[]{:S(2)}, u32[]{:S(2)}) collective-permute-start(f32[4,6,4,8,128]{4,3,2,1,0:T(8,128)S(1)} %pad_maximum_fusion.1), channel_id=1, source_target_pairs={{0,4},{4,0},{8,12},{12,8},{16,20},{20,16},{24,28},{28,24},{1,5},{5... | collective-permute-start | bytes 1179656 | tf_op jit(solution)/shard_map/ppermute | solution.py:645
  23.9 0.2 collective-permute-start.7
  24.1 4.3 %collective-permute-start.8 = (f32[54,8,128]{2,1,0:T(8,128)S(1)}, f32[54,8,128]{2,1,0:T(8,128)S(1)}, u32[]{:S(2)}, u32[]{:S(2)}) collective-permute-start(f32[54,8,128]{2,1,0:T(8,128)S(1)} %get-tuple-element.78), channel_id=1, source_target_pairs={{1,2},{2,1},{5,6},{6,5},{9,10},{10,9},{13,14},{14,13},{17,18},{18,... | collective-permute-start | bytes 663560 | tf_op jit(solution)/shard_map/ppermute | solution.py:652
  28.4 0.0 collective-permute-done.6.refs_4_
  28.4 5.9 %shard_map.77 = (f32[2,6,4,8,128]{4,3,2,1,0:T(8,128)S(1)}, f32[2,6,4,8,128]{4,3,2,1,0:T(8,128)S(1)}, f32[2,6,4,8,128]{4,3,2,1,0:T(8,128)S(1)}, f32[2,6,4,8,128]{4,3,2,1,0:T(8,128)S(1)}, f32[12,4,32,128]{3,2,1,0:T(8,128)S(1)}) custom-call(f32[2,6,4,8,128]{4,3,2,1,0:T(8,128)S(1)} %get-tuple-element.67.refs_0_, ...), custom_call_target="tpu_custom_call" | custom-call | flops 6000000000 | bytes 18000000 | tf_op jit(solution)/shard_map/pallas_call | solution.py:693
  34.3 0.0 collective-permute-done.7.even_ref
  34.3 0.0 collective-permute-done.8.odd_ref
  34.3 1.0 %collective-permute-start.12 = (f32[2,6,4,8,128]{4,3,2,1,0:T(8,128)S(1)}, f32[2,6,4,8,128]{4,3,2,1,0:T(8,128)S(1)}, u32[]{:S(2)}, u32[]{:S(2)}) collective-permute-start(f32[2,6,4,8,128]{4,3,2,1,0:T(8,128)S(1)} %get-tuple-element.87), channel_id=1, source_target_pairs={{0,8},{4,12},{8,0},{12,4},{16,24},{20,28},{24,16},{28,20},{1,9},{5... | collective-permute-start | bytes 589832 | tf_op jit(solution)/shard_map/ppermute | solution.py:628
  35.3 0.5 collective-permute-start.13
  35.8 1.2 %collective-permute-start.14 = (f32[2,6,4,8,128]{4,3,2,1,0:T(8,128)S(1)}, f32[2,6,4,8,128]{4,3,2,1,0:T(8,128)S(1)}, u32[]{:S(2)}, u32[]{:S(2)}) collective-permute-start(f32[2,6,4,8,128]{4,3,2,1,0:T(8,128)S(1)} %get-tuple-element.89), channel_id=1, source_target_pairs={{0,24},{4,28},{8,16},{12,20},{16,8},{20,12},{24,0},{28,4},{1,25},{... | collective-permute-start | bytes 589832 | tf_op jit(solution)/shard_map/ppermute | solution.py:628
  37.0 5.4 %shard_map.78 = (f32[2,6,4,8,128]{4,3,2,1,0:T(8,128)S(1)}, f32[2,6,4,8,128]{4,3,2,1,0:T(8,128)S(1)}, f32[2,6,4,8,128]{4,3,2,1,0:T(8,128)S(1)}, f32[2,6,4,8,128]{4,3,2,1,0:T(8,128)S(1)}) custom-call(f32[12,4,32,128]{3,2,1,0:T(8,128)S(1)} %get-tuple-element.72.near_ref, f32[12,4,32,128]{3,2,1,0:T(8,128)S(1)} %get-tuple-element.66.refs_5_.field_ref, ...), custom_call_target="tpu_custom_call" | custom-call | flops 6000000000 | bytes 18000000 | tf_op jit(solution)/shard_map/pallas_call | solution.py:698
  42.4 1.0 %collective-permute-start.9 = (f32[2,6,4,8,128]{4,3,2,1,0:T(8,128)S(1)}, f32[2,6,4,8,128]{4,3,2,1,0:T(8,128)S(1)}, u32[]{:S(2)}, u32[]{:S(2)}) collective-permute-start(f32[2,6,4,8,128]{4,3,2,1,0:T(8,128)S(1)} %get-tuple-element.83), channel_id=1, source_target_pairs={{0,8},{4,12},{8,0},{12,4},{16,24},{20,28},{24,16},{28,20},{1,9},{5... | collective-permute-start | bytes 589832 | tf_op jit(solution)/shard_map/ppermute | solution.py:628
  43.4 0.6 collective-permute-start.10
  43.9 0.0 collective-permute-done.12.refs_1_
  43.9 1.1 %collective-permute-start.11 = (f32[2,6,4,8,128]{4,3,2,1,0:T(8,128)S(1)}, f32[2,6,4,8,128]{4,3,2,1,0:T(8,128)S(1)}, u32[]{:S(2)}, u32[]{:S(2)}) collective-permute-start(f32[2,6,4,8,128]{4,3,2,1,0:T(8,128)S(1)} %get-tuple-element.85), channel_id=1, source_target_pairs={{0,24},{4,28},{8,16},{12,20},{16,8},{20,12},{24,0},{28,4},{1,25},{... | collective-permute-start | bytes 589832 | tf_op jit(solution)/shard_map/ppermute | solution.py:628
  45.1 0.0 collective-permute-done.13.refs_2_
  45.1 0.2 collective-permute-done.14.refs_3_
  45.4 4.1 %all-gather.1 = f32[8,6,4,8,128]{4,3,2,1,0:T(8,128)S(1)} all-gather(f32[4,6,4,8,128]{4,3,2,1,0:T(8,128)S(1)} %pad_maximum_fusion.2), channel_id=3, replica_groups={{0,4},{8,12},{16,20},{24,28},{1,5},{9,13},{17,21},{25,29},{2,6},{10,14}..., dimensions={0}, use_global_device_ids=true | all-gather | bytes 1179648 | tf_op jit(solution)/shard_map/all_gather | solution.py:639
  49.5 1.8 %shard_map.79.refs_5_ = f32[12,64,512]{2,1,0:T(8,128)} custom-call(f32[2,6,4,8,128]{4,3,2,1,0:T(8,128)S(1)} %get-tuple-element.90.refs_0_, f32[2,6,4,8,128]{4,3,2,1,0:T(8,128)S(1)} %collective-permute-done.12.refs_1_, f32[2,6,4,8,128]{4,3,2,1,0:T(8,128)S(1)} %collective-permute-done.13.refs_2_, f32[2,6,4,8,128]{4,3,2,1,0:T(8,128)S(1)} %collective-permute-done.14.refs_3_, ...), custom_call_target="tpu_custom_call" | custom-call | flops 2000000000 | bytes 6000000 | tf_op jit(solution)/shard_map/pallas_call | solution.py:707
  51.3 0.0 collective-permute-done.9.refs_1_
  51.4 0.0 collective-permute-done.10.refs_2_
  51.4 1.8 %collective-permute-done.11.refs_3_ = f32[2,6,4,8,128]{4,3,2,1,0:T(8,128)S(1)} collective-permute-done((f32[2,6,4,8,128]{4,3,2,1,0:T(8,128)S(1)}, f32[2,6,4,8,128]{4,3,2,1,0:T(8,128)S(1)}, u32[]{:S(2)}, u32[]{:S(2)}) %collective-permute-start.11) | collective-permute-done | bytes 196640 | tf_op jit(solution)/shard_map/ppermute | solution.py:628
  53.3 2.1 %collective-permute-start.15 = (f32[4,6,4,8,128]{4,3,2,1,0:T(8,128)S(1)}, f32[4,6,4,8,128]{4,3,2,1,0:T(8,128)S(1)}, u32[]{:S(2)}, u32[]{:S(2)}) collective-permute-start(f32[4,6,4,8,128]{4,3,2,1,0:T(8,128)S(1)} %pad_maximum_fusion.3), channel_id=1, source_target_pairs={{0,4},{4,0},{8,12},{12,8},{16,20},{20,16},{24,28},{28,24},{1,5},{5... | collective-permute-start | bytes 1179656 | tf_op jit(solution)/shard_map/ppermute | solution.py:645
  55.4 1.3 %collective-permute-done.15.refs_4_ = f32[4,6,4,8,128]{4,3,2,1,0:T(8,128)S(1)} collective-permute-done((f32[4,6,4,8,128]{4,3,2,1,0:T(8,128)S(1)}, f32[4,6,4,8,128]{4,3,2,1,0:T(8,128)S(1)}, u32[]{:S(2)}, u32[]{:S(2)}) %collective-permute-start.15) | collective-permute-done | bytes 393248 | tf_op jit(solution)/shard_map/ppermute | solution.py:645
  56.8 1.8 %shard_map.80 = f32[12,64,512]{2,1,0:T(8,128)} custom-call(f32[2,6,4,8,128]{4,3,2,1,0:T(8,128)S(1)} %get-tuple-element.94.refs_0_, f32[2,6,4,8,128]{4,3,2,1,0:T(8,128)S(1)} %collective-permute-done.9.refs_1_, f32[2,6,4,8,128]{4,3,2,1,0:T(8,128)S(1)} %collective-permute-done.10.refs_2_, ...), custom_call_target="tpu_custom_call", output_to_operand_aliasing={{}: (5, {})} | custom-call | flops 2000000000 | bytes 6000000 | tf_op jit(solution)/shard_map/pallas_call | solution.py:712
  (35 shorter events, 0.3 us)
Async XLA Ops:
  0.0 1.4 %copy-start = (f32[12,64,512]{2,1,0:T(8,128)S(1)}, f32[12,64,512]{2,1,0:T(8,128)}, u32[]{:S(2)}) copy-start(f32[12,64,512]{2,1,0:T(8,128)} %field_ref.3) | copy-start | bytes 4718596
  1.4 3.8 %copy-start.3 = (s32[2,12,64]{2,0,1:T(2,128)S(1)}, s32[2,12,64]{2,0,1:T(2,128)}, u32[]{:S(2)}) copy-start(s32[2,12,64]{2,0,1:T(2,128)} %param.8) | copy-start | bytes 18436
  1.4 3.8 %copy-start.4 = (f32[2,12,64]{2,0,1:T(2,128)S(1)}, f32[2,12,64]{2,0,1:T(2,128)}, u32[]{:S(2)}) copy-start(f32[2,12,64]{2,0,1:T(2,128)} %param.9) | copy-start | bytes 18436
  1.4 3.8 %copy-start.5 = (s32[2,12,64]{2,0,1:T(2,128)S(1)}, s32[2,12,64]{2,0,1:T(2,128)}, u32[]{:S(2)}) copy-start(s32[2,12,64]{2,0,1:T(2,128)} %param.10) | copy-start | bytes 18436
  1.4 3.8 %copy-start.6 = (f32[2,12,64]{2,0,1:T(2,128)S(1)}, f32[2,12,64]{2,0,1:T(2,128)}, u32[]{:S(2)}) copy-start(f32[2,12,64]{2,0,1:T(2,128)} %param.11) | copy-start | bytes 18436
  1.4 3.8 %copy-start.7 = (f32[2,12,64]{2,0,1:T(2,128)S(1)}, f32[2,12,64]{2,0,1:T(2,128)}, u32[]{:S(2)}) copy-start(f32[2,12,64]{2,0,1:T(2,128)} %param.12) | copy-start | bytes 18436
  1.4 3.8 %copy-start.2 = (f32[12,64]{1,0:T(8,128)S(1)}, f32[12,64]{1,0:T(8,128)}, u32[]{:S(2)}) copy-start(f32[12,64]{1,0:T(8,128)} %diffusivity_ref.1) | copy-start | bytes 9220
  2.5 10.5 %collective-permute-start.3 = (f32[2,6,4,8,128]{4,3,2,1,0:T(8,128)S(1)}, f32[2,6,4,8,128]{4,3,2,1,0:T(8,128)S(1)}, u32[]{:S(2)}, u32[]{:S(2)}) collective-permute-start(f32[2,6,4,8,128]{4,3,2,1,0:T(8,128)S(1)} %get-tuple-element.62), channel_id=1, source_target_pairs={{0,8},{4,12},{8,0},{12,4},{16,24},{20,28},{24,16},{28,20},{1,9},{5... | collective-permute-start | bytes 589832 | tf_op jit(solution)/shard_map/ppermute | solution.py:628
  3.7 9.5 %collective-permute-start.4 = (f32[2,6,4,8,128]{4,3,2,1,0:T(8,128)S(1)}, f32[2,6,4,8,128]{4,3,2,1,0:T(8,128)S(1)}, u32[]{:S(2)}, u32[]{:S(2)}) collective-permute-start(f32[2,6,4,8,128]{4,3,2,1,0:T(8,128)S(1)} %get-tuple-element.63), channel_id=1, source_target_pairs={{0,16},{4,20},{8,24},{12,28},{16,0},{20,4},{24,8},{28,12},{1,17},{... | collective-permute-start | bytes 589832 | tf_op jit(solution)/shard_map/ppermute | solution.py:628
  5.0 8.5 %collective-permute-start.5 = (f32[2,6,4,8,128]{4,3,2,1,0:T(8,128)S(1)}, f32[2,6,4,8,128]{4,3,2,1,0:T(8,128)S(1)}, u32[]{:S(2)}, u32[]{:S(2)}) collective-permute-start(f32[2,6,4,8,128]{4,3,2,1,0:T(8,128)S(1)} %get-tuple-element.64), channel_id=1, source_target_pairs={{0,24},{4,28},{8,16},{12,20},{16,8},{20,12},{24,0},{28,4},{1,25},{... | collective-permute-start | bytes 589832 | tf_op jit(solution)/shard_map/ppermute | solution.py:628
  5.3 4.1 %copy-start.1 = (f32[12,64,512]{2,1,0:T(8,128)S(1)}, f32[12,64,512]{2,1,0:T(8,128)}, u32[]{:S(2)}) copy-start(f32[12,64,512]{2,1,0:T(8,128)} %field_ref.3) | copy-start | bytes 4718596
  10.5 8.3 %collective-permute-start = (f32[2,6,4,8,128]{4,3,2,1,0:T(8,128)S(1)}, f32[2,6,4,8,128]{4,3,2,1,0:T(8,128)S(1)}, u32[]{:S(2)}, u32[]{:S(2)}) collective-permute-start(f32[2,6,4,8,128]{4,3,2,1,0:T(8,128)S(1)} %get-tuple-element.58), channel_id=1, source_target_pairs={{0,8},{4,12},{8,0},{12,4},{16,24},{20,28},{24,16},{28,20},{1,9},{5... | collective-permute-start | bytes 589832 | tf_op jit(solution)/shard_map/ppermute | solution.py:628
  11.7 7.0 %collective-permute-start.1 = (f32[2,6,4,8,128]{4,3,2,1,0:T(8,128)S(1)}, f32[2,6,4,8,128]{4,3,2,1,0:T(8,128)S(1)}, u32[]{:S(2)}, u32[]{:S(2)}) collective-permute-start(f32[2,6,4,8,128]{4,3,2,1,0:T(8,128)S(1)} %get-tuple-element.59), channel_id=1, source_target_pairs={{0,16},{4,20},{8,24},{12,28},{16,0},{20,4},{24,8},{28,12},{1,17},{... | collective-permute-start | bytes 589832 | tf_op jit(solution)/shard_map/ppermute | solution.py:628
  13.0 8.6 %collective-permute-start.2 = (f32[2,6,4,8,128]{4,3,2,1,0:T(8,128)S(1)}, f32[2,6,4,8,128]{4,3,2,1,0:T(8,128)S(1)}, u32[]{:S(2)}, u32[]{:S(2)}) collective-permute-start(f32[2,6,4,8,128]{4,3,2,1,0:T(8,128)S(1)} %get-tuple-element.60), channel_id=1, source_target_pairs={{0,24},{4,28},{8,16},{12,20},{16,8},{20,12},{24,0},{28,4},{1,25},{... | collective-permute-start | bytes 589832 | tf_op jit(solution)/shard_map/ppermute | solution.py:628
  21.7 6.7 %collective-permute-start.6 = (f32[4,6,4,8,128]{4,3,2,1,0:T(8,128)S(1)}, f32[4,6,4,8,128]{4,3,2,1,0:T(8,128)S(1)}, u32[]{:S(2)}, u32[]{:S(2)}) collective-permute-start(f32[4,6,4,8,128]{4,3,2,1,0:T(8,128)S(1)} %pad_maximum_fusion.1), channel_id=1, source_target_pairs={{0,4},{4,0},{8,12},{12,8},{16,20},{20,16},{24,28},{28,24},{1,5},{5... | collective-permute-start | bytes 1179656 | tf_op jit(solution)/shard_map/ppermute | solution.py:645
  23.9 10.4 %collective-permute-start.7 = (f32[54,8,128]{2,1,0:T(8,128)S(1)}, f32[54,8,128]{2,1,0:T(8,128)S(1)}, u32[]{:S(2)}, u32[]{:S(2)}) collective-permute-start(f32[54,8,128]{2,1,0:T(8,128)S(1)} %get-tuple-element.77), channel_id=1, source_target_pairs={{0,1},{1,0},{2,3},{3,2},{4,5},{5,4},{6,7},{7,6},{8,9},{9,8},{10,11... | collective-permute-start | bytes 663560 | tf_op jit(solution)/shard_map/ppermute | solution.py:652
  24.1 10.2 %collective-permute-start.8 = (f32[54,8,128]{2,1,0:T(8,128)S(1)}, f32[54,8,128]{2,1,0:T(8,128)S(1)}, u32[]{:S(2)}, u32[]{:S(2)}) collective-permute-start(f32[54,8,128]{2,1,0:T(8,128)S(1)} %get-tuple-element.78), channel_id=1, source_target_pairs={{1,2},{2,1},{5,6},{6,5},{9,10},{10,9},{13,14},{14,13},{17,18},{18,... | collective-permute-start | bytes 663560 | tf_op jit(solution)/shard_map/ppermute | solution.py:652
  34.3 9.7 %collective-permute-start.12 = (f32[2,6,4,8,128]{4,3,2,1,0:T(8,128)S(1)}, f32[2,6,4,8,128]{4,3,2,1,0:T(8,128)S(1)}, u32[]{:S(2)}, u32[]{:S(2)}) collective-permute-start(f32[2,6,4,8,128]{4,3,2,1,0:T(8,128)S(1)} %get-tuple-element.87), channel_id=1, source_target_pairs={{0,8},{4,12},{8,0},{12,4},{16,24},{20,28},{24,16},{28,20},{1,9},{5... | collective-permute-start | bytes 589832 | tf_op jit(solution)/shard_map/ppermute | solution.py:628
  35.3 9.8 %collective-permute-start.13 = (f32[2,6,4,8,128]{4,3,2,1,0:T(8,128)S(1)}, f32[2,6,4,8,128]{4,3,2,1,0:T(8,128)S(1)}, u32[]{:S(2)}, u32[]{:S(2)}) collective-permute-start(f32[2,6,4,8,128]{4,3,2,1,0:T(8,128)S(1)} %get-tuple-element.88), channel_id=1, source_target_pairs={{0,16},{4,20},{8,24},{12,28},{16,0},{20,4},{24,8},{28,12},{1,17},{... | collective-permute-start | bytes 589832 | tf_op jit(solution)/shard_map/ppermute | solution.py:628
  35.8 9.5 %collective-permute-start.14 = (f32[2,6,4,8,128]{4,3,2,1,0:T(8,128)S(1)}, f32[2,6,4,8,128]{4,3,2,1,0:T(8,128)S(1)}, u32[]{:S(2)}, u32[]{:S(2)}) collective-permute-start(f32[2,6,4,8,128]{4,3,2,1,0:T(8,128)S(1)} %get-tuple-element.89), channel_id=1, source_target_pairs={{0,24},{4,28},{8,16},{12,20},{16,8},{20,12},{24,0},{28,4},{1,25},{... | collective-permute-start | bytes 589832 | tf_op jit(solution)/shard_map/ppermute | solution.py:628
  42.4 9.0 %collective-permute-start.9 = (f32[2,6,4,8,128]{4,3,2,1,0:T(8,128)S(1)}, f32[2,6,4,8,128]{4,3,2,1,0:T(8,128)S(1)}, u32[]{:S(2)}, u32[]{:S(2)}) collective-permute-start(f32[2,6,4,8,128]{4,3,2,1,0:T(8,128)S(1)} %get-tuple-element.83), channel_id=1, source_target_pairs={{0,8},{4,12},{8,0},{12,4},{16,24},{20,28},{24,16},{28,20},{1,9},{5... | collective-permute-start | bytes 589832 | tf_op jit(solution)/shard_map/ppermute | solution.py:628
  43.4 8.0 %collective-permute-start.10 = (f32[2,6,4,8,128]{4,3,2,1,0:T(8,128)S(1)}, f32[2,6,4,8,128]{4,3,2,1,0:T(8,128)S(1)}, u32[]{:S(2)}, u32[]{:S(2)}) collective-permute-start(f32[2,6,4,8,128]{4,3,2,1,0:T(8,128)S(1)} %get-tuple-element.84), channel_id=1, source_target_pairs={{0,16},{4,20},{8,24},{12,28},{16,0},{20,4},{24,8},{28,12},{1,17},{... | collective-permute-start | bytes 589832 | tf_op jit(solution)/shard_map/ppermute | solution.py:628
  43.9 9.3 %collective-permute-start.11 = (f32[2,6,4,8,128]{4,3,2,1,0:T(8,128)S(1)}, f32[2,6,4,8,128]{4,3,2,1,0:T(8,128)S(1)}, u32[]{:S(2)}, u32[]{:S(2)}) collective-permute-start(f32[2,6,4,8,128]{4,3,2,1,0:T(8,128)S(1)} %get-tuple-element.85), channel_id=1, source_target_pairs={{0,24},{4,28},{8,16},{12,20},{16,8},{20,12},{24,0},{28,4},{1,25},{... | collective-permute-start | bytes 589832 | tf_op jit(solution)/shard_map/ppermute | solution.py:628
  53.3 3.5 %collective-permute-start.15 = (f32[4,6,4,8,128]{4,3,2,1,0:T(8,128)S(1)}, f32[4,6,4,8,128]{4,3,2,1,0:T(8,128)S(1)}, u32[]{:S(2)}, u32[]{:S(2)}) collective-permute-start(f32[4,6,4,8,128]{4,3,2,1,0:T(8,128)S(1)} %pad_maximum_fusion.3), channel_id=1, source_target_pairs={{0,4},{4,0},{8,12},{12,8},{16,20},{20,16},{24,28},{28,24},{1,5},{5... | collective-permute-start | bytes 1179656 | tf_op jit(solution)/shard_map/ppermute | solution.py:645

commit v5 on v3

--- a/solution.py
+++ b/solution.py
@@ -189,37 +189,65 @@
     return [(TILE * tile, TILE * place, TILE * count) for tile, place, count in runs]
 
 
-def pack_kernel(tiles, field_ref, *pair_refs):
+def store(refs, mate, u, plane, values):
+    if len(refs) == 8:
+        refs[mate][u, plane] = values
+    elif len(refs) == 4:
+        refs[mate >> 1][mate & 1, u, plane] = values
+    else:
+        refs[mate & 1][mate >> 1, u, plane] = values
+
+
+def arrived(refs, u, plane):
+    if len(refs) == 8:
+        return [ref[u, plane] for ref in refs]
+    swapped = refs[-1]
+    if len(swapped.shape) == 6:
+        swapped = swapped.at[1 - lax.axis_index(MESH_LON) % 2]
+    if refs[0].shape[0] == 4:
+        return [refs[0][0, u, plane], swapped[0, u, plane]] + [
+            ref[core, u, plane] for ref in refs[1:4] for core in range(2)
+        ]
+    return [
+        swapped[mate >> 1, u, plane] if mate & 1 else refs[mate >> 1][0, u, plane]
+        for mate in range(8)
+    ]
+
+
+def pack_kernel(tiles, field_ref, *refs):
     levels = field_ref.shape[0]
+    pair_refs, kept = (refs, None) if len(refs) == 2 else (refs[:4], refs[4])
     me = lax.axis_index(MESH_LON)
     lane = lane_index()
     cell_masks = lane_masks(lane, 2, 2)
     device_masks = lane_masks(lane, 4, 3)
-    base = ((lane & 3) << 5) | (((lane >> 2) & 3) << 3) | ((lane >> 4) ^ me)
+    block = (lane >> 2) & 3
+    base = ((lane & 3) << 5) | (block << 3) | ((lane >> 4) ^ me ^ block)
 
     def unit(u, carry):
-        by_group = []
-        for group in range(8):
-            k = 2 * u + group // 4
-            parts = [
-                pick(
-                    field_ref[k, at(tiles[group % 4]), LANES * q : LANES * q + LANES],
-                    base ^ ((q << 3) | group),
-                )
-                for q in range(PLANES)
-            ]
-            by_group.append(swap_blocks(parts, cell_masks))
-        for plane in range(PLANES):
-            sent = swap_blocks([parts[plane] for parts in by_group], device_masks)
-            for mate in range(8):
-                pair_refs[mate >> 1][mate & 1, u, plane] = sent[mate]
-        return carry
-
-    lax.fori_loop(0, levels // 2, unit, 0)
-
-
-def unpack_kernel(tiles, *refs):
-    message_refs, (field_ref, held, sems) = refs[:5], refs[-3:]
+        for place, tile in enumerate(tiles):
+            by_group = []
+            for half in range(2):
+                parts = [
+                    pick(
+                        field_ref[2 * u + half, at(tile), LANES * q : LANES * q + LANES],
+                        base ^ ((q << 3) | (half << 2) | q),
+                    )
+                    for q in range(PLANES)
+                ]
+                by_group.extend(swap_blocks(parts, cell_masks))
+            for mate, values in enumerate(swap_blocks(by_group, device_masks)):
+                store(pair_refs, mate, u, place, values)
+        if kept is not None:
+            for k in [2 * u, 2 * u + 1]:
+                kept[k] = field_ref[k, TILE * INNER[0] : TILE * INNER[-1] + TILE, :]
+        return carry
+
+    lax.fori_loop(0, levels // 2, unit, 0, unroll=2)
+
+
+def unpack_kernel(tiles, count, *refs):
+    message_refs, (field_ref, held, sems) = refs[:count], refs[-3:]
     levels = held.shape[0]
     runs = row_runs(tiles)
 
@@ -256,7 +284,7 @@
                     copy.start()
         return carry
 
-    lax.fori_loop(0, levels // 2, unit, 0)
+    lax.fori_loop(0, levels // 2, unit, 0, unroll=2)
 
     def end(k, carry):
         for copy in copies(k):
@@ -266,32 +294,17 @@
     lax.fori_loop(0, levels, end, 0)
 
 
-def arrived(refs, u, plane):
-    return [
-        refs[4][mate >> 1, u, plane] if mate & 1 else refs[mate >> 1][0, u, plane]
-        for mate in range(8)
-    ]
-
-
 def take_messages(message_refs, put):
-    me = lax.axis_index(MESH_LON)
-    lane = lane_index()
-    device_masks = lane_masks(lane, 4, 3)
-    base = lane ^ (me << 4)
+    device_masks = lane_masks(lane_index(), 4, 3)
 
     def unit(u, carry):
-        for plane in range(PLANES):
-            groups = swap_blocks(arrived(message_refs, u, plane), device_masks)
+        for place in range(message_refs[0].shape[-3]):
+            groups = swap_blocks(arrived(message_refs, u, place), device_masks)
             for group, values in enumerate(groups):
-                put(
-                    2 * u + group // 4,
-                    plane,
-                    group % 4,
-                    pick(values, base ^ ((group << 4) | (plane << 2))),
-                )
-        return carry
-
-    lax.fori_loop(0, message_refs[0].shape[1], unit, 0)
+                put(2 * u + group // 4, group % 4, place, values)
+        return carry
+
+    lax.fori_loop(0, message_refs[0].shape[-4], unit, 0, unroll=3)
 
 
 def give_messages(message_refs, take):
@@ -310,10 +323,10 @@
                 for group in range(8)
             ]
             for mate, values in enumerate(swap_blocks(groups, device_masks)):
-                message_refs[mate >> 1][mate & 1, u, plane] = values
-        return carry
-
-    lax.fori_loop(0, message_refs[0].shape[1], unit, 0)
+                store(message_refs, mate, u, plane, values)
+        return carry
+
+    lax.fori_loop(0, message_refs[0].shape[-4], unit, 0, unroll=3)
 
 
 def copy_tiles(source, target, pairs):
@@ -328,9 +341,10 @@
     lax.fori_loop(0, source.shape[0], level, 0)
 
 
-def advance(tile, padded, coeff_ref, coeff_row, moved, put):
+def advance(tile, padded, coeff_ref, coeff_row, moved, raw, put):
     levels = moved.shape[0]
     lane = lane_index()
+    me = lax.axis_index(MESH_LON)
     first_row = pl.multiple_of(TILE * tile + PAD, TILE)
     rows_of = pl.ds(pl.multiple_of(coeff_row, TILE), TILE)
 
@@ -349,14 +363,16 @@
         shift = coeff(k, COEFFS - 1).astype(jnp.int32)
         low_bit = shift & 1 == 1
         high_bit = shift & 2 == 2
+        first = lane - (shift >> 2)
+        least = shift & 3
+        for v in range(PLANES):
+            where = (first if v == 0 else jnp.where(least >= PLANES - v, first - 1, first)) & (
+                LANES - 1
+            )
+            turn = ((me ^ ((k & 1) * PLANES + v)) << 4 | (v << 2)) * raw
+            planes[v] = pick(planes[v], where ^ turn)
         planes = [jnp.where(low_bit, planes[v - 1], planes[v]) for v in range(PLANES)]
         planes = [jnp.where(high_bit, planes[v - 2], planes[v]) for v in range(PLANES)]
-        first = lane - (shift >> 2)
-        least = shift & 3
-        planes = [
-            pick(values, jnp.where(least > v, first - 1, first) & (LANES - 1))
-            for v, values in enumerate(planes)
-        ]
         wide = (
             [pltpu.roll(planes[3], 1, 1)]
             + planes
@@ -430,7 +446,7 @@
         def put(k, plane, row, values):
             padded[step + 1, k, plane, pl.ds(row, TILE), :] = values
 
-        advance(tile, padded.at[step], coeff_ref.at[step], TILE * tile, moved, put)
+        advance(tile, padded.at[step], coeff_ref.at[step], TILE * tile, moved, 1 - step, put)
         return carry
 
     lax.fori_loop(0, 10, one, 0)
@@ -441,7 +457,7 @@
 
 
 def last_kernel(near_ref, field_ref, even_ref, odd_ref, coeff_ref, spread_ref, *refs):
-    outgoing, (padded, moved, nearby) = refs[:4], refs[4:]
+    outgoing, (padded, moved, nearby) = refs[:-3], refs[-3:]
     levels = near_ref.shape[0]
     is_even = lax.axis_index("lat") % 2 == 0
 
@@ -487,7 +503,7 @@
         def put(k, plane, row, values):
             padded[1, k, plane, pl.ds(row, TILE), :] = values
 
-        advance(tile, padded.at[0], nearby, TILE * place, moved, put)
+        advance(tile, padded.at[0], nearby, TILE * place, moved, 1, put)
         return carry
 
     lax.fori_loop(0, 4, first, 0)
@@ -498,7 +514,7 @@
         def put(k, plane, row, values):
             padded[0, k, plane, pl.ds(row, TILE), :] = values
 
-        advance(tile, padded.at[1], coeff_ref.at[1], TILE * tile, moved, put)
+        advance(tile, padded.at[1], coeff_ref.at[1], TILE * tile, moved, 0, put)
         return carry
 
     lax.fori_loop(0, 4, second, 0)
@@ -514,11 +530,9 @@
     lat_frac_ref,
     remap_ref,
     diffusivity_ref,
-    coeff_ref,
+    turned_ref,
     edge_ref,
-    spread_ref,
     held,
-    turned_ref,
 ):
     held[...] = jnp.zeros_like(held)
     kappa = diffusivity_ref[...]
@@ -560,6 +574,25 @@
                 for k in range(levels):
                     place = 64 * (k & 1) + 16 * part + which
                     held[(step * levels + k) // 2, place : place + 1, :rows] = piece[k : k + 1]
+    pairs = steps * levels // 2
+
+    def turn(place, carry):
+        turned = held[place].T[:rows]
+        turned_ref[pl.ds(pl.multiple_of(place * rows, rows), rows), :] = turned.astype(jnp.bfloat16)
+
+        @pl.when(place < levels // 2)
+        def _():
+            edge_ref[0, place] = turned[:TILE]
+            edge_ref[1, place] = turned[rows - TILE :]
+
+        return carry
+
+    lax.fori_loop(0, pairs, turn, 0)
+
+
+def spread_kernel(turned_ref, coeff_ref, spread_ref):
+    steps, levels, _, rows, _ = coeff_ref.shape
+    pairs = steps * levels // 2
     row = lax.broadcasted_iota(jnp.int32, (LANES, LANES), 0)
 
     def choose(which, carry):
@@ -570,21 +603,6 @@
         return carry
 
     lax.fori_loop(0, COEFFS, choose, 0)
-    pairs = steps * levels // 2
-
-    def turn(place, carry):
-        turned = held[place].T[:rows]
-        turned_ref[pl.ds(pl.multiple_of(place * rows, rows), rows), :] = turned.astype(jnp.bfloat16)
-
-        @pl.when(place < levels // 2)
-        def _():
-            edge_ref[0, place] = turned[:TILE]
-            edge_ref[1, place] = turned[rows - TILE :]
-
-        return carry
-
-    lax.fori_loop(0, pairs, turn, 0)
-
     def spread(group, carry):
         for which in [group * 3 + i for i in range(3)]:
             for parity in range(2):
@@ -615,7 +633,7 @@
             pltpu.VMEM(shape, jnp.float32) if isinstance(shape, tuple) else shape
             for shape in scratch
         ],
-        compiler_params=pltpu.CompilerParams(vmem_limit_bytes=20 * 2**20),
+        compiler_params=pltpu.CompilerParams(vmem_limit_bytes=13 * 2**20),
         **options,
     )
 
@@ -625,14 +643,39 @@
     return lax.ppermute(pairs[chip], MESH_LON, [(i, i ^ (2 * chip)) for i in range(peers)])
 
 
-def arrive(pairs):
-    return pairs[:1] + [between_chips(pairs, chip) for chip in range(1, len(pairs))]
-
-
-def between_cores(pairs):
+def arrive(pairs, order=(1, 2, 3)):
+    received = list(pairs)
+    for chip in order:
+        received[chip] = between_chips(pairs, chip)
+    return received
+
+
+def core_blocks(away):
     peers = lax.axis_size(MESH_LON)
-    away = jnp.concatenate([pair[1:] for pair in pairs], axis=0)
-    return pairs + [lax.ppermute(away, MESH_LON, [(i, i ^ 1) for i in range(peers)])]
+    groups = [[i, i + 1] for i in range(0, peers, 2)]
+    return lax.all_gather(away, MESH_LON, axis_index_groups=groups)
+
+
+def cores_last(pairs):
+    return pairs + [core_blocks(jnp.concatenate([pair[1:] for pair in pairs], axis=0))]
+
+
+def cores_first(own, away):
+    both = core_blocks(away)
+    other = both[1 - lax.axis_index(MESH_LON) % 2]
+    pairs = [own] + [
+        jnp.concatenate([own[chip : chip + 1], other[chip : chip + 1]], axis=0)
+        for chip in range(1, own.shape[0])
+    ]
+    return pairs, both
+
+
+def direct(messages):
+    peers = lax.axis_size(MESH_LON)
+    return messages[:1] + [
+        lax.ppermute(messages[mate], MESH_LON, [(i, i ^ mate) for i in range(peers)])
+        for mate in range(1, peers)
+    ]
 
 
 def exchange_edges(even, odd):
@@ -646,7 +689,8 @@
     levels, rows, columns = tracers.shape
     steps = lon_shift.shape[0]
     pairs = levels // 2
-    messages = [(2, pairs, PLANES, TILE, LANES)] * 4
+    message = (pairs, PLANES, TILE, LANES)
+    in_pairs, in_cores, alone = [(2,) + message] * 4, [(4,) + message] * 2, [message] * 8
     half = (levels, PLANES, rows // 2, LANES)
     edges = (levels * PLANES + pairs, TILE, LANES)
     work = (levels, PLANES, rows + 4 * TILE, LANES)
@@ -655,31 +699,36 @@
     anywhere = pl.BlockSpec(memory_space=pl.ANY)
     vmem = pl.BlockSpec(memory_space=pltpu.VMEM)
 
-    def pack(tiles):
-        kernel = functools.partial(pack_kernel, tiles)
-        return list(call(kernel, 2, messages)(tracers))
-
-    outer, inner = pack(OUTER), pack(INNER)
-    coeff, edge, spread = call(
+    *outer, kept = call(
+        functools.partial(pack_kernel, OUTER), 2, in_pairs + [(levels, rows // 2, columns)]
+    )(tracers)
+    inner = call(functools.partial(pack_kernel, range(len(INNER))), 2, in_cores)(kept)
+    turned, edge = call(
         coeff_kernel,
-        6,
+        2,
+        [
+            jax.ShapeDtypeStruct((steps * pairs * rows, LANES), jnp.bfloat16),
+            (2, pairs, TILE, LANES),
+        ],
+        [(steps * pairs, LANES, LANES)],
+    )(lon_shift, lon_frac, lat_shift, lat_frac, remap_frac, diffusivity)
+    outer = arrive(outer)
+    inner, both = cores_first(*inner)
+    inner = arrive(inner) + [both]
+    *outer, _ = lax.optimization_barrier((*outer, edge))
+    outer = cores_last(outer)
+    field, even, odd = call(outer_kernel, 1, [half, edges, edges])(*outer, edge)
+    turned, _ = lax.optimization_barrier((turned, field))
+    coeff, spread = call(
+        spread_kernel,
+        3,
         [
             (steps, levels, COEFFS, rows, LANES),
-            (2, pairs, TILE, LANES),
             jax.ShapeDtypeStruct((COEFFS, 2, LANES, LANES), jnp.bfloat16),
         ],
-        [
-            (steps * pairs, LANES, LANES),
-            pltpu.VMEM((steps * pairs * rows, LANES), jnp.bfloat16),
-        ],
-    )(lon_shift, lon_frac, lat_shift, lat_frac, remap_frac, diffusivity)
-    outer = between_cores(arrive(outer))
-    *inner, coeff = lax.optimization_barrier((*inner, coeff))
-    inner = arrive(inner)
-    field, even, odd = call(outer_kernel, 1, [half, edges, edges])(*outer, edge)
-    inner = between_cores(inner)
+    )(turned)
     even, odd = exchange_edges(even, odd)
-    *inner, near = call(inner_kernel, 6, messages + [half], [(3,) + work, moved])(
+    *inner, near = call(inner_kernel, 6, in_pairs + [half], [(3,) + work, moved])(
         *inner, field, coeff
     )
     *inner, even, odd = lax.optimization_barrier((*inner, even, odd))
@@ -687,25 +736,30 @@
     outer = call(
         last_kernel,
         6,
-        messages,
+        in_pairs,
         [(2,) + work, moved, (levels, COEFFS, rows // 2, LANES)],
     )(near, field, even, odd, coeff, spread)
-    *inner, outer = lax.optimization_barrier((*inner, list(outer)))
-    inner = between_cores(inner)
+    *inner, _ = lax.optimization_barrier((*inner, list(outer)))
+    inner = cores_last(inner)
     done = call(
-        functools.partial(unpack_kernel, INNER), 2, [tracers.shape], held, out_specs=[anywhere]
+        functools.partial(unpack_kernel, INNER, 5),
+        2,
+        [tracers.shape],
+        held,
+        out_specs=[anywhere],
     )(*inner)[0]
-    outer[3], done = lax.optimization_barrier((outer[3], done))
-    outer = between_cores(arrive(outer))
+    *outer, done = lax.optimization_barrier((*arrive(list(outer)), done))
+    away = jnp.concatenate([pair[1:] for pair in outer], axis=0)
+    swapped = lax.ppermute(away, MESH_LON, [(i, i ^ 1) for i in range(lax.axis_size(MESH_LON))])
     return call(
-        functools.partial(unpack_kernel, OUTER),
+        functools.partial(unpack_kernel, OUTER, 5),
         2,
         [tracers.shape],
         held,
         in_specs=[vmem] * 5 + [anywhere],
         out_specs=[anywhere],
         input_output_aliases={5: 0},
-    )(*outer, done)[0]
+    )(*outer, swapped, done)[0]
 
 
 def solution(mesh):

time: 64 us -> 54.5 us (0.85)
  blocking collectives: 0 us -> 12.4 us
  waiting for transfers between devices: 15.9 us -> 3.59 us
  starting transfers between devices: 23.1 us -> 17.9 us
  Pallas kernels: 22.8 us -> 18.3 us
    all_gather x0 -> x3, blocking collectives: none -> 12.4 us  [core_blocks(): return lax.all_gather(away, MESH_LON, axis_index_groups=groups)]
    ppermute x12, waiting for transfers between devices: 14.6 us -> 2.23 us  [between_chips(): lax.ppermute(pairs[chip], MESH_LON, [(i, i ^ 2 * chip) for i in range(pee...]
    ppermute x4 -> x1, starting transfers between devices: 7.57 us -> 2.35 us  [by_tracer(): lax.ppermute(away, MESH_LON, [(i, i ^ 1) for i in range(lax.axis_size(MES...]
    pallas_call x7 -> x8, Pallas kernels: 21.7 us -> 18.1 us  [the longest x1 4.8 us: by_tracer(): call(last_kernel, 6, in_pairs, [(2,) + work, moved, (levels, COEFFS, rows...]
    pallas_call x1, Pallas kernels: 1.05 us -> 0.2 us  [by_tracer(): field, even, odd = call(outer_kernel, 1, [half, edges, edges])(*outer, edge)]
    unnamed x21 -> x19, local copies, waits for them, and re-layouts: 1.45 us -> 1.46 us
    ppermute x4 -> x1, waiting for transfers between devices: 1.36 us -> 1.35 us  [by_tracer(): lax.ppermute(away, MESH_LON, [(i, i ^ 1) for i in range(lax.axis_size(MES...]
  transfers between devices with their start and end apart: 18 -> 15, of which waited for: 9 -> 3; matrix products, arithmetic and copies ran while one was open for 0% -> 0% of each run, Pallas kernels for 31% -> 29%
where the time goes in v5:
time: 54.5 us; the launch traced here: 54.3 us
  Pallas kernels  18.3 us (34%)
  starting transfers between devices  17.9 us (33%)
  blocking collectives  12.4 us (23%)
  waiting for transfers between devices  3.59 us (7%)
  local copies, waits for them, and re-layouts  1.61 us (3%)
    all_gather x3, blocking collectives, core_blocks(): return lax.all_gather(away, MESH_LON, axis_index_groups=groups)  12.4 us
    ppermute x12, starting transfers between devices, between_chips(): lax.ppermute(pairs[chip], MESH_LON, [(i, i ^ 2 * chip) for i in range(pee...  11 us
    pallas_call x1, Pallas kernels, by_tracer(): call(last_kernel, 6, in_pairs, [(2,) + work, moved, (levels, COEFFS, rows...  4.8 us
    ppermute x2, starting transfers between devices, exchange_edges(): return (lax.ppermute(even, 'lat', near), lax.ppermute(odd, 'lat', far))  4.55 us
    pallas_call x1, Pallas kernels, by_tracer(): call(inner_kernel, 6, in_pairs + [half], [(3,) + work, moved])  4.41 us
    pallas_call x1, Pallas kernels, by_tracer(): call(spread_kernel, 3, [(steps, levels, COEFFS, rows, LANES), jax.ShapeDt...  2.66 us
    ppermute x1, starting transfers between devices, by_tracer(): lax.ppermute(away, MESH_LON, [(i, i ^ 1) for i in range(lax.axis_size(MES...  2.35 us
    ppermute x12, waiting for transfers between devices, between_chips(): lax.ppermute(pairs[chip], MESH_LON, [(i, i ^ 2 * chip) for i in range(pee...  2.23 us
  transfers between devices with their start and end apart: 15, of which 3 were waited for; matrix products, arithmetic and copies ran while one was open for 0% of the time, Pallas kernels for 29%

profile of v5, /device:TPU:9, one launch (start us, length us, event | category | flops | bytes accessed | tf_op | source)
XLA Modules:
  0.0 54.3 jit_solution(2848099272589053326)
XLA Ops:
  0.0 1.4 %copy-done = f32[12,64,512]{2,1,0:T(8,128)S(1)} copy-done((f32[12,64,512]{2,1,0:T(8,128)S(1)}, f32[12,64,512]{2,1,0:T(8,128)}, u32[]{:S(2)}) %copy-start) | copy-done | bytes 1572888
  1.4 0.8 %shard_map.73 = (f32[2,6,4,8,128]{4,3,2,1,0:T(8,128)S(1)}, f32[2,6,4,8,128]{4,3,2,1,0:T(8,128)S(1)}, f32[2,6,4,8,128]{4,3,2,1,0:T(8,128)S(1)}, f32[2,6,4,8,128]{4,3,2,1,0:T(8,128)S(1)}, f32[12,32,512]{2,1,0:T(8,128)S(1)}) custom-call(f32[12,64,512]{2,1,0:T(8,128)S(1)} %copy-done), custom_call_target="tpu_custom_call" | custom-call | flops 2000000000 | bytes 6000000 | tf_op jit(solution)/shard_map/pallas_call | solution.py:702
  2.2 1.3 %collective-permute-start.3 = (f32[2,6,4,8,128]{4,3,2,1,0:T(8,128)S(1)}, f32[2,6,4,8,128]{4,3,2,1,0:T(8,128)S(1)}, u32[]{:S(2)}, u32[]{:S(2)}) collective-permute-start(f32[2,6,4,8,128]{4,3,2,1,0:T(8,128)S(1)} %get-tuple-element.52), channel_id=1, source_target_pairs={{0,8},{4,12},{8,0},{12,4},{16,24},{20,28},{24,16},{28,20},{1,9},{5... | collective-permute-start | bytes 589832 | tf_op jit(solution)/shard_map/ppermute | solution.py:643
  3.5 1.2 %collective-permute-start.4 = (f32[2,6,4,8,128]{4,3,2,1,0:T(8,128)S(1)}, f32[2,6,4,8,128]{4,3,2,1,0:T(8,128)S(1)}, u32[]{:S(2)}, u32[]{:S(2)}) collective-permute-start(f32[2,6,4,8,128]{4,3,2,1,0:T(8,128)S(1)} %get-tuple-element.53), channel_id=1, source_target_pairs={{0,16},{4,20},{8,24},{12,28},{16,0},{20,4},{24,8},{28,12},{1,17},{... | collective-permute-start | bytes 589832 | tf_op jit(solution)/shard_map/ppermute | solution.py:643
  4.7 0.2 collective-permute-start.5
  4.9 0.8 %shard_map.74 = (f32[4,6,4,8,128]{4,3,2,1,0:T(8,128)S(1)}, f32[4,6,4,8,128]{4,3,2,1,0:T(8,128)S(1)}) custom-call(f32[12,32,512]{2,1,0:T(8,128)S(1)} %get-tuple-element.48.field_ref), custom_call_target="tpu_custom_call" | custom-call | flops 2000000000 | bytes 6000000 | tf_op jit(solution)/shard_map/pallas_call | solution.py:705
  5.7 0.0 copy-start.2
  5.7 0.0 copy-start.3
  5.7 0.0 copy-start.4
  5.7 0.0 copy-start.5
  5.7 0.0 copy-start.6
  5.8 0.0 copy-start.1
  5.8 3.6 %all-gather = f32[8,6,4,8,128]{4,3,2,1,0:T(8,128)S(1)} all-gather(f32[4,6,4,8,128]{4,3,2,1,0:T(8,128)S(1)} %get-tuple-element.50), channel_id=2, replica_groups={{0,4},{8,12},{16,20},{24,28},{1,5},{9,13},{17,21},{25,29},{2,6},{10,14}..., dimensions={0}, use_global_device_ids=true | all-gather | bytes 1179648 | tf_op jit(solution)/shard_map/all_gather | solution.py:656
  9.5 1.3 %collective-permute-start = (f32[2,6,4,8,128]{4,3,2,1,0:T(8,128)S(1)}, f32[2,6,4,8,128]{4,3,2,1,0:T(8,128)S(1)}, u32[]{:S(2)}, u32[]{:S(2)}) collective-permute-start(f32[2,6,4,8,128]{4,3,2,1,0:T(8,128)S(1)} %pad_maximum_fusion.3), channel_id=1, source_target_pairs={{0,8},{4,12},{8,0},{12,4},{16,24},{20,28},{24,16},{28,20},{1,9},{5... | collective-permute-start | bytes 589832 | tf_op jit(solution)/shard_map/ppermute | solution.py:643
  10.8 1.3 %collective-permute-start.1 = (f32[2,6,4,8,128]{4,3,2,1,0:T(8,128)S(1)}, f32[2,6,4,8,128]{4,3,2,1,0:T(8,128)S(1)}, u32[]{:S(2)}, u32[]{:S(2)}) collective-permute-start(f32[2,6,4,8,128]{4,3,2,1,0:T(8,128)S(1)} %pad_maximum_fusion.4), channel_id=1, source_target_pairs={{0,16},{4,20},{8,24},{12,28},{16,0},{20,4},{24,8},{28,12},{1,17},{... | collective-permute-start | bytes 589832 | tf_op jit(solution)/shard_map/ppermute | solution.py:643
  12.2 1.5 %shard_map.75 = (bf16[768,128]{1,0:T(8,128)(2,1)S(1)}, f32[2,6,8,128]{3,2,1,0:T(8,128)S(1)}) custom-call(s32[2,12,64]{2,1,0:T(8,128)S(1)} %copy.14.lon_shift_ref, f32[2,12,64]{2,1,0:T(8,128)S(1)} %copy.15.lon_frac_ref, s32[2,12,64]{2,1,0:T(8,128)S(1)} %copy.16.lat_shift_ref, f32[2,12,64]{2,1,0:T(8,128)S(1)} %copy.17.lat_frac_ref, ...), custom_call_target="tpu_custom_call" | custom-call | flops 2000000000 | bytes 6000000 | tf_op jit(solution)/shard_map/pallas_call | solution.py:706
  13.7 0.0 collective-permute-done.3.refs_1_
  13.7 0.3 collective-permute-start.2
  13.9 0.0 collective-permute-done.4.refs_2_
  14.0 0.0 collective-permute-done.5.refs_3_
  14.1 4.0 %all-gather.1 = f32[8,6,4,8,128]{4,3,2,1,0:T(8,128)S(1)} all-gather(f32[4,6,4,8,128]{4,3,2,1,0:T(8,128)S(1)} %pad_maximum_fusion), channel_id=3, replica_groups={{0,4},{8,12},{16,20},{24,28},{1,5},{9,13},{17,21},{25,29},{2,6},{10,14}..., dimensions={0}, use_global_device_ids=true | all-gather | bytes 1179648 | tf_op jit(solution)/shard_map/all_gather | solution.py:656
  18.0 0.2 shard_map.76
  18.2 0.2 collective-permute-start.6
  18.5 4.3 %collective-permute-start.7 = (f32[54,8,128]{2,1,0:T(8,128)S(1)}, f32[54,8,128]{2,1,0:T(8,128)S(1)}, u32[]{:S(2)}, u32[]{:S(2)}) collective-permute-start(f32[54,8,128]{2,1,0:T(8,128)S(1)} %get-tuple-element.70), channel_id=1, source_target_pairs={{1,2},{2,1},{5,6},{6,5},{9,10},{10,9},{13,14},{14,13},{17,18},{18,... | collective-permute-start | bytes 663560 | tf_op jit(solution)/shard_map/ppermute | solution.py:685
  22.8 2.7 %shard_map.77 = (f32[2,12,15,64,128]{4,3,2,1,0:T(8,128)S(1)}, bf16[15,2,128,128]{3,2,1,0:T(8,128)(2,1)S(1)}) custom-call(bf16[768,128]{1,0:T(8,128)(2,1)S(1)} %get-tuple-element.62.turned_ref), custom_call_target="tpu_custom_call" | custom-call | flops 3000000000 | bytes 9000000 | tf_op jit(solution)/shard_map/pallas_call | solution.py:722
  25.5 0.0 collective-permute-done.refs_1_
  25.5 0.0 collective-permute-done.1.refs_2_
  25.5 0.0 collective-permute-done.2.refs_3_
  25.5 4.4 %shard_map.78 = (f32[2,6,4,8,128]{4,3,2,1,0:T(8,128)S(1)}, f32[2,6,4,8,128]{4,3,2,1,0:T(8,128)S(1)}, f32[2,6,4,8,128]{4,3,2,1,0:T(8,128)S(1)}, f32[2,6,4,8,128]{4,3,2,1,0:T(8,128)S(1)}, f32[12,4,32,128]{3,2,1,0:T(8,128)S(1)}) custom-call(f32[4,6,4,8,128]{4,3,2,1,0:T(8,128)S(1)} %get-tuple-element.49.refs_0_, ...), custom_call_target="tpu_custom_call" | custom-call | flops 6000000000 | bytes 18000000 | tf_op jit(solution)/shard_map/pallas_call | solution.py:731
  29.9 0.0 collective-permute-done.6.even_ref
  29.9 0.0 collective-permute-done.7.odd_ref
  29.9 1.2 %collective-permute-start.11 = (f32[2,6,4,8,128]{4,3,2,1,0:T(8,128)S(1)}, f32[2,6,4,8,128]{4,3,2,1,0:T(8,128)S(1)}, u32[]{:S(2)}, u32[]{:S(2)}) collective-permute-start(f32[2,6,4,8,128]{4,3,2,1,0:T(8,128)S(1)} %get-tuple-element.79), channel_id=1, source_target_pairs={{0,8},{4,12},{8,0},{12,4},{16,24},{20,28},{24,16},{28,20},{1,9},{5... | collective-permute-start | bytes 589832 | tf_op jit(solution)/shard_map/ppermute | solution.py:643
  31.2 0.5 collective-permute-start.12
  31.7 1.0 %collective-permute-start.13 = (f32[2,6,4,8,128]{4,3,2,1,0:T(8,128)S(1)}, f32[2,6,4,8,128]{4,3,2,1,0:T(8,128)S(1)}, u32[]{:S(2)}, u32[]{:S(2)}) collective-permute-start(f32[2,6,4,8,128]{4,3,2,1,0:T(8,128)S(1)} %get-tuple-element.81), channel_id=1, source_target_pairs={{0,24},{4,28},{8,16},{12,20},{16,8},{20,12},{24,0},{28,4},{1,25},{... | collective-permute-start | bytes 589832 | tf_op jit(solution)/shard_map/ppermute | solution.py:643
  32.7 4.8 %shard_map.79 = (f32[2,6,4,8,128]{4,3,2,1,0:T(8,128)S(1)}, f32[2,6,4,8,128]{4,3,2,1,0:T(8,128)S(1)}, f32[2,6,4,8,128]{4,3,2,1,0:T(8,128)S(1)}, f32[2,6,4,8,128]{4,3,2,1,0:T(8,128)S(1)}) custom-call(f32[12,4,32,128]{3,2,1,0:T(8,128)S(1)} %get-tuple-element.64.near_ref, f32[12,4,32,128]{3,2,1,0:T(8,128)S(1)} %get-tuple-element.60.refs_5_.field_ref, ...), custom_call_target="tpu_custom_call" | custom-call | flops 6000000000 | bytes 18000000 | tf_op jit(solution)/shard_map/pallas_call | solution.py:736
  37.5 1.2 %collective-permute-start.8 = (f32[2,6,4,8,128]{4,3,2,1,0:T(8,128)S(1)}, f32[2,6,4,8,128]{4,3,2,1,0:T(8,128)S(1)}, u32[]{:S(2)}, u32[]{:S(2)}) collective-permute-start(f32[2,6,4,8,128]{4,3,2,1,0:T(8,128)S(1)} %get-tuple-element.75), channel_id=1, source_target_pairs={{0,8},{4,12},{8,0},{12,4},{16,24},{20,28},{24,16},{28,20},{1,9},{5... | collective-permute-start | bytes 589832 | tf_op jit(solution)/shard_map/ppermute | solution.py:643
  38.7 0.5 collective-permute-start.9
  39.2 0.0 collective-permute-done.11.refs_1_
  39.2 1.0 %collective-permute-start.10 = (f32[2,6,4,8,128]{4,3,2,1,0:T(8,128)S(1)}, f32[2,6,4,8,128]{4,3,2,1,0:T(8,128)S(1)}, u32[]{:S(2)}, u32[]{:S(2)}) collective-permute-start(f32[2,6,4,8,128]{4,3,2,1,0:T(8,128)S(1)} %get-tuple-element.77), channel_id=1, source_target_pairs={{0,24},{4,28},{8,16},{12,20},{16,8},{20,12},{24,0},{28,4},{1,25},{... | collective-permute-start | bytes 589832 | tf_op jit(solution)/shard_map/ppermute | solution.py:643
  40.2 0.0 collective-permute-done.12.refs_2_
  40.2 0.1 collective-permute-done.13.refs_3_
  40.4 4.7 %all-gather.2 = f32[8,6,4,8,128]{4,3,2,1,0:T(8,128)S(1)} all-gather(f32[4,6,4,8,128]{4,3,2,1,0:T(8,128)S(1)} %pad_maximum_fusion.1), channel_id=4, replica_groups={{0,4},{8,12},{16,20},{24,28},{1,5},{9,13},{17,21},{25,29},{2,6},{10,14}..., dimensions={0}, use_global_device_ids=true | all-gather | bytes 1179648 | tf_op jit(solution)/shard_map/all_gather | solution.py:656
  45.1 1.6 %shard_map.80.refs_5_ = f32[12,64,512]{2,1,0:T(8,128)} custom-call(f32[2,6,4,8,128]{4,3,2,1,0:T(8,128)S(1)} %get-tuple-element.82.refs_0_, f32[2,6,4,8,128]{4,3,2,1,0:T(8,128)S(1)} %collective-permute-done.11.refs_1_, f32[2,6,4,8,128]{4,3,2,1,0:T(8,128)S(1)} %collective-permute-done.12.refs_2_, f32[2,6,4,8,128]{4,3,2,1,0:T(8,128)S(1)} %collective-permute-done.13.refs_3_, ...), custom_call_target="tpu_custom_call" | custom-call | flops 2000000000 | bytes 6000000 | tf_op jit(solution)/shard_map/pallas_call | solution.py:744
  46.7 0.0 collective-permute-done.8.refs_1_
  46.7 2.1 %collective-permute-done.10.refs_3_ = f32[2,6,4,8,128]{4,3,2,1,0:T(8,128)S(1)} collective-permute-done((f32[2,6,4,8,128]{4,3,2,1,0:T(8,128)S(1)}, f32[2,6,4,8,128]{4,3,2,1,0:T(8,128)S(1)}, u32[]{:S(2)}, u32[]{:S(2)}) %collective-permute-start.10) | collective-permute-done | bytes 196640 | tf_op jit(solution)/shard_map/ppermute | solution.py:643
  48.9 2.4 %collective-permute-start.14 = (f32[4,6,4,8,128]{4,3,2,1,0:T(8,128)S(1)}, f32[4,6,4,8,128]{4,3,2,1,0:T(8,128)S(1)}, u32[]{:S(2)}, u32[]{:S(2)}) collective-permute-start(f32[4,6,4,8,128]{4,3,2,1,0:T(8,128)S(1)} %pad_maximum_fusion.2), channel_id=1, source_target_pairs={{0,4},{4,0},{8,12},{12,8},{16,20},{20,16},{24,28},{28,24},{1,5},{5... | collective-permute-start | bytes 1179656 | tf_op jit(solution)/shard_map/ppermute | solution.py:753
  51.3 1.3 %collective-permute-done.14.refs_4_ = f32[4,6,4,8,128]{4,3,2,1,0:T(8,128)S(1)} collective-permute-done((f32[4,6,4,8,128]{4,3,2,1,0:T(8,128)S(1)}, f32[4,6,4,8,128]{4,3,2,1,0:T(8,128)S(1)}, u32[]{:S(2)}, u32[]{:S(2)}) %collective-permute-start.14) | collective-permute-done | bytes 393248 | tf_op jit(solution)/shard_map/ppermute | solution.py:753
  52.6 1.6 %shard_map.81 = f32[12,64,512]{2,1,0:T(8,128)} custom-call(f32[2,6,4,8,128]{4,3,2,1,0:T(8,128)S(1)} %get-tuple-element.86.refs_0_, f32[2,6,4,8,128]{4,3,2,1,0:T(8,128)S(1)} %collective-permute-done.8.refs_1_, f32[2,6,4,8,128]{4,3,2,1,0:T(8,128)S(1)} %collective-permute-done.9.refs_2_, ...), custom_call_target="tpu_custom_call", output_to_operand_aliasing={{}: (5, {})} | custom-call | flops 2000000000 | bytes 6000000 | tf_op jit(solution)/shard_map/pallas_call | solution.py:754
  (33 shorter events, 0.3 us)
Async XLA Ops:
  0.0 1.4 %copy-start = (f32[12,64,512]{2,1,0:T(8,128)S(1)}, f32[12,64,512]{2,1,0:T(8,128)}, u32[]{:S(2)}) copy-start(f32[12,64,512]{2,1,0:T(8,128)} %field_ref.1) | copy-start | bytes 4718596
  2.2 11.5 %collective-permute-start.3 = (f32[2,6,4,8,128]{4,3,2,1,0:T(8,128)S(1)}, f32[2,6,4,8,128]{4,3,2,1,0:T(8,128)S(1)}, u32[]{:S(2)}, u32[]{:S(2)}) collective-permute-start(f32[2,6,4,8,128]{4,3,2,1,0:T(8,128)S(1)} %get-tuple-element.52), channel_id=1, source_target_pairs={{0,8},{4,12},{8,0},{12,4},{16,24},{20,28},{24,16},{28,20},{1,9},{5... | collective-permute-start | bytes 589832 | tf_op jit(solution)/shard_map/ppermute | solution.py:643
  3.5 10.5 %collective-permute-start.4 = (f32[2,6,4,8,128]{4,3,2,1,0:T(8,128)S(1)}, f32[2,6,4,8,128]{4,3,2,1,0:T(8,128)S(1)}, u32[]{:S(2)}, u32[]{:S(2)}) collective-permute-start(f32[2,6,4,8,128]{4,3,2,1,0:T(8,128)S(1)} %get-tuple-element.53), channel_id=1, source_target_pairs={{0,16},{4,20},{8,24},{12,28},{16,0},{20,4},{24,8},{28,12},{1,17},{... | collective-permute-start | bytes 589832 | tf_op jit(solution)/shard_map/ppermute | solution.py:643
  4.7 9.2 %collective-permute-start.5 = (f32[2,6,4,8,128]{4,3,2,1,0:T(8,128)S(1)}, f32[2,6,4,8,128]{4,3,2,1,0:T(8,128)S(1)}, u32[]{:S(2)}, u32[]{:S(2)}) collective-permute-start(f32[2,6,4,8,128]{4,3,2,1,0:T(8,128)S(1)} %get-tuple-element.54), channel_id=1, source_target_pairs={{0,24},{4,28},{8,16},{12,20},{16,8},{20,12},{24,0},{28,4},{1,25},{... | collective-permute-start | bytes 589832 | tf_op jit(solution)/shard_map/ppermute | solution.py:643
  5.7 6.4 %copy-start.2 = (s32[2,12,64]{2,0,1:T(2,128)S(1)}, s32[2,12,64]{2,0,1:T(2,128)}, u32[]{:S(2)}) copy-start(s32[2,12,64]{2,0,1:T(2,128)} %param.8) | copy-start | bytes 18436
  5.7 6.4 %copy-start.3 = (f32[2,12,64]{2,0,1:T(2,128)S(1)}, f32[2,12,64]{2,0,1:T(2,128)}, u32[]{:S(2)}) copy-start(f32[2,12,64]{2,0,1:T(2,128)} %param.9) | copy-start | bytes 18436
  5.7 6.4 %copy-start.4 = (s32[2,12,64]{2,0,1:T(2,128)S(1)}, s32[2,12,64]{2,0,1:T(2,128)}, u32[]{:S(2)}) copy-start(s32[2,12,64]{2,0,1:T(2,128)} %param.10) | copy-start | bytes 18436
  5.7 6.4 %copy-start.5 = (f32[2,12,64]{2,0,1:T(2,128)S(1)}, f32[2,12,64]{2,0,1:T(2,128)}, u32[]{:S(2)}) copy-start(f32[2,12,64]{2,0,1:T(2,128)} %param.11) | copy-start | bytes 18436
  5.7 6.4 %copy-start.6 = (f32[2,12,64]{2,0,1:T(2,128)S(1)}, f32[2,12,64]{2,0,1:T(2,128)}, u32[]{:S(2)}) copy-start(f32[2,12,64]{2,0,1:T(2,128)} %param.12) | copy-start | bytes 18436
  5.8 6.4 %copy-start.1 = (f32[12,64]{1,0:T(8,128)S(1)}, f32[12,64]{1,0:T(8,128)}, u32[]{:S(2)}) copy-start(f32[12,64]{1,0:T(8,128)} %diffusivity_ref.1) | copy-start | bytes 9220
  9.5 16.0 %collective-permute-start = (f32[2,6,4,8,128]{4,3,2,1,0:T(8,128)S(1)}, f32[2,6,4,8,128]{4,3,2,1,0:T(8,128)S(1)}, u32[]{:S(2)}, u32[]{:S(2)}) collective-permute-start(f32[2,6,4,8,128]{4,3,2,1,0:T(8,128)S(1)} %pad_maximum_fusion.3), channel_id=1, source_target_pairs={{0,8},{4,12},{8,0},{12,4},{16,24},{20,28},{24,16},{28,20},{1,9},{5... | collective-permute-start | bytes 589832 | tf_op jit(solution)/shard_map/ppermute | solution.py:643
  10.8 14.7 %collective-permute-start.1 = (f32[2,6,4,8,128]{4,3,2,1,0:T(8,128)S(1)}, f32[2,6,4,8,128]{4,3,2,1,0:T(8,128)S(1)}, u32[]{:S(2)}, u32[]{:S(2)}) collective-permute-start(f32[2,6,4,8,128]{4,3,2,1,0:T(8,128)S(1)} %pad_maximum_fusion.4), channel_id=1, source_target_pairs={{0,16},{4,20},{8,24},{12,28},{16,0},{20,4},{24,8},{28,12},{1,17},{... | collective-permute-start | bytes 589832 | tf_op jit(solution)/shard_map/ppermute | solution.py:643
  13.7 11.8 %collective-permute-start.2 = (f32[2,6,4,8,128]{4,3,2,1,0:T(8,128)S(1)}, f32[2,6,4,8,128]{4,3,2,1,0:T(8,128)S(1)}, u32[]{:S(2)}, u32[]{:S(2)}) collective-permute-start(f32[2,6,4,8,128]{4,3,2,1,0:T(8,128)S(1)} %pad_maximum_fusion.5), channel_id=1, source_target_pairs={{0,24},{4,28},{8,16},{12,20},{16,8},{20,12},{24,0},{28,4},{1,25},{... | collective-permute-start | bytes 589832 | tf_op jit(solution)/shard_map/ppermute | solution.py:643
  18.2 11.7 %collective-permute-start.6 = (f32[54,8,128]{2,1,0:T(8,128)S(1)}, f32[54,8,128]{2,1,0:T(8,128)S(1)}, u32[]{:S(2)}, u32[]{:S(2)}) collective-permute-start(f32[54,8,128]{2,1,0:T(8,128)S(1)} %get-tuple-element.69), channel_id=1, source_target_pairs={{0,1},{1,0},{2,3},{3,2},{4,5},{5,4},{6,7},{7,6},{8,9},{9,8},{10,11... | collective-permute-start | bytes 663560 | tf_op jit(solution)/shard_map/ppermute | solution.py:685
  18.5 11.5 %collective-permute-start.7 = (f32[54,8,128]{2,1,0:T(8,128)S(1)}, f32[54,8,128]{2,1,0:T(8,128)S(1)}, u32[]{:S(2)}, u32[]{:S(2)}) collective-permute-start(f32[54,8,128]{2,1,0:T(8,128)S(1)} %get-tuple-element.70), channel_id=1, source_target_pairs={{1,2},{2,1},{5,6},{6,5},{9,10},{10,9},{13,14},{14,13},{17,18},{18,... | collective-permute-start | bytes 663560 | tf_op jit(solution)/shard_map/ppermute | solution.py:685
  29.9 9.3 %collective-permute-start.11 = (f32[2,6,4,8,128]{4,3,2,1,0:T(8,128)S(1)}, f32[2,6,4,8,128]{4,3,2,1,0:T(8,128)S(1)}, u32[]{:S(2)}, u32[]{:S(2)}) collective-permute-start(f32[2,6,4,8,128]{4,3,2,1,0:T(8,128)S(1)} %get-tuple-element.79), channel_id=1, source_target_pairs={{0,8},{4,12},{8,0},{12,4},{16,24},{20,28},{24,16},{28,20},{1,9},{5... | collective-permute-start | bytes 589832 | tf_op jit(solution)/shard_map/ppermute | solution.py:643
  31.2 9.0 %collective-permute-start.12 = (f32[2,6,4,8,128]{4,3,2,1,0:T(8,128)S(1)}, f32[2,6,4,8,128]{4,3,2,1,0:T(8,128)S(1)}, u32[]{:S(2)}, u32[]{:S(2)}) collective-permute-start(f32[2,6,4,8,128]{4,3,2,1,0:T(8,128)S(1)} %get-tuple-element.80), channel_id=1, source_target_pairs={{0,16},{4,20},{8,24},{12,28},{16,0},{20,4},{24,8},{28,12},{1,17},{... | collective-permute-start | bytes 589832 | tf_op jit(solution)/shard_map/ppermute | solution.py:643
  31.7 8.6 %collective-permute-start.13 = (f32[2,6,4,8,128]{4,3,2,1,0:T(8,128)S(1)}, f32[2,6,4,8,128]{4,3,2,1,0:T(8,128)S(1)}, u32[]{:S(2)}, u32[]{:S(2)}) collective-permute-start(f32[2,6,4,8,128]{4,3,2,1,0:T(8,128)S(1)} %get-tuple-element.81), channel_id=1, source_target_pairs={{0,24},{4,28},{8,16},{12,20},{16,8},{20,12},{24,0},{28,4},{1,25},{... | collective-permute-start | bytes 589832 | tf_op jit(solution)/shard_map/ppermute | solution.py:643
  37.5 9.3 %collective-permute-start.8 = (f32[2,6,4,8,128]{4,3,2,1,0:T(8,128)S(1)}, f32[2,6,4,8,128]{4,3,2,1,0:T(8,128)S(1)}, u32[]{:S(2)}, u32[]{:S(2)}) collective-permute-start(f32[2,6,4,8,128]{4,3,2,1,0:T(8,128)S(1)} %get-tuple-element.75), channel_id=1, source_target_pairs={{0,8},{4,12},{8,0},{12,4},{16,24},{20,28},{24,16},{28,20},{1,9},{5... | collective-permute-start | bytes 589832 | tf_op jit(solution)/shard_map/ppermute | solution.py:643
  38.7 8.1 %collective-permute-start.9 = (f32[2,6,4,8,128]{4,3,2,1,0:T(8,128)S(1)}, f32[2,6,4,8,128]{4,3,2,1,0:T(8,128)S(1)}, u32[]{:S(2)}, u32[]{:S(2)}) collective-permute-start(f32[2,6,4,8,128]{4,3,2,1,0:T(8,128)S(1)} %get-tuple-element.76), channel_id=1, source_target_pairs={{0,16},{4,20},{8,24},{12,28},{16,0},{20,4},{24,8},{28,12},{1,17},{... | collective-permute-start | bytes 589832 | tf_op jit(solution)/shard_map/ppermute | solution.py:643
  39.2 9.6 %collective-permute-start.10 = (f32[2,6,4,8,128]{4,3,2,1,0:T(8,128)S(1)}, f32[2,6,4,8,128]{4,3,2,1,0:T(8,128)S(1)}, u32[]{:S(2)}, u32[]{:S(2)}) collective-permute-start(f32[2,6,4,8,128]{4,3,2,1,0:T(8,128)S(1)} %get-tuple-element.77), channel_id=1, source_target_pairs={{0,24},{4,28},{8,16},{12,20},{16,8},{20,12},{24,0},{28,4},{1,25},{... | collective-permute-start | bytes 589832 | tf_op jit(solution)/shard_map/ppermute | solution.py:643
  48.9 3.7 %collective-permute-start.14 = (f32[4,6,4,8,128]{4,3,2,1,0:T(8,128)S(1)}, f32[4,6,4,8,128]{4,3,2,1,0:T(8,128)S(1)}, u32[]{:S(2)}, u32[]{:S(2)}) collective-permute-start(f32[4,6,4,8,128]{4,3,2,1,0:T(8,128)S(1)} %pad_maximum_fusion.2), channel_id=1, source_target_pairs={{0,4},{4,0},{8,12},{12,8},{16,20},{20,16},{24,28},{28,24},{1,5},{5... | collective-permute-start | bytes 1179656 | tf_op jit(solution)/shard_map/ppermute | solution.py:753

commit v6 on v5

--- a/solution.py
+++ b/solution.py
@@ -2,6 +2,8 @@
 
 import jax
 import jax.numpy as jnp
+import ml_dtypes
+import numpy as np
 from jax import lax
 from jax.experimental import pallas as pl
 from jax.experimental.pallas import tpu as pltpu
@@ -284,14 +286,14 @@
                     copy.start()
         return carry
 
-    lax.fori_loop(0, levels // 2, unit, 0, unroll=2)
+    lax.fori_loop(0, levels // 2, unit, 0, unroll=3)
 
     def end(k, carry):
         for copy in copies(k):
             copy.wait()
         return carry
 
-    lax.fori_loop(0, levels, end, 0)
+    lax.fori_loop(0, levels, end, 0, unroll=True)
 
 
 def take_messages(message_refs, put):
@@ -304,7 +306,7 @@
                 put(2 * u + group // 4, group % 4, place, values)
         return carry
 
-    lax.fori_loop(0, message_refs[0].shape[-4], unit, 0, unroll=3)
+    lax.fori_loop(0, message_refs[0].shape[-4], unit, 0, unroll=True)
 
 
 def give_messages(message_refs, take):
@@ -326,7 +328,7 @@
                 store(message_refs, mate, u, plane, values)
         return carry
 
-    lax.fori_loop(0, message_refs[0].shape[-4], unit, 0, unroll=3)
+    lax.fori_loop(0, message_refs[0].shape[-4], unit, 0, unroll=True)
 
 
 def copy_tiles(source, target, pairs):
@@ -480,22 +482,19 @@
     turned = turned.astype(jnp.bfloat16)
 
     def widen(group, carry):
-        for which in [group * 3 + i for i in range(3)]:
-            for parity in range(2):
-                wide = jnp.dot(
-                    turned, spread_ref[which, parity], preferred_element_type=jnp.float32
-                )
-                for side in range(2):
-                    for pair in range(levels // 2):
-                        nearby[2 * pair + parity, which, at(3 * side), :] = wide[
-                            at(side * levels // 2 + pair)
-                        ]
+        for which in [group * 5 + i for i in range(5)]:
+            wide = jnp.dot(turned, spread_ref[which], preferred_element_type=jnp.float32)
+            for side in range(2):
+                for k in range(levels):
+                    nearby[k, which, at(3 * side), :] = wide[
+                        at((side * levels + k) // 2), k % 2 * LANES : k % 2 * LANES + LANES
+                    ]
             for k in range(levels):
                 nearby[k, which, at(1), :] = coeff_ref[0, k, which, at(0), :]
                 nearby[k, which, at(2), :] = coeff_ref[0, k, which, at(7), :]
         return carry
 
-    lax.fori_loop(0, COEFFS // 3, widen, 0)
+    lax.fori_loop(0, COEFFS // 5, widen, 0)
 
     def first(place, carry):
         tile = jnp.where(place < 2, place - 1, place + 5)
@@ -590,33 +589,31 @@
     lax.fori_loop(0, pairs, turn, 0)
 
 
-def spread_kernel(turned_ref, coeff_ref, spread_ref):
+def spread_matrices():
+    row = np.arange(LANES)[None, :, None]
+    column = np.arange(2 * LANES)[None, None, :]
+    which = np.arange(COEFFS)[:, None, None]
+    chosen = ((row & 15) == which) & ((row & 63) < 48) & (row // 64 == column // LANES)
+    return jnp.asarray(chosen.astype(ml_dtypes.bfloat16))
+
+
+def spread_kernel(turned_ref, spread_ref, coeff_ref):
     steps, levels, _, rows, _ = coeff_ref.shape
     pairs = steps * levels // 2
-    row = lax.broadcasted_iota(jnp.int32, (LANES, LANES), 0)
-
-    def choose(which, carry):
-        wanted = jnp.logical_and(row & 15 == which, row & 63 < 48)
-        for parity in range(2):
-            chosen = jnp.logical_and(wanted, row >> 6 == parity)
-            spread_ref[which, parity] = chosen.astype(jnp.float32).astype(jnp.bfloat16)
-        return carry
-
-    lax.fori_loop(0, COEFFS, choose, 0)
+
     def spread(group, carry):
-        for which in [group * 3 + i for i in range(3)]:
-            for parity in range(2):
-                wide = jnp.dot(
-                    turned_ref[...], spread_ref[which, parity], preferred_element_type=jnp.float32
-                )
-                for pair in range(pairs):
-                    both = 2 * pair + parity
-                    coeff_ref[both // levels, both % levels, which] = wide[
-                        pair * rows : pair * rows + rows
-                    ]
-        return carry
-
-    lax.fori_loop(0, COEFFS // 3, spread, 0)
+        for which in [group * 5 + i for i in range(5)]:
+            wide = jnp.dot(
+                turned_ref[...], spread_ref[which], preferred_element_type=jnp.float32
+            )
+            for both in range(2 * pairs):
+                start, lane = both // 2 * rows, both % 2 * LANES
+                coeff_ref[both // levels, both % levels, which] = wide[
+                    start : start + rows, lane : lane + LANES
+                ]
+        return carry
+
+    lax.fori_loop(0, COEFFS // 5, spread, 0)
 
 
 def call(kernel, micros, out_shapes, scratch=(), **options):
@@ -719,14 +716,8 @@
     outer = cores_last(outer)
     field, even, odd = call(outer_kernel, 1, [half, edges, edges])(*outer, edge)
     turned, _ = lax.optimization_barrier((turned, field))
-    coeff, spread = call(
-        spread_kernel,
-        3,
-        [
-            (steps, levels, COEFFS, rows, LANES),
-            jax.ShapeDtypeStruct((COEFFS, 2, LANES, LANES), jnp.bfloat16),
-        ],
-    )(turned)
+    spread = spread_matrices()
+    coeff = call(spread_kernel, 3, [(steps, levels, COEFFS, rows, LANES)])(turned, spread)[0]
     even, odd = exchange_edges(even, odd)
     *inner, near = call(inner_kernel, 6, in_pairs + [half], [(3,) + work, moved])(
         *inner, field, coeff

time: 54.5 us -> 53.6 us (0.983)
  Pallas kernels: 18.3 us -> 16.9 us
    pallas_call x1, Pallas kernels: 2.66 us -> 1.97 us  [by_tracer(): call(spread_kernel, 3, [(steps, levels, COEFFS, rows, LANES)])]
    unnamed x19 -> x21, local copies, waits for them, and re-layouts: 1.46 us -> 1.47 us
  transfers between devices with their start and end apart: 15 -> 15, of which waited for: 3 -> 3; matrix products, arithmetic and copies ran while one was open for 0% -> 0% of each run, Pallas kernels for 29% -> 27%
where the time goes in v6:
time: 53.6 us; the launch traced here: 53.4 us
  starting transfers between devices  17.8 us (33%)
  Pallas kernels  16.9 us (32%)
  blocking collectives  12.7 us (24%)
  waiting for transfers between devices  3.73 us (7%)
  local copies, waits for them, and re-layouts  1.61 us (3%)
    all_gather x3, blocking collectives, core_blocks(): return lax.all_gather(away, MESH_LON, axis_index_groups=groups)  12.7 us
    ppermute x12, starting transfers between devices, between_chips(): lax.ppermute(pairs[chip], MESH_LON, [(i, i ^ 2 * chip) for i in range(pee...  11 us
    ppermute x2, starting transfers between devices, exchange_edges(): return (lax.ppermute(even, 'lat', near), lax.ppermute(odd, 'lat', far))  4.55 us
    pallas_call x1, Pallas kernels, by_tracer(): call(last_kernel, 6, in_pairs, [(2,) + work, moved, (levels, COEFFS, rows...  4.41 us
    pallas_call x1, Pallas kernels, by_tracer(): call(inner_kernel, 6, in_pairs + [half], [(3,) + work, moved])  4.3 us
    ppermute x12, waiting for transfers between devices, between_chips(): lax.ppermute(pairs[chip], MESH_LON, [(i, i ^ 2 * chip) for i in range(pee...  2.38 us
    ppermute x1, starting transfers between devices, by_tracer(): lax.ppermute(away, MESH_LON, [(i, i ^ 1) for i in range(lax.axis_size(MES...  2.28 us
    pallas_call x1, Pallas kernels, by_tracer(): call(spread_kernel, 3, [(steps, levels, COEFFS, rows, LANES)])  1.97 us
  transfers between devices with their start and end apart: 15, of which 3 were waited for; matrix products, arithmetic and copies ran while one was open for 0% of the time, Pallas kernels for 27%

profile of v6, /device:TPU:9, one launch (start us, length us, event | category | flops | bytes accessed | tf_op | source)
XLA Modules:
  0.0 53.4 jit_solution(9026966051687729645)
XLA Ops:
  0.0 1.4 %copy-done.1 = f32[12,64,512]{2,1,0:T(8,128)S(1)} copy-done((f32[12,64,512]{2,1,0:T(8,128)S(1)}, f32[12,64,512]{2,1,0:T(8,128)}, u32[]{:S(2)}) %copy-start.1) | copy-done | bytes 1572888
  1.4 0.8 %shard_map.82 = (f32[2,6,4,8,128]{4,3,2,1,0:T(8,128)S(1)}, f32[2,6,4,8,128]{4,3,2,1,0:T(8,128)S(1)}, f32[2,6,4,8,128]{4,3,2,1,0:T(8,128)S(1)}, f32[2,6,4,8,128]{4,3,2,1,0:T(8,128)S(1)}, f32[12,32,512]{2,1,0:T(8,128)S(1)}) custom-call(f32[12,64,512]{2,1,0:T(8,128)S(1)} %copy-done.1), custom_call_target="tpu_custom_call" | custom-call | flops 2000000000 | bytes 6000000 | tf_op jit(solution)/shard_map/pallas_call | solution.py:699
  2.2 1.3 %collective-permute-start.3 = (f32[2,6,4,8,128]{4,3,2,1,0:T(8,128)S(1)}, f32[2,6,4,8,128]{4,3,2,1,0:T(8,128)S(1)}, u32[]{:S(2)}, u32[]{:S(2)}) collective-permute-start(f32[2,6,4,8,128]{4,3,2,1,0:T(8,128)S(1)} %get-tuple-element.50), channel_id=1, source_target_pairs={{0,8},{4,12},{8,0},{12,4},{16,24},{20,28},{24,16},{28,20},{1,9},{5... | collective-permute-start | bytes 589832 | tf_op jit(solution)/shard_map/ppermute | solution.py:640
  3.5 1.2 %collective-permute-start.4 = (f32[2,6,4,8,128]{4,3,2,1,0:T(8,128)S(1)}, f32[2,6,4,8,128]{4,3,2,1,0:T(8,128)S(1)}, u32[]{:S(2)}, u32[]{:S(2)}) collective-permute-start(f32[2,6,4,8,128]{4,3,2,1,0:T(8,128)S(1)} %get-tuple-element.51), channel_id=1, source_target_pairs={{0,16},{4,20},{8,24},{12,28},{16,0},{20,4},{24,8},{28,12},{1,17},{... | collective-permute-start | bytes 589832 | tf_op jit(solution)/shard_map/ppermute | solution.py:640
  4.7 0.2 collective-permute-start.5
  4.9 0.8 %shard_map.83 = (f32[4,6,4,8,128]{4,3,2,1,0:T(8,128)S(1)}, f32[4,6,4,8,128]{4,3,2,1,0:T(8,128)S(1)}) custom-call(f32[12,32,512]{2,1,0:T(8,128)S(1)} %get-tuple-element.46.field_ref), custom_call_target="tpu_custom_call" | custom-call | flops 2000000000 | bytes 6000000 | tf_op jit(solution)/shard_map/pallas_call | solution.py:702
  5.7 0.0 copy-start.3
  5.7 0.0 copy-start.4
  5.7 0.0 copy-start.5
  5.7 0.0 copy-start.6
  5.7 0.0 copy-start.7
  5.8 0.0 copy-start.2
  5.8 3.6 %all-gather = f32[8,6,4,8,128]{4,3,2,1,0:T(8,128)S(1)} all-gather(f32[4,6,4,8,128]{4,3,2,1,0:T(8,128)S(1)} %get-tuple-element.48), channel_id=2, replica_groups={{0,4},{8,12},{16,20},{24,28},{1,5},{9,13},{17,21},{25,29},{2,6},{10,14}..., dimensions={0}, use_global_device_ids=true | all-gather | bytes 1179648 | tf_op jit(solution)/shard_map/all_gather | solution.py:653
  9.5 1.3 %collective-permute-start = (f32[2,6,4,8,128]{4,3,2,1,0:T(8,128)S(1)}, f32[2,6,4,8,128]{4,3,2,1,0:T(8,128)S(1)}, u32[]{:S(2)}, u32[]{:S(2)}) collective-permute-start(f32[2,6,4,8,128]{4,3,2,1,0:T(8,128)S(1)} %pad_maximum_fusion.3), channel_id=1, source_target_pairs={{0,8},{4,12},{8,0},{12,4},{16,24},{20,28},{24,16},{28,20},{1,9},{5... | collective-permute-start | bytes 589832 | tf_op jit(solution)/shard_map/ppermute | solution.py:640
  10.8 1.3 %collective-permute-start.1 = (f32[2,6,4,8,128]{4,3,2,1,0:T(8,128)S(1)}, f32[2,6,4,8,128]{4,3,2,1,0:T(8,128)S(1)}, u32[]{:S(2)}, u32[]{:S(2)}) collective-permute-start(f32[2,6,4,8,128]{4,3,2,1,0:T(8,128)S(1)} %pad_maximum_fusion.4), channel_id=1, source_target_pairs={{0,16},{4,20},{8,24},{12,28},{16,0},{20,4},{24,8},{28,12},{1,17},{... | collective-permute-start | bytes 589832 | tf_op jit(solution)/shard_map/ppermute | solution.py:640
  12.2 1.5 %shard_map.84 = (bf16[768,128]{1,0:T(8,128)(2,1)S(1)}, f32[2,6,8,128]{3,2,1,0:T(8,128)S(1)}) custom-call(s32[2,12,64]{2,1,0:T(8,128)S(1)} %copy.15.lon_shift_ref, f32[2,12,64]{2,1,0:T(8,128)S(1)} %copy.16.lon_frac_ref, s32[2,12,64]{2,1,0:T(8,128)S(1)} %copy.17.lat_shift_ref, f32[2,12,64]{2,1,0:T(8,128)S(1)} %copy.18.lat_frac_ref, ...), custom_call_target="tpu_custom_call" | custom-call | flops 2000000000 | bytes 6000000 | tf_op jit(solution)/shard_map/pallas_call | solution.py:703
  13.7 0.0 collective-permute-done.3.refs_1_
  13.7 0.3 collective-permute-start.2
  13.9 0.0 collective-permute-done.4.refs_2_
  14.0 0.0 collective-permute-done.5.refs_3_
  14.1 4.0 %all-gather.1 = f32[8,6,4,8,128]{4,3,2,1,0:T(8,128)S(1)} all-gather(f32[4,6,4,8,128]{4,3,2,1,0:T(8,128)S(1)} %pad_maximum_fusion), channel_id=3, replica_groups={{0,4},{8,12},{16,20},{24,28},{1,5},{9,13},{17,21},{25,29},{2,6},{10,14}..., dimensions={0}, use_global_device_ids=true | all-gather | bytes 1179648 | tf_op jit(solution)/shard_map/all_gather | solution.py:653
  18.0 0.2 shard_map.85
  18.2 0.2 collective-permute-start.6
  18.5 4.3 %collective-permute-start.7 = (f32[54,8,128]{2,1,0:T(8,128)S(1)}, f32[54,8,128]{2,1,0:T(8,128)S(1)}, u32[]{:S(2)}, u32[]{:S(2)}) collective-permute-start(f32[54,8,128]{2,1,0:T(8,128)S(1)} %get-tuple-element.67), channel_id=1, source_target_pairs={{1,2},{2,1},{5,6},{6,5},{9,10},{10,9},{13,14},{14,13},{17,18},{18,... | collective-permute-start | bytes 663560 | tf_op jit(solution)/shard_map/ppermute | solution.py:682
  22.8 2.0 %shard_map.86.refs_6_.coeff_ref = f32[2,12,15,64,128]{4,3,2,1,0:T(8,128)S(1)} custom-call(bf16[768,128]{1,0:T(8,128)(2,1)S(1)} %get-tuple-element.60.turned_ref, bf16[15,128,256]{2,1,0:T(8,128)(2,1)S(1)} %copy-done), custom_call_target="tpu_custom_call" | custom-call | flops 3000000000 | bytes 9000000 | tf_op jit(solution)/shard_map/pallas_call | solution.py:720
  24.8 0.0 collective-permute-done.refs_1_
  24.8 0.0 collective-permute-done.1.refs_2_
  24.8 0.0 collective-permute-done.2.refs_3_
  24.8 4.3 %shard_map.87 = (f32[2,6,4,8,128]{4,3,2,1,0:T(8,128)S(1)}, f32[2,6,4,8,128]{4,3,2,1,0:T(8,128)S(1)}, f32[2,6,4,8,128]{4,3,2,1,0:T(8,128)S(1)}, f32[2,6,4,8,128]{4,3,2,1,0:T(8,128)S(1)}, f32[12,4,32,128]{3,2,1,0:T(8,128)S(1)}) custom-call(f32[4,6,4,8,128]{4,3,2,1,0:T(8,128)S(1)} %get-tuple-element.47.refs_0_, ...), custom_call_target="tpu_custom_call" | custom-call | flops 6000000000 | bytes 18000000 | tf_op jit(solution)/shard_map/pallas_call | solution.py:722
  29.1 0.0 collective-permute-done.6.even_ref
  29.1 0.0 collective-permute-done.7.odd_ref
  29.1 1.2 %collective-permute-start.11 = (f32[2,6,4,8,128]{4,3,2,1,0:T(8,128)S(1)}, f32[2,6,4,8,128]{4,3,2,1,0:T(8,128)S(1)}, u32[]{:S(2)}, u32[]{:S(2)}) collective-permute-start(f32[2,6,4,8,128]{4,3,2,1,0:T(8,128)S(1)} %get-tuple-element.75), channel_id=1, source_target_pairs={{0,8},{4,12},{8,0},{12,4},{16,24},{20,28},{24,16},{28,20},{1,9},{5... | collective-permute-start | bytes 589832 | tf_op jit(solution)/shard_map/ppermute | solution.py:640
  30.4 0.5 collective-permute-start.12
  30.9 1.0 %collective-permute-start.13 = (f32[2,6,4,8,128]{4,3,2,1,0:T(8,128)S(1)}, f32[2,6,4,8,128]{4,3,2,1,0:T(8,128)S(1)}, u32[]{:S(2)}, u32[]{:S(2)}) collective-permute-start(f32[2,6,4,8,128]{4,3,2,1,0:T(8,128)S(1)} %get-tuple-element.77), channel_id=1, source_target_pairs={{0,24},{4,28},{8,16},{12,20},{16,8},{20,12},{24,0},{28,4},{1,25},{... | collective-permute-start | bytes 589832 | tf_op jit(solution)/shard_map/ppermute | solution.py:640
  31.8 4.4 %shard_map.88 = (f32[2,6,4,8,128]{4,3,2,1,0:T(8,128)S(1)}, f32[2,6,4,8,128]{4,3,2,1,0:T(8,128)S(1)}, f32[2,6,4,8,128]{4,3,2,1,0:T(8,128)S(1)}, f32[2,6,4,8,128]{4,3,2,1,0:T(8,128)S(1)}) custom-call(f32[12,4,32,128]{3,2,1,0:T(8,128)S(1)} %get-tuple-element.61.near_ref, f32[12,4,32,128]{3,2,1,0:T(8,128)S(1)} %get-tuple-element.58.refs_5_.field_ref, ...), custom_call_target="tpu_custom_call" | custom-call | flops 6000000000 | bytes 18000000 | tf_op jit(solution)/shard_map/pallas_call | solution.py:727
  36.3 1.2 %collective-permute-start.8 = (f32[2,6,4,8,128]{4,3,2,1,0:T(8,128)S(1)}, f32[2,6,4,8,128]{4,3,2,1,0:T(8,128)S(1)}, u32[]{:S(2)}, u32[]{:S(2)}) collective-permute-start(f32[2,6,4,8,128]{4,3,2,1,0:T(8,128)S(1)} %get-tuple-element.71), channel_id=1, source_target_pairs={{0,8},{4,12},{8,0},{12,4},{16,24},{20,28},{24,16},{28,20},{1,9},{5... | collective-permute-start | bytes 589832 | tf_op jit(solution)/shard_map/ppermute | solution.py:640
  37.5 0.5 collective-permute-start.9
  38.0 0.0 collective-permute-done.11.refs_1_
  38.0 1.0 %collective-permute-start.10 = (f32[2,6,4,8,128]{4,3,2,1,0:T(8,128)S(1)}, f32[2,6,4,8,128]{4,3,2,1,0:T(8,128)S(1)}, u32[]{:S(2)}, u32[]{:S(2)}) collective-permute-start(f32[2,6,4,8,128]{4,3,2,1,0:T(8,128)S(1)} %get-tuple-element.73), channel_id=1, source_target_pairs={{0,24},{4,28},{8,16},{12,20},{16,8},{20,12},{24,0},{28,4},{1,25},{... | collective-permute-start | bytes 589832 | tf_op jit(solution)/shard_map/ppermute | solution.py:640
  39.0 0.0 collective-permute-done.12.refs_2_
  39.0 0.5 collective-permute-done.13.refs_3_
  39.5 5.1 %all-gather.2 = f32[8,6,4,8,128]{4,3,2,1,0:T(8,128)S(1)} all-gather(f32[4,6,4,8,128]{4,3,2,1,0:T(8,128)S(1)} %pad_maximum_fusion.1), channel_id=4, replica_groups={{0,4},{8,12},{16,20},{24,28},{1,5},{9,13},{17,21},{25,29},{2,6},{10,14}..., dimensions={0}, use_global_device_ids=true | all-gather | bytes 1179648 | tf_op jit(solution)/shard_map/all_gather | solution.py:653
  44.7 1.5 %shard_map.89.refs_5_ = f32[12,64,512]{2,1,0:T(8,128)} custom-call(f32[2,6,4,8,128]{4,3,2,1,0:T(8,128)S(1)} %get-tuple-element.78.refs_0_, f32[2,6,4,8,128]{4,3,2,1,0:T(8,128)S(1)} %collective-permute-done.11.refs_1_, f32[2,6,4,8,128]{4,3,2,1,0:T(8,128)S(1)} %collective-permute-done.12.refs_2_, f32[2,6,4,8,128]{4,3,2,1,0:T(8,128)S(1)} %collective-permute-done.13.refs_3_, ...), custom_call_target="tpu_custom_call" | custom-call | flops 2000000000 | bytes 6000000 | tf_op jit(solution)/shard_map/pallas_call | solution.py:735
  46.2 0.0 collective-permute-done.9.refs_2_
  46.2 1.9 %collective-permute-done.10.refs_3_ = f32[2,6,4,8,128]{4,3,2,1,0:T(8,128)S(1)} collective-permute-done((f32[2,6,4,8,128]{4,3,2,1,0:T(8,128)S(1)}, f32[2,6,4,8,128]{4,3,2,1,0:T(8,128)S(1)}, u32[]{:S(2)}, u32[]{:S(2)}) %collective-permute-start.10) | collective-permute-done | bytes 196640 | tf_op jit(solution)/shard_map/ppermute | solution.py:640
  48.2 2.3 %collective-permute-start.14 = (f32[4,6,4,8,128]{4,3,2,1,0:T(8,128)S(1)}, f32[4,6,4,8,128]{4,3,2,1,0:T(8,128)S(1)}, u32[]{:S(2)}, u32[]{:S(2)}) collective-permute-start(f32[4,6,4,8,128]{4,3,2,1,0:T(8,128)S(1)} %pad_maximum_fusion.2), channel_id=1, source_target_pairs={{0,4},{4,0},{8,12},{12,8},{16,20},{20,16},{24,28},{28,24},{1,5},{5... | collective-permute-start | bytes 1179656 | tf_op jit(solution)/shard_map/ppermute | solution.py:744
  50.5 1.3 %collective-permute-done.14.refs_4_ = f32[4,6,4,8,128]{4,3,2,1,0:T(8,128)S(1)} collective-permute-done((f32[4,6,4,8,128]{4,3,2,1,0:T(8,128)S(1)}, f32[4,6,4,8,128]{4,3,2,1,0:T(8,128)S(1)}, u32[]{:S(2)}, u32[]{:S(2)}) %collective-permute-start.14) | collective-permute-done | bytes 393248 | tf_op jit(solution)/shard_map/ppermute | solution.py:744
  51.8 1.5 %shard_map.90 = f32[12,64,512]{2,1,0:T(8,128)} custom-call(f32[2,6,4,8,128]{4,3,2,1,0:T(8,128)S(1)} %get-tuple-element.82.refs_0_, f32[2,6,4,8,128]{4,3,2,1,0:T(8,128)S(1)} %collective-permute-done.8.refs_1_, f32[2,6,4,8,128]{4,3,2,1,0:T(8,128)S(1)} %collective-permute-done.9.refs_2_, ...), custom_call_target="tpu_custom_call", output_to_operand_aliasing={{}: (5, {})} | custom-call | flops 2000000000 | bytes 6000000 | tf_op jit(solution)/shard_map/pallas_call | solution.py:745
  (35 shorter events, 0.3 us)
Async XLA Ops:
  0.0 1.4 %copy-start.1 = (f32[12,64,512]{2,1,0:T(8,128)S(1)}, f32[12,64,512]{2,1,0:T(8,128)}, u32[]{:S(2)}) copy-start(f32[12,64,512]{2,1,0:T(8,128)} %field_ref.1) | copy-start | bytes 4718596
  2.2 11.5 %collective-permute-start.3 = (f32[2,6,4,8,128]{4,3,2,1,0:T(8,128)S(1)}, f32[2,6,4,8,128]{4,3,2,1,0:T(8,128)S(1)}, u32[]{:S(2)}, u32[]{:S(2)}) collective-permute-start(f32[2,6,4,8,128]{4,3,2,1,0:T(8,128)S(1)} %get-tuple-element.50), channel_id=1, source_target_pairs={{0,8},{4,12},{8,0},{12,4},{16,24},{20,28},{24,16},{28,20},{1,9},{5... | collective-permute-start | bytes 589832 | tf_op jit(solution)/shard_map/ppermute | solution.py:640
  3.5 10.5 %collective-permute-start.4 = (f32[2,6,4,8,128]{4,3,2,1,0:T(8,128)S(1)}, f32[2,6,4,8,128]{4,3,2,1,0:T(8,128)S(1)}, u32[]{:S(2)}, u32[]{:S(2)}) collective-permute-start(f32[2,6,4,8,128]{4,3,2,1,0:T(8,128)S(1)} %get-tuple-element.51), channel_id=1, source_target_pairs={{0,16},{4,20},{8,24},{12,28},{16,0},{20,4},{24,8},{28,12},{1,17},{... | collective-permute-start | bytes 589832 | tf_op jit(solution)/shard_map/ppermute | solution.py:640
  4.7 9.2 %collective-permute-start.5 = (f32[2,6,4,8,128]{4,3,2,1,0:T(8,128)S(1)}, f32[2,6,4,8,128]{4,3,2,1,0:T(8,128)S(1)}, u32[]{:S(2)}, u32[]{:S(2)}) collective-permute-start(f32[2,6,4,8,128]{4,3,2,1,0:T(8,128)S(1)} %get-tuple-element.52), channel_id=1, source_target_pairs={{0,24},{4,28},{8,16},{12,20},{16,8},{20,12},{24,0},{28,4},{1,25},{... | collective-permute-start | bytes 589832 | tf_op jit(solution)/shard_map/ppermute | solution.py:640
  5.7 6.4 %copy-start.3 = (s32[2,12,64]{2,0,1:T(2,128)S(1)}, s32[2,12,64]{2,0,1:T(2,128)}, u32[]{:S(2)}) copy-start(s32[2,12,64]{2,0,1:T(2,128)} %param.9) | copy-start | bytes 18436
  5.7 6.4 %copy-start.4 = (f32[2,12,64]{2,0,1:T(2,128)S(1)}, f32[2,12,64]{2,0,1:T(2,128)}, u32[]{:S(2)}) copy-start(f32[2,12,64]{2,0,1:T(2,128)} %param.10) | copy-start | bytes 18436
  5.7 6.4 %copy-start.5 = (s32[2,12,64]{2,0,1:T(2,128)S(1)}, s32[2,12,64]{2,0,1:T(2,128)}, u32[]{:S(2)}) copy-start(s32[2,12,64]{2,0,1:T(2,128)} %param.11) | copy-start | bytes 18436
  5.7 6.4 %copy-start.6 = (f32[2,12,64]{2,0,1:T(2,128)S(1)}, f32[2,12,64]{2,0,1:T(2,128)}, u32[]{:S(2)}) copy-start(f32[2,12,64]{2,0,1:T(2,128)} %param.12) | copy-start | bytes 18436
  5.7 6.4 %copy-start.7 = (f32[2,12,64]{2,0,1:T(2,128)S(1)}, f32[2,12,64]{2,0,1:T(2,128)}, u32[]{:S(2)}) copy-start(f32[2,12,64]{2,0,1:T(2,128)} %param.13) | copy-start | bytes 18436
  5.8 6.4 %copy-start.2 = (f32[12,64]{1,0:T(8,128)S(1)}, f32[12,64]{1,0:T(8,128)}, u32[]{:S(2)}) copy-start(f32[12,64]{1,0:T(8,128)} %diffusivity_ref.1) | copy-start | bytes 9220
  9.5 15.3 %collective-permute-start = (f32[2,6,4,8,128]{4,3,2,1,0:T(8,128)S(1)}, f32[2,6,4,8,128]{4,3,2,1,0:T(8,128)S(1)}, u32[]{:S(2)}, u32[]{:S(2)}) collective-permute-start(f32[2,6,4,8,128]{4,3,2,1,0:T(8,128)S(1)} %pad_maximum_fusion.3), channel_id=1, source_target_pairs={{0,8},{4,12},{8,0},{12,4},{16,24},{20,28},{24,16},{28,20},{1,9},{5... | collective-permute-start | bytes 589832 | tf_op jit(solution)/shard_map/ppermute | solution.py:640
  10.8 14.0 %collective-permute-start.1 = (f32[2,6,4,8,128]{4,3,2,1,0:T(8,128)S(1)}, f32[2,6,4,8,128]{4,3,2,1,0:T(8,128)S(1)}, u32[]{:S(2)}, u32[]{:S(2)}) collective-permute-start(f32[2,6,4,8,128]{4,3,2,1,0:T(8,128)S(1)} %pad_maximum_fusion.4), channel_id=1, source_target_pairs={{0,16},{4,20},{8,24},{12,28},{16,0},{20,4},{24,8},{28,12},{1,17},{... | collective-permute-start | bytes 589832 | tf_op jit(solution)/shard_map/ppermute | solution.py:640
  13.7 11.1 %collective-permute-start.2 = (f32[2,6,4,8,128]{4,3,2,1,0:T(8,128)S(1)}, f32[2,6,4,8,128]{4,3,2,1,0:T(8,128)S(1)}, u32[]{:S(2)}, u32[]{:S(2)}) collective-permute-start(f32[2,6,4,8,128]{4,3,2,1,0:T(8,128)S(1)} %pad_maximum_fusion.5), channel_id=1, source_target_pairs={{0,24},{4,28},{8,16},{12,20},{16,8},{20,12},{24,0},{28,4},{1,25},{... | collective-permute-start | bytes 589832 | tf_op jit(solution)/shard_map/ppermute | solution.py:640
  18.0 4.8 %copy-start = (bf16[15,128,256]{2,1,0:T(8,128)(2,1)S(1)}, bf16[15,128,256]{2,1,0:T(8,128)(2,1)}, u32[]{:S(2)}) copy-start(bf16[15,128,256]{2,1,0:T(8,128)(2,1)} %constant.25.clone.spread_ref) | copy-start | bytes 2949124
  18.2 10.9 %collective-permute-start.6 = (f32[54,8,128]{2,1,0:T(8,128)S(1)}, f32[54,8,128]{2,1,0:T(8,128)S(1)}, u32[]{:S(2)}, u32[]{:S(2)}) collective-permute-start(f32[54,8,128]{2,1,0:T(8,128)S(1)} %get-tuple-element.66), channel_id=1, source_target_pairs={{0,1},{1,0},{2,3},{3,2},{4,5},{5,4},{6,7},{7,6},{8,9},{9,8},{10,11... | collective-permute-start | bytes 663560 | tf_op jit(solution)/shard_map/ppermute | solution.py:682
  18.5 10.7 %collective-permute-start.7 = (f32[54,8,128]{2,1,0:T(8,128)S(1)}, f32[54,8,128]{2,1,0:T(8,128)S(1)}, u32[]{:S(2)}, u32[]{:S(2)}) collective-permute-start(f32[54,8,128]{2,1,0:T(8,128)S(1)} %get-tuple-element.67), channel_id=1, source_target_pairs={{1,2},{2,1},{5,6},{6,5},{9,10},{10,9},{13,14},{14,13},{17,18},{18,... | collective-permute-start | bytes 663560 | tf_op jit(solution)/shard_map/ppermute | solution.py:682
  29.1 8.9 %collective-permute-start.11 = (f32[2,6,4,8,128]{4,3,2,1,0:T(8,128)S(1)}, f32[2,6,4,8,128]{4,3,2,1,0:T(8,128)S(1)}, u32[]{:S(2)}, u32[]{:S(2)}) collective-permute-start(f32[2,6,4,8,128]{4,3,2,1,0:T(8,128)S(1)} %get-tuple-element.75), channel_id=1, source_target_pairs={{0,8},{4,12},{8,0},{12,4},{16,24},{20,28},{24,16},{28,20},{1,9},{5... | collective-permute-start | bytes 589832 | tf_op jit(solution)/shard_map/ppermute | solution.py:640
  30.4 8.6 %collective-permute-start.12 = (f32[2,6,4,8,128]{4,3,2,1,0:T(8,128)S(1)}, f32[2,6,4,8,128]{4,3,2,1,0:T(8,128)S(1)}, u32[]{:S(2)}, u32[]{:S(2)}) collective-permute-start(f32[2,6,4,8,128]{4,3,2,1,0:T(8,128)S(1)} %get-tuple-element.76), channel_id=1, source_target_pairs={{0,16},{4,20},{8,24},{12,28},{16,0},{20,4},{24,8},{28,12},{1,17},{... | collective-permute-start | bytes 589832 | tf_op jit(solution)/shard_map/ppermute | solution.py:640
  30.9 8.6 %collective-permute-start.13 = (f32[2,6,4,8,128]{4,3,2,1,0:T(8,128)S(1)}, f32[2,6,4,8,128]{4,3,2,1,0:T(8,128)S(1)}, u32[]{:S(2)}, u32[]{:S(2)}) collective-permute-start(f32[2,6,4,8,128]{4,3,2,1,0:T(8,128)S(1)} %get-tuple-element.77), channel_id=1, source_target_pairs={{0,24},{4,28},{8,16},{12,20},{16,8},{20,12},{24,0},{28,4},{1,25},{... | collective-permute-start | bytes 589832 | tf_op jit(solution)/shard_map/ppermute | solution.py:640
  36.3 10.0 %collective-permute-start.8 = (f32[2,6,4,8,128]{4,3,2,1,0:T(8,128)S(1)}, f32[2,6,4,8,128]{4,3,2,1,0:T(8,128)S(1)}, u32[]{:S(2)}, u32[]{:S(2)}) collective-permute-start(f32[2,6,4,8,128]{4,3,2,1,0:T(8,128)S(1)} %get-tuple-element.71), channel_id=1, source_target_pairs={{0,8},{4,12},{8,0},{12,4},{16,24},{20,28},{24,16},{28,20},{1,9},{5... | collective-permute-start | bytes 589832 | tf_op jit(solution)/shard_map/ppermute | solution.py:640
  37.5 8.7 %collective-permute-start.9 = (f32[2,6,4,8,128]{4,3,2,1,0:T(8,128)S(1)}, f32[2,6,4,8,128]{4,3,2,1,0:T(8,128)S(1)}, u32[]{:S(2)}, u32[]{:S(2)}) collective-permute-start(f32[2,6,4,8,128]{4,3,2,1,0:T(8,128)S(1)} %get-tuple-element.72), channel_id=1, source_target_pairs={{0,16},{4,20},{8,24},{12,28},{16,0},{20,4},{24,8},{28,12},{1,17},{... | collective-permute-start | bytes 589832 | tf_op jit(solution)/shard_map/ppermute | solution.py:640
  38.0 10.1 %collective-permute-start.10 = (f32[2,6,4,8,128]{4,3,2,1,0:T(8,128)S(1)}, f32[2,6,4,8,128]{4,3,2,1,0:T(8,128)S(1)}, u32[]{:S(2)}, u32[]{:S(2)}) collective-permute-start(f32[2,6,4,8,128]{4,3,2,1,0:T(8,128)S(1)} %get-tuple-element.73), channel_id=1, source_target_pairs={{0,24},{4,28},{8,16},{12,20},{16,8},{20,12},{24,0},{28,4},{1,25},{... | collective-permute-start | bytes 589832 | tf_op jit(solution)/shard_map/ppermute | solution.py:640
  48.2 3.6 %collective-permute-start.14 = (f32[4,6,4,8,128]{4,3,2,1,0:T(8,128)S(1)}, f32[4,6,4,8,128]{4,3,2,1,0:T(8,128)S(1)}, u32[]{:S(2)}, u32[]{:S(2)}) collective-permute-start(f32[4,6,4,8,128]{4,3,2,1,0:T(8,128)S(1)} %pad_maximum_fusion.2), channel_id=1, source_target_pairs={{0,4},{4,0},{8,12},{12,8},{16,20},{20,16},{24,28},{28,24},{1,5},{5... | collective-permute-start | bytes 1179656 | tf_op jit(solution)/shard_map/ppermute | solution.py:744

commit v7 on v6

--- a/solution.py
+++ b/solution.py
@@ -722,7 +722,7 @@
     *inner, near = call(inner_kernel, 6, in_pairs + [half], [(3,) + work, moved])(
         *inner, field, coeff
     )
-    *inner, even, odd = lax.optimization_barrier((*inner, even, odd))
+    *inner, even = lax.optimization_barrier((*inner, even))
     inner = arrive(inner)
     outer = call(
         last_kernel,

time: 53.6 us -> 53.6 us (level)
  no operation moved by 1% of the time
where the time goes in v7:
time: 53.6 us; the launch traced here: 53.4 us
  starting transfers between devices  17.8 us (33%)
  Pallas kernels  16.9 us (32%)
  blocking collectives  12.7 us (24%)
  waiting for transfers between devices  3.74 us (7%)
  local copies, waits for them, and re-layouts  1.61 us (3%)
    all_gather x3, blocking collectives, core_blocks(): return lax.all_gather(away, MESH_LON, axis_index_groups=groups)  12.7 us
    ppermute x12, starting transfers between devices, between_chips(): lax.ppermute(pairs[chip], MESH_LON, [(i, i ^ 2 * chip) for i in range(pee...  11 us
    ppermute x2, starting transfers between devices, exchange_edges(): return (lax.ppermute(even, 'lat', near), lax.ppermute(odd, 'lat', far))  4.55 us
    pallas_call x1, Pallas kernels, by_tracer(): call(last_kernel, 6, in_pairs, [(2,) + work, moved, (levels, COEFFS, rows...  4.41 us
    pallas_call x1, Pallas kernels, by_tracer(): call(inner_kernel, 6, in_pairs + [half], [(3,) + work, moved])  4.3 us
    ppermute x12, waiting for transfers between devices, between_chips(): lax.ppermute(pairs[chip], MESH_LON, [(i, i ^ 2 * chip) for i in range(pee...  2.39 us
    ppermute x1, starting transfers between devices, by_tracer(): lax.ppermute(away, MESH_LON, [(i, i ^ 1) for i in range(lax.axis_size(MES...  2.28 us
    pallas_call x1, Pallas kernels, by_tracer(): call(spread_kernel, 3, [(steps, levels, COEFFS, rows, LANES)])  1.97 us
  transfers between devices with their start and end apart: 15, of which 3 were waited for; matrix products, arithmetic and copies ran while one was open for 0% of the time, Pallas kernels for 27%

profile of v7, /device:TPU:9, one launch (start us, length us, event | category | flops | bytes accessed | tf_op | source)
XLA Modules:
  0.0 53.4 jit_solution(2511374839366383944)
XLA Ops:
  0.0 1.4 %copy-done.1 = f32[12,64,512]{2,1,0:T(8,128)S(1)} copy-done((f32[12,64,512]{2,1,0:T(8,128)S(1)}, f32[12,64,512]{2,1,0:T(8,128)}, u32[]{:S(2)}) %copy-start.1) | copy-done | bytes 1572888
  1.4 0.8 %shard_map.82 = (f32[2,6,4,8,128]{4,3,2,1,0:T(8,128)S(1)}, f32[2,6,4,8,128]{4,3,2,1,0:T(8,128)S(1)}, f32[2,6,4,8,128]{4,3,2,1,0:T(8,128)S(1)}, f32[2,6,4,8,128]{4,3,2,1,0:T(8,128)S(1)}, f32[12,32,512]{2,1,0:T(8,128)S(1)}) custom-call(f32[12,64,512]{2,1,0:T(8,128)S(1)} %copy-done.1), custom_call_target="tpu_custom_call" | custom-call | flops 2000000000 | bytes 6000000 | tf_op jit(solution)/shard_map/pallas_call | solution.py:699
  2.2 1.3 %collective-permute-start.3 = (f32[2,6,4,8,128]{4,3,2,1,0:T(8,128)S(1)}, f32[2,6,4,8,128]{4,3,2,1,0:T(8,128)S(1)}, u32[]{:S(2)}, u32[]{:S(2)}) collective-permute-start(f32[2,6,4,8,128]{4,3,2,1,0:T(8,128)S(1)} %get-tuple-element.49), channel_id=1, source_target_pairs={{0,8},{4,12},{8,0},{12,4},{16,24},{20,28},{24,16},{28,20},{1,9},{5... | collective-permute-start | bytes 589832 | tf_op jit(solution)/shard_map/ppermute | solution.py:640
  3.5 1.2 %collective-permute-start.4 = (f32[2,6,4,8,128]{4,3,2,1,0:T(8,128)S(1)}, f32[2,6,4,8,128]{4,3,2,1,0:T(8,128)S(1)}, u32[]{:S(2)}, u32[]{:S(2)}) collective-permute-start(f32[2,6,4,8,128]{4,3,2,1,0:T(8,128)S(1)} %get-tuple-element.50), channel_id=1, source_target_pairs={{0,16},{4,20},{8,24},{12,28},{16,0},{20,4},{24,8},{28,12},{1,17},{... | collective-permute-start | bytes 589832 | tf_op jit(solution)/shard_map/ppermute | solution.py:640
  4.7 0.2 collective-permute-start.5
  4.9 0.8 %shard_map.83 = (f32[4,6,4,8,128]{4,3,2,1,0:T(8,128)S(1)}, f32[4,6,4,8,128]{4,3,2,1,0:T(8,128)S(1)}) custom-call(f32[12,32,512]{2,1,0:T(8,128)S(1)} %get-tuple-element.45.field_ref), custom_call_target="tpu_custom_call" | custom-call | flops 2000000000 | bytes 6000000 | tf_op jit(solution)/shard_map/pallas_call | solution.py:702
  5.7 0.0 copy-start.3
  5.7 0.0 copy-start.4
  5.7 0.0 copy-start.5
  5.7 0.0 copy-start.6
  5.7 0.0 copy-start.7
  5.8 0.0 copy-start.2
  5.8 3.6 %all-gather = f32[8,6,4,8,128]{4,3,2,1,0:T(8,128)S(1)} all-gather(f32[4,6,4,8,128]{4,3,2,1,0:T(8,128)S(1)} %get-tuple-element.47), channel_id=2, replica_groups={{0,4},{8,12},{16,20},{24,28},{1,5},{9,13},{17,21},{25,29},{2,6},{10,14}..., dimensions={0}, use_global_device_ids=true | all-gather | bytes 1179648 | tf_op jit(solution)/shard_map/all_gather | solution.py:653
  9.5 1.3 %collective-permute-start = (f32[2,6,4,8,128]{4,3,2,1,0:T(8,128)S(1)}, f32[2,6,4,8,128]{4,3,2,1,0:T(8,128)S(1)}, u32[]{:S(2)}, u32[]{:S(2)}) collective-permute-start(f32[2,6,4,8,128]{4,3,2,1,0:T(8,128)S(1)} %pad_maximum_fusion.3), channel_id=1, source_target_pairs={{0,8},{4,12},{8,0},{12,4},{16,24},{20,28},{24,16},{28,20},{1,9},{5... | collective-permute-start | bytes 589832 | tf_op jit(solution)/shard_map/ppermute | solution.py:640
  10.8 1.3 %collective-permute-start.1 = (f32[2,6,4,8,128]{4,3,2,1,0:T(8,128)S(1)}, f32[2,6,4,8,128]{4,3,2,1,0:T(8,128)S(1)}, u32[]{:S(2)}, u32[]{:S(2)}) collective-permute-start(f32[2,6,4,8,128]{4,3,2,1,0:T(8,128)S(1)} %pad_maximum_fusion.4), channel_id=1, source_target_pairs={{0,16},{4,20},{8,24},{12,28},{16,0},{20,4},{24,8},{28,12},{1,17},{... | collective-permute-start | bytes 589832 | tf_op jit(solution)/shard_map/ppermute | solution.py:640
  12.2 1.5 %shard_map.84 = (bf16[768,128]{1,0:T(8,128)(2,1)S(1)}, f32[2,6,8,128]{3,2,1,0:T(8,128)S(1)}) custom-call(s32[2,12,64]{2,1,0:T(8,128)S(1)} %copy.15.lon_shift_ref, f32[2,12,64]{2,1,0:T(8,128)S(1)} %copy.16.lon_frac_ref, s32[2,12,64]{2,1,0:T(8,128)S(1)} %copy.17.lat_shift_ref, f32[2,12,64]{2,1,0:T(8,128)S(1)} %copy.18.lat_frac_ref, ...), custom_call_target="tpu_custom_call" | custom-call | flops 2000000000 | bytes 6000000 | tf_op jit(solution)/shard_map/pallas_call | solution.py:703
  13.7 0.0 collective-permute-done.3.refs_1_
  13.7 0.3 collective-permute-start.2
  13.9 0.0 collective-permute-done.4.refs_2_
  14.0 0.0 collective-permute-done.5.refs_3_
  14.1 4.0 %all-gather.1 = f32[8,6,4,8,128]{4,3,2,1,0:T(8,128)S(1)} all-gather(f32[4,6,4,8,128]{4,3,2,1,0:T(8,128)S(1)} %pad_maximum_fusion), channel_id=3, replica_groups={{0,4},{8,12},{16,20},{24,28},{1,5},{9,13},{17,21},{25,29},{2,6},{10,14}..., dimensions={0}, use_global_device_ids=true | all-gather | bytes 1179648 | tf_op jit(solution)/shard_map/all_gather | solution.py:653
  18.0 0.2 shard_map.85
  18.2 0.2 collective-permute-start.6
  18.5 4.3 %collective-permute-start.7 = (f32[54,8,128]{2,1,0:T(8,128)S(1)}, f32[54,8,128]{2,1,0:T(8,128)S(1)}, u32[]{:S(2)}, u32[]{:S(2)}) collective-permute-start(f32[54,8,128]{2,1,0:T(8,128)S(1)} %get-tuple-element.67), channel_id=1, source_target_pairs={{1,2},{2,1},{5,6},{6,5},{9,10},{10,9},{13,14},{14,13},{17,18},{18,... | collective-permute-start | bytes 663560 | tf_op jit(solution)/shard_map/ppermute | solution.py:682
  22.8 2.0 %shard_map.86.refs_6_.coeff_ref = f32[2,12,15,64,128]{4,3,2,1,0:T(8,128)S(1)} custom-call(bf16[768,128]{1,0:T(8,128)(2,1)S(1)} %get-tuple-element.59.turned_ref, bf16[15,128,256]{2,1,0:T(8,128)(2,1)S(1)} %copy-done), custom_call_target="tpu_custom_call" | custom-call | flops 3000000000 | bytes 9000000 | tf_op jit(solution)/shard_map/pallas_call | solution.py:720
  24.8 0.0 collective-permute-done.refs_1_
  24.8 0.0 collective-permute-done.1.refs_2_
  24.8 0.0 collective-permute-done.2.refs_3_
  24.8 4.3 %shard_map.87 = (f32[2,6,4,8,128]{4,3,2,1,0:T(8,128)S(1)}, f32[2,6,4,8,128]{4,3,2,1,0:T(8,128)S(1)}, f32[2,6,4,8,128]{4,3,2,1,0:T(8,128)S(1)}, f32[2,6,4,8,128]{4,3,2,1,0:T(8,128)S(1)}, f32[12,4,32,128]{3,2,1,0:T(8,128)S(1)}) custom-call(f32[4,6,4,8,128]{4,3,2,1,0:T(8,128)S(1)} %get-tuple-element.46.refs_0_, ...), custom_call_target="tpu_custom_call" | custom-call | flops 6000000000 | bytes 18000000 | tf_op jit(solution)/shard_map/pallas_call | solution.py:722
  29.1 0.0 collective-permute-done.6.even_ref
  29.1 1.2 %collective-permute-start.11 = (f32[2,6,4,8,128]{4,3,2,1,0:T(8,128)S(1)}, f32[2,6,4,8,128]{4,3,2,1,0:T(8,128)S(1)}, u32[]{:S(2)}, u32[]{:S(2)}) collective-permute-start(f32[2,6,4,8,128]{4,3,2,1,0:T(8,128)S(1)} %get-tuple-element.73), channel_id=1, source_target_pairs={{0,8},{4,12},{8,0},{12,4},{16,24},{20,28},{24,16},{28,20},{1,9},{5... | collective-permute-start | bytes 589832 | tf_op jit(solution)/shard_map/ppermute | solution.py:640
  30.4 0.5 collective-permute-start.12
  30.9 1.0 %collective-permute-start.13 = (f32[2,6,4,8,128]{4,3,2,1,0:T(8,128)S(1)}, f32[2,6,4,8,128]{4,3,2,1,0:T(8,128)S(1)}, u32[]{:S(2)}, u32[]{:S(2)}) collective-permute-start(f32[2,6,4,8,128]{4,3,2,1,0:T(8,128)S(1)} %get-tuple-element.75), channel_id=1, source_target_pairs={{0,24},{4,28},{8,16},{12,20},{16,8},{20,12},{24,0},{28,4},{1,25},{... | collective-permute-start | bytes 589832 | tf_op jit(solution)/shard_map/ppermute | solution.py:640
  31.8 0.0 collective-permute-done.7.odd_ref
  31.8 4.4 %shard_map.88 = (f32[2,6,4,8,128]{4,3,2,1,0:T(8,128)S(1)}, f32[2,6,4,8,128]{4,3,2,1,0:T(8,128)S(1)}, f32[2,6,4,8,128]{4,3,2,1,0:T(8,128)S(1)}, f32[2,6,4,8,128]{4,3,2,1,0:T(8,128)S(1)}) custom-call(f32[12,4,32,128]{3,2,1,0:T(8,128)S(1)} %get-tuple-element.60.near_ref, f32[12,4,32,128]{3,2,1,0:T(8,128)S(1)} %get-tuple-element.57.refs_5_.field_ref, ...), custom_call_target="tpu_custom_call" | custom-call | flops 6000000000 | bytes 18000000 | tf_op jit(solution)/shard_map/pallas_call | solution.py:727
  36.3 1.2 %collective-permute-start.8 = (f32[2,6,4,8,128]{4,3,2,1,0:T(8,128)S(1)}, f32[2,6,4,8,128]{4,3,2,1,0:T(8,128)S(1)}, u32[]{:S(2)}, u32[]{:S(2)}) collective-permute-start(f32[2,6,4,8,128]{4,3,2,1,0:T(8,128)S(1)} %get-tuple-element.69), channel_id=1, source_target_pairs={{0,8},{4,12},{8,0},{12,4},{16,24},{20,28},{24,16},{28,20},{1,9},{5... | collective-permute-start | bytes 589832 | tf_op jit(solution)/shard_map/ppermute | solution.py:640
  37.5 0.5 collective-permute-start.9
  38.0 0.0 collective-permute-done.11.refs_1_
  38.0 1.0 %collective-permute-start.10 = (f32[2,6,4,8,128]{4,3,2,1,0:T(8,128)S(1)}, f32[2,6,4,8,128]{4,3,2,1,0:T(8,128)S(1)}, u32[]{:S(2)}, u32[]{:S(2)}) collective-permute-start(f32[2,6,4,8,128]{4,3,2,1,0:T(8,128)S(1)} %get-tuple-element.71), channel_id=1, source_target_pairs={{0,24},{4,28},{8,16},{12,20},{16,8},{20,12},{24,0},{28,4},{1,25},{... | collective-permute-start | bytes 589832 | tf_op jit(solution)/shard_map/ppermute | solution.py:640
  39.0 0.0 collective-permute-done.12.refs_2_
  39.0 0.5 collective-permute-done.13.refs_3_
  39.5 5.1 %all-gather.2 = f32[8,6,4,8,128]{4,3,2,1,0:T(8,128)S(1)} all-gather(f32[4,6,4,8,128]{4,3,2,1,0:T(8,128)S(1)} %pad_maximum_fusion.1), channel_id=4, replica_groups={{0,4},{8,12},{16,20},{24,28},{1,5},{9,13},{17,21},{25,29},{2,6},{10,14}..., dimensions={0}, use_global_device_ids=true | all-gather | bytes 1179648 | tf_op jit(solution)/shard_map/all_gather | solution.py:653
  44.6 1.5 %shard_map.89.refs_5_ = f32[12,64,512]{2,1,0:T(8,128)} custom-call(f32[2,6,4,8,128]{4,3,2,1,0:T(8,128)S(1)} %get-tuple-element.76.refs_0_, f32[2,6,4,8,128]{4,3,2,1,0:T(8,128)S(1)} %collective-permute-done.11.refs_1_, f32[2,6,4,8,128]{4,3,2,1,0:T(8,128)S(1)} %collective-permute-done.12.refs_2_, f32[2,6,4,8,128]{4,3,2,1,0:T(8,128)S(1)} %collective-permute-done.13.refs_3_, ...), custom_call_target="tpu_custom_call" | custom-call | flops 2000000000 | bytes 6000000 | tf_op jit(solution)/shard_map/pallas_call | solution.py:735
  46.2 0.0 collective-permute-done.8.refs_1_
  46.2 1.9 %collective-permute-done.10.refs_3_ = f32[2,6,4,8,128]{4,3,2,1,0:T(8,128)S(1)} collective-permute-done((f32[2,6,4,8,128]{4,3,2,1,0:T(8,128)S(1)}, f32[2,6,4,8,128]{4,3,2,1,0:T(8,128)S(1)}, u32[]{:S(2)}, u32[]{:S(2)}) %collective-permute-start.10) | collective-permute-done | bytes 196640 | tf_op jit(solution)/shard_map/ppermute | solution.py:640
  48.2 2.3 %collective-permute-start.14 = (f32[4,6,4,8,128]{4,3,2,1,0:T(8,128)S(1)}, f32[4,6,4,8,128]{4,3,2,1,0:T(8,128)S(1)}, u32[]{:S(2)}, u32[]{:S(2)}) collective-permute-start(f32[4,6,4,8,128]{4,3,2,1,0:T(8,128)S(1)} %pad_maximum_fusion.2), channel_id=1, source_target_pairs={{0,4},{4,0},{8,12},{12,8},{16,20},{20,16},{24,28},{28,24},{1,5},{5... | collective-permute-start | bytes 1179656 | tf_op jit(solution)/shard_map/ppermute | solution.py:744
  50.5 1.3 %collective-permute-done.14.refs_4_ = f32[4,6,4,8,128]{4,3,2,1,0:T(8,128)S(1)} collective-permute-done((f32[4,6,4,8,128]{4,3,2,1,0:T(8,128)S(1)}, f32[4,6,4,8,128]{4,3,2,1,0:T(8,128)S(1)}, u32[]{:S(2)}, u32[]{:S(2)}) %collective-permute-start.14) | collective-permute-done | bytes 393248 | tf_op jit(solution)/shard_map/ppermute | solution.py:744
  51.8 1.5 %shard_map.90 = f32[12,64,512]{2,1,0:T(8,128)} custom-call(f32[2,6,4,8,128]{4,3,2,1,0:T(8,128)S(1)} %get-tuple-element.80.refs_0_, f32[2,6,4,8,128]{4,3,2,1,0:T(8,128)S(1)} %collective-permute-done.8.refs_1_, f32[2,6,4,8,128]{4,3,2,1,0:T(8,128)S(1)} %collective-permute-done.9.refs_2_, ...), custom_call_target="tpu_custom_call", output_to_operand_aliasing={{}: (5, {})} | custom-call | flops 2000000000 | bytes 6000000 | tf_op jit(solution)/shard_map/pallas_call | solution.py:745
  (35 shorter events, 0.3 us)
Async XLA Ops:
  0.0 1.4 %copy-start.1 = (f32[12,64,512]{2,1,0:T(8,128)S(1)}, f32[12,64,512]{2,1,0:T(8,128)}, u32[]{:S(2)}) copy-start(f32[12,64,512]{2,1,0:T(8,128)} %field_ref.1) | copy-start | bytes 4718596
  2.2 11.5 %collective-permute-start.3 = (f32[2,6,4,8,128]{4,3,2,1,0:T(8,128)S(1)}, f32[2,6,4,8,128]{4,3,2,1,0:T(8,128)S(1)}, u32[]{:S(2)}, u32[]{:S(2)}) collective-permute-start(f32[2,6,4,8,128]{4,3,2,1,0:T(8,128)S(1)} %get-tuple-element.49), channel_id=1, source_target_pairs={{0,8},{4,12},{8,0},{12,4},{16,24},{20,28},{24,16},{28,20},{1,9},{5... | collective-permute-start | bytes 589832 | tf_op jit(solution)/shard_map/ppermute | solution.py:640
  3.5 10.5 %collective-permute-start.4 = (f32[2,6,4,8,128]{4,3,2,1,0:T(8,128)S(1)}, f32[2,6,4,8,128]{4,3,2,1,0:T(8,128)S(1)}, u32[]{:S(2)}, u32[]{:S(2)}) collective-permute-start(f32[2,6,4,8,128]{4,3,2,1,0:T(8,128)S(1)} %get-tuple-element.50), channel_id=1, source_target_pairs={{0,16},{4,20},{8,24},{12,28},{16,0},{20,4},{24,8},{28,12},{1,17},{... | collective-permute-start | bytes 589832 | tf_op jit(solution)/shard_map/ppermute | solution.py:640
  4.7 9.2 %collective-permute-start.5 = (f32[2,6,4,8,128]{4,3,2,1,0:T(8,128)S(1)}, f32[2,6,4,8,128]{4,3,2,1,0:T(8,128)S(1)}, u32[]{:S(2)}, u32[]{:S(2)}) collective-permute-start(f32[2,6,4,8,128]{4,3,2,1,0:T(8,128)S(1)} %get-tuple-element.51), channel_id=1, source_target_pairs={{0,24},{4,28},{8,16},{12,20},{16,8},{20,12},{24,0},{28,4},{1,25},{... | collective-permute-start | bytes 589832 | tf_op jit(solution)/shard_map/ppermute | solution.py:640
  5.7 6.4 %copy-start.3 = (s32[2,12,64]{2,0,1:T(2,128)S(1)}, s32[2,12,64]{2,0,1:T(2,128)}, u32[]{:S(2)}) copy-start(s32[2,12,64]{2,0,1:T(2,128)} %param.9) | copy-start | bytes 18436
  5.7 6.4 %copy-start.4 = (f32[2,12,64]{2,0,1:T(2,128)S(1)}, f32[2,12,64]{2,0,1:T(2,128)}, u32[]{:S(2)}) copy-start(f32[2,12,64]{2,0,1:T(2,128)} %param.10) | copy-start | bytes 18436
  5.7 6.4 %copy-start.5 = (s32[2,12,64]{2,0,1:T(2,128)S(1)}, s32[2,12,64]{2,0,1:T(2,128)}, u32[]{:S(2)}) copy-start(s32[2,12,64]{2,0,1:T(2,128)} %param.11) | copy-start | bytes 18436
  5.7 6.4 %copy-start.6 = (f32[2,12,64]{2,0,1:T(2,128)S(1)}, f32[2,12,64]{2,0,1:T(2,128)}, u32[]{:S(2)}) copy-start(f32[2,12,64]{2,0,1:T(2,128)} %param.12) | copy-start | bytes 18436
  5.7 6.4 %copy-start.7 = (f32[2,12,64]{2,0,1:T(2,128)S(1)}, f32[2,12,64]{2,0,1:T(2,128)}, u32[]{:S(2)}) copy-start(f32[2,12,64]{2,0,1:T(2,128)} %param.13) | copy-start | bytes 18436
  5.8 6.4 %copy-start.2 = (f32[12,64]{1,0:T(8,128)S(1)}, f32[12,64]{1,0:T(8,128)}, u32[]{:S(2)}) copy-start(f32[12,64]{1,0:T(8,128)} %diffusivity_ref.1) | copy-start | bytes 9220
  9.5 15.3 %collective-permute-start = (f32[2,6,4,8,128]{4,3,2,1,0:T(8,128)S(1)}, f32[2,6,4,8,128]{4,3,2,1,0:T(8,128)S(1)}, u32[]{:S(2)}, u32[]{:S(2)}) collective-permute-start(f32[2,6,4,8,128]{4,3,2,1,0:T(8,128)S(1)} %pad_maximum_fusion.3), channel_id=1, source_target_pairs={{0,8},{4,12},{8,0},{12,4},{16,24},{20,28},{24,16},{28,20},{1,9},{5... | collective-permute-start | bytes 589832 | tf_op jit(solution)/shard_map/ppermute | solution.py:640
  10.8 14.0 %collective-permute-start.1 = (f32[2,6,4,8,128]{4,3,2,1,0:T(8,128)S(1)}, f32[2,6,4,8,128]{4,3,2,1,0:T(8,128)S(1)}, u32[]{:S(2)}, u32[]{:S(2)}) collective-permute-start(f32[2,6,4,8,128]{4,3,2,1,0:T(8,128)S(1)} %pad_maximum_fusion.4), channel_id=1, source_target_pairs={{0,16},{4,20},{8,24},{12,28},{16,0},{20,4},{24,8},{28,12},{1,17},{... | collective-permute-start | bytes 589832 | tf_op jit(solution)/shard_map/ppermute | solution.py:640
  13.7 11.1 %collective-permute-start.2 = (f32[2,6,4,8,128]{4,3,2,1,0:T(8,128)S(1)}, f32[2,6,4,8,128]{4,3,2,1,0:T(8,128)S(1)}, u32[]{:S(2)}, u32[]{:S(2)}) collective-permute-start(f32[2,6,4,8,128]{4,3,2,1,0:T(8,128)S(1)} %pad_maximum_fusion.5), channel_id=1, source_target_pairs={{0,24},{4,28},{8,16},{12,20},{16,8},{20,12},{24,0},{28,4},{1,25},{... | collective-permute-start | bytes 589832 | tf_op jit(solution)/shard_map/ppermute | solution.py:640
  18.0 4.8 %copy-start = (bf16[15,128,256]{2,1,0:T(8,128)(2,1)S(1)}, bf16[15,128,256]{2,1,0:T(8,128)(2,1)}, u32[]{:S(2)}) copy-start(bf16[15,128,256]{2,1,0:T(8,128)(2,1)} %constant.25.clone.spread_ref) | copy-start | bytes 2949124
  18.2 10.9 %collective-permute-start.6 = (f32[54,8,128]{2,1,0:T(8,128)S(1)}, f32[54,8,128]{2,1,0:T(8,128)S(1)}, u32[]{:S(2)}, u32[]{:S(2)}) collective-permute-start(f32[54,8,128]{2,1,0:T(8,128)S(1)} %get-tuple-element.65), channel_id=1, source_target_pairs={{0,1},{1,0},{2,3},{3,2},{4,5},{5,4},{6,7},{7,6},{8,9},{9,8},{10,11... | collective-permute-start | bytes 663560 | tf_op jit(solution)/shard_map/ppermute | solution.py:682
  18.5 13.4 %collective-permute-start.7 = (f32[54,8,128]{2,1,0:T(8,128)S(1)}, f32[54,8,128]{2,1,0:T(8,128)S(1)}, u32[]{:S(2)}, u32[]{:S(2)}) collective-permute-start(f32[54,8,128]{2,1,0:T(8,128)S(1)} %get-tuple-element.67), channel_id=1, source_target_pairs={{1,2},{2,1},{5,6},{6,5},{9,10},{10,9},{13,14},{14,13},{17,18},{18,... | collective-permute-start | bytes 663560 | tf_op jit(solution)/shard_map/ppermute | solution.py:682
  29.1 8.9 %collective-permute-start.11 = (f32[2,6,4,8,128]{4,3,2,1,0:T(8,128)S(1)}, f32[2,6,4,8,128]{4,3,2,1,0:T(8,128)S(1)}, u32[]{:S(2)}, u32[]{:S(2)}) collective-permute-start(f32[2,6,4,8,128]{4,3,2,1,0:T(8,128)S(1)} %get-tuple-element.73), channel_id=1, source_target_pairs={{0,8},{4,12},{8,0},{12,4},{16,24},{20,28},{24,16},{28,20},{1,9},{5... | collective-permute-start | bytes 589832 | tf_op jit(solution)/shard_map/ppermute | solution.py:640
  30.4 8.6 %collective-permute-start.12 = (f32[2,6,4,8,128]{4,3,2,1,0:T(8,128)S(1)}, f32[2,6,4,8,128]{4,3,2,1,0:T(8,128)S(1)}, u32[]{:S(2)}, u32[]{:S(2)}) collective-permute-start(f32[2,6,4,8,128]{4,3,2,1,0:T(8,128)S(1)} %get-tuple-element.74), channel_id=1, source_target_pairs={{0,16},{4,20},{8,24},{12,28},{16,0},{20,4},{24,8},{28,12},{1,17},{... | collective-permute-start | bytes 589832 | tf_op jit(solution)/shard_map/ppermute | solution.py:640
  30.9 8.6 %collective-permute-start.13 = (f32[2,6,4,8,128]{4,3,2,1,0:T(8,128)S(1)}, f32[2,6,4,8,128]{4,3,2,1,0:T(8,128)S(1)}, u32[]{:S(2)}, u32[]{:S(2)}) collective-permute-start(f32[2,6,4,8,128]{4,3,2,1,0:T(8,128)S(1)} %get-tuple-element.75), channel_id=1, source_target_pairs={{0,24},{4,28},{8,16},{12,20},{16,8},{20,12},{24,0},{28,4},{1,25},{... | collective-permute-start | bytes 589832 | tf_op jit(solution)/shard_map/ppermute | solution.py:640
  36.3 9.9 %collective-permute-start.8 = (f32[2,6,4,8,128]{4,3,2,1,0:T(8,128)S(1)}, f32[2,6,4,8,128]{4,3,2,1,0:T(8,128)S(1)}, u32[]{:S(2)}, u32[]{:S(2)}) collective-permute-start(f32[2,6,4,8,128]{4,3,2,1,0:T(8,128)S(1)} %get-tuple-element.69), channel_id=1, source_target_pairs={{0,8},{4,12},{8,0},{12,4},{16,24},{20,28},{24,16},{28,20},{1,9},{5... | collective-permute-start | bytes 589832 | tf_op jit(solution)/shard_map/ppermute | solution.py:640
  37.5 8.7 %collective-permute-start.9 = (f32[2,6,4,8,128]{4,3,2,1,0:T(8,128)S(1)}, f32[2,6,4,8,128]{4,3,2,1,0:T(8,128)S(1)}, u32[]{:S(2)}, u32[]{:S(2)}) collective-permute-start(f32[2,6,4,8,128]{4,3,2,1,0:T(8,128)S(1)} %get-tuple-element.70), channel_id=1, source_target_pairs={{0,16},{4,20},{8,24},{12,28},{16,0},{20,4},{24,8},{28,12},{1,17},{... | collective-permute-start | bytes 589832 | tf_op jit(solution)/shard_map/ppermute | solution.py:640
  38.0 10.1 %collective-permute-start.10 = (f32[2,6,4,8,128]{4,3,2,1,0:T(8,128)S(1)}, f32[2,6,4,8,128]{4,3,2,1,0:T(8,128)S(1)}, u32[]{:S(2)}, u32[]{:S(2)}) collective-permute-start(f32[2,6,4,8,128]{4,3,2,1,0:T(8,128)S(1)} %get-tuple-element.71), channel_id=1, source_target_pairs={{0,24},{4,28},{8,16},{12,20},{16,8},{20,12},{24,0},{28,4},{1,25},{... | collective-permute-start | bytes 589832 | tf_op jit(solution)/shard_map/ppermute | solution.py:640
  48.2 3.6 %collective-permute-start.14 = (f32[4,6,4,8,128]{4,3,2,1,0:T(8,128)S(1)}, f32[4,6,4,8,128]{4,3,2,1,0:T(8,128)S(1)}, u32[]{:S(2)}, u32[]{:S(2)}) collective-permute-start(f32[4,6,4,8,128]{4,3,2,1,0:T(8,128)S(1)} %pad_maximum_fusion.2), channel_id=1, source_target_pairs={{0,4},{4,0},{8,12},{12,8},{16,20},{20,16},{24,28},{28,24},{1,5},{5... | collective-permute-start | bytes 1179656 | tf_op jit(solution)/shard_map/ppermute | solution.py:744

commit v8 on v7

--- a/solution.py
+++ b/solution.py
@@ -245,7 +245,7 @@
                 kept[k] = field_ref[k, TILE * INNER[0] : TILE * INNER[-1] + TILE, :]
         return carry
 
-    lax.fori_loop(0, levels // 2, unit, 0, unroll=2)
+    lax.fori_loop(0, levels // 2, unit, 0, unroll=True)
 
 
 def unpack_kernel(tiles, count, *refs):

time: 53.6 us -> 53.4 us (level)
  no operation moved by 1% of the time
where the time goes in v8:
time: 53.4 us; the launch traced here: 53.2 us
  starting transfers between devices  17.7 us (33%)
  Pallas kernels  16.6 us (31%)
  blocking collectives  12.9 us (24%)
  waiting for transfers between devices  3.81 us (7%)
  local copies, waits for them, and re-layouts  1.61 us (3%)
    all_gather x3, blocking collectives, core_blocks(): return lax.all_gather(away, MESH_LON, axis_index_groups=groups)  12.9 us
    ppermute x12, starting transfers between devices, between_chips(): lax.ppermute(pairs[chip], MESH_LON, [(i, i ^ 2 * chip) for i in range(pee...  11 us
    ppermute x2, starting transfers between devices, exchange_edges(): return (lax.ppermute(even, 'lat', near), lax.ppermute(odd, 'lat', far))  4.55 us
    pallas_call x1, Pallas kernels, by_tracer(): call(last_kernel, 6, in_pairs, [(2,) + work, moved, (levels, COEFFS, rows...  4.41 us
    pallas_call x1, Pallas kernels, by_tracer(): call(inner_kernel, 6, in_pairs + [half], [(3,) + work, moved])  4.3 us
    ppermute x12, waiting for transfers between devices, between_chips(): lax.ppermute(pairs[chip], MESH_LON, [(i, i ^ 2 * chip) for i in range(pee...  2.46 us
    ppermute x1, starting transfers between devices, by_tracer(): lax.ppermute(away, MESH_LON, [(i, i ^ 1) for i in range(lax.axis_size(MES...  2.2 us
    pallas_call x1, Pallas kernels, by_tracer(): call(spread_kernel, 3, [(steps, levels, COEFFS, rows, LANES)])  1.97 us
  transfers between devices with their start and end apart: 15, of which 3 were waited for; matrix products, arithmetic and copies ran while one was open for 0% of the time, Pallas kernels for 27%

profile of v8, /device:TPU:9, one launch (start us, length us, event | category | flops | bytes accessed | tf_op | source)
XLA Modules:
  0.0 53.2 jit_solution(14026062344279073352)
XLA Ops:
  0.0 1.4 %copy-done.1 = f32[12,64,512]{2,1,0:T(8,128)S(1)} copy-done((f32[12,64,512]{2,1,0:T(8,128)S(1)}, f32[12,64,512]{2,1,0:T(8,128)}, u32[]{:S(2)}) %copy-start.1) | copy-done | bytes 1572888
  1.4 0.6 %shard_map.82 = (f32[2,6,4,8,128]{4,3,2,1,0:T(8,128)S(1)}, f32[2,6,4,8,128]{4,3,2,1,0:T(8,128)S(1)}, f32[2,6,4,8,128]{4,3,2,1,0:T(8,128)S(1)}, f32[2,6,4,8,128]{4,3,2,1,0:T(8,128)S(1)}, f32[12,32,512]{2,1,0:T(8,128)S(1)}) custom-call(f32[12,64,512]{2,1,0:T(8,128)S(1)} %copy-done.1), custom_call_target="tpu_custom_call" | custom-call | flops 2000000000 | bytes 6000000 | tf_op jit(solution)/shard_map/pallas_call | solution.py:699
  2.0 1.3 %collective-permute-start.3 = (f32[2,6,4,8,128]{4,3,2,1,0:T(8,128)S(1)}, f32[2,6,4,8,128]{4,3,2,1,0:T(8,128)S(1)}, u32[]{:S(2)}, u32[]{:S(2)}) collective-permute-start(f32[2,6,4,8,128]{4,3,2,1,0:T(8,128)S(1)} %get-tuple-element.49), channel_id=1, source_target_pairs={{0,8},{4,12},{8,0},{12,4},{16,24},{20,28},{24,16},{28,20},{1,9},{5... | collective-permute-start | bytes 589832 | tf_op jit(solution)/shard_map/ppermute | solution.py:640
  3.3 1.2 %collective-permute-start.4 = (f32[2,6,4,8,128]{4,3,2,1,0:T(8,128)S(1)}, f32[2,6,4,8,128]{4,3,2,1,0:T(8,128)S(1)}, u32[]{:S(2)}, u32[]{:S(2)}) collective-permute-start(f32[2,6,4,8,128]{4,3,2,1,0:T(8,128)S(1)} %get-tuple-element.50), channel_id=1, source_target_pairs={{0,16},{4,20},{8,24},{12,28},{16,0},{20,4},{24,8},{28,12},{1,17},{... | collective-permute-start | bytes 589832 | tf_op jit(solution)/shard_map/ppermute | solution.py:640
  4.5 0.2 collective-permute-start.5
  4.7 0.6 %shard_map.83 = (f32[4,6,4,8,128]{4,3,2,1,0:T(8,128)S(1)}, f32[4,6,4,8,128]{4,3,2,1,0:T(8,128)S(1)}) custom-call(f32[12,32,512]{2,1,0:T(8,128)S(1)} %get-tuple-element.45.field_ref), custom_call_target="tpu_custom_call" | custom-call | flops 2000000000 | bytes 6000000 | tf_op jit(solution)/shard_map/pallas_call | solution.py:702
  5.4 0.0 copy-start.3
  5.4 0.0 copy-start.4
  5.4 0.0 copy-start.5
  5.4 0.0 copy-start.6
  5.4 0.0 copy-start.7
  5.4 0.0 copy-start.2
  5.5 3.6 %all-gather = f32[8,6,4,8,128]{4,3,2,1,0:T(8,128)S(1)} all-gather(f32[4,6,4,8,128]{4,3,2,1,0:T(8,128)S(1)} %get-tuple-element.47), channel_id=2, replica_groups={{0,4},{8,12},{16,20},{24,28},{1,5},{9,13},{17,21},{25,29},{2,6},{10,14}..., dimensions={0}, use_global_device_ids=true | all-gather | bytes 1179648 | tf_op jit(solution)/shard_map/all_gather | solution.py:653
  9.2 1.3 %collective-permute-start = (f32[2,6,4,8,128]{4,3,2,1,0:T(8,128)S(1)}, f32[2,6,4,8,128]{4,3,2,1,0:T(8,128)S(1)}, u32[]{:S(2)}, u32[]{:S(2)}) collective-permute-start(f32[2,6,4,8,128]{4,3,2,1,0:T(8,128)S(1)} %pad_maximum_fusion.3), channel_id=1, source_target_pairs={{0,8},{4,12},{8,0},{12,4},{16,24},{20,28},{24,16},{28,20},{1,9},{5... | collective-permute-start | bytes 589832 | tf_op jit(solution)/shard_map/ppermute | solution.py:640
  10.4 1.3 %collective-permute-start.1 = (f32[2,6,4,8,128]{4,3,2,1,0:T(8,128)S(1)}, f32[2,6,4,8,128]{4,3,2,1,0:T(8,128)S(1)}, u32[]{:S(2)}, u32[]{:S(2)}) collective-permute-start(f32[2,6,4,8,128]{4,3,2,1,0:T(8,128)S(1)} %pad_maximum_fusion.4), channel_id=1, source_target_pairs={{0,16},{4,20},{8,24},{12,28},{16,0},{20,4},{24,8},{28,12},{1,17},{... | collective-permute-start | bytes 589832 | tf_op jit(solution)/shard_map/ppermute | solution.py:640
  11.9 1.5 %shard_map.84 = (bf16[768,128]{1,0:T(8,128)(2,1)S(1)}, f32[2,6,8,128]{3,2,1,0:T(8,128)S(1)}) custom-call(s32[2,12,64]{2,1,0:T(8,128)S(1)} %copy.15.lon_shift_ref, f32[2,12,64]{2,1,0:T(8,128)S(1)} %copy.16.lon_frac_ref, s32[2,12,64]{2,1,0:T(8,128)S(1)} %copy.17.lat_shift_ref, f32[2,12,64]{2,1,0:T(8,128)S(1)} %copy.18.lat_frac_ref, ...), custom_call_target="tpu_custom_call" | custom-call | flops 2000000000 | bytes 6000000 | tf_op jit(solution)/shard_map/pallas_call | solution.py:703
  13.3 0.0 collective-permute-done.3.refs_1_
  13.4 0.3 collective-permute-start.2
  13.6 0.0 collective-permute-done.4.refs_2_
  13.6 0.0 collective-permute-done.5.refs_3_
  13.7 4.1 %all-gather.1 = f32[8,6,4,8,128]{4,3,2,1,0:T(8,128)S(1)} all-gather(f32[4,6,4,8,128]{4,3,2,1,0:T(8,128)S(1)} %pad_maximum_fusion), channel_id=3, replica_groups={{0,4},{8,12},{16,20},{24,28},{1,5},{9,13},{17,21},{25,29},{2,6},{10,14}..., dimensions={0}, use_global_device_ids=true | all-gather | bytes 1179648 | tf_op jit(solution)/shard_map/all_gather | solution.py:653
  17.9 0.2 shard_map.85
  18.1 0.2 collective-permute-start.6
  18.3 4.3 %collective-permute-start.7 = (f32[54,8,128]{2,1,0:T(8,128)S(1)}, f32[54,8,128]{2,1,0:T(8,128)S(1)}, u32[]{:S(2)}, u32[]{:S(2)}) collective-permute-start(f32[54,8,128]{2,1,0:T(8,128)S(1)} %get-tuple-element.67), channel_id=1, source_target_pairs={{1,2},{2,1},{5,6},{6,5},{9,10},{10,9},{13,14},{14,13},{17,18},{18,... | collective-permute-start | bytes 663560 | tf_op jit(solution)/shard_map/ppermute | solution.py:682
  22.6 2.0 %shard_map.86.refs_6_.coeff_ref = f32[2,12,15,64,128]{4,3,2,1,0:T(8,128)S(1)} custom-call(bf16[768,128]{1,0:T(8,128)(2,1)S(1)} %get-tuple-element.59.turned_ref, bf16[15,128,256]{2,1,0:T(8,128)(2,1)S(1)} %copy-done), custom_call_target="tpu_custom_call" | custom-call | flops 3000000000 | bytes 9000000 | tf_op jit(solution)/shard_map/pallas_call | solution.py:720
  24.6 0.0 collective-permute-done.refs_1_
  24.6 0.0 collective-permute-done.1.refs_2_
  24.6 0.0 collective-permute-done.2.refs_3_
  24.6 4.3 %shard_map.87 = (f32[2,6,4,8,128]{4,3,2,1,0:T(8,128)S(1)}, f32[2,6,4,8,128]{4,3,2,1,0:T(8,128)S(1)}, f32[2,6,4,8,128]{4,3,2,1,0:T(8,128)S(1)}, f32[2,6,4,8,128]{4,3,2,1,0:T(8,128)S(1)}, f32[12,4,32,128]{3,2,1,0:T(8,128)S(1)}) custom-call(f32[4,6,4,8,128]{4,3,2,1,0:T(8,128)S(1)} %get-tuple-element.46.refs_0_, ...), custom_call_target="tpu_custom_call" | custom-call | flops 6000000000 | bytes 18000000 | tf_op jit(solution)/shard_map/pallas_call | solution.py:722
  28.9 0.0 collective-permute-done.6.even_ref
  29.0 1.2 %collective-permute-start.11 = (f32[2,6,4,8,128]{4,3,2,1,0:T(8,128)S(1)}, f32[2,6,4,8,128]{4,3,2,1,0:T(8,128)S(1)}, u32[]{:S(2)}, u32[]{:S(2)}) collective-permute-start(f32[2,6,4,8,128]{4,3,2,1,0:T(8,128)S(1)} %get-tuple-element.73), channel_id=1, source_target_pairs={{0,8},{4,12},{8,0},{12,4},{16,24},{20,28},{24,16},{28,20},{1,9},{5... | collective-permute-start | bytes 589832 | tf_op jit(solution)/shard_map/ppermute | solution.py:640
  30.2 0.4 collective-permute-start.12
  30.5 1.1 %collective-permute-start.13 = (f32[2,6,4,8,128]{4,3,2,1,0:T(8,128)S(1)}, f32[2,6,4,8,128]{4,3,2,1,0:T(8,128)S(1)}, u32[]{:S(2)}, u32[]{:S(2)}) collective-permute-start(f32[2,6,4,8,128]{4,3,2,1,0:T(8,128)S(1)} %get-tuple-element.75), channel_id=1, source_target_pairs={{0,24},{4,28},{8,16},{12,20},{16,8},{20,12},{24,0},{28,4},{1,25},{... | collective-permute-start | bytes 589832 | tf_op jit(solution)/shard_map/ppermute | solution.py:640
  31.7 0.0 collective-permute-done.7.odd_ref
  31.7 4.4 %shard_map.88 = (f32[2,6,4,8,128]{4,3,2,1,0:T(8,128)S(1)}, f32[2,6,4,8,128]{4,3,2,1,0:T(8,128)S(1)}, f32[2,6,4,8,128]{4,3,2,1,0:T(8,128)S(1)}, f32[2,6,4,8,128]{4,3,2,1,0:T(8,128)S(1)}) custom-call(f32[12,4,32,128]{3,2,1,0:T(8,128)S(1)} %get-tuple-element.60.near_ref, f32[12,4,32,128]{3,2,1,0:T(8,128)S(1)} %get-tuple-element.57.refs_5_.field_ref, ...), custom_call_target="tpu_custom_call" | custom-call | flops 6000000000 | bytes 18000000 | tf_op jit(solution)/shard_map/pallas_call | solution.py:727
  36.1 1.2 %collective-permute-start.8 = (f32[2,6,4,8,128]{4,3,2,1,0:T(8,128)S(1)}, f32[2,6,4,8,128]{4,3,2,1,0:T(8,128)S(1)}, u32[]{:S(2)}, u32[]{:S(2)}) collective-permute-start(f32[2,6,4,8,128]{4,3,2,1,0:T(8,128)S(1)} %get-tuple-element.69), channel_id=1, source_target_pairs={{0,8},{4,12},{8,0},{12,4},{16,24},{20,28},{24,16},{28,20},{1,9},{5... | collective-permute-start | bytes 589832 | tf_op jit(solution)/shard_map/ppermute | solution.py:640
  37.3 0.4 collective-permute-start.9
  37.7 0.0 collective-permute-done.11.refs_1_
  37.7 1.1 %collective-permute-start.10 = (f32[2,6,4,8,128]{4,3,2,1,0:T(8,128)S(1)}, f32[2,6,4,8,128]{4,3,2,1,0:T(8,128)S(1)}, u32[]{:S(2)}, u32[]{:S(2)}) collective-permute-start(f32[2,6,4,8,128]{4,3,2,1,0:T(8,128)S(1)} %get-tuple-element.71), channel_id=1, source_target_pairs={{0,24},{4,28},{8,16},{12,20},{16,8},{20,12},{24,0},{28,4},{1,25},{... | collective-permute-start | bytes 589832 | tf_op jit(solution)/shard_map/ppermute | solution.py:640
  38.8 0.0 collective-permute-done.12.refs_2_
  38.8 0.5 %collective-permute-done.13.refs_3_ = f32[2,6,4,8,128]{4,3,2,1,0:T(8,128)S(1)} collective-permute-done((f32[2,6,4,8,128]{4,3,2,1,0:T(8,128)S(1)}, f32[2,6,4,8,128]{4,3,2,1,0:T(8,128)S(1)}, u32[]{:S(2)}, u32[]{:S(2)}) %collective-permute-start.13) | collective-permute-done | bytes 196640 | tf_op jit(solution)/shard_map/ppermute | solution.py:640
  39.4 5.1 %all-gather.2 = f32[8,6,4,8,128]{4,3,2,1,0:T(8,128)S(1)} all-gather(f32[4,6,4,8,128]{4,3,2,1,0:T(8,128)S(1)} %pad_maximum_fusion.1), channel_id=4, replica_groups={{0,4},{8,12},{16,20},{24,28},{1,5},{9,13},{17,21},{25,29},{2,6},{10,14}..., dimensions={0}, use_global_device_ids=true | all-gather | bytes 1179648 | tf_op jit(solution)/shard_map/all_gather | solution.py:653
  44.5 1.5 %shard_map.89.refs_5_ = f32[12,64,512]{2,1,0:T(8,128)} custom-call(f32[2,6,4,8,128]{4,3,2,1,0:T(8,128)S(1)} %get-tuple-element.76.refs_0_, f32[2,6,4,8,128]{4,3,2,1,0:T(8,128)S(1)} %collective-permute-done.11.refs_1_, f32[2,6,4,8,128]{4,3,2,1,0:T(8,128)S(1)} %collective-permute-done.12.refs_2_, f32[2,6,4,8,128]{4,3,2,1,0:T(8,128)S(1)} %collective-permute-done.13.refs_3_, ...), custom_call_target="tpu_custom_call" | custom-call | flops 2000000000 | bytes 6000000 | tf_op jit(solution)/shard_map/pallas_call | solution.py:735
  46.1 0.0 collective-permute-done.8.refs_1_
  46.1 1.9 %collective-permute-done.10.refs_3_ = f32[2,6,4,8,128]{4,3,2,1,0:T(8,128)S(1)} collective-permute-done((f32[2,6,4,8,128]{4,3,2,1,0:T(8,128)S(1)}, f32[2,6,4,8,128]{4,3,2,1,0:T(8,128)S(1)}, u32[]{:S(2)}, u32[]{:S(2)}) %collective-permute-start.10) | collective-permute-done | bytes 196640 | tf_op jit(solution)/shard_map/ppermute | solution.py:640
  48.1 2.2 %collective-permute-start.14 = (f32[4,6,4,8,128]{4,3,2,1,0:T(8,128)S(1)}, f32[4,6,4,8,128]{4,3,2,1,0:T(8,128)S(1)}, u32[]{:S(2)}, u32[]{:S(2)}) collective-permute-start(f32[4,6,4,8,128]{4,3,2,1,0:T(8,128)S(1)} %pad_maximum_fusion.2), channel_id=1, source_target_pairs={{0,4},{4,0},{8,12},{12,8},{16,20},{20,16},{24,28},{28,24},{1,5},{5... | collective-permute-start | bytes 1179656 | tf_op jit(solution)/shard_map/ppermute | solution.py:744
  50.3 1.3 %collective-permute-done.14.refs_4_ = f32[4,6,4,8,128]{4,3,2,1,0:T(8,128)S(1)} collective-permute-done((f32[4,6,4,8,128]{4,3,2,1,0:T(8,128)S(1)}, f32[4,6,4,8,128]{4,3,2,1,0:T(8,128)S(1)}, u32[]{:S(2)}, u32[]{:S(2)}) %collective-permute-start.14) | collective-permute-done | bytes 393248 | tf_op jit(solution)/shard_map/ppermute | solution.py:744
  51.6 1.5 %shard_map.90 = f32[12,64,512]{2,1,0:T(8,128)} custom-call(f32[2,6,4,8,128]{4,3,2,1,0:T(8,128)S(1)} %get-tuple-element.80.refs_0_, f32[2,6,4,8,128]{4,3,2,1,0:T(8,128)S(1)} %collective-permute-done.8.refs_1_, f32[2,6,4,8,128]{4,3,2,1,0:T(8,128)S(1)} %collective-permute-done.9.refs_2_, ...), custom_call_target="tpu_custom_call", output_to_operand_aliasing={{}: (5, {})} | custom-call | flops 2000000000 | bytes 6000000 | tf_op jit(solution)/shard_map/pallas_call | solution.py:745
  (35 shorter events, 0.3 us)
Async XLA Ops:
  0.0 1.4 %copy-start.1 = (f32[12,64,512]{2,1,0:T(8,128)S(1)}, f32[12,64,512]{2,1,0:T(8,128)}, u32[]{:S(2)}) copy-start(f32[12,64,512]{2,1,0:T(8,128)} %field_ref.1) | copy-start | bytes 4718596
  2.0 11.3 %collective-permute-start.3 = (f32[2,6,4,8,128]{4,3,2,1,0:T(8,128)S(1)}, f32[2,6,4,8,128]{4,3,2,1,0:T(8,128)S(1)}, u32[]{:S(2)}, u32[]{:S(2)}) collective-permute-start(f32[2,6,4,8,128]{4,3,2,1,0:T(8,128)S(1)} %get-tuple-element.49), channel_id=1, source_target_pairs={{0,8},{4,12},{8,0},{12,4},{16,24},{20,28},{24,16},{28,20},{1,9},{5... | collective-permute-start | bytes 589832 | tf_op jit(solution)/shard_map/ppermute | solution.py:640
  3.3 10.3 %collective-permute-start.4 = (f32[2,6,4,8,128]{4,3,2,1,0:T(8,128)S(1)}, f32[2,6,4,8,128]{4,3,2,1,0:T(8,128)S(1)}, u32[]{:S(2)}, u32[]{:S(2)}) collective-permute-start(f32[2,6,4,8,128]{4,3,2,1,0:T(8,128)S(1)} %get-tuple-element.50), channel_id=1, source_target_pairs={{0,16},{4,20},{8,24},{12,28},{16,0},{20,4},{24,8},{28,12},{1,17},{... | collective-permute-start | bytes 589832 | tf_op jit(solution)/shard_map/ppermute | solution.py:640
  4.5 9.1 %collective-permute-start.5 = (f32[2,6,4,8,128]{4,3,2,1,0:T(8,128)S(1)}, f32[2,6,4,8,128]{4,3,2,1,0:T(8,128)S(1)}, u32[]{:S(2)}, u32[]{:S(2)}) collective-permute-start(f32[2,6,4,8,128]{4,3,2,1,0:T(8,128)S(1)} %get-tuple-element.51), channel_id=1, source_target_pairs={{0,24},{4,28},{8,16},{12,20},{16,8},{20,12},{24,0},{28,4},{1,25},{... | collective-permute-start | bytes 589832 | tf_op jit(solution)/shard_map/ppermute | solution.py:640
  5.4 6.4 %copy-start.3 = (s32[2,12,64]{2,0,1:T(2,128)S(1)}, s32[2,12,64]{2,0,1:T(2,128)}, u32[]{:S(2)}) copy-start(s32[2,12,64]{2,0,1:T(2,128)} %param.9) | copy-start | bytes 18436
  5.4 6.4 %copy-start.4 = (f32[2,12,64]{2,0,1:T(2,128)S(1)}, f32[2,12,64]{2,0,1:T(2,128)}, u32[]{:S(2)}) copy-start(f32[2,12,64]{2,0,1:T(2,128)} %param.10) | copy-start | bytes 18436
  5.4 6.4 %copy-start.5 = (s32[2,12,64]{2,0,1:T(2,128)S(1)}, s32[2,12,64]{2,0,1:T(2,128)}, u32[]{:S(2)}) copy-start(s32[2,12,64]{2,0,1:T(2,128)} %param.11) | copy-start | bytes 18436
  5.4 6.4 %copy-start.6 = (f32[2,12,64]{2,0,1:T(2,128)S(1)}, f32[2,12,64]{2,0,1:T(2,128)}, u32[]{:S(2)}) copy-start(f32[2,12,64]{2,0,1:T(2,128)} %param.12) | copy-start | bytes 18436
  5.4 6.4 %copy-start.7 = (f32[2,12,64]{2,0,1:T(2,128)S(1)}, f32[2,12,64]{2,0,1:T(2,128)}, u32[]{:S(2)}) copy-start(f32[2,12,64]{2,0,1:T(2,128)} %param.13) | copy-start | bytes 18436
  5.4 6.4 %copy-start.2 = (f32[12,64]{1,0:T(8,128)S(1)}, f32[12,64]{1,0:T(8,128)}, u32[]{:S(2)}) copy-start(f32[12,64]{1,0:T(8,128)} %diffusivity_ref.1) | copy-start | bytes 9220
  9.2 15.5 %collective-permute-start = (f32[2,6,4,8,128]{4,3,2,1,0:T(8,128)S(1)}, f32[2,6,4,8,128]{4,3,2,1,0:T(8,128)S(1)}, u32[]{:S(2)}, u32[]{:S(2)}) collective-permute-start(f32[2,6,4,8,128]{4,3,2,1,0:T(8,128)S(1)} %pad_maximum_fusion.3), channel_id=1, source_target_pairs={{0,8},{4,12},{8,0},{12,4},{16,24},{20,28},{24,16},{28,20},{1,9},{5... | collective-permute-start | bytes 589832 | tf_op jit(solution)/shard_map/ppermute | solution.py:640
  10.4 14.2 %collective-permute-start.1 = (f32[2,6,4,8,128]{4,3,2,1,0:T(8,128)S(1)}, f32[2,6,4,8,128]{4,3,2,1,0:T(8,128)S(1)}, u32[]{:S(2)}, u32[]{:S(2)}) collective-permute-start(f32[2,6,4,8,128]{4,3,2,1,0:T(8,128)S(1)} %pad_maximum_fusion.4), channel_id=1, source_target_pairs={{0,16},{4,20},{8,24},{12,28},{16,0},{20,4},{24,8},{28,12},{1,17},{... | collective-permute-start | bytes 589832 | tf_op jit(solution)/shard_map/ppermute | solution.py:640
  13.4 11.3 %collective-permute-start.2 = (f32[2,6,4,8,128]{4,3,2,1,0:T(8,128)S(1)}, f32[2,6,4,8,128]{4,3,2,1,0:T(8,128)S(1)}, u32[]{:S(2)}, u32[]{:S(2)}) collective-permute-start(f32[2,6,4,8,128]{4,3,2,1,0:T(8,128)S(1)} %pad_maximum_fusion.5), channel_id=1, source_target_pairs={{0,24},{4,28},{8,16},{12,20},{16,8},{20,12},{24,0},{28,4},{1,25},{... | collective-permute-start | bytes 589832 | tf_op jit(solution)/shard_map/ppermute | solution.py:640
  17.9 4.8 %copy-start = (bf16[15,128,256]{2,1,0:T(8,128)(2,1)S(1)}, bf16[15,128,256]{2,1,0:T(8,128)(2,1)}, u32[]{:S(2)}) copy-start(bf16[15,128,256]{2,1,0:T(8,128)(2,1)} %constant.25.clone.spread_ref) | copy-start | bytes 2949124
  18.1 10.9 %collective-permute-start.6 = (f32[54,8,128]{2,1,0:T(8,128)S(1)}, f32[54,8,128]{2,1,0:T(8,128)S(1)}, u32[]{:S(2)}, u32[]{:S(2)}) collective-permute-start(f32[54,8,128]{2,1,0:T(8,128)S(1)} %get-tuple-element.65), channel_id=1, source_target_pairs={{0,1},{1,0},{2,3},{3,2},{4,5},{5,4},{6,7},{7,6},{8,9},{9,8},{10,11... | collective-permute-start | bytes 663560 | tf_op jit(solution)/shard_map/ppermute | solution.py:682
  18.3 13.4 %collective-permute-start.7 = (f32[54,8,128]{2,1,0:T(8,128)S(1)}, f32[54,8,128]{2,1,0:T(8,128)S(1)}, u32[]{:S(2)}, u32[]{:S(2)}) collective-permute-start(f32[54,8,128]{2,1,0:T(8,128)S(1)} %get-tuple-element.67), channel_id=1, source_target_pairs={{1,2},{2,1},{5,6},{6,5},{9,10},{10,9},{13,14},{14,13},{17,18},{18,... | collective-permute-start | bytes 663560 | tf_op jit(solution)/shard_map/ppermute | solution.py:682
  29.0 8.7 %collective-permute-start.11 = (f32[2,6,4,8,128]{4,3,2,1,0:T(8,128)S(1)}, f32[2,6,4,8,128]{4,3,2,1,0:T(8,128)S(1)}, u32[]{:S(2)}, u32[]{:S(2)}) collective-permute-start(f32[2,6,4,8,128]{4,3,2,1,0:T(8,128)S(1)} %get-tuple-element.73), channel_id=1, source_target_pairs={{0,8},{4,12},{8,0},{12,4},{16,24},{20,28},{24,16},{28,20},{1,9},{5... | collective-permute-start | bytes 589832 | tf_op jit(solution)/shard_map/ppermute | solution.py:640
  30.2 8.6 %collective-permute-start.12 = (f32[2,6,4,8,128]{4,3,2,1,0:T(8,128)S(1)}, f32[2,6,4,8,128]{4,3,2,1,0:T(8,128)S(1)}, u32[]{:S(2)}, u32[]{:S(2)}) collective-permute-start(f32[2,6,4,8,128]{4,3,2,1,0:T(8,128)S(1)} %get-tuple-element.74), channel_id=1, source_target_pairs={{0,16},{4,20},{8,24},{12,28},{16,0},{20,4},{24,8},{28,12},{1,17},{... | collective-permute-start | bytes 589832 | tf_op jit(solution)/shard_map/ppermute | solution.py:640
  30.5 8.8 %collective-permute-start.13 = (f32[2,6,4,8,128]{4,3,2,1,0:T(8,128)S(1)}, f32[2,6,4,8,128]{4,3,2,1,0:T(8,128)S(1)}, u32[]{:S(2)}, u32[]{:S(2)}) collective-permute-start(f32[2,6,4,8,128]{4,3,2,1,0:T(8,128)S(1)} %get-tuple-element.75), channel_id=1, source_target_pairs={{0,24},{4,28},{8,16},{12,20},{16,8},{20,12},{24,0},{28,4},{1,25},{... | collective-permute-start | bytes 589832 | tf_op jit(solution)/shard_map/ppermute | solution.py:640
  36.1 10.0 %collective-permute-start.8 = (f32[2,6,4,8,128]{4,3,2,1,0:T(8,128)S(1)}, f32[2,6,4,8,128]{4,3,2,1,0:T(8,128)S(1)}, u32[]{:S(2)}, u32[]{:S(2)}) collective-permute-start(f32[2,6,4,8,128]{4,3,2,1,0:T(8,128)S(1)} %get-tuple-element.69), channel_id=1, source_target_pairs={{0,8},{4,12},{8,0},{12,4},{16,24},{20,28},{24,16},{28,20},{1,9},{5... | collective-permute-start | bytes 589832 | tf_op jit(solution)/shard_map/ppermute | solution.py:640
  37.3 8.8 %collective-permute-start.9 = (f32[2,6,4,8,128]{4,3,2,1,0:T(8,128)S(1)}, f32[2,6,4,8,128]{4,3,2,1,0:T(8,128)S(1)}, u32[]{:S(2)}, u32[]{:S(2)}) collective-permute-start(f32[2,6,4,8,128]{4,3,2,1,0:T(8,128)S(1)} %get-tuple-element.70), channel_id=1, source_target_pairs={{0,16},{4,20},{8,24},{12,28},{16,0},{20,4},{24,8},{28,12},{1,17},{... | collective-permute-start | bytes 589832 | tf_op jit(solution)/shard_map/ppermute | solution.py:640
  37.7 10.3 %collective-permute-start.10 = (f32[2,6,4,8,128]{4,3,2,1,0:T(8,128)S(1)}, f32[2,6,4,8,128]{4,3,2,1,0:T(8,128)S(1)}, u32[]{:S(2)}, u32[]{:S(2)}) collective-permute-start(f32[2,6,4,8,128]{4,3,2,1,0:T(8,128)S(1)} %get-tuple-element.71), channel_id=1, source_target_pairs={{0,24},{4,28},{8,16},{12,20},{16,8},{20,12},{24,0},{28,4},{1,25},{... | collective-permute-start | bytes 589832 | tf_op jit(solution)/shard_map/ppermute | solution.py:640
  48.1 3.5 %collective-permute-start.14 = (f32[4,6,4,8,128]{4,3,2,1,0:T(8,128)S(1)}, f32[4,6,4,8,128]{4,3,2,1,0:T(8,128)S(1)}, u32[]{:S(2)}, u32[]{:S(2)}) collective-permute-start(f32[4,6,4,8,128]{4,3,2,1,0:T(8,128)S(1)} %pad_maximum_fusion.2), channel_id=1, source_target_pairs={{0,4},{4,0},{8,12},{12,8},{16,20},{20,16},{24,28},{28,24},{1,5},{5... | collective-permute-start | bytes 1179656 | tf_op jit(solution)/shard_map/ppermute | solution.py:744
